TPU v7x, 128 devices: a whole 4x4x4 slice. The times are simulated.
128 devices in a mesh: dp: 4 (over z_lo, core), fsdp: 32 (over y, x, z_hi).
Axes of the slice: x: 4, y: 4, z: 4 (z_hi: 2, z_lo: 2; z = z_hi * 2 + z_lo), core: 2. Of those that a mesh axis runs over, the one named last changes fastest.
Arguments:
- inputs: bfloat16 [32768, 1024], P(('dp', 'fsdp')), may hold values from -6 to 6
- cotangent: bfloat16 [32768, 1024], P(('dp', 'fsdp')), may hold values from -24 to 24
- lengths: int32 [128, 8], P(('dp', 'fsdp')), may hold values from 1 to 128, 256 in all within a row
- norm1_gain: bfloat16 [1024], P(('dp', 'fsdp')), may hold values from 0.25 to 1.75
- norm1_bias: bfloat16 [1024], P(('dp', 'fsdp')), may hold values from -1.75 to 1.75
- norm2_gain: bfloat16 [1024], P(('dp', 'fsdp')), may hold values from 0.25 to 1.75
- norm2_bias: bfloat16 [1024], P(('dp', 'fsdp')), may hold values from -1.75 to 1.75
- qkv_weight: bfloat16 [3145728], P(('dp', 'fsdp')), may hold values from -0.1875 to 0.1875
- qkv_bias: bfloat16 [3072], P(('dp', 'fsdp')), may hold values from -3 to 3
- dense_weight: bfloat16 [1048576], P(('dp', 'fsdp')), may hold values from -0.75 to 0.75
- dense_bias: bfloat16 [1024], P(('dp', 'fsdp')), may hold values from -3 to 3
- up_weight: bfloat16 [4194304], P(('dp', 'fsdp')), may hold values from -0.1875 to 0.1875
- up_bias: bfloat16 [4096], P(('dp', 'fsdp')), may hold values from -3 to 3
- down_weight: bfloat16 [4194304], P(('dp', 'fsdp')), may hold values from -0.09375 to 0.09375
- down_bias: bfloat16 [1024], P(('dp', 'fsdp')), may hold values from -3 to 3
Outputs:
- block_output: bfloat16 [32768, 1024], P(('dp', 'fsdp'))
- input_grad: float32 [32768, 1024], P(('dp', 'fsdp'))
- norm1_gain_grad: float32 [1024], P(('dp', 'fsdp'))
- norm1_bias_grad: float32 [1024], P(('dp', 'fsdp'))
- norm2_gain_grad: float32 [1024], P(('dp', 'fsdp'))
- norm2_bias_grad: float32 [1024], P(('dp', 'fsdp'))
- qkv_weight_grad: float32 [3145728], P(('dp', 'fsdp'))
- qkv_bias_grad: float32 [3072], P(('dp', 'fsdp'))
- dense_weight_grad: float32 [1048576], P(('dp', 'fsdp'))
- dense_bias_grad: float32 [1024], P(('dp', 'fsdp'))
- up_weight_grad: float32 [4194304], P(('dp', 'fsdp'))
- up_bias_grad: float32 [4096], P(('dp', 'fsdp'))
- down_weight_grad: float32 [4194304], P(('dp', 'fsdp'))
- down_bias_grad: float32 [1024], P(('dp', 'fsdp'))
Inputs may be any that keep to these rules, and one draw needn't show every extreme that they name: Each row's entries sum to 256; the first 7 are document lengths, the last the padding at the row's end.
All inputs are finite; a program needn't handle non-finite values.
Results may differ from a plain program's by a relative error of at most 0.017.
Values may be sent and summed in bfloat16 or wider, within the bound.
No kernel may reach another device: no remote copies, remote signals or barrier semaphores. Data moves between devices by JAX's collectives and lax.ppermute only.
A program may use at most 256 MiB of HBM per device.

v0:
```python
import jax
import jax.numpy as jnp
from jax import lax
from jax.sharding import PartitionSpec as P

D = 1024
HEADS = 16
HEAD_DIM = 64
ROT = 16
FF = 4096
ROW = 256
SEGS = 8


root_half = 0.7071067811865476
inv_root_tau = 0.3989422804014327


def documents(seg_lens):
    ends = jnp.cumsum(seg_lens)
    starts = ends - seg_lens
    places = jnp.arange(ROW, dtype=jnp.int32)
    doc_ids = jnp.sum((places[:, None] >= ends[None, :]).astype(jnp.int32), axis=1)
    matches = doc_ids[:, None] == jnp.arange(SEGS, dtype=jnp.int32)[None, :]
    firsts = jnp.sum(jnp.where(matches, starts[None, :], 0), axis=1)
    return (doc_ids, places - firsts)


def rotary(doc_pos):
    half = ROT // 2
    freqs = 10000.0 ** (-(jnp.arange(half, dtype=jnp.float32) * 2.0) / ROT)
    angle = doc_pos.astype(jnp.float32)[:, None] * freqs[None, :]
    angle = jnp.concatenate([angle, angle], axis=-1)[:, None, :]
    return (jnp.cos(angle), jnp.sin(angle))


def rope(values, cosine, sine):
    half = ROT // 2
    leading = values[..., :ROT]
    turned = jnp.concatenate([-leading[..., half:], leading[..., :half]], axis=-1)
    return jnp.concatenate([leading * cosine + turned * sine, values[..., ROT:]], axis=-1)


def rope_back(grads, cosine, sine):
    half = ROT // 2
    leading = grads[..., :ROT]
    moved = leading * sine
    turned = jnp.concatenate([moved[..., half:], -moved[..., :half]], axis=-1)
    return jnp.concatenate([leading * cosine + turned, grads[..., ROT:]], axis=-1)


def normalize(states):
    average = jnp.mean(states, axis=-1, keepdims=True)
    centred = states - average
    inv_std = lax.rsqrt(jnp.mean(centred * centred, axis=-1, keepdims=True) + 1e-05)
    return (centred * inv_std, inv_std)


def norm_back(scaled, normed, inv_std):
    first = jnp.mean(scaled, axis=-1, keepdims=True)
    second = jnp.mean(scaled * normed, axis=-1, keepdims=True)
    return inv_std * (scaled - first - normed * second)


def gelu_slope(hidden_pre):
    cumul = 0.5 * (1.0 + jax.scipy.special.erf(hidden_pre * root_half))
    density = jnp.exp(-0.5 * hidden_pre * hidden_pre) * inv_root_tau
    return cumul + hidden_pre * density


def outer_sum(left, right):
    return lax.dot_general(
        left, right, (((0,), (0,)), ((), ())), preferred_element_type=jnp.float32
    )


def times_back(left, right):
    return lax.dot_general(
        left, right, (((1,), (1,)), ((), ())), preferred_element_type=jnp.float32
    )


def collect(pieces):
    return (
        lax.all_gather(pieces[0], ("dp", "fsdp"), axis=0, tiled=True),
        lax.all_gather(pieces[1], ("dp", "fsdp"), axis=0, tiled=True),
        lax.all_gather(pieces[2], ("dp", "fsdp"), axis=0, tiled=True),
        lax.all_gather(pieces[3], ("dp", "fsdp"), axis=0, tiled=True),
        lax.all_gather(pieces[4], ("dp", "fsdp"), axis=0, tiled=True),
        lax.all_gather(pieces[5], ("dp", "fsdp"), axis=0, tiled=True),
        lax.all_gather(pieces[6], ("dp", "fsdp"), axis=0, tiled=True),
        lax.all_gather(pieces[7], ("dp", "fsdp"), axis=0, tiled=True),
        lax.all_gather(pieces[8], ("dp", "fsdp"), axis=0, tiled=True),
        lax.all_gather(pieces[9], ("dp", "fsdp"), axis=0, tiled=True),
        lax.all_gather(pieces[10], ("dp", "fsdp"), axis=0, tiled=True),
        lax.all_gather(pieces[11], ("dp", "fsdp"), axis=0, tiled=True),
    )


def spread_grads(pieces):
    return (
        lax.psum_scatter(pieces[0], ("dp", "fsdp"), scatter_dimension=0, tiled=True),
        lax.psum_scatter(pieces[1], ("dp", "fsdp"), scatter_dimension=0, tiled=True),
        lax.psum_scatter(pieces[2], ("dp", "fsdp"), scatter_dimension=0, tiled=True),
        lax.psum_scatter(pieces[3], ("dp", "fsdp"), scatter_dimension=0, tiled=True),
        lax.psum_scatter(pieces[4], ("dp", "fsdp"), scatter_dimension=0, tiled=True),
        lax.psum_scatter(pieces[5], ("dp", "fsdp"), scatter_dimension=0, tiled=True),
        lax.psum_scatter(pieces[6], ("dp", "fsdp"), scatter_dimension=0, tiled=True),
        lax.psum_scatter(pieces[7], ("dp", "fsdp"), scatter_dimension=0, tiled=True),
        lax.psum_scatter(pieces[8], ("dp", "fsdp"), scatter_dimension=0, tiled=True),
        lax.psum_scatter(pieces[9], ("dp", "fsdp"), scatter_dimension=0, tiled=True),
        lax.psum_scatter(pieces[10], ("dp", "fsdp"), scatter_dimension=0, tiled=True),
        lax.psum_scatter(pieces[11], ("dp", "fsdp"), scatter_dimension=0, tiled=True),
    )


def unpack(whole):
    return (
        whole[0].astype(jnp.float32),
        whole[1].astype(jnp.float32),
        whole[2].astype(jnp.float32),
        whole[3].astype(jnp.float32),
        whole[4].reshape(D, 3 * D),
        whole[5].astype(jnp.float32),
        whole[6].reshape(D, D),
        whole[7].astype(jnp.float32),
        whole[8].reshape(D, FF),
        whole[9].astype(jnp.float32),
        whole[10].reshape(FF, D),
        whole[11].astype(jnp.float32),
    )


def score_block(queries, keys_rot, allowed):
    scores = jnp.einsum(
        "qhd,khd->hqk", queries, keys_rot, preferred_element_type=jnp.float32
    ) * HEAD_DIM ** (-0.5)
    return jnp.where(allowed[None], scores, -1000000000.0)


def body(
    inputs,
    cotangent,
    lengths,
    norm1_gain,
    norm1_bias,
    norm2_gain,
    norm2_bias,
    qkv_weight,
    qkv_bias,
    dense_weight,
    dense_bias,
    up_weight,
    up_bias,
    down_weight,
    down_bias,
):
    shards = (
        norm1_gain,
        norm1_bias,
        norm2_gain,
        norm2_bias,
        qkv_weight,
        qkv_bias,
        dense_weight,
        dense_bias,
        up_weight,
        up_bias,
        down_weight,
        down_bias,
    )
    params = unpack(collect(shards))
    (
        gain_one,
        bias_one,
        gain_two,
        bias_two,
        w_qkv,
        b_qkv,
        w_dense,
        b_dense,
        w_up,
        b_up,
        w_down,
        b_down,
    ) = params
    count = inputs.shape[0]
    states = inputs.astype(jnp.float32)
    doc_ids, doc_pos = documents(lengths[0])
    keep = (doc_ids < SEGS - 1).astype(jnp.float32)
    places = jnp.arange(count, dtype=jnp.int32)
    allowed = (doc_ids[:, None] == doc_ids[None, :]) & (places[None, :] <= places[:, None])
    normed, inv_std = normalize(states)
    attn_in = (normed * gain_one + bias_one).astype(jnp.bfloat16)
    mlp_in = (normed * gain_two + bias_two).astype(jnp.bfloat16)
    projected = jnp.dot(attn_in, w_qkv, preferred_element_type=jnp.float32) + b_qkv
    triple = projected.reshape(count, 3, HEADS, HEAD_DIM)
    cosine, sine = rotary(doc_pos)
    queries = rope(triple[:, 0], cosine, sine).astype(jnp.bfloat16)
    keys_rot = rope(triple[:, 1], cosine, sine).astype(jnp.bfloat16)
    values = triple[:, 2].astype(jnp.bfloat16)
    scores = score_block(queries, keys_rot, allowed)
    highest = jnp.max(scores, axis=-1, keepdims=True)
    shifted = jnp.exp(scores - highest)
    totals = jnp.sum(shifted, axis=-1, keepdims=True)
    log_total = highest + jnp.log(totals)
    probs = (shifted / totals).astype(jnp.bfloat16)
    context = (
        jnp.einsum("hqk,khd->qhd", probs, values, preferred_element_type=jnp.float32)
        .astype(jnp.bfloat16)
        .reshape(count, D)
    )
    attn_out = jnp.dot(context, w_dense, preferred_element_type=jnp.float32) + b_dense
    hidden_pre = jnp.dot(mlp_in, w_up, preferred_element_type=jnp.float32) + b_up
    hidden = jax.nn.gelu(hidden_pre, approximate=False).astype(jnp.bfloat16)
    mlp_out = jnp.dot(hidden, w_down, preferred_element_type=jnp.float32) + b_down
    block_output = (states + attn_out + mlp_out).astype(jnp.bfloat16)
    again = unpack(collect(shards))
    upstream = cotangent.astype(jnp.float32) * keep[:, None]
    up_low = upstream.astype(jnp.bfloat16)
    grad_down = outer_sum(hidden, up_low)
    grad_out_bias = jnp.sum(upstream, axis=0)
    grad_hidden = times_back(up_low, again[10])
    grad_pre = (grad_hidden * gelu_slope(hidden_pre)).astype(jnp.bfloat16)
    grad_up = outer_sum(mlp_in, grad_pre)
    grad_up_bias = jnp.sum(grad_pre.astype(jnp.float32), axis=0)
    grad_mlp_in = times_back(grad_pre, again[8])
    grad_dense = outer_sum(context, up_low)
    grad_context = times_back(up_low, again[6]).astype(jnp.bfloat16).reshape(count, HEADS, HEAD_DIM)
    scores = score_block(queries, keys_rot, allowed)
    probs_full = jnp.exp(scores - log_total)
    grad_values = jnp.einsum(
        "hqk,qhd->khd",
        probs_full.astype(jnp.bfloat16),
        grad_context,
        preferred_element_type=jnp.float32,
    )
    grad_probs = jnp.einsum(
        "qhd,khd->hqk", grad_context, values, preferred_element_type=jnp.float32
    )
    inner_term = jnp.sum(grad_probs * probs_full, axis=-1, keepdims=True)
    grad_scores = (probs_full * (grad_probs - inner_term)).astype(jnp.bfloat16)
    grad_queries = jnp.einsum(
        "hqk,khd->qhd", grad_scores, keys_rot, preferred_element_type=jnp.float32
    ) * HEAD_DIM ** (-0.5)
    grad_keys = jnp.einsum(
        "hqk,qhd->khd", grad_scores, queries, preferred_element_type=jnp.float32
    ) * HEAD_DIM ** (-0.5)
    grad_triple = jnp.stack(
        [rope_back(grad_queries, cosine, sine), rope_back(grad_keys, cosine, sine), grad_values],
        axis=1,
    )
    grad_triple = grad_triple.reshape(count, 3 * D).astype(jnp.bfloat16)
    grad_qkv = outer_sum(attn_in, grad_triple)
    grad_qkv_bias = jnp.sum(grad_triple.astype(jnp.float32), axis=0)
    grad_attn_in = times_back(grad_triple, again[4])
    grad_gain_one = jnp.sum(grad_attn_in * normed, axis=0)
    grad_bias_one = jnp.sum(grad_attn_in, axis=0)
    grad_gain_two = jnp.sum(grad_mlp_in * normed, axis=0)
    grad_bias_two = jnp.sum(grad_mlp_in, axis=0)
    scaled = grad_attn_in * again[0] + grad_mlp_in * again[2]
    input_grad = upstream + norm_back(scaled, normed, inv_std)
    owned = spread_grads(
        (
            grad_gain_one,
            grad_bias_one,
            grad_gain_two,
            grad_bias_two,
            grad_qkv.reshape(-1),
            grad_qkv_bias,
            grad_dense.reshape(-1),
            grad_out_bias,
            grad_up.reshape(-1),
            grad_up_bias,
            grad_down.reshape(-1),
            grad_out_bias,
        )
    )
    return (
        block_output,
        input_grad,
        owned[0],
        owned[1],
        owned[2],
        owned[3],
        owned[4],
        owned[5],
        owned[6],
        owned[7],
        owned[8],
        owned[9],
        owned[10],
        owned[11],
    )


def solution(mesh):
    return jax.shard_map(
        body,
        mesh=mesh,
        in_specs=(
            P(("dp", "fsdp"), None),
            P(("dp", "fsdp"), None),
            P(("dp", "fsdp"), None),
            P(("dp", "fsdp")),
            P(("dp", "fsdp")),
            P(("dp", "fsdp")),
            P(("dp", "fsdp")),
            P(("dp", "fsdp")),
            P(("dp", "fsdp")),
            P(("dp", "fsdp")),
            P(("dp", "fsdp")),
            P(("dp", "fsdp")),
            P(("dp", "fsdp")),
            P(("dp", "fsdp")),
            P(("dp", "fsdp")),
        ),
        out_specs=(
            P(("dp", "fsdp"), None),
            P(("dp", "fsdp"), None),
            P(("dp", "fsdp")),
            P(("dp", "fsdp")),
            P(("dp", "fsdp")),
            P(("dp", "fsdp")),
            P(("dp", "fsdp")),
            P(("dp", "fsdp")),
            P(("dp", "fsdp")),
            P(("dp", "fsdp")),
            P(("dp", "fsdp")),
            P(("dp", "fsdp")),
            P(("dp", "fsdp")),
            P(("dp", "fsdp")),
        ),
        check_vma=False,
    )
```

profile of v0, /device:TPU:1, one launch (start us, length us, event | category | flops | bytes accessed | tf_op | source)
XLA Modules:
  0.0 1676.1 jit_solution(2732410012276892290)
XLA Ops:
  7.2 0.7 all-gather.7.cloned.1.call-update
  8.0 0.7 all-gather.5.cloned.1.call-update
  8.7 0.7 all-gather.9.cloned.1.call-update
  10.0 0.8 dynamic-update-slice
  10.9 0.8 dynamic-update-slice.1
  11.7 0.8 dynamic-update-slice.7
  12.6 0.8 dynamic-update-slice.4
  13.4 0.8 dynamic-update-slice.5
  14.2 0.8 dynamic-update-slice.3
  15.1 0.8 dynamic-update-slice.2
  15.9 0.8 dynamic-update-slice.6
  16.8 69.4 %all-reduce.21 = (bf16[4096]{0:T(1024)(128)(2,1)S(1)}, bf16[1024]{0:T(1024)(128)(2,1)S(1)}, bf16[1024]{0:T(1024)(128)(2,1)S(1)}, bf16[1024]{0:T(1024)(128)(2,1)S...) all-reduce(bf16[4096]{0:T(1024)(128)(2,1)S(1)} %dynamic-update-slic, ...), channel_id=1, replica_groups=mesh['dp'=4,'fsdp'=32] {'dp','fsdp'}, use_global_device_ids=true, to_apply=%add.6 | all-reduce | flops 13312 | bytes 53248
  86.2 0.8 reduce-window.4
  87.1 0.7 fusion.61
  88.0 1.2 convert_reduce_fusion.2
  89.2 1.3 fusion.47
  90.7 222.9 %all-gather.7.cloned.1.call-done = bf16[1048576]{0:T(1024)(128)(2,1)} async-done(((bf16[8192]{0:T(1024)(128)(2,1)}), bf16[1048576]{0:T(1024)(128)(2,1)}) %all-gather.7.cloned.1.call-update) | async-done | bytes 2097168 | tf_op jit(solution)/shard_map/all_gather | solution.py:91
  313.6 2.8 reshape.240
  316.4 1.6 convolution_convert_fusion
  318.0 1.2 copy.52
  319.2 308.0 %all-gather.5.cloned.1.call-done = bf16[3145728]{0:T(1024)(128)(2,1)} async-done(((bf16[24576]{0:T(1024)(128)(2,1)}), bf16[3145728]{0:T(1024)(128)(2,1)}) %all-gather.5.cloned.1.call-update) | async-done | bytes 6291472 | tf_op jit(solution)/shard_map/all_gather | solution.py:89
  627.2 10.3 reshape.235
  637.6 6.4 convolution_add_fusion.1
  643.9 3.7 copy.50
  647.7 1.7 slice_bitcast_fusion.1
  649.7 0.9 fusion.78
  650.5 0.6 fusion.15
  651.5 1.0 multiply_reduce_fusion
  652.5 1.0 multiply_convert_fusion
  654.1 0.8 fusion.24
  654.9 0.8 fusion.28
  656.0 0.8 convolution_bitcast_fusion.3
  656.8 2.9 copy.61
  660.0 0.8 fusion.21
  661.3 6.6 convolution_bitcast_fusion.2
  667.9 12.3 copy.60
  680.2 262.1 %all-gather.9.cloned.1.call-done = bf16[4194304]{0:T(1024)(128)(2,1)} async-done(((bf16[32768]{0:T(1024)(128)(2,1)}), bf16[4194304]{0:T(1024)(128)(2,1)}) %all-gather.9.cloned.1.call-update) | async-done | bytes 8388624 | tf_op jit(solution)/shard_map/all_gather | solution.py:93
  942.3 13.3 reshape.241
  955.6 15.4 fusion.3
  971.1 285.6 %all-gather.11.cloned.1.call-done = bf16[4194304]{0:T(1024)(128)(2,1)} async-done(((bf16[32768]{0:T(1024)(128)(2,1)}), bf16[4194304]{0:T(1024)(128)(2,1)}) %all-gather.11.cloned.1.call-update) | async-done | bytes 8388624 | tf_op jit(solution)/shard_map/all_gather | solution.py:95
  1256.7 13.3 reshape.242
  1270.0 6.6 convert_reduce_fusion
  1276.6 1.3 copy-done.9
  1277.9 2.5 convolution_bitcast_fusion.1
  1280.4 7.3 copy.62
  1287.7 2.5 convolution_bitcast_fusion
  1290.2 8.0 copy.63
  1298.4 4.8 fusion.79
  1303.1 6.2 fusion.73
  1309.4 1.4 fusion.48
  1310.8 67.0 %all-reduce.19 = (f32[1024]{0:T(1024)S(1)}, f32[1024]{0:T(1024)S(1)}, f32[1024]{0:T(1024)S(1)}, f32[1024]{0:T(1024)S(1)}, f32[3072]{0:T(1024)S(1)}, /*index=5*/f32[1024]{0:T(1024)S(1)}, f32[4096]{0:T(1024)S(1)}) all-reduce(f32[1024]{0:T(1024)S(1)} %get-tuple-element.47, ...), channel_id=2, replica_groups=mesh['dp'=4,'fsdp'=32] {'dp','fsdp'}, use_global_device_ids=true, to_apply=%region_11.12.clone | all-reduce | flops 12288 | bytes 98304
  1377.8 0.6 dynamic-slice
  1378.4 0.6 dynamic-slice.1
  1379.0 0.6 dynamic-slice.2
  1379.6 0.6 dynamic-slice.3
  1380.2 0.6 dynamic-slice.9
  1380.7 0.6 dynamic-slice.5
  1381.3 7.0 convolution_add_fusion.3
  1388.3 1.6 fusion.27
  1389.9 273.0 %all-reduce.24.cloned.1.call-done = (f32[3145728]{0:T(1024)}, f32[1048576]{0:T(1024)}, f32[4194304]{0:T(1024)}, f32[4194304]{0:T(1024)}) async-done(((f32[3145728]{0:T(1024)}, f32[1048576]{0:T(1024)}, f32[4194304]{0:T(1024)}, f32[4194304]{0:T(1024)}), (f32[3145728]{0:T(1024)}, f32[1048576]{0:T(1024)}, f32[4194304]{0:T(1024)}, f32[4194304]{0:T(1024)})) %all-reduce.24.cloned.1.call-update) | async-done | bytes 50331664
  1662.8 1.6 dynamic-slice.8
  1664.4 1.6 dynamic-slice.10
  1666.0 1.5 dynamic-slice.4
  1667.5 1.4 dynamic-slice.6
  (76 shorter events, 4.1 us)
Async XLA Ops:
  7.2 309.2 %copy-start.4 = (bf16[256,1024]{1,0:T(8,128)(2,1)S(1)}, bf16[256,1024]{1,0:T(8,128)(2,1)}, u32[]{:S(2)}) copy-start(bf16[256,1024]{1,0:T(8,128)(2,1)} %param.16) | copy-start | bytes 1572868
  7.2 306.4 %all-gather.7.cloned.1.call-start = ((), (), s32[]{:S(2)}) async-start(), calls=%async_computation.1 | async-start | bytes 2113536 | tf_op jit(solution)/shard_map/all_gather | solution.py:91
  7.9 619.3 %all-gather.5.cloned.1.call-start = ((), (), s32[]{:S(2)}) async-start(), calls=%async_computation | async-start | bytes 6340608 | tf_op jit(solution)/shard_map/all_gather | solution.py:89
  8.7 933.6 %all-gather.9.cloned.1.call-start = ((), (), s32[]{:S(2)}) async-start(), calls=%async_computation.2 | async-start | bytes 8454144 | tf_op jit(solution)/shard_map/all_gather | solution.py:93
  9.4 1247.3 %all-gather.11.cloned.1.call-start = ((), (), s32[]{:S(2)}) async-start(), calls=%async_computation.3 | async-start | bytes 8454144 | tf_op jit(solution)/shard_map/all_gather | solution.py:95
  10.0 1652.9 %all-reduce.24.cloned.1.call-start = ((), (), s32[]{:S(2)}) async-start(), calls=%async_computation.4 | async-start | bytes 100663296
  316.4 321.1 %copy-start.2 = (bf16[1024,1024]{1,0:T(8,128)(2,1)}, bf16[1024,1024]{1,0:T(8,128)(2,1)S(1)}, u32[]{:S(2)}) copy-start(bf16[1024,1024]{1,0:T(8,128)(2,1)S(1)} %reshape.240) | copy-start | bytes 6291460
  319.2 318.3 %copy-start = (bf16[256,1024]{1,0:T(8,128)(2,1)S(1)}, bf16[256,1024]{1,0:T(8,128)(2,1)}, u32[]{:S(2)}) copy-start(bf16[256,1024]{1,0:T(8,128)(2,1)} %param.15) | copy-start | bytes 1572868
  649.7 1.9 copy-start.1
  654.9 1.0 copy-start.5
  655.7 3.9 copy-start.6
  1276.5 1.3 copy-start.9
  1280.4 7.3 copy-start.8
  1298.4 4.8 copy-start.10
  1378.4 290.5 %copy-start.11 = (f32[8]{0:T(128)}, f32[8]{0:T(128)S(1)}, u32[]{:S(2)}) copy-start(f32[8]{0:T(128)S(1)} %dynamic-slice.7) | copy-start | bytes 100
  1381.3 7.0 copy-start.3
  1381.3 7.0 copy-start.7
Sparse Core Ops, SparseCore 0:
  9.7 303.8 all-gather.6
  315.3 311.9 all-gather.4
  628.9 313.3 all-gather.8
  943.8 312.7 all-gather.10
  1298.4 364.4 all-reduce.23
where the time goes:
time: 1680 us
  waiting for transfers between devices  1350 us (80%)
  blocking collectives  136 us (8%)
  local copies, waits for them, and re-layouts  96 us (6%)
  matrix products  66.5 us (4%)
    all_gather x1, waiting for transfers between devices, collect(): lax.all_gather(pieces[4], ('dp', 'fsdp'), axis=0, tiled=True)  308 us
    all_gather x1, waiting for transfers between devices, collect(): lax.all_gather(pieces[10], ('dp', 'fsdp'), axis=0, tiled=True)  286 us
    unnamed x6, waiting for transfers between devices  276 us
    all_gather x1, waiting for transfers between devices, collect(): lax.all_gather(pieces[8], ('dp', 'fsdp'), axis=0, tiled=True)  262 us
    all_gather x1, waiting for transfers between devices, collect(): lax.all_gather(pieces[6], ('dp', 'fsdp'), axis=0, tiled=True)  223 us
    unnamed x2, blocking collectives  136 us
    unnamed x56, local copies, waits for them, and re-layouts  49.4 us
  transfers between devices with their start and end apart: 5, of which 5 were waited for; matrix products, arithmetic and copies ran while one was open for 7% of the time, Pallas kernels for 0%

commit v1 on v0

v1 whole, which is shorter than its diff:
```python
import jax
import jax.numpy as jnp
from jax import lax
from jax.experimental import pallas as pl
from jax.experimental.pallas import tpu as pltpu
from jax.sharding import PartitionSpec as P

D = 1024
HEADS = 16
HEAD_DIM = 64
ROT = 16
FF = 4096
ROW = 256
SEGS = 8
TP = 4
QC = 3 * D // TP
HC = FF // TP
LOCAL_HEADS = HEADS // TP
SMALL = 104
AXES = ("dp", "fsdp")
VMEM = 48 * 1024 * 1024

f32 = jnp.float32
bf16 = jnp.bfloat16


def dev(d, y, x, zh):
    return d * 32 + y * 8 + x * 2 + zh


def outer_groups():
    groups = []
    for d in range(4):
        for k in range(4):
            for zh in range(2):
                if d % 2 == 0:
                    groups.append([dev(d, i, k, zh) for i in range(4)])
                else:
                    groups.append([dev(d, k, i, zh) for i in range(4)])
    return groups


def inner_groups():
    groups = []
    for d in range(4):
        for k in range(4):
            if d % 2 == 0:
                groups.append([dev(d, k, i, zh) for i in range(4) for zh in range(2)])
            else:
                groups.append([dev(d, i, k, zh) for i in range(4) for zh in range(2)])
    return groups


def a2a(values, groups):
    return lax.all_to_all(values, AXES, 0, 0, tiled=True, axis_index_groups=groups)


def flip_core(values):
    return lax.ppermute(values, "dp", [(0, 1), (1, 0), (2, 3), (3, 2)])


def flip_chip(values):
    return lax.ppermute(values, "dp", [(0, 2), (2, 0), (1, 3), (3, 1)])


def dot(left, right):
    return jnp.dot(left, right, preferred_element_type=f32)


def dot_nt(left, right):
    return lax.dot_general(left, right, (((1,), (1,)), ((), ())), preferred_element_type=f32)


def dot_tn(left, right):
    return lax.dot_general(left, right, (((0,), (0,)), ((), ())), preferred_element_type=f32)


def params(flops, nbytes, trans=0):
    return dict(
        compiler_params=pltpu.CompilerParams(vmem_limit_bytes=VMEM),
        cost_estimate=pl.CostEstimate(
            flops=int(flops), bytes_accessed=int(nbytes), transcendentals=int(trans)
        ),
    )


def normalize(x):
    average = jnp.mean(x, axis=-1, keepdims=True)
    centred = x - average
    inv_std = lax.rsqrt(jnp.mean(centred * centred, axis=-1, keepdims=True) + 1e-05)
    return centred * inv_std, inv_std


def assemble_a_kernel(core_ref, buf_ref, wqkv_ref, wd_ref, small_ref):
    for d in range(4):
        for p in range(3):
            row = (d * 3 + p) * 16
            wqkv_ref[d, 0, 0, :, p * 256 : (p + 1) * 256] = buf_ref[0, 0, row : row + 16, :]
    for cg in range(4):
        row = 192 + cg * 16
        wd_ref[0, 0, :, cg * 256 : (cg + 1) * 256] = buf_ref[0, 0, row : row + 16, :]
    small_ref[0, 0] = buf_ref[0, 0, 256:272, :]


def swapped(y, x, core_ref):
    c = core_ref[0]
    return y + c * (x - y), x + c * (y - x)


def assemble_a(buf, core):
    grid_spec = pltpu.PrefetchScalarGridSpec(
        num_scalar_prefetch=1,
        grid=(4, 4),
        in_specs=[pl.BlockSpec((1, 1, 272, 256), lambda y, x, c: (*swapped(y, x, c), 0, 0))],
        out_specs=[
            pl.BlockSpec((4, 1, 1, 16, QC), lambda y, x, c: (0, y, x, 0, 0)),
            pl.BlockSpec((1, 1, 16, D), lambda y, x, c: (y, x, 0, 0)),
            pl.BlockSpec((1, 1, 16, 256), lambda y, x, c: (y, x, 0, 0)),
        ],
    )
    wqkv, wd, small = pl.pallas_call(
        assemble_a_kernel,
        grid_spec=grid_spec,
        out_shape=[
            jax.ShapeDtypeStruct((4, 4, 4, 16, QC), bf16),
            jax.ShapeDtypeStruct((4, 4, 16, D), bf16),
            jax.ShapeDtypeStruct((4, 4, 16, 256), bf16),
        ],
        **params(0, 5e6),
    )(core, buf)
    return wqkv.reshape(D, QC), wd.reshape(D // TP, D), small


def assemble_b_kernel(core_ref, buf_ref, wup_ref, wdown_ref):
    for d in range(4):
        for cg in range(4):
            row = (d * 4 + cg) * 16
            wup_ref[d, 0, 0, :, cg * 256 : (cg + 1) * 256] = buf_ref[0, 0, row : row + 16, :]
    for cg in range(4):
        row = 256 + cg * 64
        wdown_ref[0, 0, :, cg * 256 : (cg + 1) * 256] = buf_ref[0, 0, row : row + 64, :]


def assemble_b(buf, core):
    grid_spec = pltpu.PrefetchScalarGridSpec(
        num_scalar_prefetch=1,
        grid=(4, 4),
        in_specs=[pl.BlockSpec((1, 1, 512, 256), lambda y, x, c: (*swapped(y, x, c), 0, 0))],
        out_specs=[
            pl.BlockSpec((4, 1, 1, 16, HC), lambda y, x, c: (0, y, x, 0, 0)),
            pl.BlockSpec((1, 1, 64, D), lambda y, x, c: (y, x, 0, 0)),
        ],
    )
    wup, wdown = pl.pallas_call(
        assemble_b_kernel,
        grid_spec=grid_spec,
        out_shape=[
            jax.ShapeDtypeStruct((4, 4, 4, 16, HC), bf16),
            jax.ShapeDtypeStruct((4, 4, 64, D), bf16),
        ],
        **params(0, 8e6),
    )(core, buf)
    return wup.reshape(D, HC), wdown.reshape(HC, D)


def turn(u, cosine, sin_left, sin_right):
    return (
        u * cosine
        + pltpu.roll(u, u.shape[1] - ROT // 2, 1) * sin_left
        + pltpu.roll(u, ROT // 2, 1) * sin_right
    )


def attention_kernel(
    ends_ref,
    x_ref,
    cot_ref,
    wqkv_ref,
    wd_ref,
    vec_ref,
    qb_ref,
    cos_ref,
    sl_ref,
    sr_ref,
    ain_ref,
    min_ref,
    gb_ref,
    ctx_ref,
    dqkv_ref,
    sums_ref,
):
    r = pl.program_id(0)
    xhat, _ = normalize(x_ref[0].astype(f32))
    attn_in = (xhat * vec_ref[0:1] + vec_ref[1:2]).astype(bf16)
    ain_ref[...] = attn_in
    min_ref[...] = (xhat * vec_ref[2:3] + vec_ref[3:4]).astype(bf16)
    qkv = dot(attn_in, wqkv_ref[...]) + qb_ref[0:1]
    ends = [ends_ref[r * SEGS + j] for j in range(SEGS - 1)]
    rows = lax.broadcasted_iota(jnp.int32, (ROW, 1), 0)
    cols = lax.broadcasted_iota(jnp.int32, (1, ROW), 1)
    row_doc = sum([(rows >= e).astype(jnp.int32) for e in ends])
    col_doc = sum([(cols >= e).astype(jnp.int32) for e in ends])
    allowed = (row_doc == col_doc) & (cols <= rows)
    kept = jnp.where(rows < ends[-1], cot_ref[0].astype(f32), 0.0)
    gb = kept.astype(bf16)
    gb_ref[...] = gb
    dctx = dot_nt(gb, wd_ref[...]).astype(bf16)
    cosine, left, right = cos_ref[0], sl_ref[0], sr_ref[0]
    q = turn(qkv[:, 0:256], cosine, left, right).astype(bf16)
    k = turn(qkv[:, 256:512], cosine, left, right).astype(bf16)
    v = qkv[:, 512:768].astype(bf16)
    scale = HEAD_DIM**-0.5
    ctx, dq, dk, dv = [], [], [], []
    for h in range(LOCAL_HEADS):
        at = slice(h * HEAD_DIM, (h + 1) * HEAD_DIM)
        qh, kh, vh, dch = q[:, at], k[:, at], v[:, at], dctx[:, at]
        scores = jnp.where(allowed, dot_nt(qh, kh) * scale, -1000000000.0)
        shifted = jnp.exp(scores - jnp.max(scores, axis=-1, keepdims=True))
        probs = shifted * (1.0 / jnp.sum(shifted, axis=-1, keepdims=True))
        low = probs.astype(bf16)
        ctx.append(dot(low, vh))
        dv.append(dot_tn(low, dch))
        dprobs = dot_nt(dch, vh)
        inner = jnp.sum(dprobs * probs, axis=-1, keepdims=True)
        ds = (probs * (dprobs - inner)).astype(bf16)
        dq.append(dot(ds, kh) * scale)
        dk.append(dot_tn(ds, qh) * scale)
    ctx_ref[...] = jnp.concatenate(ctx, axis=1).astype(bf16)
    dqs = turn(jnp.concatenate(dq, axis=1), cosine, -left, -right)
    dks = turn(jnp.concatenate(dk, axis=1), cosine, -left, -right)
    dqkv = jnp.concatenate([dqs, dks] + dv, axis=1).astype(bf16)
    dqkv_ref[...] = dqkv

    @pl.when(r == 0)
    def _():
        sums_ref[...] = jnp.zeros_like(sums_ref)
        sums_ref[0:1, :] = jnp.sum(kept, axis=0, keepdims=True)

    sums_ref[1:2, 0:QC] += jnp.sum(dqkv.astype(f32), axis=0, keepdims=True)


def attention(ends, x4, cot4, wqkv, wd, vec, qb, cosine, left, right):
    row = lambda r, e: (r, 0)
    row3 = lambda r, e: (r, 0, 0)
    fixed = lambda r, e: (0, 0)
    grid_spec = pltpu.PrefetchScalarGridSpec(
        num_scalar_prefetch=1,
        grid=(TP,),
        in_specs=[
            pl.BlockSpec((1, ROW, D), row3),
            pl.BlockSpec((1, ROW, D), row3),
            pl.BlockSpec((D, QC), fixed),
            pl.BlockSpec((D // TP, D), fixed),
            pl.BlockSpec((8, D), fixed),
            pl.BlockSpec((8, QC), fixed),
            pl.BlockSpec((1, ROW, 256), row3),
            pl.BlockSpec((1, ROW, 256), row3),
            pl.BlockSpec((1, ROW, 256), row3),
        ],
        out_specs=[
            pl.BlockSpec((ROW, D), row),
            pl.BlockSpec((ROW, D), row),
            pl.BlockSpec((ROW, D), row),
            pl.BlockSpec((ROW, 256), row),
            pl.BlockSpec((ROW, QC), row),
            pl.BlockSpec((8, D), fixed),
        ],
    )
    tokens = TP * ROW
    return pl.pallas_call(
        attention_kernel,
        grid_spec=grid_spec,
        out_shape=[
            jax.ShapeDtypeStruct((tokens, D), bf16),
            jax.ShapeDtypeStruct((tokens, D), bf16),
            jax.ShapeDtypeStruct((tokens, D), bf16),
            jax.ShapeDtypeStruct((tokens, 256), bf16),
            jax.ShapeDtypeStruct((tokens, QC), bf16),
            jax.ShapeDtypeStruct((8, D), f32),
        ],
        **params(4e9, 2e7, 1e6),
    )(ends, x4, cot4, wqkv, wd, vec, qb, cosine, left, right)


def grads_a_kernel(core_ref, ain_ref, dqkv_ref, ctx_ref, gb_ref, out_ref):
    d = pl.program_id(0)
    c = core_ref[0]
    dqkv_grad = dot_tn(ain_ref[...], dqkv_ref[...]).astype(bf16)
    dense_grad = dot_tn(ctx_ref[...], gb_ref[...]).astype(bf16)
    base = pl.multiple_of(d * 48, 16)
    dense_base = pl.multiple_of(192 + d * 16, 16)
    for y in range(4):
        for x in range(4):
            b, a = y + c * (x - y), x + c * (y - x)
            at = slice((y * 4 + x) * 16, (y * 4 + x + 1) * 16)
            for p in range(3):
                out_ref[b, a, pl.ds(base + p * 16, 16), :] = dqkv_grad[at, p * 256 : (p + 1) * 256]
            out_ref[b, a, pl.ds(dense_base, 16), :] = dense_grad[at]


def grads_a(core, attn_in, dqkv, ctx, gb):
    tokens = TP * ROW
    grid_spec = pltpu.PrefetchScalarGridSpec(
        num_scalar_prefetch=1,
        grid=(4,),
        in_specs=[
            pl.BlockSpec((tokens, 256), lambda d, c: (0, d)),
            pl.BlockSpec((tokens, QC), lambda d, c: (0, 0)),
            pl.BlockSpec((tokens, 256), lambda d, c: (0, 0)),
            pl.BlockSpec((tokens, 256), lambda d, c: (0, d)),
        ],
        out_specs=pl.BlockSpec((4, 4, 256, 256), lambda d, c: (0, 0, 0, 0)),
    )
    return pl.pallas_call(
        grads_a_kernel,
        grid_spec=grid_spec,
        out_shape=jax.ShapeDtypeStruct((4, 4, 256, 256), bf16),
        **params(2.2e9, 1e7),
    )(core, attn_in, dqkv, ctx, gb)


def grads_down_kernel(core_ref, hidden_ref, gb_ref, out_ref):
    y = pl.program_id(0)
    c = core_ref[0]
    grad = dot_tn(hidden_ref[...], gb_ref[...]).astype(bf16)
    for x in range(4):
        b, a = y + c * (x - y), x + c * (y - x)
        for cg in range(4):
            out_ref[b, a, cg * 64 : (cg + 1) * 64, :] = grad[
                x * 64 : (x + 1) * 64, cg * 256 : (cg + 1) * 256
            ]


def grads_down(core, hidden, gb):
    tokens = TP * ROW
    grid_spec = pltpu.PrefetchScalarGridSpec(
        num_scalar_prefetch=1,
        grid=(4,),
        in_specs=[
            pl.BlockSpec((tokens, 256), lambda y, c: (0, y)),
            pl.BlockSpec((tokens, D), lambda y, c: (0, 0)),
        ],
        out_specs=pl.BlockSpec((4, 4, 256, 256), lambda y, c: (0, 0, 0, 0)),
    )
    return pl.pallas_call(
        grads_down_kernel,
        grid_spec=grid_spec,
        out_shape=jax.ShapeDtypeStruct((4, 4, 256, 256), bf16),
        **params(2.2e9, 6e6),
    )(core, hidden, gb)


def grads_up_kernel(core_ref, min_ref, dpre_ref, small_ref, out_ref):
    d = pl.program_id(0)
    c = core_ref[0]
    grad = dot_tn(min_ref[...], dpre_ref[...]).astype(bf16)
    base = pl.multiple_of(d * 64, 16)
    for y in range(4):
        for x in range(4):
            b, a = y + c * (x - y), x + c * (y - x)
            at = slice((y * 4 + x) * 16, (y * 4 + x + 1) * 16)
            for cg in range(4):
                out_ref[b, a, pl.ds(base + cg * 16, 16), :] = grad[at, cg * 256 : (cg + 1) * 256]

    @pl.when(d == 0)
    def _():
        for y in range(4):
            for x in range(4):
                b, a = y + c * (x - y), x + c * (y - x)
                out_ref[b, a, 256:272, :] = small_ref[y, x]


def grads_up(core, mlp_in, dpre, small):
    tokens = TP * ROW
    grid_spec = pltpu.PrefetchScalarGridSpec(
        num_scalar_prefetch=1,
        grid=(4,),
        in_specs=[
            pl.BlockSpec((tokens, 256), lambda d, c: (0, d)),
            pl.BlockSpec((tokens, HC), lambda d, c: (0, 0)),
            pl.BlockSpec((4, 4, 16, 256), lambda d, c: (0, 0, 0, 0)),
        ],
        out_specs=pl.BlockSpec((4, 4, 272, 256), lambda d, c: (0, 0, 0, 0)),
    )
    return pl.pallas_call(
        grads_up_kernel,
        grid_spec=grid_spec,
        out_shape=jax.ShapeDtypeStruct((4, 4, 272, 256), bf16),
        **params(2.2e9, 6e6),
    )(core, mlp_in, dpre, small)


def hidden_kernel(min_ref, gb_ref, wup_ref, wdown_ref, ub_ref, hidden_ref, dpre_ref, sums_ref):
    t = pl.program_id(1)
    pre = dot(min_ref[...], wup_ref[...]) + ub_ref[0:1]
    back = dot_nt(gb_ref[...], wdown_ref[...])
    size = jnp.abs(pre) * 0.7071067811865476
    bell = jnp.exp(-0.5 * pre * pre)
    s = 1.0 / (1.0 + 0.3275911 * size)
    poly = s * (
        0.127414796
        + s * (-0.142248368 + s * (0.7107068705 + s * (-0.7265760135 + s * 0.5307027145)))
    )
    tail = poly * bell
    cumul = jnp.where(pre >= 0.0, 1.0 - tail, tail)
    hidden_ref[...] = (pre * cumul).astype(bf16)
    dpre = (back * (cumul + pre * (bell * 0.3989422804014327))).astype(bf16)
    dpre_ref[...] = dpre

    @pl.when(t == 0)
    def _():
        sums_ref[...] = jnp.zeros_like(sums_ref)

    sums_ref[0:1, :] += jnp.sum(dpre.astype(f32), axis=0, keepdims=True)


def hidden_units(mlp_in, gb, wup, wdown, ub):
    tokens = TP * ROW
    return pl.pallas_call(
        hidden_kernel,
        grid=(4, 4),
        in_specs=[
            pl.BlockSpec((256, D), lambda j, t: (t, 0)),
            pl.BlockSpec((256, D), lambda j, t: (t, 0)),
            pl.BlockSpec((D, 256), lambda j, t: (0, j)),
            pl.BlockSpec((256, D), lambda j, t: (j, 0)),
            pl.BlockSpec((8, 256), lambda j, t: (0, j)),
        ],
        out_specs=[
            pl.BlockSpec((256, 256), lambda j, t: (t, j)),
            pl.BlockSpec((256, 256), lambda j, t: (t, j)),
            pl.BlockSpec((8, 256), lambda j, t: (0, j)),
        ],
        out_shape=[
            jax.ShapeDtypeStruct((tokens, HC), bf16),
            jax.ShapeDtypeStruct((tokens, HC), bf16),
            jax.ShapeDtypeStruct((8, HC), f32),
        ],
        **params(8e9, 2e7, 2e6),
    )(mlp_in, gb, wup, wdown, ub)


def outputs_kernel(
    x_ref,
    ctx_ref,
    hidden_ref,
    dqkv_ref,
    dpre_ref,
    wd_ref,
    wdown_ref,
    wqkv_ref,
    wup_ref,
    vec_ref,
    out_ref,
    sums_ref,
):
    t = pl.program_id(0)
    forward = dot(ctx_ref[...], wd_ref[...]) + dot(hidden_ref[...], wdown_ref[...])
    out_ref[0, 0] = forward.astype(bf16)
    dattn = dot_nt(dqkv_ref[...], wqkv_ref[...])
    dmlp = dot_nt(dpre_ref[...], wup_ref[...])
    xhat, _ = normalize(x_ref[0].astype(f32))

    @pl.when(t == 0)
    def _():
        sums_ref[...] = jnp.zeros_like(sums_ref)

    sums_ref[0:1, :] += jnp.sum(dattn * xhat, axis=0, keepdims=True)
    sums_ref[1:2, :] += jnp.sum(dattn, axis=0, keepdims=True)
    sums_ref[2:3, :] += jnp.sum(dmlp * xhat, axis=0, keepdims=True)
    sums_ref[3:4, :] += jnp.sum(dmlp, axis=0, keepdims=True)
    out_ref[0, 1] = (dattn * vec_ref[0:1] + dmlp * vec_ref[2:3]).astype(bf16)


def outputs(x4, ctx, hidden, dqkv, dpre, wd, wdown, wqkv, wup, vec):
    row = lambda t: (t, 0)
    fixed = lambda t: (0, 0)
    return pl.pallas_call(
        outputs_kernel,
        grid=(TP,),
        in_specs=[
            pl.BlockSpec((1, ROW, D), lambda t: (t, 0, 0)),
            pl.BlockSpec((ROW, 256), row),
            pl.BlockSpec((ROW, HC), row),
            pl.BlockSpec((ROW, QC), row),
            pl.BlockSpec((ROW, HC), row),
            pl.BlockSpec((D // TP, D), fixed),
            pl.BlockSpec((HC, D), fixed),
            pl.BlockSpec((D, QC), fixed),
            pl.BlockSpec((D, HC), fixed),
            pl.BlockSpec((8, D), fixed),
        ],
        out_specs=[
            pl.BlockSpec((1, 2, ROW, D), lambda t: (t, 0, 0, 0)),
            pl.BlockSpec((8, D), fixed),
        ],
        out_shape=[
            jax.ShapeDtypeStruct((TP, 2, ROW, D), bf16),
            jax.ShapeDtypeStruct((8, D), f32),
        ],
        **params(6.5e9, 2e7),
    )(x4, ctx, hidden, dqkv, dpre, wd, wdown, wqkv, wup, vec)


def rotary_tables(ends, starts_len):
    places = jnp.arange(ROW, dtype=jnp.int32)
    passed = places[None, :, None] >= ends[:, None, : SEGS - 1]
    first = jnp.max(jnp.where(passed, ends[:, None, : SEGS - 1], 0), axis=-1)
    place = (places[None, :] - first).astype(f32)
    half = ROT // 2
    freqs = 10000.0 ** (-(jnp.arange(half, dtype=f32) * 2.0) / ROT)
    angle = place[:, :, None] * freqs
    cosine, sine = jnp.cos(angle), jnp.sin(angle)
    zeros = jnp.zeros_like(sine)
    rest = jnp.zeros((TP, ROW, HEAD_DIM - ROT), f32)
    wide = lambda parts: jnp.tile(jnp.concatenate(parts, axis=-1), (1, 1, LOCAL_HEADS))
    return (
        wide([cosine, cosine, rest + 1.0]),
        wide([-sine, zeros, rest]),
        wide([zeros, sine, rest]),
    )


def widen(vector, rows=8):
    return jnp.pad(vector[None, :], ((0, rows - 1), (0, 0)))


def body(
    inputs,
    cotangent,
    lengths,
    norm1_gain,
    norm1_bias,
    norm2_gain,
    norm2_bias,
    qkv_weight,
    qkv_bias,
    dense_weight,
    dense_bias,
    up_weight,
    up_bias,
    down_weight,
    down_bias,
):
    me = lax.axis_index("dp")
    core = (me % 2).astype(jnp.int32)
    core1 = core[None]
    outer, inner = outer_groups(), inner_groups()

    x_pair = jnp.stack([inputs, flip_chip(inputs)])
    x4 = jnp.concatenate([x_pair, flip_core(x_pair)])
    cot_pair = jnp.stack([cotangent, flip_chip(cotangent)])
    cot4 = jnp.concatenate([cot_pair, flip_core(cot_pair)])

    qkv_piece = qkv_weight.reshape(8, 3, 4, 256).transpose(2, 1, 0, 3).reshape(4, 24, 256)
    up_piece = up_weight.reshape(8, 4, 4, 256).transpose(1, 2, 0, 3).reshape(4, 32, 256)
    vector = jnp.concatenate(
        [
            norm1_gain,
            norm1_bias,
            norm2_gain,
            norm2_bias,
            qkv_bias,
            dense_bias,
            up_bias,
            down_bias,
            lengths[0].astype(bf16),
        ]
    )
    vector = jnp.pad(vector, (0, 256 - SMALL - SEGS))
    small_piece = jnp.broadcast_to(widen(vector)[None], (4, 8, 256))
    first = lax.all_to_all(
        jnp.concatenate([qkv_piece, up_piece, small_piece], axis=1), "dp", 0, 0, tiled=True
    )
    dense_piece = dense_weight.reshape(8, 4, 256).transpose(1, 0, 2).reshape(32, 256)
    down_piece = down_weight.reshape(32, 4, 256).transpose(1, 0, 2).reshape(128, 256)
    vectors = first[:, 56, :]
    block = jnp.concatenate(
        [
            first[:, :24].reshape(96, 256),
            dense_piece,
            jnp.pad(vectors, ((0, 4), (0, 0))),
            first[:, 24:56].reshape(128, 256),
            down_piece,
        ]
    )
    second = a2a(jnp.broadcast_to(block[None], (8, 392, 256)).reshape(8 * 392, 256), inner)
    second = second.reshape(4, 2, 392, 256)
    units = lambda v, n: v.reshape(4, 2, n, 8, 256).transpose(0, 2, 1, 3, 4).reshape(4, n * 16, 256)
    block_a = units(second[:, :, :136], 17)
    block_up = units(second[:, :, 136:264], 16)
    block_down = second[:, :, 264:].reshape(4, 2, 4, 32, 256).transpose(0, 2, 1, 3, 4)
    block_b = jnp.concatenate([block_up, block_down.reshape(4, 256, 256)], axis=1)
    third_a = a2a(jnp.broadcast_to(block_a[None], (4, 4, 272, 256)), outer)
    third_b = a2a(jnp.broadcast_to(block_b[None], (4, 4, 512, 256)), outer)

    lens = vectors[:, SMALL : SMALL + SEGS].astype(f32)
    order = jnp.array([0, 2, 1, 3], jnp.int32) ^ me
    pick = (order[:, None] == jnp.arange(4, dtype=jnp.int32)[None, :]).astype(f32)
    lens4 = jnp.sum(pick[:, :, None] * lens[None], axis=1)
    ends = jnp.cumsum(lens4, axis=1).astype(jnp.int32)
    cosine, left, right = rotary_tables(ends, None)

    wqkv, wd, small = assemble_a(third_a, core1)
    small = small.reshape(4, 4, 2, 8, 256)[:, :, :, :4, :SMALL]
    small = small.transpose(3, 0, 1, 2, 4).reshape(128, SMALL).astype(f32)
    vec = jnp.pad(small[:, :32].reshape(128, 4, 8).transpose(1, 0, 2).reshape(4, D), ((0, 4), (0, 0)))
    qkv_b = small[:, 32:56].reshape(3, 4, 256)
    up_b = small[:, 64:96].reshape(4, HC)
    own = (jnp.arange(4, dtype=jnp.int32) == me).astype(f32)
    qkv_b = jnp.sum(qkv_b * own[None, :, None], axis=1).reshape(QC)
    up_b = jnp.sum(up_b * own[:, None], axis=0)
    out_b = small[:, 56:64].reshape(D) + small[:, 96:104].reshape(D)

    attn_in, mlp_in, gb, ctx, dqkv, sums_a = attention(
        ends.reshape(-1), x4, cot4, wqkv, wd, vec, widen(qkv_b), cosine, left, right
    )
    sent_a = a2a(grads_a(core1, attn_in, dqkv, ctx, gb), outer)

    wup, wdown = assemble_b(third_b, core1)
    hidden, dpre, sums_b = hidden_units(mlp_in, gb, wup, wdown, widen(up_b))
    sent_down = a2a(grads_down(core1, hidden, gb), outer)
    both, sums_c = outputs(x4, ctx, hidden, dqkv, dpre, wd, wdown, wqkv, wup, vec)

    halves = both[:2].astype(f32) + flip_core(both[2:]).astype(f32)
    mine, theirs = halves[0], halves[1].astype(bf16)
    total = mine + flip_chip(theirs).astype(f32)
    states = inputs.astype(f32)
    block_output = (states + total[0] + out_b[None, :]).astype(bf16)
    normed, inv_std = normalize(states)
    scaled = total[1]
    mean_e = jnp.mean(scaled, axis=-1, keepdims=True)
    mean_ex = jnp.mean(scaled * normed, axis=-1, keepdims=True)
    rows = jnp.arange(ROW, dtype=jnp.int32)
    keep = rows < ends[0, SEGS - 2]
    upstream = jnp.where(keep[:, None], cotangent.astype(f32), 0.0)
    input_grad = upstream + inv_std * (scaled - mean_e - normed * mean_ex)

    cut = lambda v, n: v.reshape(128, n)
    qkv_bg = (sums_a[1, :QC].reshape(3, 1, 256) * own[None, :, None]).reshape(-1)
    up_bg = (sums_b[0][None, :] * own[:, None]).reshape(-1)
    table = jnp.concatenate(
        [
            cut(sums_c[0], 8),
            cut(sums_c[1], 8),
            cut(sums_c[2], 8),
            cut(sums_c[3], 8),
            cut(qkv_bg, 24),
            cut(sums_a[0], 8),
            cut(up_bg, 32),
            cut(sums_a[0], 8),
        ],
        axis=1,
    )
    table = jnp.pad(table, ((0, 0), (0, 128 - SMALL)))

    def split(values):
        high = lax.reduce_precision(values, 8, 7)
        return jnp.concatenate([high, values - high], axis=-1).astype(bf16)

    rows_small = split(table).reshape(4, 4, 4, 2, 256).transpose(1, 2, 3, 0, 4)
    rows_small = jnp.pad(rows_small, ((0, 0), (0, 0), (0, 0), (0, 4), (0, 0))).reshape(4, 4, 16, 256)
    sent_up = a2a(grads_up(core1, mlp_in, dpre, rows_small), outer)

    def add(values):
        return jnp.sum(values.astype(f32), axis=0)

    def halve(values, n, size):
        return values.reshape(4, n, 2, size, 256).transpose(0, 2, 1, 3, 4).reshape(8, n * size, 256)

    def rejoin(values):
        return values[..., :128] + values[..., 128:]

    sum_a = halve(add(sent_a), 16, 8).astype(bf16)
    sum_down = halve(add(sent_down), 4, 32).astype(bf16)
    sum_up = add(sent_up)
    sum_small = split(rejoin(sum_up[:, 256:272]).reshape(8, 8, 128))
    sum_up = halve(sum_up[:, :256], 16, 8).astype(bf16)
    fourth = a2a(jnp.concatenate([sum_a, sum_up, sum_small, sum_down], axis=1), inner)
    final = add(fourth.reshape(8, 392, 256))
    dense_grad = final[96:128].reshape(4, 8, 256).transpose(1, 0, 2).reshape(-1)
    down_grad = final[264:392].reshape(4, 32, 256).transpose(1, 0, 2).reshape(-1)
    small_sum = jnp.pad(rejoin(final[256:264])[:4], ((0, 0), (0, 128)))
    last = jnp.concatenate(
        [
            final[0:96].reshape(4, 24, 256),
            final[128:256].reshape(4, 32, 256),
            jnp.pad(small_sum[:, None, :], ((0, 0), (0, 7), (0, 0))),
        ],
        axis=1,
    )
    last = lax.all_to_all(last, "dp", 0, 0, tiled=True)
    qkv_grad = last[:, :24].reshape(4, 3, 8, 256).transpose(2, 1, 0, 3).reshape(-1)
    up_grad = last[:, 24:56].reshape(4, 4, 8, 256).transpose(2, 0, 1, 3).reshape(-1)
    tiny = jnp.sum(last[:, 56, :SMALL], axis=0)
    return (
        block_output,
        input_grad,
        tiny[0:8],
        tiny[8:16],
        tiny[16:24],
        tiny[24:32],
        qkv_grad,
        tiny[32:56],
        dense_grad,
        tiny[56:64],
        up_grad,
        tiny[64:96],
        down_grad,
        tiny[96:104],
    )


def solution(mesh):
    flat = P(("dp", "fsdp"))
    rows = P(("dp", "fsdp"), None)
    return jax.shard_map(
        body,
        mesh=mesh,
        in_specs=(rows,) * 3 + (flat,) * 12,
        out_specs=(rows,) * 2 + (flat,) * 12,
        check_vma=False,
    )
```

time: 1680 us -> 289 us (0.17)
  waiting for transfers between devices: 1350 us -> 36.2 us
  blocking collectives: 136 us -> 27.3 us
  Pallas kernels: 0 us -> 78.2 us
  matrix products: 66.5 us -> 0 us
  starting transfers between devices: 0.19 us -> 47.9 us
  local copies, waits for them, and re-layouts: 96 us -> 61.9 us
  other arithmetic: 8.43 us -> 31.3 us
    all_gather x4 -> x0, waiting for transfers between devices: 1080 us -> none  [the longest x1 308 us: collect(): lax.all_gather(pieces[4], ('dp', 'fsdp'), axis=0, tiled=True)]
    unnamed x6 -> x0, waiting for transfers between devices: 276 us -> none
    unnamed x2 -> x0, blocking collectives: 136 us -> none
    pallas_call x0 -> x8, Pallas kernels: none -> 78.2 us  [the longest x1 21.8 us: attention(): pl.pallas_call(attention_kernel, grid_spec=grid_spec, out_shape=[jax.Shap...]
    dot_general x18 -> x0, matrix products: 66.5 us -> none  [the longest x4 19.1 us: times_back(): lax.dot_general(left, right, (((1,), (1,)), ((), ())), preferred_element_...]
    all_to_all x0 -> x8, starting transfers between devices: none -> 41.8 us  [the longest x6 26.7 us: a2a(): lax.all_to_all(values, AXES, 0, 0, tiled=True, axis_index_groups=groups)]
    reshape x4 -> x8, local copies, waits for them, and re-layouts: 39.8 us -> 3.74 us  [the longest x1 0.89 us: body(): down_weight.reshape(32, 4, 256).transpose(1, 0, 2).reshape(128, 256)]
    all_to_all x0 -> x1, blocking collectives: none -> 27.3 us  [a2a(): lax.all_to_all(values, AXES, 0, 0, tiled=True, axis_index_groups=groups)]
  transfers between devices with their start and end apart: 5 -> 14, of which waited for: 5 -> 5; matrix products, arithmetic and copies ran while one was open for 7% -> 21% of each run, Pallas kernels for 0% -> 28%
where the time goes in v1:
time: 289 us; the launch traced here: 284 us
  Pallas kernels  78.2 us (27%)
  local copies, waits for them, and re-layouts  61.9 us (21%)
  starting transfers between devices  47.9 us (17%)
  waiting for transfers between devices  36.2 us (13%)
  other arithmetic  31.3 us (11%)
  blocking collectives  27.3 us (9%)
    all_to_all x1, blocking collectives, a2a(): lax.all_to_all(values, AXES, 0, 0, tiled=True, axis_index_groups=groups)  27.3 us
    all_to_all x6, starting transfers between devices, a2a(): lax.all_to_all(values, AXES, 0, 0, tiled=True, axis_index_groups=groups)  26.7 us
    all_to_all x6, waiting for transfers between devices, a2a(): lax.all_to_all(values, AXES, 0, 0, tiled=True, axis_index_groups=groups)  24.1 us
    unnamed x58, local copies, waits for them, and re-layouts  22.6 us
    pallas_call x1, Pallas kernels, attention(): pl.pallas_call(attention_kernel, grid_spec=grid_spec, out_shape=[jax.Shap...  21.8 us
    pallas_call x1, Pallas kernels, hidden_units(): pl.pallas_call(hidden_kernel, grid=(4, 4), in_specs=[pl.BlockSpec((256, D...  17.5 us
    pallas_call x1, Pallas kernels, outputs(): pl.pallas_call(outputs_kernel, grid=(TP,), in_specs=[pl.BlockSpec((1, ROW...  13.2 us
    another operation x6, local copies, waits for them, and re-layouts, rotary_tables(): jnp.tile(jnp.concatenate(parts, axis=-1), (1, 1, LOCAL_HEADS))  11.1 us
  transfers between devices with their start and end apart: 14, of which 5 were waited for; matrix products, arithmetic and copies ran while one was open for 21% of the time, Pallas kernels for 28%

profile of v1, /device:TPU:1, one launch (start us, length us, event | category | flops | bytes accessed | tf_op | source)
XLA Modules:
  0.0 284.3 jit_solution(12429015593554475570)
XLA Ops:
  0.6 0.9 reshape.281
  3.1 5.4 %concatenate.52 = bf16[112]{0:T(256)(128)(2,1)S(1)} concatenate(bf16[8]{0:T(256)(128)(2,1)} %param.19, bf16[8]{0:T(256)(128)(2,1)} %param.20, bf16[8]{0:T(256)(128)(2,1)} %param.21, bf16[8]{0:T(256)(128)(2,1)} %param.22, bf16[24]{0:T(256)(128)(2,1)} %param.24, bf16[8]{0:T(256)(128)(2,1)} %param.26, bf16[32]{0:T(256)(128)(2,1)} %param.28, bf16[8]{0:T(256)(128)(2,1)} %param.30, ...), dimensions={0} | concatenate | bytes 448 | tf_op jit(solution)/shard_map/concatenate | solution.py:557
  9.2 4.7 %all-to-all-start = ((bf16[4,64,256]{2,1,0:T(8,128)(2,1)}), bf16[4,64,256]{2,1,0:T(8,128)(2,1)S(1)}, u32[]{:S(2)}, u32[]{:S(2)}) async-start(bf16[4,64,256]{2,1,0:T(8,128)(2,1)} %pad_maximum_fusion.6), calls=%async_computation | async-start | bytes 262144 | tf_op jit(solution)/shard_map/all_to_all | solution.py:572
  14.7 0.9 reshape.287
  15.6 2.0 all-to-all-done
  17.7 27.3 %all_to_all.46 = bf16[8,392,256]{2,1,0:T(8,128)(2,1)S(1)} all-to-all(bf16[8,392,256]{2,1,0:T(8,128)(2,1)S(1)} %broadcast_in_dim.43), channel_id=1, replica_groups={{0,1,2,3,4,5,6,7},{8,9,10,11,12,13,14,15},{16,17,18,19,20,21,22,23},{24..., dimensions={0} | all-to-all | bytes 3211264 | tf_op jit(solution)/shard_map/all_to_all | solution.py:55
  45.1 1.2 copy-done.16
  46.3 1.5 broadcast_in_dim.45
  47.9 4.2 %all-to-all-start.2 = ((bf16[4,4,272,256]{3,2,1,0:T(8,128)(2,1)}), bf16[4,4,272,256]{3,2,1,0:T(8,128)(2,1)S(1)}, u32[]{:S(2)}, u32[]{:S(2)}) async-start(bf16[4,4,272,256]{3,2,1,0:T(8,128)(2,1)} %broadcast_in_dim.45), calls=%async_computation.2 | async-start | bytes 4456448 | tf_op jit(solution)/shard_map/all_to_all | solution.py:55
  52.5 1.1 collective-permute-start.2
  53.5 1.3 slice_bitcast_fusion.3
  54.9 1.0 pad_maximum_fusion.5
  55.9 12.5 %all-to-all-done.2.buf_ref = bf16[4,4,272,256]{3,2,1,0:T(8,128)(2,1)S(1)} async-done(((bf16[4,4,272,256]{3,2,1,0:T(8,128)(2,1)}), bf16[4,4,272,256]{3,2,1,0:T(8,128)(2,1)S(1)}, u32[]{:S(2)}, u32[]{:S(2)}) %all-to-all-start.2) | async-done | bytes 2228256 | tf_op jit(solution)/shard_map/all_to_all | solution.py:55
  68.4 3.6 %broadcast_in_dim.49 = bf16[4,4,512,256]{3,2,1,0:T(8,128)(2,1)} broadcast(bf16[4,512,256]{2,1,0:T(8,128)(2,1)} %pad_maximum_fusion.5), dimensions={1,2,3} | broadcast | bytes 5242880 | tf_op jit(solution)/shard_map/broadcast_in_dim | solution.py:595
  72.0 4.9 %all-to-all-start.3 = ((bf16[4,4,512,256]{3,2,1,0:T(8,128)(2,1)}), bf16[4,4,512,256]{3,2,1,0:T(8,128)(2,1)}, u32[]{:S(2)}, u32[]{:S(2)}) async-start(bf16[4,4,512,256]{3,2,1,0:T(8,128)(2,1)} %broadcast_in_dim.49), calls=%async_computation.3 | async-start | bytes 8388608 | tf_op jit(solution)/shard_map/all_to_all | solution.py:55
  77.7 2.1 pad_maximum_fusion.3
  79.9 3.1 %collective-permute-start.1 = (bf16[2,256,1024]{2,1,0:T(8,128)(2,1)}, bf16[2,256,1024]{2,1,0:T(8,128)(2,1)}, u32[]{:S(2)}, u32[]{:S(2)}) collective-permute-start(bf16[2,256,1024]{2,1,0:T(8,128)(2,1)} %pad_maximum_fusion.3), channel_id=1, source_target_pairs={{0,32},{32,0},{64,96},{96,64},{1,33},{33,1},{65,97},{97,65},{2,34}... | collective-permute-start | bytes 3145736 | tf_op jit(solution)/shard_map/ppermute | solution.py:59
  83.0 2.1 pad_maximum_fusion.4
  86.7 1.2 tile.12
  87.9 1.6 copy.73.cos_ref
  89.4 2.1 tile.14
  91.5 2.5 copy.74.sl_ref
  94.1 1.2 tile.31
  95.2 2.5 copy.75.sr_ref
  97.8 3.2 %pad_maximum_fusion.x_ref = bf16[4,256,1024]{2,1,0:T(8,128)(2,1)} fusion(bf16[2,256,1024]{2,1,0:T(8,128)(2,1)} %collective-permute-done.1, bf16[1,256,1024]{2,1,0:T(8,128)(2,1)} %bitcast.1, bf16[1,256,1024]{2,1,0:T(8,128)(2,1)} %bitcast.134), kind=kLoop, calls=%fused_computation.6 | loop fusion | flops 2097152 | bytes 4194304 | tf_op jit(solution)/shard_map/concatenate | solution.py:551
  101.0 2.9 %pad_maximum_fusion.1.cot_ref = bf16[4,256,1024]{2,1,0:T(8,128)(2,1)} fusion(bf16[2,256,1024]{2,1,0:T(8,128)(2,1)} %collective-permute-done.3, bf16[1,256,1024]{2,1,0:T(8,128)(2,1)} %bitcast.8, bf16[1,256,1024]{2,1,0:T(8,128)(2,1)S(1)} %bitcast.139), kind=kLoop, calls=%fused_computation.7 | loop fusion | flops 2097152 | bytes 4194304 | tf_op jit(solution)/shard_map/concatenate | solution.py:553
  104.5 1.2 copy-done.4
  107.3 1.2 copy-done
  108.6 1.2 copy-done.1
  109.8 1.0 copy-done.7
  110.8 21.8 %shard_map.264 = (bf16[1024,1024]{1,0:T(8,128)(2,1)}, bf16[1024,1024]{1,0:T(8,128)(2,1)}, bf16[1024,1024]{1,0:T(8,128)(2,1)}, bf16[1024,256]{1,0:T(8,128)(2,1)S(...) custom-call(s32[32]{0:T(128)S(1)} %convert_element_type.139.ends_ref, ...), custom_call_target="tpu_custom_call" | custom-call | flops 4000000000 | bytes 20000000 | tf_op jit(solution)/shard_map/pallas_call | solution.py:270
  132.6 6.1 %shard_map.268 = bf16[4,4,256,256]{3,2,1,0:T(8,128)(2,1)} custom-call(s32[1]{0:T(128)} %bitcast.9.core_ref, bf16[1024,1024]{1,0:T(8,128)(2,1)} %get-tuple-element.42.ain_ref, bf16[1024,768]{1,0:T(8,128)(2,1)S(1)} %get-tuple-element.39.dqkv_ref, bf16[1024,256]{1,0:T(8,128)(2,1)S(1)} %get-tuple-element.33.ctx_ref, bf16[1024,1024]{1,0:T(8,128)(2,1)} %get-tuple-element.35.gb_ref), custom_call_target="tpu_custom_call" | custom-call | flops 2200000000 | bytes 10000000 | tf_op jit(solution)/shard_map/pallas_call | solution.py:314
  138.7 4.7 %all-to-all-start.4 = ((bf16[4,4,256,256]{3,2,1,0:T(8,128)(2,1)}), bf16[4,4,256,256]{3,2,1,0:T(8,128)(2,1)}, u32[]{:S(2)}, u32[]{:S(2)}) async-start(bf16[4,4,256,256]{3,2,1,0:T(8,128)(2,1)} %shard_map.268), calls=%async_computation.4 | async-start | bytes 4194304 | tf_op jit(solution)/shard_map/all_to_all | solution.py:55
  143.8 8.2 %shard_map.265 = (bf16[4,4,4,16,1024]{4,3,2,1,0:T(8,128)(2,1)S(1)}, bf16[4,4,64,1024]{3,2,1,0:T(8,128)(2,1)S(1)}) custom-call(s32[1]{0:T(128)} %bitcast.9.core_ref, bf16[4,4,512,256]{3,2,1,0:T(8,128)(2,1)} %all-to-all-done.3.buf_ref), custom_call_target="tpu_custom_call" | custom-call | bytes 8000000 | tf_op jit(solution)/shard_map/pallas_call | solution.py:154
  152.0 1.3 copy-done.2
  153.3 1.3 copy-done.3
  154.6 17.5 %shard_map.266 = (bf16[1024,1024]{1,0:T(8,128)(2,1)S(1)}, bf16[1024,1024]{1,0:T(8,128)(2,1)S(1)}, f32[8,1024]{1,0:T(8,128)S(1)}) custom-call(bf16[1024,1024]{1,0:T(8,128)(2,1)} %get-tuple-element.34.min_ref, bf16[1024,1024]{1,0:T(8,128)(2,1)} %get-tuple-element.35.gb_ref, bf16[1024,1024]{1,0:T(8,128)(2,1)} %bitcast.126, bf16[1024,1024]{1,0:T(8,128)(2,1)} %bitcast.128, ...), custom_call_target="tpu_custom_call" | custom-call | flops 8000000000 | bytes 20000000 | tf_op jit(solution)/shard_map/pallas_call | solution.py:419
  172.1 1.3 copy-done.10
  173.4 6.2 %shard_map.270 = bf16[4,4,256,256]{3,2,1,0:T(8,128)(2,1)} custom-call(s32[1]{0:T(128)} %bitcast.9.core_ref, bf16[1024,1024]{1,0:T(8,128)(2,1)S(1)} %get-tuple-element.38.hidden_ref, bf16[1024,1024]{1,0:T(8,128)(2,1)} %get-tuple-element.35.gb_ref), custom_call_target="tpu_custom_call" | custom-call | flops 2200000000 | bytes 6000000 | tf_op jit(solution)/shard_map/pallas_call | solution.py:345
  179.6 1.3 copy-done.12
  180.9 4.6 %all-to-all-start.6 = ((bf16[4,4,256,256]{3,2,1,0:T(8,128)(2,1)}), bf16[4,4,256,256]{3,2,1,0:T(8,128)(2,1)}, u32[]{:S(2)}, u32[]{:S(2)}) async-start(bf16[4,4,256,256]{3,2,1,0:T(8,128)(2,1)} %shard_map.270), calls=%async_computation.6 | async-start | bytes 4194304 | tf_op jit(solution)/shard_map/all_to_all | solution.py:55
  185.8 1.4 copy-done.5
  187.2 13.2 %shard_map.267 = (bf16[4,2,256,1024]{3,2,1,0:T(8,128)(2,1)}, f32[8,1024]{1,0:T(8,128)S(1)}) custom-call(bf16[4,256,1024]{2,1,0:T(8,128)(2,1)} %pad_maximum_fusion.x_ref, bf16[1024,256]{1,0:T(8,128)(2,1)S(1)} %get-tuple-element.33.ctx_ref, bf16[1024,1024]{1,0:T(8,128)(2,1)} %copy-done.12, bf16[1024,768]{1,0:T(8,128)(2,1)S(1)} %get-tuple-element.39.dqkv_ref, ...), custom_call_target="tpu_custom_call" | custom-call | flops 6499999744 | bytes 20000000 | tf_op jit(solution)/shard_map/pallas_call | solution.py:478
  201.4 1.6 copy-done.9
  203.0 1.6 copy-done.11
  204.6 4.7 %shard_map.269 = bf16[4,4,272,256]{3,2,1,0:T(8,128)(2,1)} custom-call(s32[1]{0:T(128)} %bitcast.9.core_ref, bf16[1024,1024]{1,0:T(8,128)(2,1)S(1)} %copy-done.9, bf16[1024,1024]{1,0:T(8,128)(2,1)S(1)} %copy-done.11, bf16[4,4,16,256]{3,2,1,0:T(8,128)(2,1)S(1)} %pad_bitcast_fusion.small_ref), custom_call_target="tpu_custom_call" | custom-call | flops 2200000000 | bytes 6000000 | tf_op jit(solution)/shard_map/pallas_call | solution.py:385
  209.3 4.2 %all-to-all-start.5 = ((bf16[4,4,272,256]{3,2,1,0:T(8,128)(2,1)}), bf16[4,4,272,256]{3,2,1,0:T(8,128)(2,1)S(1)}, u32[]{:S(2)}, u32[]{:S(2)}) async-start(bf16[4,4,272,256]{3,2,1,0:T(8,128)(2,1)} %shard_map.269), calls=%async_computation.5 | async-start | bytes 4456448 | tf_op jit(solution)/shard_map/all_to_all | solution.py:55
  213.5 3.2 %slice.170 = bf16[2,2,256,1024]{3,2,1,0:T(8,128)(2,1)} slice(bf16[4,2,256,1024]{3,2,1,0:T(8,128)(2,1)} %get-tuple-element.41), slice={[2:4], [0:2], [0:256], [0:1024]} | slice | bytes 4194304 | tf_op jit(solution)/shard_map/slice | solution.py:625
  216.7 1.5 collective-permute-start.4
  218.3 2.8 reduce_sum.121
  221.2 1.1 copy.78
  222.3 2.8 reduce_sum.123
  225.1 1.9 copy.81
  227.0 2.9 %all-to-all-done.5 = bf16[4,4,272,256]{3,2,1,0:T(8,128)(2,1)S(1)} async-done(((bf16[4,4,272,256]{3,2,1,0:T(8,128)(2,1)}), bf16[4,4,272,256]{3,2,1,0:T(8,128)(2,1)S(1)}, u32[]{:S(2)}, u32[]{:S(2)}) %all-to-all-start.5) | async-done | bytes 2228256 | tf_op jit(solution)/shard_map/all_to_all | solution.py:55
  230.9 1.3 pad_maximum_fusion.2
  232.2 4.2 %all-to-all-start.7 = ((bf16[8,392,256]{2,1,0:T(8,128)(2,1)}), bf16[8,392,256]{2,1,0:T(8,128)(2,1)S(1)}, u32[]{:S(2)}, u32[]{:S(2)}) async-start(bf16[8,392,256]{2,1,0:T(8,128)(2,1)} %pad_maximum_fusion.2), calls=%async_computation.7 | async-start | bytes 3211264 | tf_op jit(solution)/shard_map/all_to_all | solution.py:55
  237.9 3.1 %convert_add_fusion = f32[2,2,256,1024]{3,2,1,0:T(8,128)S(1)} fusion(bf16[2,2,256,1024]{3,2,1,0:T(8,128)(2,1)} %collective-permute-done.4, bf16[4,2,256,1024]{3,2,1,0:T(8,128)(2,1)} %get-tuple-element.41), kind=kLoop, calls=%fused_computation.1 | loop fusion | flops 3145728 | bytes 8388608 | tf_op jit(solution)/shard_map/add | solution.py:625
  241.1 1.9 copy-done.15
  243.0 1.1 fusion.12
  244.3 8.7 %all-to-all-done.7 = bf16[8,392,256]{2,1,0:T(8,128)(2,1)S(1)} async-done(((bf16[8,392,256]{2,1,0:T(8,128)(2,1)}), bf16[8,392,256]{2,1,0:T(8,128)(2,1)S(1)}, u32[]{:S(2)}, u32[]{:S(2)}) %all-to-all-start.7) | async-done | bytes 1605664 | tf_op jit(solution)/shard_map/all_to_all | solution.py:55
  254.1 10.5 %all-to-all-start.8 = ((f32[4,64,256]{2,1,0:T(8,128)}), f32[4,64,256]{2,1,0:T(8,128)S(1)}, u32[]{:S(2)}, u32[]{:S(2)}) async-start(f32[4,64,256]{2,1,0:T(8,128)} %select_maximum_fusion), calls=%async_computation.8 | async-start | bytes 524288 | tf_op jit(solution)/shard_map/all_to_all | solution.py:692
  266.0 10.2 %collective-permute-done.5 = bf16[2,256,1024]{2,1,0:T(8,128)(2,1)} collective-permute-done((bf16[2,256,1024]{2,1,0:T(8,128)(2,1)}, bf16[2,256,1024]{2,1,0:T(8,128)(2,1)}, u32[]{:S(2)}, u32[]{:S(2)}) %collective-permute-start.5) | collective-permute-done | bytes 1048608 | tf_op jit(solution)/shard_map/ppermute | solution.py:63
  276.2 2.2 fusion
  279.4 1.6 fusion.8
  (166 shorter events, 19.5 us)
Async XLA Ops:
  9.2 8.3 %all-to-all-start = ((bf16[4,64,256]{2,1,0:T(8,128)(2,1)}), bf16[4,64,256]{2,1,0:T(8,128)(2,1)S(1)}, u32[]{:S(2)}, u32[]{:S(2)}) async-start(bf16[4,64,256]{2,1,0:T(8,128)(2,1)} %pad_maximum_fusion.6), calls=%async_computation | async-start | bytes 262144 | tf_op jit(solution)/shard_map/all_to_all | solution.py:572
  45.1 1.2 copy-start.16
  47.9 4.2 %copy-start.13 = (bf16[256,1024]{1,0:T(8,128)(2,1)S(1)}, bf16[256,1024]{1,0:T(8,128)(2,1)}, u32[]{:S(2)}) copy-start(bf16[256,1024]{1,0:T(8,128)(2,1)} %param.16) | copy-start | bytes 1572868
  47.9 4.6 %copy-start.17 = (bf16[256,1024]{1,0:T(8,128)(2,1)S(1)}, bf16[256,1024]{1,0:T(8,128)(2,1)}, u32[]{:S(2)}) copy-start(bf16[256,1024]{1,0:T(8,128)(2,1)} %param.17) | copy-start | bytes 1572868
  47.9 5.7 %copy-start.22 = (s32[4]{0:T(128)S(1)}, s32[4]{0:T(128)}, u32[]{:S(2)}) copy-start(s32[4]{0:T(128)} %constant.53.clone) | copy-start | bytes 52
  47.9 20.6 %all-to-all-start.2 = ((bf16[4,4,272,256]{3,2,1,0:T(8,128)(2,1)}), bf16[4,4,272,256]{3,2,1,0:T(8,128)(2,1)S(1)}, u32[]{:S(2)}, u32[]{:S(2)}) async-start(bf16[4,4,272,256]{3,2,1,0:T(8,128)(2,1)} %broadcast_in_dim.45), calls=%async_computation.2 | async-start | bytes 4456448 | tf_op jit(solution)/shard_map/all_to_all | solution.py:55
  52.1 25.7 %collective-permute-start = (bf16[256,1024]{1,0:T(8,128)(2,1)S(1)}, bf16[256,1024]{1,0:T(8,128)(2,1)}, u32[]{:S(2)}, u32[]{:S(2)}) collective-permute-start(bf16[256,1024]{1,0:T(8,128)(2,1)S(1)} %copy-done.13), channel_id=1, source_target_pairs={{0,64},{64,0},{32,96},{96,32},{1,65},{65,1},{33,97},{97,33},{2,66}... | collective-permute-start | bytes 1572872 | tf_op jit(solution)/shard_map/ppermute | solution.py:63
  52.5 30.5 %collective-permute-start.2 = (bf16[256,1024]{1,0:T(8,128)(2,1)S(1)}, bf16[256,1024]{1,0:T(8,128)(2,1)}, u32[]{:S(2)}, u32[]{:S(2)}) collective-permute-start(bf16[256,1024]{1,0:T(8,128)(2,1)S(1)} %copy-done.17), channel_id=1, source_target_pairs={{0,64},{64,0},{32,96},{96,32},{1,65},{65,1},{33,97},{97,33},{2,66}... | collective-permute-start | bytes 1572872 | tf_op jit(solution)/shard_map/ppermute | solution.py:63
  72.0 66.7 %all-to-all-start.3 = ((bf16[4,4,512,256]{3,2,1,0:T(8,128)(2,1)}), bf16[4,4,512,256]{3,2,1,0:T(8,128)(2,1)}, u32[]{:S(2)}, u32[]{:S(2)}) async-start(bf16[4,4,512,256]{3,2,1,0:T(8,128)(2,1)} %broadcast_in_dim.49), calls=%async_computation.3 | async-start | bytes 8388608 | tf_op jit(solution)/shard_map/all_to_all | solution.py:55
  77.7 8.1 %copy-start.21 = (f32[64]{0:T(128)S(1)}, f32[64]{0:T(128)}, u32[]{:S(2)}) copy-start(f32[64]{0:T(128)} %pad.70.clone) | copy-start | bytes 772
  79.9 17.9 %collective-permute-start.1 = (bf16[2,256,1024]{2,1,0:T(8,128)(2,1)}, bf16[2,256,1024]{2,1,0:T(8,128)(2,1)}, u32[]{:S(2)}, u32[]{:S(2)}) collective-permute-start(bf16[2,256,1024]{2,1,0:T(8,128)(2,1)} %pad_maximum_fusion.3), channel_id=1, source_target_pairs={{0,32},{32,0},{64,96},{96,64},{1,33},{33,1},{65,97},{97,65},{2,34}... | collective-permute-start | bytes 3145736 | tf_op jit(solution)/shard_map/ppermute | solution.py:59
  85.1 15.9 %collective-permute-start.3 = (bf16[2,256,1024]{2,1,0:T(8,128)(2,1)}, bf16[2,256,1024]{2,1,0:T(8,128)(2,1)}, u32[]{:S(2)}, u32[]{:S(2)}) collective-permute-start(bf16[2,256,1024]{2,1,0:T(8,128)(2,1)} %pad_maximum_fusion.4), channel_id=1, source_target_pairs={{0,32},{32,0},{64,96},{96,64},{1,33},{33,1},{65,97},{97,65},{2,34}... | collective-permute-start | bytes 3145736 | tf_op jit(solution)/shard_map/ppermute | solution.py:59
  97.8 3.2 %copy-start.18 = (bf16[256,1024]{1,0:T(8,128)(2,1)S(1)}, bf16[256,1024]{1,0:T(8,128)(2,1)}, u32[]{:S(2)}) copy-start(bf16[256,1024]{1,0:T(8,128)(2,1)} %param.17) | copy-start | bytes 1572868
  104.5 1.2 copy-start.4
  105.7 0.8 copy-start.6
  107.3 1.2 copy-start
  108.5 1.2 copy-start.1
  109.8 1.0 copy-start.7
  138.7 42.2 %all-to-all-start.4 = ((bf16[4,4,256,256]{3,2,1,0:T(8,128)(2,1)}), bf16[4,4,256,256]{3,2,1,0:T(8,128)(2,1)}, u32[]{:S(2)}, u32[]{:S(2)}) async-start(bf16[4,4,256,256]{3,2,1,0:T(8,128)(2,1)} %shard_map.268), calls=%async_computation.4 | async-start | bytes 4194304 | tf_op jit(solution)/shard_map/all_to_all | solution.py:55
  152.0 1.3 copy-start.2
  153.3 1.3 copy-start.3
  172.1 1.3 copy-start.10
  179.6 1.3 copy-start.12
  180.9 4.9 %copy-start.8 = (bf16[4,4,16,1024]{3,2,1,0:T(8,128)(2,1)S(1)}, bf16[4,4,16,1024]{3,2,1,0:T(8,128)(2,1)}, u32[]{:S(2)}) copy-start(bf16[4,4,16,1024]{3,2,1,0:T(8,128)(2,1)} %copy-done.6) | copy-start | bytes 1572868
  180.9 28.4 %all-to-all-start.6 = ((bf16[4,4,256,256]{3,2,1,0:T(8,128)(2,1)}), bf16[4,4,256,256]{3,2,1,0:T(8,128)(2,1)}, u32[]{:S(2)}, u32[]{:S(2)}) async-start(bf16[4,4,256,256]{3,2,1,0:T(8,128)(2,1)} %shard_map.270), calls=%async_computation.6 | async-start | bytes 4194304 | tf_op jit(solution)/shard_map/all_to_all | solution.py:55
  185.8 1.4 copy-start.5
  201.4 1.6 copy-start.9
  203.0 1.6 copy-start.11
  209.3 20.5 %all-to-all-start.5 = ((bf16[4,4,272,256]{3,2,1,0:T(8,128)(2,1)}), bf16[4,4,272,256]{3,2,1,0:T(8,128)(2,1)S(1)}, u32[]{:S(2)}, u32[]{:S(2)}) async-start(bf16[4,4,272,256]{3,2,1,0:T(8,128)(2,1)} %shard_map.269), calls=%async_computation.5 | async-start | bytes 4456448 | tf_op jit(solution)/shard_map/all_to_all | solution.py:55
  213.5 4.7 %copy-start.14 = (bf16[256,1024]{1,0:T(8,128)(2,1)S(1)}, bf16[256,1024]{1,0:T(8,128)(2,1)}, u32[]{:S(2)}) copy-start(bf16[256,1024]{1,0:T(8,128)(2,1)} %param.16) | copy-start | bytes 1572868
  216.7 21.2 %collective-permute-start.4 = (bf16[2,2,256,1024]{3,2,1,0:T(8,128)(2,1)}, bf16[2,2,256,1024]{3,2,1,0:T(8,128)(2,1)}, u32[]{:S(2)}, u32[]{:S(2)}) collective-permute-start(bf16[2,2,256,1024]{3,2,1,0:T(8,128)(2,1)} %slice.170), channel_id=1, source_target_pairs={{0,32},{32,0},{64,96},{96,64},{1,33},{33,1},{65,97},{97,65},{2,34}... | collective-permute-start | bytes 6291464 | tf_op jit(solution)/shard_map/ppermute | solution.py:59
  229.8 1.0 copy-start.20
  232.2 20.9 %all-to-all-start.7 = ((bf16[8,392,256]{2,1,0:T(8,128)(2,1)}), bf16[8,392,256]{2,1,0:T(8,128)(2,1)S(1)}, u32[]{:S(2)}, u32[]{:S(2)}) async-start(bf16[8,392,256]{2,1,0:T(8,128)(2,1)} %pad_maximum_fusion.2), calls=%async_computation.7 | async-start | bytes 3211264 | tf_op jit(solution)/shard_map/all_to_all | solution.py:55
  241.0 1.9 copy-start.15
  244.1 32.1 %collective-permute-start.5 = (bf16[2,256,1024]{2,1,0:T(8,128)(2,1)}, bf16[2,256,1024]{2,1,0:T(8,128)(2,1)}, u32[]{:S(2)}, u32[]{:S(2)}) collective-permute-start(bf16[2,256,1024]{2,1,0:T(8,128)(2,1)} %fusion.12), channel_id=1, source_target_pairs={{0,64},{64,0},{32,96},{96,32},{1,65},{65,1},{33,97},{97,33},{2,66}... | collective-permute-start | bytes 3145736 | tf_op jit(solution)/shard_map/ppermute | solution.py:63
  254.1 26.9 %all-to-all-start.8 = ((f32[4,64,256]{2,1,0:T(8,128)}), f32[4,64,256]{2,1,0:T(8,128)S(1)}, u32[]{:S(2)}, u32[]{:S(2)}) async-start(f32[4,64,256]{2,1,0:T(8,128)} %select_maximum_fusion), calls=%async_computation.8 | async-start | bytes 524288 | tf_op jit(solution)/shard_map/all_to_all | solution.py:692
  278.3 1.0 copy-start.19

commit v2 on v0

v2 whole, which is shorter than its diff:
```python
import jax
import jax.numpy as jnp
import ml_dtypes
import numpy as np
from jax import lax
from jax.experimental import pallas as pl
from jax.experimental.pallas import tpu as pltpu
from jax.sharding import PartitionSpec as P

D = 1024
HEADS = 16
HEAD_DIM = 64
ROT = 16
FF = 4096
ROW = 256
SEGS = 8
TP = 4
QC = 3 * D // TP
HC = FF // TP
LOCAL_HEADS = HEADS // TP
AXES = ("dp", "fsdp")
VMEM = 36 * 1024 * 1024

f32 = jnp.float32
bf16 = jnp.bfloat16


def dev(d, y, x, zh):
    return d * 32 + y * 8 + x * 2 + zh


def outer_groups(flip=0):
    groups = []
    for d in range(4):
        for k in range(4):
            for zh in range(2):
                if d % 2 == flip:
                    groups.append([dev(d, i, k, zh) for i in range(4)])
                else:
                    groups.append([dev(d, k, i, zh) for i in range(4)])
    return groups


def inner_groups():
    return outer_groups(flip=1)


def stack_groups():
    return [
        [dev(d, y, x, zh) for d in range(4) for zh in range(2)] for y in range(4) for x in range(4)
    ]


def plane_groups():
    return [
        [dev(d, y, x, zh) for y in range(4) for x in range(4)] for d in range(4) for zh in range(2)
    ]


def outer_flip(values, step):
    pairs = [(g[i], g[i ^ step]) for g in outer_groups() for i in range(4)]
    return lax.ppermute(values, AXES, pairs)


def a2a(values, groups):
    return lax.all_to_all(values, AXES, 0, 0, tiled=True, axis_index_groups=groups)


def flip_core(values):
    return lax.ppermute(values, "dp", [(0, 1), (1, 0), (2, 3), (3, 2)])


def flip_chip(values):
    return lax.ppermute(values, "dp", [(0, 2), (2, 0), (1, 3), (3, 1)])


def flip_far(values):
    return lax.ppermute(values, "fsdp", [(i, i ^ 1) for i in range(32)])


def dot(left, right):
    return jnp.dot(left, right, preferred_element_type=f32)


def dot_nt(left, right):
    return lax.dot_general(left, right, (((1,), (1,)), ((), ())), preferred_element_type=f32)


def dot_tn(left, right):
    return lax.dot_general(left, right, (((0,), (0,)), ((), ())), preferred_element_type=f32)


def in_hbm(values):
    return pltpu.with_memory_space_constraint(values, pltpu.HBM)


VMEM_SPEC = pl.BlockSpec(memory_space=pltpu.VMEM)
SMEM_SPEC = pl.BlockSpec(memory_space=pltpu.SMEM)
HBM_SPEC = pl.BlockSpec(memory_space=pltpu.HBM)
SPECS = {"s": SMEM_SPEC, "v": VMEM_SPEC, "h": HBM_SPEC}


def call(kernel, out_shape, *args, places=None, outs=None, scratch=(), flops=0, nbytes=0, trans=0):
    places = places or "s" + "v" * (len(args) - 1)
    out_specs = jax.tree.map(lambda _: VMEM_SPEC, out_shape)
    if outs is not None:
        out_specs = [SPECS[o] for o in outs]
        out_shape = [
            pltpu.HBM(v.shape, v.dtype) if o == "h" else v for o, v in zip(outs, out_shape)
        ]
    args = [in_hbm(v) if p == "h" else v for p, v in zip(places, args)]
    return pl.pallas_call(
        kernel,
        in_specs=[SPECS[p] for p in places],
        out_specs=out_specs,
        out_shape=out_shape,
        scratch_shapes=list(scratch),
        compiler_params=pltpu.CompilerParams(vmem_limit_bytes=VMEM),
        cost_estimate=pl.CostEstimate(
            flops=int(flops), bytes_accessed=int(nbytes), transcendentals=int(trans)
        ),
    )(*args)


def shaped(*shape, dtype=bf16):
    return jax.ShapeDtypeStruct(shape, dtype)


def normalize(x):
    average = jnp.mean(x, axis=-1, keepdims=True)
    centred = x - average
    inv_std = lax.rsqrt(jnp.mean(centred * centred, axis=-1, keepdims=True) + 1e-05)
    return centred * inv_std, inv_std


STARTS = (0, 4, 8, 12, 16, 28, 32, 48)
SIZES = (8, 8, 8, 8, 24, 8, 32, 8)
IMAGE = 64
LENS = 52
SLOT = QC + HC + IMAGE // 8 * 256


def tile(n):
    return pl.ds(pl.multiple_of(n * 256, 256), 256)


def swapped(y, x, c):
    return y + c * (x - y), x + c * (y - x)


def prepare_kernel(
    place_ref, qkv_ref, up_ref, dense_in, down_in, len_in, n1g, n1b, n2g, n2b, qb, db, ub, dnb,
    out_ref, pieces_ref, image_ref, *rest
):
    sources = (len_in, n1g, n1b, n2g, n2b, qb, db, ub, dnb)
    holders, sem = rest[:9], rest[9]
    copies = [
        pltpu.make_async_copy(src, dst, sem.at[i])
        for i, (src, dst) in enumerate(zip(sources, holders))
    ]
    for copy in copies:
        copy.start()
    for d in range(4):
        for zh in range(2):
            s = d * 2 + zh
            for p in range(3):
                at = p * D + d * 256
                out_ref[s, :, p * 256 : (p + 1) * 256] = qkv_ref[:, at : at + 256]
            out_ref[s, :, QC : QC + HC] = up_ref[:, d * HC : (d + 1) * HC]
    pieces_ref[0:32, :] = down_in[...]
    pieces_ref[32:40, :] = dense_in[...]
    image_ref[...] = jnp.zeros_like(image_ref)
    for copy in copies:
        copy.wait()
    p = place_ref[0]
    for start, size, ref in zip(STARTS, SIZES, holders[1:]):
        first = p * size
        row, lane = start + first // 256, first % 256
        wide = 512 if size == 24 else 256
        values = jnp.concatenate(
            [ref[...].astype(f32), jnp.zeros((1, wide - size), f32)], axis=1
        )
        values = pltpu.roll(values, lane, 1)
        image_ref[pl.ds(row, 1), :] = values[:, :256]
        if wide == 512:
            image_ref[pl.ds(row + 1, 1), :] = values[:, 256:]
    lens = jnp.concatenate(
        [holders[0][...].astype(f32), jnp.zeros((1, 256 - SEGS), f32)], axis=1
    )
    image_ref[LENS : LENS + 1, :] = pltpu.roll(lens, place_ref[1] * SEGS, 1)
    for g in range(IMAGE // 8):
        block = image_ref[g * 8 : (g + 1) * 8, :].astype(bf16)
        at = QC + HC + g * 256
        for s in range(8):
            out_ref[s, :, at : at + 256] = block


def prepare(place, qkv, up, dense, down, lengths, vectors):
    vectors = [v[None, :] for v in vectors]
    return call(
        prepare_kernel,
        [shaped(8, 8, SLOT), shaped(40, D)],
        place,
        qkv,
        up,
        dense,
        down,
        lengths,
        *vectors,
        places="svvvv" + "h" * 9,
        scratch=[pltpu.VMEM((IMAGE, 256), f32), pltpu.VMEM((1, SEGS), jnp.int32)]
        + [pltpu.VMEM(v.shape, bf16) for v in vectors]
        + [pltpu.SemaphoreType.DMA((9,))],
        nbytes=1e6,
    )


def spread_kernel(far_ref, first_ref, mine_ref, theirs_ref, out_ref, lens_ref):
    far = far_ref[0] == 1
    mine, theirs = mine_ref[...].astype(f32), theirs_ref[...].astype(f32)
    low, high = jnp.where(far, theirs, mine), jnp.where(far, mine, theirs)
    down = jnp.concatenate([low[:32], high[:32]], axis=0).astype(bf16)
    dense = jnp.concatenate([low[32:], high[32:]], axis=0).astype(bf16)
    images = []
    for g in range(IMAGE // 8):
        at = QC + HC + g * 256
        parts = [first_ref[d, :, at : at + 256].astype(f32) for d in range(4)]
        total = sum(parts)
        images.append(total[:8] + total[8:])
    image = jnp.concatenate(images, axis=0)
    lens_ref[...] = image[LENS : LENS + 1, :].astype(jnp.int32)
    image = image.astype(bf16)
    for i in range(4):
        for d in range(4):
            for p in range(3):
                row = (d * 3 + p) * 16
                out_ref[i, row : row + 16, :] = first_ref[d, :, p * 256 : (p + 1) * 256]
            for cg in range(4):
                row = 256 + (d * 4 + cg) * 16
                at = QC + cg * 256
                out_ref[i, row : row + 16, :] = first_ref[d, :, at : at + 256]
        for cg in range(4):
            at = slice(cg * 256, (cg + 1) * 256)
            out_ref[i, 192 + cg * 16 : 208 + cg * 16, :] = dense[:, at]
            out_ref[i, 512 + cg * 64 : 576 + cg * 64, :] = down[:, at]
        out_ref[i, 768 : 768 + IMAGE, :] = image


def spread(far, first, mine, theirs):
    return call(
        spread_kernel,
        [shaped(4, 768 + IMAGE, 256), shaped(1, 256, dtype=jnp.int32)],
        far,
        first,
        mine,
        theirs,
        nbytes=2e6,
    )


def widen_kernel(in_ref, a_ref, b_ref):
    image = sum([in_ref[a, 768 : 768 + IMAGE, :].astype(f32) for a in range(4)]).astype(bf16)

    @pl.loop(0, 4)
    def _(i):
        for a in range(4):
            a_ref[i, a * 256 : (a + 1) * 256, :] = in_ref[a, 0:256, :]
            b_ref[i, a * 512 : (a + 1) * 512, :] = in_ref[a, 256:768, :]
        a_ref[i, 1024 : 1024 + IMAGE, :] = image


def widen(second):
    return call(
        widen_kernel,
        [shaped(4, 1024 + IMAGE, 256), shaped(4, 2048, 256)],
        second,
        places="v",
        nbytes=8e6,
    )


def assemble_a(me, buf_ref, wqkv_ref, wd_ref):
    c = me % 2
    for y in range(4):
        for x in range(4):
            b, a = swapped(y, x, c)
            yx = y * 4 + x
            base = a * 256
            for d in range(4):
                for p in range(3):
                    row = pl.multiple_of(base + (d * 3 + p) * 16, 16)
                    wqkv_ref[d * 256 + yx * 16 : d * 256 + yx * 16 + 16, p * 256 : (p + 1) * 256] = (
                        buf_ref[b, pl.ds(row, 16), :]
                    )
            for cg in range(4):
                row = pl.multiple_of(base + 192 + cg * 16, 16)
                wd_ref[yx * 16 : yx * 16 + 16, cg * 256 : (cg + 1) * 256] = buf_ref[
                    b, pl.ds(row, 16), :
                ]


def read_vectors(me, buf_ref, vec_ref, qb_ref, ub_ref):
    image = sum([buf_ref[b, 1024 : 1024 + IMAGE, :].astype(f32) for b in range(4)])

    def long(start):
        return jnp.concatenate([image[start + i : start + i + 1, :] for i in range(4)], axis=1)

    vec_ref[...] = jnp.zeros_like(vec_ref)
    for i in range(4):
        vec_ref[i : i + 1, :] = long(4 * i)
    vec_ref[4:5, :] = long(28) + long(48)
    own = [jnp.where(me == d, 1.0, 0.0) for d in range(4)]
    rows = [sum([image[16 + p * 4 + d : 17 + p * 4 + d] * own[d] for d in range(4)]) for p in range(3)]
    qb_ref[...] = jnp.concatenate(rows, axis=1)
    ub_ref[...] = sum([long(32 + 4 * d) * own[d] for d in range(4)])


def assemble_b(me, buf_ref, wup_ref, wdown_ref):
    c = me % 2
    for y in range(4):
        for x in range(4):
            b, a = swapped(y, x, c)
            yx = y * 4 + x
            base = a * 512
            for d in range(4):
                for cg in range(4):
                    row = pl.multiple_of(base + (d * 4 + cg) * 16, 16)
                    wup_ref[d * 256 + yx * 16 : d * 256 + yx * 16 + 16, cg * 256 : (cg + 1) * 256] = (
                        buf_ref[b, pl.ds(row, 16), :]
                    )
            for cg in range(4):
                row = pl.multiple_of(base + 256 + cg * 64, 16)
                wdown_ref[yx * 64 : yx * 64 + 64, cg * 256 : (cg + 1) * 256] = buf_ref[
                    b, pl.ds(row, 64), :
                ]


def turn(u, cosine, sin_left, sin_right):
    return (
        u * cosine
        + pltpu.roll(u, u.shape[1] - ROT // 2, 1) * sin_left
        + pltpu.roll(u, ROT // 2, 1) * sin_right
    )


def rotary_tables():
    places = np.arange(ROW, dtype=np.float32)
    freqs = (10000.0 ** (-(np.arange(ROT // 2, dtype=np.float32) * 2.0) / ROT)).astype(np.float32)
    angle = (places[:, None] * freqs[None, :]).astype(np.float32)
    cosine, sine = np.cos(angle), np.sin(angle)
    zeros = np.zeros_like(sine)
    rest = np.zeros((ROW, HEAD_DIM - ROT), np.float32)
    parts = [[cosine, cosine, rest + 1.0], [-sine, zeros, rest], [zeros, sine, rest]]
    columns = []
    for part in parts:
        whole = np.tile(np.concatenate(part, axis=1), (1, 2)).astype(np.float32)
        high = whole.astype(ml_dtypes.bfloat16)
        columns += [high, (whole - high.astype(np.float32)).astype(ml_dtypes.bfloat16)]
    return np.concatenate(columns, axis=1)


def attention_kernel(
    info_ref,
    x0,
    x1,
    x2,
    x3,
    c0,
    c1,
    c2,
    c3,
    buf_ref,
    rot_ref,
    sent_out,
    min_out,
    gb_out,
    ctx_out,
    dqkv_out,
    wqkv_out,
    wd_out,
    vec_ref,
    ub_ref,
    sums_ref,
    x_ref,
    cot_ref,
    wqkv_ref,
    wd_ref,
    qb_ref,
    ain_ref,
    min_ref,
    gb_ref,
    ctx_ref,
    dqkv_ref,
    sent_ref,
    in_sem,
    out_sem,
    weight_sem,
    sent_sem,
):
    me = info_ref[64]
    loads = []
    for i, (one, other) in enumerate(zip((x0, x1, x2, x3), (c0, c1, c2, c3))):
        loads.append(pltpu.make_async_copy(one, x_ref.at[i], in_sem.at[i, 0]))
        loads.append(pltpu.make_async_copy(other, cot_ref.at[i], in_sem.at[i, 1]))
    for load in loads:
        load.start()
    assemble_a(me, buf_ref, wqkv_ref, wd_ref)
    read_vectors(me, buf_ref, vec_ref, qb_ref, ub_ref)
    weights = [
        pltpu.make_async_copy(wqkv_ref, wqkv_out, weight_sem.at[0]),
        pltpu.make_async_copy(wd_ref, wd_out, weight_sem.at[1]),
    ]
    for copy in weights:
        copy.start()
    stores = ((min_ref, min_out), (gb_ref, gb_out), (ctx_ref, ctx_out), (dqkv_ref, dqkv_out))

    def store(n, r):
        rows = pl.ds(pl.multiple_of(r * ROW, ROW), ROW)
        src, dst = stores[n]
        return pltpu.make_async_copy(src.at[rows, :], dst.at[rows, :], out_sem.at[n, r])

    sums_ref[...] = jnp.zeros_like(sums_ref)

    @pl.loop(0, TP)
    def _(r):
        pltpu.make_async_copy(x0, x_ref.at[r], in_sem.at[r, 0]).wait()
        pltpu.make_async_copy(c0, cot_ref.at[r], in_sem.at[r, 1]).wait()
        here = pl.ds(pl.multiple_of(r * ROW, ROW), ROW)
        xhat, _ = normalize(x_ref[r].astype(f32))
        attn_in = (xhat * vec_ref[0:1] + vec_ref[1:2]).astype(bf16)
        ain_ref[here, :] = attn_in
        min_ref[here, :] = (xhat * vec_ref[2:3] + vec_ref[3:4]).astype(bf16)
        qkv = dot(attn_in, wqkv_ref[...]) + qb_ref[...]
        d = me ^ ((r & 1) * 2 + r // 2)
        base = (d * 2 + info_ref[65]) * SEGS
        ends, end = [], 0
        for j in range(SEGS - 1):
            end = end + info_ref[base + j]
            ends.append(end)
        rows = lax.broadcasted_iota(jnp.int32, (ROW, 1), 0)
        cols = lax.broadcasted_iota(jnp.int32, (1, ROW), 1)
        row_doc = sum([(rows >= e).astype(jnp.int32) for e in ends])
        col_doc = sum([(cols >= e).astype(jnp.int32) for e in ends])
        allowed = (row_doc == col_doc) & (cols <= rows)
        start = jnp.zeros_like(rows)
        for e in ends:
            start = jnp.maximum(start, jnp.where(rows >= e, e, 0))
        kept = jnp.where(rows < ends[-1], cot_ref[r].astype(f32), 0.0)
        gb = kept.astype(bf16)
        gb_ref[here, :] = gb
        dctx = dot_nt(gb, wd_ref[...]).astype(bf16)
        chosen = ((rows - start) == cols).astype(f32).astype(bf16)
        table = dot(chosen, rot_ref[...])
        pair = lambda n: table[:, n * 256 : n * 256 + 128] + table[:, n * 256 + 128 : n * 256 + 256]
        cosine, left, right = [jnp.concatenate([pair(n)] * 2, axis=1) for n in range(3)]
        q = turn(qkv[:, 0:256], cosine, left, right).astype(bf16)
        k = turn(qkv[:, 256:512], cosine, left, right).astype(bf16)
        v = qkv[:, 512:768].astype(bf16)
        scale = HEAD_DIM**-0.5
        ctx, dq, dk, dv = [], [], [], []
        for h in range(LOCAL_HEADS):
            at = slice(h * HEAD_DIM, (h + 1) * HEAD_DIM)
            qh, kh, vh, dch = q[:, at], k[:, at], v[:, at], dctx[:, at]
            scores = jnp.where(allowed, dot_nt(qh, kh) * scale, -1000000000.0)
            shifted = jnp.exp(scores - jnp.max(scores, axis=-1, keepdims=True))
            probs = shifted * (1.0 / jnp.sum(shifted, axis=-1, keepdims=True))
            low = probs.astype(bf16)
            ctx.append(dot(low, vh))
            dv.append(dot_tn(low, dch))
            dprobs = dot_nt(dch, vh)
            inner = jnp.sum(dprobs * probs, axis=-1, keepdims=True)
            ds = (probs * (dprobs - inner)).astype(bf16)
            dq.append(dot(ds, kh) * scale)
            dk.append(dot_tn(ds, qh) * scale)
        ctx_ref[here, :] = jnp.concatenate(ctx, axis=1).astype(bf16)
        dqs = turn(jnp.concatenate(dq, axis=1), cosine, -left, -right)
        dks = turn(jnp.concatenate(dk, axis=1), cosine, -left, -right)
        dqkv = jnp.concatenate([dqs, dks] + dv, axis=1).astype(bf16)
        dqkv_ref[here, :] = dqkv

        @pl.when(r == 0)
        def _():
            sums_ref[0:1, :] = jnp.sum(kept, axis=0, keepdims=True)

        sums_ref[1:2, 0:QC] += jnp.sum(dqkv.astype(f32), axis=0, keepdims=True)
        for n in range(4):
            store(n, r).start()

    c = me % 2

    def sent(d, n):
        rows = pl.ds(pl.multiple_of(d * 48, 16), 48)
        if n == 1:
            rows = pl.ds(pl.multiple_of(192 + d * 16, 16), 16)
        return pltpu.make_async_copy(
            sent_ref.at[:, :, rows, :], sent_out.at[:, :, rows, :], sent_sem.at[d, n]
        )

    @pl.loop(0, 4)
    def _(d):
        qkv_grad = dot_tn(ain_ref[:, tile(d)], dqkv_ref[...]).astype(bf16)
        dense_grad = dot_tn(ctx_ref[...], gb_ref[:, tile(d)]).astype(bf16)
        base = pl.multiple_of(d * 48, 16)
        dense_base = pl.multiple_of(192 + d * 16, 16)
        for y in range(4):
            for x in range(4):
                b, a = swapped(y, x, c)
                at = slice((y * 4 + x) * 16, (y * 4 + x + 1) * 16)
                for p in range(3):
                    sent_ref[b, a, pl.ds(base + p * 16, 16), :] = qkv_grad[
                        at, p * 256 : (p + 1) * 256
                    ]
                sent_ref[b, a, pl.ds(dense_base, 16), :] = dense_grad[at]
        sent(d, 0).start()
        sent(d, 1).start()

    for copy in weights:
        copy.wait()

    @pl.loop(0, 4)
    def _(i):
        for n in range(4):
            store(n, i).wait()
        sent(i, 0).wait()
        sent(i, 1).wait()


def attention(info, xs, cots, buf):
    tokens = TP * ROW
    dma = pltpu.SemaphoreType.DMA
    return call(
        attention_kernel,
        [
            shaped(4, 4, 256, 256),
            shaped(tokens, D),
            shaped(tokens, D),
            shaped(tokens, 256),
            shaped(tokens, QC),
            shaped(D, QC),
            shaped(D // TP, D),
            shaped(8, D, dtype=f32),
            shaped(1, HC, dtype=f32),
            shaped(8, D, dtype=f32),
        ],
        info,
        *xs,
        *cots,
        buf,
        jnp.asarray(rotary_tables()),
        places="s" + "h" * 8 + "vv",
        outs="hhhhhhhvvv",
        scratch=[
            pltpu.VMEM((TP, ROW, D), bf16),
            pltpu.VMEM((TP, ROW, D), bf16),
            pltpu.VMEM((D, QC), bf16),
            pltpu.VMEM((D // TP, D), bf16),
            pltpu.VMEM((1, QC), f32),
            pltpu.VMEM((tokens, D), bf16),
            pltpu.VMEM((tokens, D), bf16),
            pltpu.VMEM((tokens, D), bf16),
            pltpu.VMEM((tokens, 256), bf16),
            pltpu.VMEM((tokens, QC), bf16),
            pltpu.VMEM((4, 4, 256, 256), bf16),
            dma((4, 2)),
            dma((4, 4)),
            dma((2,)),
            dma((4, 2)),
        ],
        flops=6e9,
        nbytes=2e7,
        trans=1e6,
    )


def mlp_kernel(
    me_ref,
    buf_in,
    min_in,
    gb_in,
    ub_ref,
    sent_out,
    hidden_out,
    dpre_out,
    wup_out,
    wdown_out,
    sums_ref,
    buf_ref,
    min_ref,
    gb_ref,
    wup_ref,
    wdown_ref,
    hidden_ref,
    dpre_ref,
    sent_ref,
    buf_sem,
    in_sem,
    out_sem,
    weight_sem,
    sent_sem,
):
    me = me_ref[0]
    c = me % 2
    parts = [pltpu.make_async_copy(buf_in.at[b], buf_ref.at[b], buf_sem.at[b]) for b in range(4)]

    def load(t, n):
        src, dst = ((min_in, min_ref), (gb_in, gb_ref))[n]
        return pltpu.make_async_copy(src.at[tile(t), :], dst.at[tile(t), :], in_sem.at[t, n])

    for part in parts:
        part.start()
    for t in range(4):
        for n in range(2):
            load(t, n).start()
    for part in parts:
        part.wait()
    assemble_b(me, buf_ref, wup_ref, wdown_ref)
    weights = [
        pltpu.make_async_copy(wup_ref, wup_out, weight_sem.at[0]),
        pltpu.make_async_copy(wdown_ref, wdown_out, weight_sem.at[1]),
    ]
    for copy in weights:
        copy.start()
    sums_ref[...] = jnp.zeros_like(sums_ref)

    def store(j, n):
        src, dst = ((hidden_ref, hidden_out), (dpre_ref, dpre_out))[n]
        return pltpu.make_async_copy(src.at[:, tile(j)], dst.at[:, tile(j)], out_sem.at[j, n])

    @pl.loop(0, 16)
    def _(i):
        jn, tn = i // 4, i % 4
        j, t = tile(jn), tile(tn)

        @pl.when(i < 4)
        def _():
            load(tn, 0).wait()
            load(tn, 1).wait()

        pre = dot(min_ref[t, :], wup_ref[:, j]) + ub_ref[:, j]
        back = dot_nt(gb_ref[t, :], wdown_ref[j, :])
        size = jnp.abs(pre) * 0.7071067811865476
        bell = jnp.exp(-0.5 * pre * pre)
        s = 1.0 / (1.0 + 0.3275911 * size)
        poly = s * (
            0.127414796
            + s * (-0.142248368 + s * (0.7107068705 + s * (-0.7265760135 + s * 0.5307027145)))
        )
        tail = poly * bell
        cumul = jnp.where(pre >= 0.0, 1.0 - tail, tail)
        hidden_ref[t, j] = (pre * cumul).astype(bf16)
        dpre = (back * (cumul + pre * (bell * 0.3989422804014327))).astype(bf16)
        dpre_ref[t, j] = dpre
        sums_ref[0:1, j] += jnp.sum(dpre.astype(f32), axis=0, keepdims=True)

        @pl.when(tn == 3)
        def _():
            store(jn, 0).start()
            store(jn, 1).start()

    @pl.loop(0, 4)
    def _(y):
        grad = dot_tn(hidden_ref[:, tile(y)], gb_ref[...]).astype(bf16)
        for x in range(4):
            b, a = swapped(y, x, c)
            for cg in range(4):
                sent_ref[b, a, 256 + cg * 64 : 256 + (cg + 1) * 64, :] = grad[
                    x * 64 : (x + 1) * 64, cg * 256 : (cg + 1) * 256
                ]

    def sent(rows, n):
        return pltpu.make_async_copy(
            sent_ref.at[:, :, rows, :], sent_out.at[:, :, rows, :], sent_sem.at[n]
        )

    below = sent(pl.ds(256, 256), 4)
    below.start()

    def above(d):
        return sent(pl.ds(pl.multiple_of(d * 64, 64), 64), d)

    @pl.loop(0, 4)
    def _(d):
        grad = dot_tn(min_ref[:, tile(d)], dpre_ref[...]).astype(bf16)
        for y in range(4):
            for x in range(4):
                b, a = swapped(y, x, c)
                at = slice((y * 4 + x) * 16, (y * 4 + x + 1) * 16)
                for cg in range(4):
                    row = pl.multiple_of(d * 64 + cg * 16, 16)
                    sent_ref[b, a, pl.ds(row, 16), :] = grad[at, cg * 256 : (cg + 1) * 256]
        above(d).start()

    for copy in weights:
        copy.wait()

    @pl.loop(0, 4)
    def _(i):
        store(i, 0).wait()
        store(i, 1).wait()
        above(i).wait()

    below.wait()


def mlp(me, buf, mlp_in, gb, ub):
    tokens = TP * ROW
    dma = pltpu.SemaphoreType.DMA
    return call(
        mlp_kernel,
        [
            shaped(4, 4, 512, 256),
            shaped(tokens, HC),
            shaped(tokens, HC),
            shaped(D, HC),
            shaped(HC, D),
            shaped(8, HC, dtype=f32),
        ],
        me,
        buf,
        mlp_in,
        gb,
        ub,
        places="shhhv",
        outs="hhhhhv",
        scratch=[
            pltpu.VMEM((4, 2048, 256), bf16),
            pltpu.VMEM((tokens, D), bf16),
            pltpu.VMEM((tokens, D), bf16),
            pltpu.VMEM((D, HC), bf16),
            pltpu.VMEM((HC, D), bf16),
            pltpu.VMEM((tokens, HC), bf16),
            pltpu.VMEM((tokens, HC), bf16),
            pltpu.VMEM((4, 4, 512, 256), bf16),
            dma((4,)),
            dma((4, 2)),
            dma((4, 2)),
            dma((2,)),
            dma((5,)),
        ],
        flops=1.3e10,
        nbytes=2e7,
        trans=2e6,
    )


def outputs_kernel(
    me_ref,
    x0,
    x1,
    x2,
    x3,
    ctx_in,
    hidden_in,
    dqkv_in,
    dpre_in,
    wd_in,
    wdown_in,
    wqkv_in,
    wup_in,
    vec_ref,
    sums_a_ref,
    sums_b_ref,
    theirs_out,
    mine_out,
    image_ref,
    x_ref,
    ctx_ref,
    hidden_ref,
    dqkv_ref,
    dpre_ref,
    wd_ref,
    wdown_ref,
    wqkv_ref,
    wup_ref,
    both_ref,
    sums_ref,
    weight_sem,
    in_sem,
    out_sem,
):
    pairs = ((wqkv_in, wqkv_ref), (wup_in, wup_ref), (wdown_in, wdown_ref), (wd_in, wd_ref))
    weights = [
        pltpu.make_async_copy(src, dst, weight_sem.at[i]) for i, (src, dst) in enumerate(pairs)
    ]
    inputs = (
        (dqkv_in, dqkv_ref),
        (dpre_in, dpre_ref),
        (hidden_in, hidden_ref),
        (ctx_in, ctx_ref),
    )

    def load(t, n):
        src, dst = inputs[n]
        return pltpu.make_async_copy(src.at[tile(t), :], dst.at[tile(t), :], in_sem.at[t, n])

    rows = [
        pltpu.make_async_copy(src, x_ref.at[i], in_sem.at[i, 4])
        for i, src in enumerate((x0, x1, x2, x3))
    ]
    order = (2, 3, 0, 1)
    for n in range(4):
        load(order[0], n).start()
        weights[n].start()
    rows[order[0]].start()
    for t in order[1:]:
        for n in range(4):
            load(t, n).start()
        rows[t].start()
    sums_ref[...] = jnp.zeros_like(sums_ref)

    def store(i):
        return pltpu.make_async_copy(both_ref.at[i], theirs_out.at[i], out_sem.at[i])

    def store_mine(i):
        return pltpu.make_async_copy(both_ref.at[i + 2], mine_out.at[i], out_sem.at[i + 2])

    for weight in weights:
        weight.wait()

    @pl.loop(0, TP)
    def _(i):
        t = (i + 2) % 4
        pltpu.make_async_copy(x0, x_ref.at[t], in_sem.at[t, 4]).wait()
        for n in range(4):
            load(t, n).wait()
        here = tile(t)
        dattn = dot_nt(dqkv_ref[here, :], wqkv_ref[...])
        dmlp = dot_nt(dpre_ref[here, :], wup_ref[...])
        xhat, _ = normalize(x_ref[t].astype(f32))
        sums_ref[0:1, :] += jnp.sum(dattn * xhat, axis=0, keepdims=True)
        sums_ref[1:2, :] += jnp.sum(dattn, axis=0, keepdims=True)
        sums_ref[2:3, :] += jnp.sum(dmlp * xhat, axis=0, keepdims=True)
        sums_ref[3:4, :] += jnp.sum(dmlp, axis=0, keepdims=True)
        both_ref[i, 1] = (dattn * vec_ref[0:1] + dmlp * vec_ref[2:3]).astype(bf16)
        forward = dot(ctx_ref[here, :], wd_ref[...]) + dot(hidden_ref[here, :], wdown_ref[...])
        both_ref[i, 0] = forward.astype(bf16)

        @pl.when(i < 2)
        def _():
            store(i).start()

        @pl.when(i >= 2)
        def _():
            store_mine(i - 2).start()

    me = me_ref[0]
    image_ref[...] = jnp.zeros_like(image_ref)

    def put(row, ref, line, count):
        for i in range(count):
            image_ref[pl.ds(row + i, 1), :] = ref[line : line + 1, i * 256 : (i + 1) * 256]

    for i in range(4):
        put(4 * i, sums_ref, i, 4)
    for p in range(3):
        image_ref[pl.ds(16 + p * 4 + me, 1), :] = sums_a_ref[1:2, p * 256 : (p + 1) * 256]
    put(28, sums_a_ref, 0, 4)
    put(32 + 4 * me, sums_b_ref, 0, 4)
    put(48, sums_a_ref, 0, 4)
    for i in range(2):
        store(i).wait()
        store_mine(i).wait()


def outputs(me, xs, ctx, hidden, dqkv, dpre, wd, wdown, wqkv, wup, vec, sums_a, sums_b):
    tokens = TP * ROW
    dma = pltpu.SemaphoreType.DMA
    half = shaped(2, 2, ROW, D)
    return call(
        outputs_kernel,
        [half, half, shaped(IMAGE, 256, dtype=f32)],
        me,
        *xs,
        ctx,
        hidden,
        dqkv,
        dpre,
        wd,
        wdown,
        wqkv,
        wup,
        vec,
        sums_a,
        sums_b,
        places="s" + "h" * 12 + "vvv",
        outs="hhv",
        scratch=[
            pltpu.VMEM((TP, ROW, D), bf16),
            pltpu.VMEM((tokens, 256), bf16),
            pltpu.VMEM((tokens, HC), bf16),
            pltpu.VMEM((tokens, QC), bf16),
            pltpu.VMEM((tokens, HC), bf16),
            pltpu.VMEM((D // TP, D), bf16),
            pltpu.VMEM((HC, D), bf16),
            pltpu.VMEM((D, QC), bf16),
            pltpu.VMEM((D, HC), bf16),
            pltpu.VMEM((TP, 2, ROW, D), bf16),
            pltpu.VMEM((8, D), f32),
            dma((4,)),
            dma((4, 5)),
            dma((4,)),
        ],
        flops=6.5e9,
        nbytes=2e7,
    )


def half_kernel(mine0_ref, got0_ref, mine1_ref, got1_ref, kept_ref, send_ref):
    kept_ref[...] = mine0_ref[0].astype(f32) + got0_ref[0].astype(f32)
    send_ref[...] = (mine1_ref[0].astype(f32) + got1_ref[0].astype(f32)).astype(bf16)


def half_sum(mine, got):
    mine, got = in_hbm(mine), in_hbm(got)
    first = pl.BlockSpec((1, 1, ROW, D // 2), lambda i, k: (0, i, 0, k))
    second = pl.BlockSpec((1, 1, ROW, D // 2), lambda i, k: (1, i, 0, k))
    out = pl.BlockSpec((1, ROW, D // 2), lambda i, k: (i, 0, k))
    return pl.pallas_call(
        half_kernel,
        grid=(2, 2),
        in_specs=[first, first, second, second],
        out_specs=[out, out],
        out_shape=[pltpu.HBM((2, ROW, D), f32), pltpu.HBM((2, ROW, D), bf16)],
        compiler_params=pltpu.CompilerParams(vmem_limit_bytes=VMEM),
        cost_estimate=pl.CostEstimate(flops=0, bytes_accessed=8000000, transcendentals=0),
    )(mine, got, mine, got)


def close_kernel(len_ref, x_ref, cot_ref, kept_ref, got_ref, vec_ref, out_ref, grad_ref):
    x = x_ref[...].astype(f32)
    out_ref[...] = (x + kept_ref[0] + got_ref[0].astype(f32) + vec_ref[4:5]).astype(bf16)
    e = kept_ref[1] + got_ref[1].astype(f32)
    xhat, inv_std = normalize(x)
    mean_e = jnp.mean(e, axis=-1, keepdims=True)
    mean_ex = jnp.mean(e * xhat, axis=-1, keepdims=True)
    used = sum([len_ref[0, j] for j in range(SEGS - 1)])
    rows = lax.broadcasted_iota(jnp.int32, (ROW, 1), 0)
    kept = jnp.where(rows < used, cot_ref[...].astype(f32), 0.0)
    grad_ref[...] = kept + inv_std * (e - mean_e - xhat * mean_ex)


def close(lengths, x, cot, kept, got, vec):
    return call(
        close_kernel,
        [shaped(ROW, D), shaped(ROW, D, dtype=f32)],
        lengths,
        x,
        cot,
        kept,
        got,
        vec,
        nbytes=6e6,
    )


def add_kernel(a_ref, b_ref, image_ref, out_ref):
    total = sum([a_ref[i, 0].astype(f32) for i in range(4)])
    out_ref[0, 0:256, :] = total.astype(bf16)
    total = sum([b_ref[i, 0].astype(f32) for i in range(4)])
    out_ref[0, 256:768, :] = total.astype(bf16)
    image = image_ref[...]
    high = image.astype(bf16)
    out_ref[0, 768 : 768 + IMAGE, :] = high
    out_ref[0, 768 + IMAGE : 768 + 2 * IMAGE, :] = (image - high.astype(f32)).astype(bf16)


def add(sent_a, sent_b, image):
    rows = 768 + 2 * IMAGE
    return pl.pallas_call(
        add_kernel,
        grid=(4,),
        in_specs=[
            pl.BlockSpec((4, 1, 256, 256), lambda a: (0, a, 0, 0)),
            pl.BlockSpec((4, 1, 512, 256), lambda a: (0, a, 0, 0)),
            pl.BlockSpec((IMAGE, 256), lambda a: (0, 0)),
        ],
        out_specs=pl.BlockSpec((1, rows, 256), lambda a: (a, 0, 0)),
        out_shape=pltpu.HBM((4, rows, 256), bf16),
        compiler_params=pltpu.CompilerParams(vmem_limit_bytes=VMEM),
        cost_estimate=pl.CostEstimate(flops=0, bytes_accessed=8000000, transcendentals=0),
    )(in_hbm(sent_a), in_hbm(sent_b), image)


def part_kernel(far_ref, in_ref, slots_ref, keep_ref, send_ref, total_ref):
    far = far_ref[0]
    total_ref[...] = sum([in_ref[i].astype(f32) for i in range(4)])
    image = total_ref[768 : 768 + IMAGE, :] + total_ref[768 + IMAGE : 768 + 2 * IMAGE, :]
    for d in range(4):
        for zh in range(2):
            s = d * 2 + zh
            for p in range(3):
                row = (d * 3 + p) * 16 + zh * 8
                slots_ref[s, p * 8 : p * 8 + 8, :] = total_ref[row : row + 8, :]
            for cg in range(4):
                row = 256 + (d * 4 + cg) * 16 + zh * 8
                slots_ref[s, 24 + cg * 8 : 32 + cg * 8, :] = total_ref[row : row + 8, :]
            slots_ref[s, 56 : 56 + IMAGE, :] = image
    for ref, half in ((keep_ref, far), (send_ref, 1 - far)):
        for cg in range(4):
            row = pl.multiple_of(192 + cg * 16 + half * 8, 8)
            ref[cg * 8 : cg * 8 + 8, :] = total_ref[pl.ds(row, 8), :]
            row = pl.multiple_of(512 + cg * 64 + half * 32, 8)
            ref[32 + cg * 32 : 64 + cg * 32, :] = total_ref[pl.ds(row, 32), :]


def part(far, received):
    return call(
        part_kernel,
        [shaped(8, 56 + IMAGE, 256, dtype=f32), shaped(160, 256, dtype=f32), shaped(160, 256, dtype=f32)],
        far,
        received,
        scratch=[pltpu.VMEM((768 + 2 * IMAGE, 256), f32)],
        nbytes=4e6,
    )


def finish_kernel(place_ref, slots_ref, keep_ref, got_ref, qkv_ref, up_ref, dense_ref, down_ref, *rest):
    tiny_refs, image_ref = rest[:8], rest[8]
    image_ref[...] = sum([slots_ref[s, 56 : 56 + IMAGE, :] for s in range(8)])
    for d in range(4):
        for p in range(3):
            at = p * D + d * 256
            rows = slice(p * 8, p * 8 + 8)
            qkv_ref[:, at : at + 256] = slots_ref[2 * d, rows, :] + slots_ref[2 * d + 1, rows, :]
        for cg in range(4):
            at = d * HC + cg * 256
            rows = slice(24 + cg * 8, 32 + cg * 8)
            up_ref[:, at : at + 256] = slots_ref[2 * d, rows, :] + slots_ref[2 * d + 1, rows, :]
    for cg in range(4):
        at = slice(cg * 256, (cg + 1) * 256)
        rows = slice(cg * 8, cg * 8 + 8)
        dense_ref[:, at] = keep_ref[rows, :] + got_ref[rows, :]
        rows = slice(32 + cg * 32, 64 + cg * 32)
        down_ref[:, at] = keep_ref[rows, :] + got_ref[rows, :]
    p = place_ref[0]
    for start, size, ref in zip(STARTS, SIZES, tiny_refs):
        first = p * size
        row, lane = start + first // 256, first % 256
        values = image_ref[pl.ds(row, 1), :]
        if size == 24:
            values = jnp.concatenate([values, image_ref[pl.ds(row + 1, 1), :]], axis=1)
        ref[...] = pltpu.roll(values, values.shape[1] - lane, 1)[:, :size]


def finish(place, slots, keep, got):
    return call(
        finish_kernel,
        [
            shaped(8, 3 * D, dtype=f32),
            shaped(8, FF, dtype=f32),
            shaped(8, D, dtype=f32),
            shaped(32, D, dtype=f32),
        ]
        + [shaped(1, size, dtype=f32) for size in SIZES],
        place,
        slots,
        keep,
        got,
        scratch=[pltpu.VMEM((IMAGE, 256), f32)],
        nbytes=2e6,
    )


def body(
    inputs,
    cotangent,
    lengths,
    norm1_gain,
    norm1_bias,
    norm2_gain,
    norm2_bias,
    qkv_weight,
    qkv_bias,
    dense_weight,
    dense_bias,
    up_weight,
    up_bias,
    down_weight,
    down_bias,
):
    me = lax.axis_index("dp").astype(jnp.int32)
    index = lax.axis_index("fsdp").astype(jnp.int32)
    half = index % 2
    far = half[None]
    me1 = me[None]
    place = jnp.stack([me * 32 + index, me * 2 + half])
    outer, inner = outer_groups(), inner_groups()

    vectors = (
        norm1_gain,
        norm1_bias,
        norm2_gain,
        norm2_bias,
        qkv_bias,
        dense_bias,
        up_bias,
        down_bias,
    )
    slots, pieces = prepare(
        place,
        qkv_weight.reshape(8, 3 * D),
        up_weight.reshape(8, FF),
        dense_weight.reshape(8, D),
        down_weight.reshape(32, D),
        lengths,
        vectors,
    )
    far_pieces = flip_far(pieces)
    first = a2a(slots, stack_groups())
    block, lens = spread(far, first.reshape(4, 16, SLOT), pieces, far_pieces)
    info = jnp.concatenate([lens[0, :64], me1, far])

    block, x0, c0 = lax.optimization_barrier((block, inputs, cotangent))
    x1, c1 = flip_chip(x0), flip_chip(c0)
    second = a2a(block, inner)
    second, x1, c1 = lax.optimization_barrier((second, x1, c1))
    x2, x3 = flip_core(x0), flip_core(x1)
    c2, c3 = flip_core(c0), flip_core(c1)
    xs, cots = (x0, x1, x2, x3), (c0, c1, c2, c3)
    wide_a, wide_b = widen(second)
    third_a = a2a(wide_a, outer)
    third_b = a2a(wide_b, outer)

    sent_a, mlp_in, gb, ctx, dqkv, wqkv, wd, vec, up_b, sums_a = attention(info, xs, cots, third_a)
    sent_a = a2a(sent_a, outer)
    sent_b, hidden, dpre, wup, wdown, sums_b = mlp(me1, third_b, mlp_in, gb, up_b)
    sent_b = a2a(sent_b, outer)
    theirs, mine, image = outputs(
        me1, xs, ctx, hidden, dqkv, dpre, wd, wdown, wqkv, wup, vec, sums_a, sums_b
    )

    kept, send = half_sum(mine, flip_core(theirs))
    other = flip_chip(send)

    image = image + outer_flip(image, 1)
    image = image + outer_flip(image, 2)
    fourth = a2a(add(sent_a, sent_b, image), inner)
    slots, keep, send = part(far, fourth)
    block_output, input_grad = close(lengths, inputs, cotangent, kept, other, vec)
    results = finish(place, a2a(slots, stack_groups()), keep, flip_far(send))
    flat = [r.reshape(-1) for r in results]
    return (
        block_output,
        input_grad,
        flat[4],
        flat[5],
        flat[6],
        flat[7],
        flat[0],
        flat[8],
        flat[2],
        flat[9],
        flat[1],
        flat[10],
        flat[3],
        flat[11],
    )


def solution(mesh):
    flat = P(("dp", "fsdp"))
    rows = P(("dp", "fsdp"), None)
    return jax.shard_map(
        body,
        mesh=mesh,
        in_specs=(rows,) * 3 + (flat,) * 12,
        out_specs=(rows,) * 2 + (flat,) * 12,
        check_vma=False,
    )
```

time: 1680 us -> 234 us (0.14)
  waiting for transfers between devices: 1350 us -> 65.3 us
  blocking collectives: 136 us -> 19.5 us
  local copies, waits for them, and re-layouts: 96 us -> 13.9 us
  Pallas kernels: 0 us -> 79 us
  matrix products: 66.5 us -> 0 us
  starting transfers between devices: 0.19 us -> 53.6 us
    all_gather x4 -> x0, waiting for transfers between devices: 1080 us -> none  [the longest x1 308 us: collect(): lax.all_gather(pieces[4], ('dp', 'fsdp'), axis=0, tiled=True)]
    unnamed x6 -> x0, waiting for transfers between devices: 276 us -> none
    unnamed x2 -> x0, blocking collectives: 136 us -> none
    pallas_call x0 -> x11, Pallas kernels: none -> 79 us  [the longest x9 69.8 us: call(): pl.pallas_call(kernel, in_specs=[SPECS[p] for p in places], out_specs=out...]
    dot_general x18 -> x0, matrix products: 66.5 us -> none  [the longest x4 19.1 us: times_back(): lax.dot_general(left, right, (((1,), (1,)), ((), ())), preferred_element_...]
    ppermute x0 -> x12, waiting for transfers between devices: none -> 55.7 us  [the longest x3 21.5 us: flip_chip(): return lax.ppermute(values, 'dp', [(0, 2), (2, 0), (1, 3), (3, 1)])]
    unnamed x56 -> x40, local copies, waits for them, and re-layouts: 49.4 us -> 10.6 us
    all_to_all x0 -> x7, starting transfers between devices: none -> 36.6 us  [a2a(): lax.all_to_all(values, AXES, 0, 0, tiled=True, axis_index_groups=groups)]
  transfers between devices with their start and end apart: 5 -> 19, of which waited for: 5 -> 11; matrix products, arithmetic and copies ran while one was open for 7% -> 0% of each run, Pallas kernels for 0% -> 32%
where the time goes in v2:
time: 234 us; the launch traced here: 232 us
  Pallas kernels  79 us (34%)
  waiting for transfers between devices  65.3 us (28%)
  starting transfers between devices  53.6 us (23%)
  blocking collectives  19.5 us (8%)
  local copies, waits for them, and re-layouts  13.9 us (6%)
    pallas_call x9, Pallas kernels, call(): pl.pallas_call(kernel, in_specs=[SPECS[p] for p in places], out_specs=out...  69.8 us
    all_to_all x7, starting transfers between devices, a2a(): lax.all_to_all(values, AXES, 0, 0, tiled=True, axis_index_groups=groups)  36.6 us
    ppermute x3, waiting for transfers between devices, flip_chip(): return lax.ppermute(values, 'dp', [(0, 2), (2, 0), (1, 3), (3, 1)])  21.5 us
    ppermute x2, waiting for transfers between devices, flip_far(): return lax.ppermute(values, 'fsdp', [(i, i ^ 1) for i in range(32)])  19.5 us
    all_to_all x1, blocking collectives, a2a(): lax.all_to_all(values, AXES, 0, 0, tiled=True, axis_index_groups=groups)  19.5 us
    ppermute x2, waiting for transfers between devices, outer_flip(): return lax.ppermute(values, AXES, pairs)  11.4 us
    unnamed x40, local copies, waits for them, and re-layouts  10.6 us
    all_to_all x7, waiting for transfers between devices, a2a(): lax.all_to_all(values, AXES, 0, 0, tiled=True, axis_index_groups=groups)  9.59 us
  transfers between devices with their start and end apart: 19, of which 11 were waited for; matrix products, arithmetic and copies ran while one was open for 0% of the time, Pallas kernels for 32%

profile of v2, /device:TPU:1, one launch (start us, length us, event | category | flops | bytes accessed | tf_op | source)
XLA Modules:
  0.0 232.3 jit_solution(3135446118814407885)
XLA Ops:
  0.7 0.7 reshape.81.dense_in
  1.4 0.8 reshape.79.qkv_ref
  2.2 0.9 reshape.80.up_ref
  3.1 0.9 reshape.82.down_in
  4.0 0.1 pad_add_fusion.place_ref
  4.1 2.3 shard_map.263
  6.4 6.8 %all-to-all-start = ((bf16[8,8,3840]{2,1,0:T(8,128)(2,1)}), bf16[8,8,3840]{2,1,0:T(8,128)(2,1)S(1)}, u32[]{:S(2)}, u32[]{:S(2)}) async-start(bf16[8,8,3840]{2,1,0:T(8,128)(2,1)} %get-tuple-element.64), calls=%async_computation | async-start | bytes 983040 | tf_op jit(solution)/shard_map/all_to_all | solution.py:66
  13.2 2.9 %collective-permute-start = (bf16[40,1024]{1,0:T(8,128)(2,1)S(1)}, bf16[40,1024]{1,0:T(8,128)(2,1)S(1)}, u32[]{:S(2)}, u32[]{:S(2)}) collective-permute-start(bf16[40,1024]{1,0:T(8,128)(2,1)S(1)} %get-tuple-element.65.mine_ref), channel_id=1, source_target_pairs={{0,1},{1,0},{2,3},{3,2},{4,5},{5,4},{6,7},{7,6},{8,9},{9,8},{10,11... | collective-permute-start | bytes 245768 | tf_op jit(solution)/shard_map/ppermute | solution.py:78
  16.1 8.0 %collective-permute-done.theirs_ref = bf16[40,1024]{1,0:T(8,128)(2,1)S(1)} collective-permute-done((bf16[40,1024]{1,0:T(8,128)(2,1)S(1)}, bf16[40,1024]{1,0:T(8,128)(2,1)S(1)}, u32[]{:S(2)}, u32[]{:S(2)}) %collective-permute-start) | collective-permute-done | bytes 81952 | tf_op jit(solution)/shard_map/ppermute | solution.py:78
  24.1 0.0 all-to-all-done
  24.1 1.4 shard_map.264
  25.4 4.2 %all-to-all-start.1 = ((bf16[4,832,256]{2,1,0:T(8,128)(2,1)}), bf16[4,832,256]{2,1,0:T(8,128)(2,1)S(1)}, u32[]{:S(2)}, u32[]{:S(2)}) async-start(bf16[4,832,256]{2,1,0:T(8,128)(2,1)} %get-tuple-element.68), calls=%async_computation.1 | async-start | bytes 3407872 | tf_op jit(solution)/shard_map/all_to_all | solution.py:66
  29.6 0.3 collective-permute-start.2
  29.9 1.2 collective-permute-start.1
  31.1 11.0 %collective-permute-done.2.c1 = bf16[256,1024]{1,0:T(8,128)(2,1)S(1)} collective-permute-done((bf16[256,1024]{1,0:T(8,128)(2,1)S(1)}, bf16[256,1024]{1,0:T(8,128)(2,1)S(1)}, u32[]{:S(2)}, u32[]{:S(2)}) %collective-permute-start.2) | collective-permute-done | bytes 524320 | tf_op jit(solution)/shard_map/ppermute | solution.py:74
  42.1 0.8 copy-done.15
  42.9 10.5 %collective-permute-done.1.x1 = bf16[256,1024]{1,0:T(8,128)(2,1)} collective-permute-done((bf16[256,1024]{1,0:T(8,128)(2,1)S(1)}, bf16[256,1024]{1,0:T(8,128)(2,1)}, u32[]{:S(2)}, u32[]{:S(2)}) %collective-permute-start.1) | collective-permute-done | bytes 524320 | tf_op jit(solution)/shard_map/ppermute | solution.py:74
  53.4 0.0 all-to-all-done.1.in_ref
  53.4 0.4 shard_map.265
  53.9 19.5 %all_to_all.40.buf_ref = bf16[4,1088,256]{2,1,0:T(8,128)(2,1)S(1)} all-to-all(bf16[4,1088,256]{2,1,0:T(8,128)(2,1)S(1)} %get-tuple-element.74), channel_id=1, replica_groups={{0,8,16,24},{1,9,17,25},{2,10,18,26},{3,11,19,27},{4,12,20,28},{5,13,21..., dimensions={0} | all-to-all | bytes 4456448 | tf_op jit(solution)/shard_map/all_to_all | solution.py:66
  73.4 4.9 %all-to-all-start.3 = ((bf16[4,2048,256]{2,1,0:T(8,128)(2,1)}), bf16[4,2048,256]{2,1,0:T(8,128)(2,1)}, u32[]{:S(2)}, u32[]{:S(2)}) async-start(bf16[4,2048,256]{2,1,0:T(8,128)(2,1)} %copy-done), calls=%async_computation.3 | async-start | bytes 8388608 | tf_op jit(solution)/shard_map/all_to_all | solution.py:66
  78.3 4.0 %collective-permute-start.5 = (bf16[256,1024]{1,0:T(8,128)(2,1)S(1)}, bf16[256,1024]{1,0:T(8,128)(2,1)S(1)}, u32[]{:S(2)}, u32[]{:S(2)}) collective-permute-start(bf16[256,1024]{1,0:T(8,128)(2,1)S(1)} %copy-done.5), channel_id=1, source_target_pairs={{0,32},{32,0},{64,96},{96,64},{1,33},{33,1},{65,97},{97,65},{2,34}... | collective-permute-start | bytes 1572872 | tf_op jit(solution)/shard_map/ppermute | solution.py:70
  82.2 0.1 collective-permute-start.3
  82.3 0.4 collective-permute-start.6
  82.8 0.1 collective-permute-start.4
  82.9 0.1 pad_add_fusion.1.info_ref
  82.9 0.9 collective-permute-done.5.c2
  83.8 1.5 collective-permute-done.3.x2
  85.3 0.2 collective-permute-done.6.c3
  85.5 0.7 collective-permute-done.4.x3
  86.2 0.1 copy-done.17
  86.3 0.8 copy-done.14
  87.1 1.0 copy-done.11
  88.1 25.4 %shard_map.266 = (bf16[4,4,256,256]{3,2,1,0:T(8,128)(2,1)}, bf16[1024,1024]{1,0:T(8,128)(2,1)}, bf16[1024,1024]{1,0:T(8,128)(2,1)}, bf16[1024,256]{1,0:T(8,128)(...) custom-call(s32[66]{0:T(128)S(1)} %pad_add_fusion.1.info_ref, ...), custom_call_target="tpu_custom_call" | custom-call | flops 6000000000 | bytes 20000000 | tf_op jit(solution)/shard_map/pallas_call | solution.py:112
  113.5 0.0 all-to-all-done.3.buf_in
  113.5 4.0 %all-to-all-start.4 = ((bf16[4,4,256,256]{3,2,1,0:T(8,128)(2,1)}), bf16[4,4,256,256]{3,2,1,0:T(8,128)(2,1)S(1)}, u32[]{:S(2)}, u32[]{:S(2)}) async-start(bf16[4,4,256,256]{3,2,1,0:T(8,128)(2,1)} %get-tuple-element.96), calls=%async_computation.4 | async-start | bytes 4194304 | tf_op jit(solution)/shard_map/all_to_all | solution.py:66
  117.5 21.6 %shard_map.267 = (bf16[4,4,512,256]{3,2,1,0:T(8,128)(2,1)}, bf16[1024,1024]{1,0:T(8,128)(2,1)}, bf16[1024,1024]{1,0:T(8,128)(2,1)}, bf16[1024,1024]{1,0:T(8,128)...) custom-call(s32[1]{0:T(128)} %bitcast.me_ref, bf16[4,2048,256]{2,1,0:T(8,128)(2,1)} %all-to-all-done.3.buf_in, ...), custom_call_target="tpu_custom_call" | custom-call | flops 12999999488 | bytes 20000000 | tf_op jit(solution)/shard_map/pallas_call | solution.py:112
  139.2 1.3 copy-done.12
  140.5 5.0 %all-to-all-start.5 = ((bf16[4,4,512,256]{3,2,1,0:T(8,128)(2,1)}), bf16[4,4,512,256]{3,2,1,0:T(8,128)(2,1)}, u32[]{:S(2)}, u32[]{:S(2)}) async-start(bf16[4,4,512,256]{3,2,1,0:T(8,128)(2,1)} %get-tuple-element.97), calls=%async_computation.5 | async-start | bytes 8388608 | tf_op jit(solution)/shard_map/all_to_all | solution.py:66
  145.6 14.6 %shard_map.268 = (bf16[2,2,256,1024]{3,2,1,0:T(8,128)(2,1)}, bf16[2,2,256,1024]{3,2,1,0:T(8,128)(2,1)}, f32[64,256]{1,0:T(8,128)S(1)}) custom-call(s32[1]{0:T(128)} %bitcast.me_ref, bf16[256,1024]{1,0:T(8,128)(2,1)} %x_ref.1, bf16[256,1024]{1,0:T(8,128)(2,1)} %collective-permute-done.1.x1, bf16[256,1024]{1,0:T(8,128)(2,1)} %copy-done.13, ...), custom_call_target="tpu_custom_call" | custom-call | flops 6499999744 | bytes 20000000 | tf_op jit(solution)/shard_map/pallas_call | solution.py:112
  160.2 1.1 collective-permute-start.7
  161.3 1.2 collective-permute-start.9
  162.6 9.2 %collective-permute-done.9 = f32[64,256]{1,0:T(8,128)S(1)} collective-permute-done((f32[64,256]{1,0:T(8,128)S(1)}, f32[64,256]{1,0:T(8,128)S(1)}, u32[]{:S(2)}, u32[]{:S(2)}) %collective-permute-start.9) | collective-permute-done | bytes 65568 | tf_op jit(solution)/shard_map/ppermute | solution.py:62
  171.7 2.5 %collective-permute-start.10 = (f32[64,256]{1,0:T(8,128)S(1)}, f32[64,256]{1,0:T(8,128)S(1)}, u32[]{:S(2)}, u32[]{:S(2)}) collective-permute-start(f32[64,256]{1,0:T(8,128)S(1)} %add.19), channel_id=1, source_target_pairs={{0,16},{8,24},{16,0},{24,8},{1,17},{9,25},{17,1},{25,9},{2,18},{10... | collective-permute-start | bytes 196616 | tf_op jit(solution)/shard_map/ppermute | solution.py:62
  174.2 2.2 collective-permute-done.10
  176.5 4.9 %shard_map.271 = bf16[4,896,256]{2,1,0:T(8,128)(2,1)} custom-call(bf16[4,4,256,256]{3,2,1,0:T(8,128)(2,1)} %copy-done.12, bf16[4,4,512,256]{3,2,1,0:T(8,128)(2,1)} %all-to-all-done.5.b_ref, f32[64,256]{1,0:T(8,128)S(1)} %add.20.image_ref), custom_call_target="tpu_custom_call" | custom-call | bytes 8000000 | tf_op jit(solution)/shard_map/pallas_call | solution.py:969
  181.4 4.1 %all-to-all-start.6 = ((bf16[4,896,256]{2,1,0:T(8,128)(2,1)}), bf16[4,896,256]{2,1,0:T(8,128)(2,1)S(1)}, u32[]{:S(2)}, u32[]{:S(2)}) async-start(bf16[4,896,256]{2,1,0:T(8,128)(2,1)} %shard_map.271), calls=%async_computation.6 | async-start | bytes 3670016 | tf_op jit(solution)/shard_map/all_to_all | solution.py:66
  185.5 4.3 %shard_map.269 = (f32[2,256,1024]{2,1,0:T(8,128)}, bf16[2,256,1024]{2,1,0:T(8,128)(2,1)}) custom-call(bf16[2,2,256,1024]{3,2,1,0:T(8,128)(2,1)} %get-tuple-element.90.mine0_ref.mine1_ref, bf16[2,2,256,1024]{3,2,1,0:T(8,128)(2,1)} %collective-permute-done.7.got0_ref.got1_ref, bf16[2,2,256,1024]{3,2,1,0:T(8,128)(2,1)} %get-tuple-element.90.mine0_ref.mine1_ref, ...), custom_call_target="tpu_custom_call" | custom-call | bytes 8000000 | tf_op jit(solution)/shard_map/pallas_call | solution.py:918
  189.8 0.3 collective-permute-start.8
  190.1 9.6 %all-to-all-done.6.in_ref = bf16[4,896,256]{2,1,0:T(8,128)(2,1)S(1)} async-done(((bf16[4,896,256]{2,1,0:T(8,128)(2,1)}), bf16[4,896,256]{2,1,0:T(8,128)(2,1)S(1)}, u32[]{:S(2)}, u32[]{:S(2)}) %all-to-all-start.6) | async-done | bytes 1835040 | tf_op jit(solution)/shard_map/all_to_all | solution.py:66
  199.7 0.5 shard_map.272
  200.2 1.0 copy-done.2
  201.2 0.7 copy-done.7
  201.8 0.7 copy-done.10
  202.5 7.6 %all-to-all-start.7 = ((f32[8,120,256]{2,1,0:T(8,128)}), f32[8,120,256]{2,1,0:T(8,128)S(1)}, u32[]{:S(2)}, u32[]{:S(2)}) async-start(f32[8,120,256]{2,1,0:T(8,128)} %copy-done.2), calls=%async_computation.7 | async-start | bytes 1966080 | tf_op jit(solution)/shard_map/all_to_all | solution.py:66
  210.1 2.9 %collective-permute-start.11 = (f32[160,256]{1,0:T(8,128)}, f32[160,256]{1,0:T(8,128)S(1)}, u32[]{:S(2)}, u32[]{:S(2)}) collective-permute-start(f32[160,256]{1,0:T(8,128)} %copy-done.10), channel_id=1, source_target_pairs={{0,1},{1,0},{2,3},{3,2},{4,5},{5,4},{6,7},{7,6},{8,9},{9,8},{10,11... | collective-permute-start | bytes 491528 | tf_op jit(solution)/shard_map/ppermute | solution.py:78
  213.0 1.6 copy-done.1
  214.6 2.4 %shard_map.270 = (bf16[256,1024]{1,0:T(8,128)(2,1)}, f32[256,1024]{1,0:T(8,128)}) custom-call(s32[1,8]{1,0:T(1,128)S(1)} %copy-done.9, bf16[256,1024]{1,0:T(8,128)(2,1)S(1)} %copy-done.4, bf16[256,1024]{1,0:T(8,128)(2,1)S(1)} %copy-done.6, f32[2,256,1024]{2,1,0:T(8,128)S(1)} %copy-done.1, bf16[2,256,1024]{2,1,0:T(8,128)(2,1)S(1)} %collective-permute-done.8.got_ref, ...), custom_call_target="tpu_custom_call" | custom-call | bytes 6000000 | tf_op jit(solution)/shard_map/pallas_call | solution.py:112
  216.9 11.5 %collective-permute-done.11.got_ref = f32[160,256]{1,0:T(8,128)S(1)} collective-permute-done((f32[160,256]{1,0:T(8,128)}, f32[160,256]{1,0:T(8,128)S(1)}, u32[]{:S(2)}, u32[]{:S(2)}) %collective-permute-start.11) | collective-permute-done | bytes 163872 | tf_op jit(solution)/shard_map/ppermute | solution.py:78
  228.5 1.2 shard_map.273
  229.7 0.6 copy.35
  230.3 0.7 copy.30
  231.0 0.7 copy.32
  231.6 0.7 copy.33
  (35 shorter events, 0.1 us)
Async XLA Ops:
  6.4 17.7 %all-to-all-start = ((bf16[8,8,3840]{2,1,0:T(8,128)(2,1)}), bf16[8,8,3840]{2,1,0:T(8,128)(2,1)S(1)}, u32[]{:S(2)}, u32[]{:S(2)}) async-start(bf16[8,8,3840]{2,1,0:T(8,128)(2,1)} %get-tuple-element.64), calls=%async_computation | async-start | bytes 983040 | tf_op jit(solution)/shard_map/all_to_all | solution.py:66
  13.2 16.4 %copy-start.5 = (bf16[256,1024]{1,0:T(8,128)(2,1)S(1)}, bf16[256,1024]{1,0:T(8,128)(2,1)}, u32[]{:S(2)}) copy-start(bf16[256,1024]{1,0:T(8,128)(2,1)} %cot_ref.1) | copy-start | bytes 1572868
  13.2 16.7 %copy-start.3 = (bf16[256,1024]{1,0:T(8,128)(2,1)S(1)}, bf16[256,1024]{1,0:T(8,128)(2,1)}, u32[]{:S(2)}) copy-start(bf16[256,1024]{1,0:T(8,128)(2,1)} %x_ref.1) | copy-start | bytes 1572868
  13.2 10.9 %collective-permute-start = (bf16[40,1024]{1,0:T(8,128)(2,1)S(1)}, bf16[40,1024]{1,0:T(8,128)(2,1)S(1)}, u32[]{:S(2)}, u32[]{:S(2)}) collective-permute-start(bf16[40,1024]{1,0:T(8,128)(2,1)S(1)} %get-tuple-element.65.mine_ref), channel_id=1, source_target_pairs={{0,1},{1,0},{2,3},{3,2},{4,5},{5,4},{6,7},{7,6},{8,9},{9,8},{10,11... | collective-permute-start | bytes 245768 | tf_op jit(solution)/shard_map/ppermute | solution.py:78
  25.4 28.0 %all-to-all-start.1 = ((bf16[4,832,256]{2,1,0:T(8,128)(2,1)}), bf16[4,832,256]{2,1,0:T(8,128)(2,1)S(1)}, u32[]{:S(2)}, u32[]{:S(2)}) async-start(bf16[4,832,256]{2,1,0:T(8,128)(2,1)} %get-tuple-element.68), calls=%async_computation.1 | async-start | bytes 3407872 | tf_op jit(solution)/shard_map/all_to_all | solution.py:66
  29.6 12.4 %collective-permute-start.2 = (bf16[256,1024]{1,0:T(8,128)(2,1)S(1)}, bf16[256,1024]{1,0:T(8,128)(2,1)S(1)}, u32[]{:S(2)}, u32[]{:S(2)}) collective-permute-start(bf16[256,1024]{1,0:T(8,128)(2,1)S(1)} %copy-done.5), channel_id=1, source_target_pairs={{0,64},{64,0},{32,96},{96,32},{1,65},{65,1},{33,97},{97,33},{2,66}... | collective-permute-start | bytes 1572872 | tf_op jit(solution)/shard_map/ppermute | solution.py:74
  29.9 23.5 %collective-permute-start.1 = (bf16[256,1024]{1,0:T(8,128)(2,1)S(1)}, bf16[256,1024]{1,0:T(8,128)(2,1)}, u32[]{:S(2)}, u32[]{:S(2)}) collective-permute-start(bf16[256,1024]{1,0:T(8,128)(2,1)S(1)} %copy-done.3), channel_id=1, source_target_pairs={{0,64},{64,0},{32,96},{96,32},{1,65},{65,1},{33,97},{97,33},{2,66}... | collective-permute-start | bytes 1572872 | tf_op jit(solution)/shard_map/ppermute | solution.py:74
  42.1 0.8 copy-start.15
  53.9 19.5 %copy-start = (bf16[4,2048,256]{2,1,0:T(8,128)(2,1)}, bf16[4,2048,256]{2,1,0:T(8,128)(2,1)S(1)}, u32[]{:S(2)}) copy-start(bf16[4,2048,256]{2,1,0:T(8,128)(2,1)S(1)} %get-tuple-element.76) | copy-start | bytes 12582916
  73.4 40.1 %all-to-all-start.3 = ((bf16[4,2048,256]{2,1,0:T(8,128)(2,1)}), bf16[4,2048,256]{2,1,0:T(8,128)(2,1)}, u32[]{:S(2)}, u32[]{:S(2)}) async-start(bf16[4,2048,256]{2,1,0:T(8,128)(2,1)} %copy-done), calls=%async_computation.3 | async-start | bytes 8388608 | tf_op jit(solution)/shard_map/all_to_all | solution.py:66
  78.3 5.5 %collective-permute-start.5 = (bf16[256,1024]{1,0:T(8,128)(2,1)S(1)}, bf16[256,1024]{1,0:T(8,128)(2,1)S(1)}, u32[]{:S(2)}, u32[]{:S(2)}) collective-permute-start(bf16[256,1024]{1,0:T(8,128)(2,1)S(1)} %copy-done.5), channel_id=1, source_target_pairs={{0,32},{32,0},{64,96},{96,64},{1,33},{33,1},{65,97},{97,65},{2,34}... | collective-permute-start | bytes 1572872 | tf_op jit(solution)/shard_map/ppermute | solution.py:70
  82.2 3.0 %collective-permute-start.3 = (bf16[256,1024]{1,0:T(8,128)(2,1)S(1)}, bf16[256,1024]{1,0:T(8,128)(2,1)S(1)}, u32[]{:S(2)}, u32[]{:S(2)}) collective-permute-start(bf16[256,1024]{1,0:T(8,128)(2,1)S(1)} %copy-done.3), channel_id=1, source_target_pairs={{0,32},{32,0},{64,96},{96,64},{1,33},{33,1},{65,97},{97,65},{2,34}... | collective-permute-start | bytes 1572872 | tf_op jit(solution)/shard_map/ppermute | solution.py:70
  82.3 3.2 %collective-permute-start.6 = (bf16[256,1024]{1,0:T(8,128)(2,1)}, bf16[256,1024]{1,0:T(8,128)(2,1)S(1)}, u32[]{:S(2)}, u32[]{:S(2)}) collective-permute-start(bf16[256,1024]{1,0:T(8,128)(2,1)} %copy-done.15), channel_id=1, source_target_pairs={{0,32},{32,0},{64,96},{96,64},{1,33},{33,1},{65,97},{97,65},{2,34}... | collective-permute-start | bytes 1572872 | tf_op jit(solution)/shard_map/ppermute | solution.py:70
  82.8 3.5 %collective-permute-start.4 = (bf16[256,1024]{1,0:T(8,128)(2,1)}, bf16[256,1024]{1,0:T(8,128)(2,1)S(1)}, u32[]{:S(2)}, u32[]{:S(2)}) collective-permute-start(bf16[256,1024]{1,0:T(8,128)(2,1)} %collective-permute-done.1.x1), channel_id=1, source_target_pairs={{0,32},{32,0},{64,96},{96,64},{1,33},{33,1},{65,97},{97,65},{2,34}... | collective-permute-start | bytes 1572872 | tf_op jit(solution)/shard_map/ppermute | solution.py:70
  83.8 2.5 %copy-start.16 = (bf16[256,1024]{1,0:T(8,128)(2,1)}, bf16[256,1024]{1,0:T(8,128)(2,1)S(1)}, u32[]{:S(2)}) copy-start(bf16[256,1024]{1,0:T(8,128)(2,1)S(1)} %collective-permute-done.5.c2) | copy-start | bytes 1572868
  85.3 1.0 copy-start.13
  85.5 0.8 copy-start.17
  86.3 0.8 copy-start.14
  87.1 1.0 copy-start.11
  113.5 25.7 %all-to-all-start.4 = ((bf16[4,4,256,256]{3,2,1,0:T(8,128)(2,1)}), bf16[4,4,256,256]{3,2,1,0:T(8,128)(2,1)S(1)}, u32[]{:S(2)}, u32[]{:S(2)}) async-start(bf16[4,4,256,256]{3,2,1,0:T(8,128)(2,1)} %get-tuple-element.96), calls=%async_computation.4 | async-start | bytes 4194304 | tf_op jit(solution)/shard_map/all_to_all | solution.py:66
  139.2 1.4 copy-start.12
  140.5 35.9 %all-to-all-start.5 = ((bf16[4,4,512,256]{3,2,1,0:T(8,128)(2,1)}), bf16[4,4,512,256]{3,2,1,0:T(8,128)(2,1)}, u32[]{:S(2)}, u32[]{:S(2)}) async-start(bf16[4,4,512,256]{3,2,1,0:T(8,128)(2,1)} %get-tuple-element.97), calls=%async_computation.5 | async-start | bytes 8388608 | tf_op jit(solution)/shard_map/all_to_all | solution.py:66
  160.2 25.2 %collective-permute-start.7 = (bf16[2,2,256,1024]{3,2,1,0:T(8,128)(2,1)}, bf16[2,2,256,1024]{3,2,1,0:T(8,128)(2,1)}, u32[]{:S(2)}, u32[]{:S(2)}) collective-permute-start(bf16[2,2,256,1024]{3,2,1,0:T(8,128)(2,1)} %get-tuple-element.91), channel_id=1, source_target_pairs={{0,32},{32,0},{64,96},{96,64},{1,33},{33,1},{65,97},{97,65},{2,34}... | collective-permute-start | bytes 6291464 | tf_op jit(solution)/shard_map/ppermute | solution.py:70
  161.3 10.4 %collective-permute-start.9 = (f32[64,256]{1,0:T(8,128)S(1)}, f32[64,256]{1,0:T(8,128)S(1)}, u32[]{:S(2)}, u32[]{:S(2)}) collective-permute-start(f32[64,256]{1,0:T(8,128)S(1)} %get-tuple-element.98), channel_id=1, source_target_pairs={{0,8},{8,0},{16,24},{24,16},{1,9},{9,1},{17,25},{25,17},{2,10},{10... | collective-permute-start | bytes 196616 | tf_op jit(solution)/shard_map/ppermute | solution.py:62
  171.7 4.7 %collective-permute-start.10 = (f32[64,256]{1,0:T(8,128)S(1)}, f32[64,256]{1,0:T(8,128)S(1)}, u32[]{:S(2)}, u32[]{:S(2)}) collective-permute-start(f32[64,256]{1,0:T(8,128)S(1)} %add.19), channel_id=1, source_target_pairs={{0,16},{8,24},{16,0},{24,8},{1,17},{9,25},{17,1},{25,9},{2,18},{10... | collective-permute-start | bytes 196616 | tf_op jit(solution)/shard_map/ppermute | solution.py:62
  181.4 18.4 %all-to-all-start.6 = ((bf16[4,896,256]{2,1,0:T(8,128)(2,1)}), bf16[4,896,256]{2,1,0:T(8,128)(2,1)S(1)}, u32[]{:S(2)}, u32[]{:S(2)}) async-start(bf16[4,896,256]{2,1,0:T(8,128)(2,1)} %shard_map.271), calls=%async_computation.6 | async-start | bytes 3670016 | tf_op jit(solution)/shard_map/all_to_all | solution.py:66
  189.8 23.1 %copy-start.4 = (bf16[256,1024]{1,0:T(8,128)(2,1)S(1)}, bf16[256,1024]{1,0:T(8,128)(2,1)}, u32[]{:S(2)}) copy-start(bf16[256,1024]{1,0:T(8,128)(2,1)} %x_ref.1) | copy-start | bytes 1572868
  189.8 23.1 %copy-start.9 = (s32[1,8]{1,0:T(1,128)S(1)}, s32[1,8]{1,0:T(1,128)}, u32[]{:S(2)}) copy-start(s32[1,8]{1,0:T(1,128)} %len_ref.1) | copy-start | bytes 100
  189.8 23.1 %collective-permute-start.8 = (bf16[2,256,1024]{2,1,0:T(8,128)(2,1)}, bf16[2,256,1024]{2,1,0:T(8,128)(2,1)S(1)}, u32[]{:S(2)}, u32[]{:S(2)}) collective-permute-start(bf16[2,256,1024]{2,1,0:T(8,128)(2,1)} %get-tuple-element.93), channel_id=1, source_target_pairs={{0,64},{64,0},{32,96},{96,32},{1,65},{65,1},{33,97},{97,33},{2,66}... | collective-permute-start | bytes 3145736 | tf_op jit(solution)/shard_map/ppermute | solution.py:74
  200.2 1.0 copy-start.2
  201.2 0.7 copy-start.7
  201.8 0.7 copy-start.10
  202.5 10.4 %copy-start.6 = (bf16[256,1024]{1,0:T(8,128)(2,1)S(1)}, bf16[256,1024]{1,0:T(8,128)(2,1)}, u32[]{:S(2)}) copy-start(bf16[256,1024]{1,0:T(8,128)(2,1)} %cot_ref.1) | copy-start | bytes 1572868
  202.5 26.0 %all-to-all-start.7 = ((f32[8,120,256]{2,1,0:T(8,128)}), f32[8,120,256]{2,1,0:T(8,128)S(1)}, u32[]{:S(2)}, u32[]{:S(2)}) async-start(f32[8,120,256]{2,1,0:T(8,128)} %copy-done.2), calls=%async_computation.7 | async-start | bytes 1966080 | tf_op jit(solution)/shard_map/all_to_all | solution.py:66
  210.1 18.4 %collective-permute-start.11 = (f32[160,256]{1,0:T(8,128)}, f32[160,256]{1,0:T(8,128)S(1)}, u32[]{:S(2)}, u32[]{:S(2)}) collective-permute-start(f32[160,256]{1,0:T(8,128)} %copy-done.10), channel_id=1, source_target_pairs={{0,1},{1,0},{2,3},{3,2},{4,5},{5,4},{6,7},{7,6},{8,9},{9,8},{10,11... | collective-permute-start | bytes 491528 | tf_op jit(solution)/shard_map/ppermute | solution.py:78
  213.0 1.6 copy-start.1
  214.5 13.9 %copy-start.8 = (f32[160,256]{1,0:T(8,128)S(1)}, f32[160,256]{1,0:T(8,128)}, u32[]{:S(2)}) copy-start(f32[160,256]{1,0:T(8,128)} %copy-done.7) | copy-start | bytes 491524

commit v3 on v2

v3 whole, which is shorter than its diff:
```python
import jax
import jax.numpy as jnp
import ml_dtypes
import numpy as np
from jax import lax
from jax.experimental import pallas as pl
from jax.experimental.pallas import tpu as pltpu
from jax.sharding import PartitionSpec as P

D = 1024
HEADS = 16
HEAD_DIM = 64
ROT = 16
FF = 4096
ROW = 256
SEGS = 8
TP = 4
QC = 3 * D // TP
HC = FF // TP
LOCAL_HEADS = HEADS // TP
AXES = ("dp", "fsdp")
VMEM = 44 * 1024 * 1024

f32 = jnp.float32
bf16 = jnp.bfloat16


def dev(d, y, x, zh):
    return d * 32 + y * 8 + x * 2 + zh


def outer_groups(flip=0):
    groups = []
    for d in range(4):
        for k in range(4):
            for zh in range(2):
                if d % 2 == flip:
                    groups.append([dev(d, i, k, zh) for i in range(4)])
                else:
                    groups.append([dev(d, k, i, zh) for i in range(4)])
    return groups


def inner_groups():
    return outer_groups(flip=1)


def stack_groups():
    return [
        [dev(d, y, x, zh) for d in range(4) for zh in range(2)] for y in range(4) for x in range(4)
    ]


def plane_groups():
    return [
        [dev(d, y, x, zh) for y in range(4) for x in range(4)] for d in range(4) for zh in range(2)
    ]


def a2a(values, groups):
    return lax.all_to_all(values, AXES, 0, 0, tiled=True, axis_index_groups=groups)


def flip_core(values):
    return lax.ppermute(values, "dp", [(0, 1), (1, 0), (2, 3), (3, 2)])


def flip_chip(values):
    return lax.ppermute(values, "dp", [(0, 2), (2, 0), (1, 3), (3, 1)])


def flip_far(values):
    return lax.ppermute(values, "fsdp", [(i, i ^ 1) for i in range(32)])


def dot(left, right):
    return jnp.dot(left, right, preferred_element_type=f32)


def dot_nt(left, right):
    return lax.dot_general(left, right, (((1,), (1,)), ((), ())), preferred_element_type=f32)


def dot_tn(left, right):
    return lax.dot_general(left, right, (((0,), (0,)), ((), ())), preferred_element_type=f32)


def in_hbm(values):
    return pltpu.with_memory_space_constraint(values, pltpu.HBM)


VMEM_SPEC = pl.BlockSpec(memory_space=pltpu.VMEM)
SMEM_SPEC = pl.BlockSpec(memory_space=pltpu.SMEM)
HBM_SPEC = pl.BlockSpec(memory_space=pltpu.HBM)
SPECS = {"s": SMEM_SPEC, "v": VMEM_SPEC, "u": VMEM_SPEC, "h": HBM_SPEC}


def call(kernel, out_shape, *args, places=None, outs=None, scratch=(), flops=0, nbytes=0, trans=0):
    places = places or "s" + "v" * (len(args) - 1)
    out_specs = jax.tree.map(lambda _: VMEM_SPEC, out_shape)
    if outs is not None:
        out_specs = [SPECS[o] for o in outs]
        out_shape = [
            v if o == "v" else pltpu.HBM(v.shape, v.dtype) for o, v in zip(outs, out_shape)
        ]
    args = [in_hbm(v) if p == "h" else v for p, v in zip(places, args)]
    return pl.pallas_call(
        kernel,
        in_specs=[SPECS[p] for p in places],
        out_specs=out_specs,
        out_shape=out_shape,
        scratch_shapes=list(scratch),
        compiler_params=pltpu.CompilerParams(vmem_limit_bytes=VMEM),
        cost_estimate=pl.CostEstimate(
            flops=int(flops), bytes_accessed=int(nbytes), transcendentals=int(trans)
        ),
    )(*args)


def shaped(*shape, dtype=bf16):
    return jax.ShapeDtypeStruct(shape, dtype)


def normalize(x):
    average = jnp.mean(x, axis=-1, keepdims=True)
    centred = x - average
    inv_std = lax.rsqrt(jnp.mean(centred * centred, axis=-1, keepdims=True) + 1e-05)
    return centred * inv_std, inv_std


STARTS = (0, 4, 8, 12, 16, 28, 32, 48)
SIZES = (8, 8, 8, 8, 24, 8, 32, 8)
IMAGE = 64
LENS = 64
SLOT = QC + HC + 128


def tile(n):
    return pl.ds(pl.multiple_of(n * 256, 256), 256)


def swapped(y, x, c):
    return y + c * (x - y), x + c * (y - x)


def prepare_kernel(
    qkv_ref, up_ref, dense_in, down_in, len_in, n1g, n1b, n2g, n2b, qb, db, ub, dnb,
    out_ref, pieces_ref, tile_ref, *rest
):
    sources = (len_in, n1g, n1b, n2g, n2b, qb, db, ub, dnb)
    holders, sem = rest[:9], rest[9]
    copies = [
        pltpu.make_async_copy(src, dst, sem.at[i])
        for i, (src, dst) in enumerate(zip(sources, holders))
    ]
    for copy in copies:
        copy.start()
    for d in range(4):
        for zh in range(2):
            s = d * 2 + zh
            for p in range(3):
                at = p * D + d * 256
                out_ref[s, :, p * 256 : (p + 1) * 256] = qkv_ref[:, at : at + 256]
            out_ref[s, :, QC : QC + HC] = up_ref[:, d * HC : (d + 1) * HC]
    pieces_ref[0:32, :] = down_in[...]
    pieces_ref[32:40, :] = dense_in[...]
    tile_ref[...] = jnp.zeros_like(tile_ref)
    for copy in copies:
        copy.wait()
    for i, (size, ref) in enumerate(zip(SIZES, holders[1:])):
        tile_ref[i : i + 1, 0:size] = ref[...].astype(f32)
    tile_ref[0:1, LENS : LENS + SEGS] = holders[0][...].astype(f32)
    block = tile_ref[...].astype(bf16)
    for s in range(8):
        out_ref[s, :, QC + HC : SLOT] = block


def prepare(qkv, up, dense, down, lengths, vectors):
    vectors = [v[None, :] for v in vectors]
    return call(
        prepare_kernel,
        [shaped(8, 8, SLOT), shaped(40, D)],
        qkv,
        up,
        dense,
        down,
        lengths,
        *vectors,
        places="vvvv" + "h" * 9,
        scratch=[pltpu.VMEM((8, 128), f32), pltpu.VMEM((1, SEGS), jnp.int32)]
        + [pltpu.VMEM(v.shape, bf16) for v in vectors]
        + [pltpu.SemaphoreType.DMA((9,))],
        nbytes=1e6,
    )


def locate(p, start, size):
    first = p * size
    return start + first // 256, first % 256


def spread_kernel(index_ref, first_ref, mine_ref, theirs_ref, out_ref, lens_ref, image_ref):
    index = index_ref[0]
    far = index % 2 == 1
    mine, theirs = mine_ref[...].astype(f32), theirs_ref[...].astype(f32)
    low, high = jnp.where(far, theirs, mine), jnp.where(far, mine, theirs)
    down = jnp.concatenate([low[:32], high[:32]], axis=0).astype(bf16)
    dense = jnp.concatenate([low[32:], high[32:]], axis=0).astype(bf16)
    image_ref[...] = jnp.zeros_like(image_ref)
    lens = []
    for d in range(4):
        both = first_ref[d, :, QC + HC : SLOT].astype(f32)
        for zh in range(2):
            p = d * 32 + index // 2 * 2 + zh
            tile = both[zh * 8 : zh * 8 + 8]
            lens.append(tile[0:1, LENS : LENS + SEGS])
            for i, (start, size) in enumerate(zip(STARTS, SIZES)):
                row, lane = locate(p, start, size)
                wide = 512 if size == 24 else 256
                blank = jnp.zeros((1, wide - size), f32)
                values = jnp.concatenate([tile[i : i + 1, :size], blank], axis=1)
                values = pltpu.roll(values, lane, 1)
                image_ref[pl.ds(row, 1), :] += values[:, :256]
                if wide == 512:
                    image_ref[pl.ds(row + 1, 1), :] += values[:, 256:]
    lens_ref[...] = jnp.concatenate(lens, axis=1).astype(jnp.int32)
    image = image_ref[...].astype(bf16)
    for i in range(4):
        for d in range(4):
            for p in range(3):
                row = (d * 3 + p) * 16
                out_ref[i, row : row + 16, :] = first_ref[d, :, p * 256 : (p + 1) * 256]
            for cg in range(4):
                row = 256 + (d * 4 + cg) * 16
                at = QC + cg * 256
                out_ref[i, row : row + 16, :] = first_ref[d, :, at : at + 256]
        for cg in range(4):
            at = slice(cg * 256, (cg + 1) * 256)
            out_ref[i, 192 + cg * 16 : 208 + cg * 16, :] = dense[:, at]
            out_ref[i, 512 + cg * 64 : 576 + cg * 64, :] = down[:, at]
        out_ref[i, 768 : 768 + IMAGE, :] = image


def spread(index, first, mine, theirs):
    return call(
        spread_kernel,
        [shaped(4, 768 + IMAGE, 256), shaped(1, 64, dtype=jnp.int32)],
        index,
        first,
        mine,
        theirs,
        scratch=[pltpu.VMEM((IMAGE, 256), f32)],
        nbytes=2e6,
    )


def widen_a_kernel(in_ref, out_ref):
    image = sum([in_ref[a, 768 : 768 + IMAGE, :].astype(f32) for a in range(4)]).astype(bf16)
    for i in range(4):
        for a in range(4):
            out_ref[i, a * 256 : (a + 1) * 256, :] = in_ref[a, 0:256, :]
        out_ref[i, 1024 : 1024 + IMAGE, :] = image


def widen_a(second):
    return call(
        widen_a_kernel, [shaped(4, 1024 + IMAGE, 256)], second, places="v", outs="u", nbytes=4e6
    )[0]


def widen_b_kernel(in_ref, out_ref):
    @pl.loop(0, 4)
    def _(i):
        for a in range(4):
            out_ref[i, a * 512 : (a + 1) * 512, :] = in_ref[a, 256:768, :]


def widen_b(second):
    return call(
        widen_b_kernel, [shaped(4, 2048, 256)], second, places="v", outs="u", nbytes=6e6
    )[0]


def assemble_a(me, buf_ref, wqkv_ref, wd_ref):
    c = me % 2
    for y in range(4):
        for x in range(4):
            b, a = swapped(y, x, c)
            yx = y * 4 + x
            base = a * 256
            for d in range(4):
                for p in range(3):
                    row = pl.multiple_of(base + (d * 3 + p) * 16, 16)
                    wqkv_ref[d * 256 + yx * 16 : d * 256 + yx * 16 + 16, p * 256 : (p + 1) * 256] = (
                        buf_ref[b, pl.ds(row, 16), :]
                    )
            for cg in range(4):
                row = pl.multiple_of(base + 192 + cg * 16, 16)
                wd_ref[yx * 16 : yx * 16 + 16, cg * 256 : (cg + 1) * 256] = buf_ref[
                    b, pl.ds(row, 16), :
                ]


def read_vectors(me, buf_ref, vec_ref, qb_ref, ub_ref):
    image = sum([buf_ref[b, 1024 : 1024 + IMAGE, :].astype(f32) for b in range(4)])

    def long(start):
        return jnp.concatenate([image[start + i : start + i + 1, :] for i in range(4)], axis=1)

    vec_ref[...] = jnp.zeros_like(vec_ref)
    for i in range(4):
        vec_ref[i : i + 1, :] = long(4 * i)
    vec_ref[4:5, :] = long(28) + long(48)
    own = [jnp.where(me == d, 1.0, 0.0) for d in range(4)]
    rows = [sum([image[16 + p * 4 + d : 17 + p * 4 + d] * own[d] for d in range(4)]) for p in range(3)]
    qb_ref[...] = jnp.concatenate(rows, axis=1)
    ub_ref[...] = sum([long(32 + 4 * d) * own[d] for d in range(4)])


def assemble_b(me, buf_ref, wup_ref, wdown_ref):
    c = me % 2
    for y in range(4):
        for x in range(4):
            b, a = swapped(y, x, c)
            yx = y * 4 + x
            base = a * 512
            for d in range(4):
                for cg in range(4):
                    row = pl.multiple_of(base + (d * 4 + cg) * 16, 16)
                    wup_ref[d * 256 + yx * 16 : d * 256 + yx * 16 + 16, cg * 256 : (cg + 1) * 256] = (
                        buf_ref[b, pl.ds(row, 16), :]
                    )
            for cg in range(4):
                row = pl.multiple_of(base + 256 + cg * 64, 16)
                wdown_ref[yx * 64 : yx * 64 + 64, cg * 256 : (cg + 1) * 256] = buf_ref[
                    b, pl.ds(row, 64), :
                ]


def turn(u, cosine, sin_left, sin_right):
    return (
        u * cosine
        + pltpu.roll(u, u.shape[1] - ROT // 2, 1) * sin_left
        + pltpu.roll(u, ROT // 2, 1) * sin_right
    )


def rotary_tables():
    places = np.arange(ROW, dtype=np.float32)
    freqs = (10000.0 ** (-(np.arange(ROT // 2, dtype=np.float32) * 2.0) / ROT)).astype(np.float32)
    angle = (places[:, None] * freqs[None, :]).astype(np.float32)
    cosine, sine = np.cos(angle), np.sin(angle)
    zeros = np.zeros_like(sine)
    rest = np.zeros((ROW, HEAD_DIM - ROT), np.float32)
    parts = [[cosine, cosine, rest + 1.0], [-sine, zeros, rest], [zeros, sine, rest]]
    columns = []
    for part in parts:
        whole = np.tile(np.concatenate(part, axis=1), (1, 2)).astype(np.float32)
        high = whole.astype(ml_dtypes.bfloat16)
        columns += [high, (whole - high.astype(np.float32)).astype(ml_dtypes.bfloat16)]
    return np.concatenate(columns, axis=1)


def row_sums(values):
    total = jnp.sum(values, axis=1, keepdims=True)
    return jnp.transpose(jnp.broadcast_to(total, (256, 128)))[0:1, :]


def through(sums, matrix):
    high = sums.astype(bf16)
    low = (sums - high.astype(f32)).astype(bf16)
    both = jnp.concatenate([high.astype(f32), low.astype(f32)] + [jnp.zeros_like(sums)] * 6, axis=0)
    out = dot_nt(both.astype(bf16), matrix)
    return out[0:1] + out[1:2]


def attention_kernel(
    info_ref,
    x0,
    x1,
    x2,
    x3,
    c0,
    c1,
    c2,
    c3,
    buf_ref,
    rot_ref,
    sent_out,
    min_out,
    gb_out,
    ctx_out,
    dqkv_out,
    wd_out,
    wqkv_out,
    xhat_out,
    vec_ref,
    ub_ref,
    sums_ref,
    x_ref,
    cot_ref,
    wqkv_ref,
    wd_ref,
    qb_ref,
    min_ref,
    gb_ref,
    ctx_ref,
    dqkv_ref,
    xhat_ref,
    sent_ref,
    in_sem,
    out_sem,
    weight_sem,
    sent_sem,
    vec_col_ref,
):
    me = info_ref[64]
    loads = []
    for i, (one, other) in enumerate(zip((x0, x1, x2, x3), (c0, c1, c2, c3))):
        loads.append(pltpu.make_async_copy(one, x_ref.at[i], in_sem.at[i, 0]))
        loads.append(pltpu.make_async_copy(other, cot_ref.at[i], in_sem.at[i, 1]))
    for load in loads[:2]:
        load.start()
    assemble_a(me, buf_ref, wqkv_ref, wd_ref)
    for load in loads[2:]:
        load.start()
    read_vectors(me, buf_ref, vec_ref, qb_ref, ub_ref)
    weights = [
        pltpu.make_async_copy(wd_ref, wd_out, weight_sem.at[0]),
        pltpu.make_async_copy(wqkv_ref, wqkv_out, weight_sem.at[1]),
    ]
    for copy in weights:
        copy.start()
    stores = (
        (min_ref, min_out),
        (gb_ref, gb_out),
        (ctx_ref, ctx_out),
        (xhat_ref, xhat_out),
        (dqkv_ref, dqkv_out),
    )

    def store(n, r):
        rows = pl.ds(pl.multiple_of(r * ROW, ROW), ROW)
        src, dst = stores[n]
        return pltpu.make_async_copy(src.at[rows, :], dst.at[rows, :], out_sem.at[n, r])

    sums_ref[...] = jnp.zeros_like(sums_ref)

    @pl.loop(0, TP)
    def _(r):
        pltpu.make_async_copy(x0, x_ref.at[r], in_sem.at[r, 0]).wait()
        pltpu.make_async_copy(c0, cot_ref.at[r], in_sem.at[r, 1]).wait()
        here = pl.ds(pl.multiple_of(r * ROW, ROW), ROW)
        xhat, _ = normalize(x_ref[r].astype(f32))
        xhat_ref[here, :] = xhat.astype(bf16)
        attn_in = (xhat * vec_ref[0:1] + vec_ref[1:2]).astype(bf16)
        min_ref[here, :] = (xhat * vec_ref[2:3] + vec_ref[3:4]).astype(bf16)
        qkv = dot(attn_in, wqkv_ref[...]) + qb_ref[...]
        d = me ^ ((r & 1) * 2 + r // 2)
        base = (d * 2 + info_ref[65]) * SEGS
        ends, end = [], 0
        for j in range(SEGS - 1):
            end = end + info_ref[base + j]
            ends.append(end)
        rows = lax.broadcasted_iota(jnp.int32, (ROW, 1), 0)
        cols = lax.broadcasted_iota(jnp.int32, (1, ROW), 1)
        row_doc = sum([(rows >= e).astype(jnp.int32) for e in ends])
        col_doc = sum([(cols >= e).astype(jnp.int32) for e in ends])
        allowed = (row_doc == col_doc) & (rows <= cols)
        start = jnp.zeros_like(rows)
        for e in ends:
            start = jnp.maximum(start, jnp.where(rows >= e, e, 0))
        kept = jnp.where(rows < ends[-1], cot_ref[r].astype(f32), 0.0)
        gb = kept.astype(bf16)
        gb_ref[here, :] = gb
        dctx = dot_nt(gb, wd_ref[...]).astype(bf16)
        chosen = ((rows - start) == cols).astype(f32).astype(bf16)
        table = dot(chosen, rot_ref[...])
        pair = lambda n: table[:, n * 256 : n * 256 + 128] + table[:, n * 256 + 128 : n * 256 + 256]
        cosine, left, right = [jnp.concatenate([pair(n)] * 2, axis=1) for n in range(3)]
        scale = HEAD_DIM**-0.5
        q = (turn(qkv[:, 0:256], cosine, left, right).astype(bf16).astype(f32) * scale).astype(bf16)
        k = turn(qkv[:, 256:512], cosine, left, right).astype(bf16)
        v = qkv[:, 512:768].astype(bf16)
        lanes = lax.broadcasted_iota(jnp.int32, (1, 256), 1) // HEAD_DIM
        ctx, dq, dk, dv = [jnp.zeros((ROW, 256), f32)] * 4
        heads = range(LOCAL_HEADS)
        only = [(lanes == h).astype(f32).astype(bf16) for h in heads]
        qs, dcs = [q * m for m in only], [dctx * m for m in only]
        s_all = dot_nt(k, jnp.concatenate(qs, axis=0))
        dp_all = dot_nt(v, jnp.concatenate(dcs, axis=0))
        cut = [slice(h * ROW, (h + 1) * ROW) for h in heads]
        scores = [jnp.where(allowed, s_all[:, c], -1000000000.0) for c in cut]
        dprobs = [dp_all[:, c] for c in cut]
        probs = []
        for h in heads:
            shifted = jnp.exp(scores[h] - jnp.max(scores[h], axis=0, keepdims=True))
            probs.append(shifted * (1.0 / jnp.sum(shifted, axis=0, keepdims=True)))
        lows = [p.astype(bf16) for p in probs]
        ds = []
        for h in heads:
            inner = jnp.sum(dprobs[h] * probs[h], axis=0, keepdims=True)
            ds.append((probs[h] * (dprobs[h] - inner)).astype(bf16))
        p_all = jnp.concatenate(lows, axis=0)
        ds_all = jnp.concatenate(ds, axis=0)
        ctx = dot_tn(p_all, jnp.concatenate([v * m for m in only], axis=0))
        dq = dot_tn(ds_all, jnp.concatenate([k * m for m in only], axis=0))
        dv = dot(jnp.concatenate(lows, axis=1), jnp.concatenate(dcs, axis=0))
        dk = dot(jnp.concatenate(ds, axis=1), jnp.concatenate(qs, axis=0))
        ctx_ref[here, :] = ctx.astype(bf16)
        dqs = turn(dq * scale, cosine, -left, -right)
        dks = turn(dk, cosine, -left, -right)
        dqkv = jnp.concatenate([dqs, dks, dv], axis=1).astype(bf16)
        dqkv_ref[here, :] = dqkv

        @pl.when(r == 0)
        def _():
            sums_ref[0:1, :] = jnp.sum(kept, axis=0, keepdims=True)

        sums_ref[1:2, 0:QC] += jnp.sum(dqkv.astype(f32), axis=0, keepdims=True)
        for n in range(5):
            store(n, r).start()

    c = me % 2
    sums_ref[3:4, :] = through(sums_ref[1:2, 0:QC], wqkv_ref[...])
    columns = jnp.transpose(vec_ref[...])
    vec_col_ref[...] = columns

    def sent(d, n):
        rows = pl.ds(pl.multiple_of(d * 48, 16), 48)
        if n == 1:
            rows = pl.ds(pl.multiple_of(192 + d * 16, 16), 16)
        return pltpu.make_async_copy(
            sent_ref.at[:, :, rows, :], sent_out.at[:, :, rows, :], sent_sem.at[d, n]
        )

    @pl.loop(0, 4)
    def _(d):
        raw = dot_tn(xhat_ref[:, tile(d)], dqkv_ref[...])
        gain, bias = vec_col_ref[tile(d), 0:1], vec_col_ref[tile(d), 1:2]
        qkv_grad = (raw * gain + bias * sums_ref[1:2, 0:QC]).astype(bf16)
        sums_ref[2:3, tile(d)] = row_sums(raw * wqkv_ref[tile(d), :].astype(f32))
        dense_grad = dot_tn(ctx_ref[...], gb_ref[:, tile(d)]).astype(bf16)
        base = pl.multiple_of(d * 48, 16)
        dense_base = pl.multiple_of(192 + d * 16, 16)
        for y in range(4):
            for x in range(4):
                b, a = swapped(y, x, c)
                at = slice((y * 4 + x) * 16, (y * 4 + x + 1) * 16)
                for p in range(3):
                    sent_ref[b, a, pl.ds(base + p * 16, 16), :] = qkv_grad[
                        at, p * 256 : (p + 1) * 256
                    ]
                sent_ref[b, a, pl.ds(dense_base, 16), :] = dense_grad[at]
        sent(d, 0).start()
        sent(d, 1).start()

    for copy in weights:
        copy.wait()

    @pl.loop(0, 4)
    def _(i):
        for n in range(5):
            store(n, i).wait()
        sent(i, 0).wait()
        sent(i, 1).wait()


def attention(info, xs, cots, buf):
    tokens = TP * ROW
    dma = pltpu.SemaphoreType.DMA
    return call(
        attention_kernel,
        [
            shaped(4, 4, 256, 256),
            shaped(tokens, D),
            shaped(tokens, D),
            shaped(tokens, 256),
            shaped(tokens, QC),
            shaped(D // TP, D),
            shaped(D, QC),
            shaped(tokens, D),
            shaped(8, D, dtype=f32),
            shaped(1, HC, dtype=f32),
            shaped(8, D, dtype=f32),
        ],
        info,
        *xs,
        *cots,
        buf,
        jnp.asarray(rotary_tables()),
        places="s" + "h" * 8 + "vv",
        outs="hhhhhhhhvvv",
        scratch=[
            pltpu.VMEM((TP, ROW, D), bf16),
            pltpu.VMEM((TP, ROW, D), bf16),
            pltpu.VMEM((D, QC), bf16),
            pltpu.VMEM((D // TP, D), bf16),
            pltpu.VMEM((1, QC), f32),
            pltpu.VMEM((tokens, D), bf16),
            pltpu.VMEM((tokens, D), bf16),
            pltpu.VMEM((tokens, 256), bf16),
            pltpu.VMEM((tokens, QC), bf16),
            pltpu.VMEM((tokens, D), bf16),
            pltpu.VMEM((4, 4, 256, 256), bf16),
            dma((4, 2)),
            dma((5, 4)),
            dma((2,)),
            dma((4, 2)),
            pltpu.VMEM((D, 8), f32),
        ],
        flops=6e9,
        nbytes=2e7,
        trans=1e6,
    )


def mlp_kernel(
    me_ref,
    buf_in,
    min_in,
    gb_in,
    xhat_in,
    ub_ref,
    vec_ref,
    sums_a_ref,
    sent_out,
    hidden_out,
    dpre_out,
    wup_out,
    wdown_out,
    buf_ref,
    min_ref,
    gb_ref,
    wup_ref,
    wdown_ref,
    hidden_ref,
    dpre_ref,
    sent_ref,
    xhat_ref,
    sums_ref,
    image_ref,
    parts_ref,
    vec_col_ref,
    buf_sem,
    in_sem,
    out_sem,
    weight_sem,
    sent_sem,
    image_sem,
):
    me = me_ref[0]
    c = me % 2
    parts = [pltpu.make_async_copy(buf_in.at[b], buf_ref.at[b], buf_sem.at[b]) for b in range(4)]

    def load(t, n):
        src, dst = ((min_in, min_ref), (gb_in, gb_ref), (xhat_in, xhat_ref))[n]
        return pltpu.make_async_copy(src.at[tile(t), :], dst.at[tile(t), :], in_sem.at[t, n])

    for part in parts:
        part.start()
    for t in range(4):
        for n in range(2):
            load(t, n).start()
    for part in parts:
        part.wait()
    for t in range(4):
        load(t, 2).start()
    assemble_b(me, buf_ref, wup_ref, wdown_ref)
    weights = [
        pltpu.make_async_copy(wup_ref, wup_out, weight_sem.at[0]),
        pltpu.make_async_copy(wdown_ref, wdown_out, weight_sem.at[1]),
    ]
    for copy in weights:
        copy.start()
    sums_ref[...] = jnp.zeros_like(sums_ref)

    def store(t, n):
        src, dst = ((hidden_ref, hidden_out), (dpre_ref, dpre_out))[n]
        return pltpu.make_async_copy(src.at[tile(t), :], dst.at[tile(t), :], out_sem.at[t, n])

    @pl.loop(0, TP)
    def _(tn):
        t = tile(tn)
        load(tn, 0).wait()
        load(tn, 1).wait()

        def products(n):
            at = slice(n * 256, (n + 1) * 256)
            pre = dot(min_ref[t, :], wup_ref[:, at]) + ub_ref[:, at]
            return pre, dot_nt(gb_ref[t, :], wdown_ref[at, :])

        ahead = products(0)
        for n in range(4):
            at = slice(n * 256, (n + 1) * 256)
            pre, back = ahead
            if n < 3:
                ahead = products(n + 1)
            size = jnp.abs(pre) * 0.7071067811865476
            bell = jnp.exp(-0.5 * pre * pre)
            s = 1.0 / (1.0 + 0.3275911 * size)
            poly = s * (
                0.127414796
                + s * (-0.142248368 + s * (0.7107068705 + s * (-0.7265760135 + s * 0.5307027145)))
            )
            tail = poly * bell
            cumul = jnp.where(pre >= 0.0, 1.0 - tail, tail)
            hidden_ref[t, at] = (pre * cumul).astype(bf16)
            dpre = (back * (cumul + pre * (bell * 0.3989422804014327))).astype(bf16)
            dpre_ref[t, at] = dpre
            sums_ref[0:1, at] += jnp.sum(dpre.astype(f32), axis=0, keepdims=True)
        store(tn, 0).start()
        store(tn, 1).start()

    @pl.loop(0, 4)
    def _(y):
        grad = dot_tn(hidden_ref[:, tile(y)], gb_ref[...]).astype(bf16)
        for x in range(4):
            b, a = swapped(y, x, c)
            for cg in range(4):
                sent_ref[b, a, 256 + cg * 64 : 256 + (cg + 1) * 64, :] = grad[
                    x * 64 : (x + 1) * 64, cg * 256 : (cg + 1) * 256
                ]

    def sent(a, rows, n):
        base = a * 512 + rows.start
        return pltpu.make_async_copy(
            sent_ref.at[:, a, rows, :],
            sent_out.at[:, pl.ds(pl.multiple_of(base, 16), rows.size), :],
            sent_sem.at[a, n],
        )

    for a in range(4):
        sent(a, pl.ds(256, 256), 4).start()

    sums_ref[2:3, :] = through(sums_ref[0:1, :], wup_ref[...])
    vec_col_ref[...] = jnp.transpose(vec_ref[...])
    for t in range(4):
        load(t, 2).wait()

    def above(a, d):
        return sent(a, pl.ds(pl.multiple_of(d * 64, 64), 64), d)

    @pl.loop(0, 4)
    def _(d):
        raw = dot_tn(xhat_ref[:, tile(d)], dpre_ref[...])
        gain, bias = vec_col_ref[tile(d), 2:3], vec_col_ref[tile(d), 3:4]
        grad = (raw * gain + bias * sums_ref[0:1, :]).astype(bf16)
        sums_ref[1:2, tile(d)] = row_sums(raw * wup_ref[tile(d), :].astype(f32))
        for y in range(4):
            for x in range(4):
                b, a = swapped(y, x, c)
                at = slice((y * 4 + x) * 16, (y * 4 + x + 1) * 16)
                for cg in range(4):
                    row = pl.multiple_of(d * 64 + cg * 16, 16)
                    sent_ref[b, a, pl.ds(row, 16), :] = grad[at, cg * 256 : (cg + 1) * 256]
        for a in range(4):
            above(a, d).start()

    image_ref[...] = jnp.zeros_like(image_ref)

    def put(row, ref, line, count):
        for i in range(count):
            image_ref[pl.ds(row + i, 1), :] = ref[line : line + 1, i * 256 : (i + 1) * 256]

    put(0, sums_a_ref, 2, 4)
    put(4, sums_a_ref, 3, 4)
    put(8, sums_ref, 1, 4)
    put(12, sums_ref, 2, 4)
    for p in range(3):
        image_ref[pl.ds(16 + p * 4 + me, 1), :] = sums_a_ref[1:2, p * 256 : (p + 1) * 256]
    put(28, sums_a_ref, 0, 4)
    put(32 + 4 * me, sums_ref, 0, 4)
    put(48, sums_a_ref, 0, 4)
    image = image_ref[...]
    high = image.astype(bf16)
    parts_ref[0:IMAGE, :] = high
    parts_ref[IMAGE : 2 * IMAGE, :] = (image - high.astype(f32)).astype(bf16)
    images = [
        pltpu.make_async_copy(parts_ref, sent_out.at[b, pl.ds(2048, 2 * IMAGE), :], image_sem.at[b])
        for b in range(4)
    ]
    for copy in images:
        copy.start()
    for copy in weights:
        copy.wait()
    for i in range(TP):
        store(i, 0).wait()
        store(i, 1).wait()
        for n in range(4):
            above(i, n).wait()
        sent(i, pl.ds(256, 256), 4).wait()
    for copy in images:
        copy.wait()


def mlp(me, buf, mlp_in, gb, xhat, ub, vec, sums):
    tokens = TP * ROW
    dma = pltpu.SemaphoreType.DMA
    return call(
        mlp_kernel,
        [
            shaped(4, 2048 + 2 * IMAGE, 256),
            shaped(tokens, HC),
            shaped(tokens, HC),
            shaped(D, HC),
            shaped(HC, D),
        ],
        me,
        buf,
        mlp_in,
        gb,
        xhat,
        ub,
        vec,
        sums,
        places="s" + "h" * 4 + "vvv",
        outs="hhhhh",
        scratch=[
            pltpu.VMEM((4, 2048, 256), bf16),
            pltpu.VMEM((tokens, D), bf16),
            pltpu.VMEM((tokens, D), bf16),
            pltpu.VMEM((D, HC), bf16),
            pltpu.VMEM((HC, D), bf16),
            pltpu.VMEM((tokens, HC), bf16),
            pltpu.VMEM((tokens, HC), bf16),
            pltpu.VMEM((4, 4, 512, 256), bf16),
            pltpu.VMEM((tokens, D), bf16),
            pltpu.VMEM((8, D), f32),
            pltpu.VMEM((IMAGE, 256), f32),
            pltpu.VMEM((2 * IMAGE, 256), bf16),
            pltpu.VMEM((D, 8), f32),
            dma((4,)),
            dma((4, 3)),
            dma((4, 2)),
            dma((2,)),
            dma((4, 5)),
            dma((4,)),
        ],
        flops=9e9,
        nbytes=2e7,
        trans=2e6,
    )


def outputs_kernel(
    ctx_in,
    hidden_in,
    dqkv_in,
    dpre_in,
    wd_in,
    wdown_in,
    wqkv_in,
    wup_in,
    vec_ref,
    theirs_out,
    mine_out,
    ctx_ref,
    hidden_ref,
    dqkv_ref,
    dpre_ref,
    wd_ref,
    wdown_ref,
    wqkv_ref,
    wup_ref,
    both_ref,
    weight_sem,
    in_sem,
    out_sem,
):
    pairs = ((wqkv_in, wqkv_ref), (wup_in, wup_ref), (wd_in, wd_ref), (wdown_in, wdown_ref))
    weights = [
        pltpu.make_async_copy(src, dst, weight_sem.at[i]) for i, (src, dst) in enumerate(pairs)
    ]
    inputs = (
        (dqkv_in, dqkv_ref),
        (dpre_in, dpre_ref),
        (ctx_in, ctx_ref),
        (hidden_in, hidden_ref),
    )

    def load(t, n):
        src, dst = inputs[n]
        return pltpu.make_async_copy(src.at[tile(t), :], dst.at[tile(t), :], in_sem.at[t, n])

    def finished(i, n):
        dst = (theirs_out, mine_out)[n]
        return pltpu.make_async_copy(both_ref.at[i], dst.at[i - 2 * n], out_sem.at[i])

    for i in range(TP):
        for n in range(4):
            load((i + 2) % 4, n).start()
            if i == 0:
                weights[n].start()
    for weight in weights:
        weight.wait()

    @pl.loop(0, TP)
    def _(i):
        t = (i + 2) % 4
        for n in range(4):
            load(t, n).wait()
        here = tile(t)
        dattn = dot_nt(dqkv_ref[here, :], wqkv_ref[...])
        dmlp = dot_nt(dpre_ref[here, :], wup_ref[...])
        both_ref[i, 1] = (dattn * vec_ref[0:1] + dmlp * vec_ref[2:3]).astype(bf16)
        forward = dot(ctx_ref[here, :], wd_ref[...]) + dot(hidden_ref[here, :], wdown_ref[...])
        both_ref[i, 0] = forward.astype(bf16)

        @pl.when(i < 2)
        def _():
            finished(i, 0).start()

        @pl.when(i >= 2)
        def _():
            finished(i, 1).start()

    for i in range(TP):
        finished(i, i // 2).wait()


def outputs(ctx, hidden, dqkv, dpre, wd, wdown, wqkv, wup, vec):
    tokens = TP * ROW
    dma = pltpu.SemaphoreType.DMA
    return call(
        outputs_kernel,
        [shaped(2, 2, ROW, D), shaped(2, 2, ROW, D)],
        ctx,
        hidden,
        dqkv,
        dpre,
        wd,
        wdown,
        wqkv,
        wup,
        vec,
        places="h" * 8 + "v",
        outs="hh",
        scratch=[
            pltpu.VMEM((tokens, 256), bf16),
            pltpu.VMEM((tokens, HC), bf16),
            pltpu.VMEM((tokens, QC), bf16),
            pltpu.VMEM((tokens, HC), bf16),
            pltpu.VMEM((D // TP, D), bf16),
            pltpu.VMEM((HC, D), bf16),
            pltpu.VMEM((D, QC), bf16),
            pltpu.VMEM((D, HC), bf16),
            pltpu.VMEM((TP, 2, ROW, D), bf16),
            dma((4,)),
            dma((4, 4)),
            dma((4,)),
        ],
        flops=6.5e9,
        nbytes=1.6e7,
    )


def half_kernel(a0_ref, b0_ref, a1_ref, b1_ref, kept_ref, send_ref):
    kept_ref[...] = a0_ref[...].astype(f32) + b0_ref[...].astype(f32)
    send_ref[...] = (a1_ref[...].astype(f32) + b1_ref[...].astype(f32)).astype(bf16)


def half_sum(mine, got):
    mine, got = in_hbm(mine), in_hbm(got)
    first = pl.BlockSpec((1, 1, ROW // 2, D), lambda n, k: (0, n, k, 0))
    second = pl.BlockSpec((1, 1, ROW // 2, D), lambda n, k: (1, n, k, 0))
    out = pl.BlockSpec((1, 1, ROW // 2, D), lambda n, k: (0, n, k, 0))
    return pl.pallas_call(
        half_kernel,
        grid=(2, 2),
        in_specs=[first, first, second, second],
        out_specs=[out, out],
        out_shape=[pltpu.HBM((1, 2, ROW, D), f32), pltpu.HBM((1, 2, ROW, D), bf16)],
        compiler_params=pltpu.CompilerParams(vmem_limit_bytes=VMEM),
        cost_estimate=pl.CostEstimate(flops=0, bytes_accessed=8000000, transcendentals=0),
    )(mine, got, mine, got)


def close_kernel(len_ref, x_ref, cot_ref, kept_ref, got_ref, vec_ref, out_ref, grad_ref):
    x = x_ref[...].astype(f32)
    out_ref[...] = (x + kept_ref[0, 0] + got_ref[0, 0].astype(f32) + vec_ref[4:5]).astype(bf16)
    e = kept_ref[0, 1] + got_ref[0, 1].astype(f32)
    xhat, inv_std = normalize(x)
    mean_e = jnp.mean(e, axis=-1, keepdims=True)
    mean_ex = jnp.mean(e * xhat, axis=-1, keepdims=True)
    used = sum([len_ref[0, j] for j in range(SEGS - 1)])
    rows = pl.program_id(0) * x.shape[0] + lax.broadcasted_iota(jnp.int32, (x.shape[0], 1), 0)
    kept = jnp.where(rows < used, cot_ref[...].astype(f32), 0.0)
    grad_ref[...] = kept + inv_std * (e - mean_e - xhat * mean_ex)


def close(lengths, x, cot, kept, got, vec):
    row = pl.BlockSpec((ROW // 4, D), lambda k: (k, 0))
    both = pl.BlockSpec((1, 2, ROW // 4, D), lambda k: (0, 0, k, 0))
    return pl.pallas_call(
        close_kernel,
        grid=(4,),
        in_specs=[SMEM_SPEC, row, row, both, both, pl.BlockSpec((8, D), lambda k: (0, 0))],
        out_specs=[row, row],
        out_shape=[pltpu.HBM((ROW, D), bf16), pltpu.HBM((ROW, D), f32)],
        compiler_params=pltpu.CompilerParams(vmem_limit_bytes=VMEM),
        cost_estimate=pl.CostEstimate(flops=0, bytes_accessed=6000000, transcendentals=0),
    )(lengths, *[in_hbm(v) for v in (x, cot, kept, got)], vec)


def add_early_kernel(a_ref, out_ref):
    out_ref[0] = sum([a_ref[i, 0].astype(f32) for i in range(4)]).astype(bf16)


def add_early(sent_a):
    return pl.pallas_call(
        add_early_kernel,
        grid=(4,),
        in_specs=[pl.BlockSpec((4, 1, 256, 256), lambda a: (0, a, 0, 0))],
        out_specs=pl.BlockSpec((1, 256, 256), lambda a: (a, 0, 0)),
        out_shape=pltpu.HBM((4, 256, 256), bf16),
        compiler_params=pltpu.CompilerParams(vmem_limit_bytes=VMEM),
        cost_estimate=pl.CostEstimate(flops=0, bytes_accessed=3000000, transcendentals=0),
    )(in_hbm(sent_a))


def add(early, sent_b):
    rows = 768 + 2 * IMAGE

    def kernel(early_ref, b_ref, image_ref, out_ref, sums_ref):
        out_ref[0, 0:256, :] = early_ref[0]
        total = sum([b_ref[i].astype(f32) for i in range(4)])
        out_ref[0, 256:768, :] = total.astype(bf16)

        @pl.when(pl.program_id(0) == 0)
        def _():
            image = sum([image_ref[i].astype(f32) for i in range(4)])
            image = image[:IMAGE] + image[IMAGE:]
            high = image.astype(bf16)
            sums_ref[0:IMAGE, :] = high
            sums_ref[IMAGE : 2 * IMAGE, :] = (image - high.astype(f32)).astype(bf16)

        out_ref[0, 768:rows, :] = sums_ref[...]

    return pl.pallas_call(
        kernel,
        grid=(4,),
        in_specs=[
            pl.BlockSpec((1, 256, 256), lambda a: (a, 0, 0)),
            pl.BlockSpec((4, 512, 256), lambda a: (0, a, 0)),
            pl.BlockSpec((4, 2 * IMAGE, 256), lambda a: (0, 2048 // (2 * IMAGE), 0)),
        ],
        out_specs=pl.BlockSpec((1, rows, 256), lambda a: (a, 0, 0)),
        out_shape=pltpu.HBM((4, rows, 256), bf16),
        scratch_shapes=[pltpu.VMEM((2 * IMAGE, 256), bf16)],
        compiler_params=pltpu.CompilerParams(vmem_limit_bytes=VMEM),
        cost_estimate=pl.CostEstimate(flops=0, bytes_accessed=6000000, transcendentals=0),
    )(in_hbm(early), in_hbm(sent_b), in_hbm(sent_b))


LAST = QC + HC + 4 * 256


def image_rows(d):
    return [start + d for start in STARTS[:4]] + [28 + d, 48 + d] + [
        32 + 4 * d + i for i in range(4)
    ] + [16 + 3 * d + i for i in range(3)]


def part_kernel(far_ref, in_ref, slots_ref, keep_ref, send_ref, total_ref, rows_ref):
    far = far_ref[0]
    total_ref[...] = sum([in_ref[i].astype(f32) for i in range(4)])
    rows_ref[...] = jnp.zeros_like(rows_ref)
    for d in range(4):
        for i, row in enumerate(image_rows(d)):
            high = total_ref[768 + row : 769 + row, :]
            low = total_ref[768 + IMAGE + row : 769 + IMAGE + row, :]
            rows_ref[d, i : i + 1, :] = high + low
        image = rows_ref[d]
        high = image.astype(bf16)
        low = (image - high.astype(f32)).astype(bf16)
        for zh in range(2):
            s = d * 2 + zh
            for p in range(3):
                row = (d * 3 + p) * 16 + zh * 8
                slots_ref[s, :, p * 256 : (p + 1) * 256] = total_ref[row : row + 8, :].astype(bf16)
            for cg in range(4):
                row = 256 + (d * 4 + cg) * 16 + zh * 8
                at = QC + cg * 256
                slots_ref[s, :, at : at + 256] = total_ref[row : row + 8, :].astype(bf16)
            for n, block in enumerate((high[:8], high[8:], low[:8], low[8:])):
                at = QC + HC + n * 256
                slots_ref[s, :, at : at + 256] = block
    for ref, half in ((keep_ref, far), (send_ref, 1 - far)):
        for cg in range(4):
            at = slice(cg * 256, (cg + 1) * 256)
            row = pl.multiple_of(192 + cg * 16 + half * 8, 8)
            ref[32:40, at] = total_ref[pl.ds(row, 8), :].astype(ref.dtype)
            row = pl.multiple_of(512 + cg * 64 + half * 32, 8)
            ref[0:32, at] = total_ref[pl.ds(row, 32), :].astype(ref.dtype)


def part(far, received):
    return call(
        part_kernel,
        [shaped(8, 8, LAST), shaped(40, D, dtype=f32), shaped(40, D)],
        far,
        received,
        outs="uuu",
        scratch=[pltpu.VMEM((768 + 2 * IMAGE, 256), f32), pltpu.VMEM((4, 16, 256), f32)],
        nbytes=4e6,
    )


def finish_kernel(place_ref, slots_ref, keep_ref, got_ref, qkv_ref, up_ref, dense_ref, down_ref, *rest):
    tiny_refs, image_ref = rest[:8], rest[8]
    image = [jnp.zeros((8, 256), f32)] * 2
    for s in range(8):
        for n in range(4):
            at = QC + HC + n * 256
            image[n % 2] = image[n % 2] + slots_ref[s, :, at : at + 256].astype(f32)
    image_ref[0:8, :] = image[0]
    image_ref[8:16, :] = image[1]
    for d in range(4):
        both = slots_ref[2 * d, :, 0 : QC + HC].astype(f32) + slots_ref[
            2 * d + 1, :, 0 : QC + HC
        ].astype(f32)
        for p in range(3):
            at = p * D + d * 256
            qkv_ref[:, at : at + 256] = both[:, p * 256 : (p + 1) * 256]
        up_ref[:, d * HC : (d + 1) * HC] = both[:, QC:]
    total = keep_ref[...] + got_ref[...].astype(f32)
    dense_ref[...] = total[32:40]
    down_ref[...] = total[0:32]
    p = place_ref[0]
    f = p % 32
    lines = (0, 1, 2, 3, 10 + f * 24 // 256, 4, 6 + f // 8, 5)
    for line, size, ref in zip(lines, SIZES, tiny_refs):
        lane = (p * size) % 256
        values = image_ref[pl.ds(line, 1), :]
        if size == 24:
            values = jnp.concatenate([values, image_ref[pl.ds(line + 1, 1), :]], axis=1)
        ref[...] = pltpu.roll(values, values.shape[1] - lane, 1)[:, :size]


def finish(place, slots, keep, got):
    return call(
        finish_kernel,
        [
            shaped(8, 3 * D, dtype=f32),
            shaped(8, FF, dtype=f32),
            shaped(8, D, dtype=f32),
            shaped(32, D, dtype=f32),
        ]
        + [shaped(1, size, dtype=f32) for size in SIZES],
        place,
        slots,
        keep,
        got,
        scratch=[pltpu.VMEM((16, 256), f32)],
        nbytes=2e6,
    )


def body(
    inputs,
    cotangent,
    lengths,
    norm1_gain,
    norm1_bias,
    norm2_gain,
    norm2_bias,
    qkv_weight,
    qkv_bias,
    dense_weight,
    dense_bias,
    up_weight,
    up_bias,
    down_weight,
    down_bias,
):
    me = lax.axis_index("dp").astype(jnp.int32)
    index = lax.axis_index("fsdp").astype(jnp.int32)
    far = (index % 2)[None]
    me1 = me[None]
    outer, inner = outer_groups(), inner_groups()

    vectors = (
        norm1_gain,
        norm1_bias,
        norm2_gain,
        norm2_bias,
        qkv_bias,
        dense_bias,
        up_bias,
        down_bias,
    )
    slots, pieces = prepare(
        qkv_weight.reshape(8, 3 * D),
        up_weight.reshape(8, FF),
        dense_weight.reshape(8, D),
        down_weight.reshape(32, D),
        lengths,
        vectors,
    )
    far_pieces = flip_far(pieces)
    first = a2a(slots, stack_groups())
    block, lens = spread(index[None], first.reshape(4, 16, SLOT), pieces, far_pieces)
    info = jnp.concatenate([lens[0], me1, far])

    block, x0 = lax.optimization_barrier((block, inputs))
    x1 = flip_chip(x0)
    second = a2a(block, inner)
    second, x1, c0 = lax.optimization_barrier((second, x1, cotangent))
    c1 = flip_chip(c0)
    third_a = a2a(widen_a(second), outer)
    x2, x3 = flip_core(x0), flip_core(x1)
    c2, c3 = flip_core(c0), flip_core(c1)
    xs, cots = (x0, x1, x2, x3), (c0, c1, c2, c3)
    wide_b, xs, cots = lax.optimization_barrier((widen_b(second), xs, cots))
    third_b = a2a(wide_b, outer)

    sent_a, mlp_in, gb, ctx, dqkv, wd, wqkv, xhat, vec, up_b, sums = attention(
        info, xs, cots, third_a
    )
    sent_a = a2a(sent_a, outer)
    sent_b, hidden, dpre, wup, wdown = mlp(me1, third_b, mlp_in, gb, xhat, up_b, vec, sums)
    sent_b = a2a(sent_b, outer)

    theirs, mine = outputs(ctx, hidden, dqkv, dpre, wd, wdown, wqkv, wup, vec)
    kept, send = half_sum(mine, flip_core(theirs))

    early, send, sent_b = lax.optimization_barrier((add_early(sent_a), send, sent_b))
    got = flip_chip(send)
    fourth = a2a(add(early, sent_b), inner)
    slots, keep, rest = part(far, fourth)
    block_output, input_grad = close(lengths, inputs, cotangent, kept, got, vec)
    place = (me * 32 + index)[None]
    results = finish(place, a2a(slots, stack_groups()), keep, flip_far(rest))
    flat = [r.reshape(-1) for r in results]
    return (
        block_output,
        input_grad,
        flat[4],
        flat[5],
        flat[6],
        flat[7],
        flat[0],
        flat[8],
        flat[2],
        flat[9],
        flat[1],
        flat[10],
        flat[3],
        flat[11],
    )


def solution(mesh):
    flat = P(("dp", "fsdp"))
    rows = P(("dp", "fsdp"), None)
    return jax.shard_map(
        body,
        mesh=mesh,
        in_specs=(rows,) * 3 + (flat,) * 12,
        out_specs=(rows,) * 2 + (flat,) * 12,
        check_vma=False,
    )
```

time: 234 us -> 200 us (0.85)
  blocking collectives: 19.5 us -> 0 us
  waiting for transfers between devices: 65.3 us -> 54.2 us
  local copies, waits for them, and re-layouts: 13.9 us -> 11.5 us
    all_to_all x1 -> x0, blocking collectives: 19.5 us -> none  [a2a(): lax.all_to_all(values, AXES, 0, 0, tiled=True, axis_index_groups=groups)]
    all_to_all x7 -> x8, waiting for transfers between devices: 9.59 us -> 26.5 us  [a2a(): lax.all_to_all(values, AXES, 0, 0, tiled=True, axis_index_groups=groups)]
    ppermute x2, waiting for transfers between devices: 19.5 us -> 6.31 us  [flip_far(): return lax.ppermute(values, 'fsdp', [(i, i ^ 1) for i in range(32)])]
    ppermute x2 -> x0, waiting for transfers between devices: 11.4 us -> none  [outer_flip(): return lax.ppermute(values, AXES, pairs)]
    pallas_call x1 -> x3, Pallas kernels: 4.89 us -> 12.8 us  [the longest x1 4.63 us: close(): pl.pallas_call(close_kernel, grid=(4,), in_specs=[SMEM_SPEC, row, row, bo...]
    pallas_call x9, Pallas kernels: 69.8 us -> 62 us  [call(): pl.pallas_call(kernel, in_specs=[SPECS[p] for p in places], out_specs=out...]
    ppermute x2 -> x0, starting transfers between devices: 3.7 us -> none  [outer_flip(): return lax.ppermute(values, AXES, pairs)]
    all_to_all x7 -> x8, starting transfers between devices: 36.6 us -> 39.9 us  [a2a(): lax.all_to_all(values, AXES, 0, 0, tiled=True, axis_index_groups=groups)]
  transfers between devices with their start and end apart: 19 -> 18, of which waited for: 11 -> 9; matrix products, arithmetic and copies ran while one was open for 0% -> 0% of each run, Pallas kernels for 32% -> 35%
where the time goes in v3:
time: 200 us; the launch traced here: 199 us
  Pallas kernels  79.1 us (40%)
  waiting for transfers between devices  54.2 us (27%)
  starting transfers between devices  53.5 us (27%)
  local copies, waits for them, and re-layouts  11.5 us (6%)
    pallas_call x9, Pallas kernels, call(): pl.pallas_call(kernel, in_specs=[SPECS[p] for p in places], out_specs=out...  62 us
    all_to_all x8, starting transfers between devices, a2a(): lax.all_to_all(values, AXES, 0, 0, tiled=True, axis_index_groups=groups)  39.9 us
    all_to_all x8, waiting for transfers between devices, a2a(): lax.all_to_all(values, AXES, 0, 0, tiled=True, axis_index_groups=groups)  26.5 us
    ppermute x3, waiting for transfers between devices, flip_chip(): return lax.ppermute(values, 'dp', [(0, 2), (2, 0), (1, 3), (3, 1)])  20.9 us
    unnamed x30, local copies, waits for them, and re-layouts  8.15 us
    ppermute x5, starting transfers between devices, flip_core(): return lax.ppermute(values, 'dp', [(0, 1), (1, 0), (2, 3), (3, 2)])  6.81 us
    ppermute x2, waiting for transfers between devices, flip_far(): return lax.ppermute(values, 'fsdp', [(i, i ^ 1) for i in range(32)])  6.31 us
    ppermute x2, starting transfers between devices, flip_far(): return lax.ppermute(values, 'fsdp', [(i, i ^ 1) for i in range(32)])  5.77 us
  transfers between devices with their start and end apart: 18, of which 9 were waited for; matrix products, arithmetic and copies ran while one was open for 0% of the time, Pallas kernels for 35%

profile of v3, /device:TPU:1, one launch (start us, length us, event | category | flops | bytes accessed | tf_op | source)
XLA Modules:
  0.0 199.1 jit_solution(12976225965318498848)
XLA Ops:
  0.6 0.7 reshape.81.dense_in
  1.4 0.8 reshape.79.qkv_ref
  2.2 0.9 reshape.80.up_ref
  3.1 0.9 reshape.82.down_in
  4.0 1.6 shard_map.263
  5.6 0.0 copy-start.6
  5.6 7.0 %all-to-all-start = ((bf16[8,8,1920]{2,1,0:T(8,128)(2,1)}), bf16[8,8,1920]{2,1,0:T(8,128)(2,1)S(1)}, u32[]{:S(2)}, u32[]{:S(2)}) async-start(bf16[8,8,1920]{2,1,0:T(8,128)(2,1)} %get-tuple-element.72), calls=%async_computation | async-start | bytes 491520 | tf_op jit(solution)/shard_map/all_to_all | solution.py:61
  12.6 2.9 %collective-permute-start = (bf16[40,1024]{1,0:T(8,128)(2,1)S(1)}, bf16[40,1024]{1,0:T(8,128)(2,1)S(1)}, u32[]{:S(2)}, u32[]{:S(2)}) collective-permute-start(bf16[40,1024]{1,0:T(8,128)(2,1)S(1)} %get-tuple-element.73.mine_ref), channel_id=1, source_target_pairs={{0,1},{1,0},{2,3},{3,2},{4,5},{5,4},{6,7},{7,6},{8,9},{9,8},{10,11... | collective-permute-start | bytes 245768 | tf_op jit(solution)/shard_map/ppermute | solution.py:73
  15.5 5.4 %collective-permute-done.theirs_ref = bf16[40,1024]{1,0:T(8,128)(2,1)S(1)} collective-permute-done((bf16[40,1024]{1,0:T(8,128)(2,1)S(1)}, bf16[40,1024]{1,0:T(8,128)(2,1)S(1)}, u32[]{:S(2)}, u32[]{:S(2)}) %collective-permute-start) | collective-permute-done | bytes 81952 | tf_op jit(solution)/shard_map/ppermute | solution.py:73
  20.8 0.0 all-to-all-done
  20.8 1.7 shard_map.264
  22.6 4.2 %all-to-all-start.1 = ((bf16[4,832,256]{2,1,0:T(8,128)(2,1)}), bf16[4,832,256]{2,1,0:T(8,128)(2,1)S(1)}, u32[]{:S(2)}, u32[]{:S(2)}) async-start(bf16[4,832,256]{2,1,0:T(8,128)(2,1)} %get-tuple-element.76), calls=%async_computation.1 | async-start | bytes 3407872 | tf_op jit(solution)/shard_map/all_to_all | solution.py:61
  26.8 0.3 collective-permute-start.1
  27.0 12.2 %collective-permute-done.1.x1 = bf16[256,1024]{1,0:T(8,128)(2,1)S(1)} collective-permute-done((bf16[256,1024]{1,0:T(8,128)(2,1)S(1)}, bf16[256,1024]{1,0:T(8,128)(2,1)S(1)}, u32[]{:S(2)}, u32[]{:S(2)}) %collective-permute-start.1) | collective-permute-done | bytes 524320 | tf_op jit(solution)/shard_map/ppermute | solution.py:69
  39.2 1.1 all-to-all-done.1.in_ref
  40.3 1.5 shard_map.266
  41.9 4.6 %all-to-all-start.2 = ((bf16[4,1088,256]{2,1,0:T(8,128)(2,1)}), bf16[4,1088,256]{2,1,0:T(8,128)(2,1)}, u32[]{:S(2)}, u32[]{:S(2)}) async-start(bf16[4,1088,256]{2,1,0:T(8,128)(2,1)} %shard_map.266), calls=%async_computation.2 | async-start | bytes 4456448 | tf_op jit(solution)/shard_map/all_to_all | solution.py:61
  46.5 0.4 collective-permute-start.4
  46.9 2.1 %collective-permute-start.2 = (bf16[256,1024]{1,0:T(8,128)(2,1)S(1)}, bf16[256,1024]{1,0:T(8,128)(2,1)S(1)}, u32[]{:S(2)}, u32[]{:S(2)}) collective-permute-start(bf16[256,1024]{1,0:T(8,128)(2,1)S(1)} %copy-done.6), channel_id=1, source_target_pairs={{0,32},{32,0},{64,96},{96,64},{1,33},{33,1},{65,97},{97,65},{2,34}... | collective-permute-start | bytes 1572872 | tf_op jit(solution)/shard_map/ppermute | solution.py:65
  49.0 0.0 collective-permute-start.5
  49.0 0.5 collective-permute-start.3
  49.5 8.8 %collective-permute-done.4.c1 = bf16[256,1024]{1,0:T(8,128)(2,1)S(1)} collective-permute-done((bf16[256,1024]{1,0:T(8,128)(2,1)S(1)}, bf16[256,1024]{1,0:T(8,128)(2,1)S(1)}, u32[]{:S(2)}, u32[]{:S(2)}) %collective-permute-start.4) | collective-permute-done | bytes 524320 | tf_op jit(solution)/shard_map/ppermute | solution.py:69
  58.3 2.7 %collective-permute-start.6 = (bf16[256,1024]{1,0:T(8,128)(2,1)S(1)}, bf16[256,1024]{1,0:T(8,128)(2,1)}, u32[]{:S(2)}, u32[]{:S(2)}) collective-permute-start(bf16[256,1024]{1,0:T(8,128)(2,1)S(1)} %collective-permute-done.4.c1), channel_id=1, source_target_pairs={{0,32},{32,0},{64,96},{96,64},{1,33},{33,1},{65,97},{97,65},{2,34}... | collective-permute-start | bytes 1572872 | tf_op jit(solution)/shard_map/ppermute | solution.py:65
  60.9 2.2 %shard_map.265 = bf16[4,2048,256]{2,1,0:T(8,128)(2,1)} custom-call(bf16[4,832,256]{2,1,0:T(8,128)(2,1)S(1)} %all-to-all-done.1.in_ref), custom_call_target="tpu_custom_call" | custom-call | bytes 6000000 | tf_op jit(solution)/shard_map/pallas_call | solution.py:107
  63.2 0.0 collective-permute-done.2.x2
  63.2 0.0 collective-permute-done.3.x3
  63.2 0.0 collective-permute-done.5.c2
  63.2 0.8 copy-done.10
  64.0 0.2 copy-done.12
  64.2 0.8 copy-done.11
  65.0 0.0 collective-permute-done.6.c3
  65.0 0.0 all-to-all-done.2.buf_ref
  65.0 4.8 %all-to-all-start.3 = ((bf16[4,2048,256]{2,1,0:T(8,128)(2,1)}), bf16[4,2048,256]{2,1,0:T(8,128)(2,1)}, u32[]{:S(2)}, u32[]{:S(2)}) async-start(bf16[4,2048,256]{2,1,0:T(8,128)(2,1)} %shard_map.265), calls=%async_computation.3 | async-start | bytes 8388608 | tf_op jit(solution)/shard_map/all_to_all | solution.py:61
  69.9 0.1 pad_add_fusion.info_ref
  70.0 19.3 %shard_map.267 = (bf16[4,4,256,256]{3,2,1,0:T(8,128)(2,1)}, bf16[1024,1024]{1,0:T(8,128)(2,1)}, bf16[1024,1024]{1,0:T(8,128)(2,1)}, bf16[1024,256]{1,0:T(8,128)(...) custom-call(s32[66]{0:T(128)S(1)} %pad_add_fusion.info_ref, ...), custom_call_target="tpu_custom_call" | custom-call | flops 6000000000 | bytes 20000000 | tf_op jit(solution)/shard_map/pallas_call | solution.py:107
  89.3 7.5 %all-to-all-done.3.buf_in = bf16[4,2048,256]{2,1,0:T(8,128)(2,1)} async-done(((bf16[4,2048,256]{2,1,0:T(8,128)(2,1)}), bf16[4,2048,256]{2,1,0:T(8,128)(2,1)}, u32[]{:S(2)}, u32[]{:S(2)}) %all-to-all-start.3) | async-done | bytes 4194336 | tf_op jit(solution)/shard_map/all_to_all | solution.py:61
  96.8 3.8 %all-to-all-start.4 = ((bf16[4,4,256,256]{3,2,1,0:T(8,128)(2,1)}), bf16[4,4,256,256]{3,2,1,0:T(8,128)(2,1)S(1)}, u32[]{:S(2)}, u32[]{:S(2)}) async-start(bf16[4,4,256,256]{3,2,1,0:T(8,128)(2,1)} %get-tuple-element.107), calls=%async_computation.4 | async-start | bytes 4194304 | tf_op jit(solution)/shard_map/all_to_all | solution.py:61
  100.6 20.5 %shard_map.268 = (bf16[4,2176,256]{2,1,0:T(8,128)(2,1)}, bf16[1024,1024]{1,0:T(8,128)(2,1)}, bf16[1024,1024]{1,0:T(8,128)(2,1)}, bf16[1024,1024]{1,0:T(8,128)(2,1)}, bf16[1024,1024]{1,0:T(8,128)(2,1)}) custom-call(s32[1]{0:T(128)} %bitcast.11.me_ref, bf16[4,2048,256]{2,1,0:T(8,128)(2,1)} %all-to-all-done.3.buf_in, ...), custom_call_target="tpu_custom_call" | custom-call | flops 8999999488 | bytes 20000000 | tf_op jit(solution)/shard_map/pallas_call | solution.py:107
  121.1 0.0 all-to-all-done.4.a_ref
  121.1 1.3 copy-done.3
  122.4 4.9 %all-to-all-start.5 = ((bf16[4,2176,256]{2,1,0:T(8,128)(2,1)}), bf16[4,2176,256]{2,1,0:T(8,128)(2,1)}, u32[]{:S(2)}, u32[]{:S(2)}) async-start(bf16[4,2176,256]{2,1,0:T(8,128)(2,1)} %get-tuple-element.109), calls=%async_computation.5 | async-start | bytes 8912896 | tf_op jit(solution)/shard_map/all_to_all | solution.py:61
  127.3 13.1 %shard_map.269 = (bf16[2,2,256,1024]{3,2,1,0:T(8,128)(2,1)}, bf16[2,2,256,1024]{3,2,1,0:T(8,128)(2,1)}) custom-call(bf16[1024,256]{1,0:T(8,128)(2,1)} %get-tuple-element.89.ctx_in, bf16[1024,1024]{1,0:T(8,128)(2,1)} %get-tuple-element.97.hidden_in, bf16[1024,768]{1,0:T(8,128)(2,1)} %get-tuple-element.98.dqkv_in, ...), custom_call_target="tpu_custom_call" | custom-call | flops 6499999744 | bytes 16000000 | tf_op jit(solution)/shard_map/pallas_call | solution.py:107
  140.4 1.5 collective-permute-start.7
  141.9 3.6 %shard_map.271.early_ref = bf16[4,256,256]{2,1,0:T(8,128)(2,1)} custom-call(bf16[4,4,256,256]{3,2,1,0:T(8,128)(2,1)} %copy-done.3), custom_call_target="tpu_custom_call" | custom-call | bytes 3000000 | tf_op jit(solution)/shard_map/pallas_call | solution.py:1011
  145.5 0.4 collective-permute-done.7.b0_ref.b1_ref
  145.9 1.4 copy-done.4
  147.3 4.3 %shard_map.270 = (f32[1,2,256,1024]{3,2,1,0:T(8,128)}, bf16[1,2,256,1024]{3,2,1,0:T(8,128)(2,1)}) custom-call(bf16[2,2,256,1024]{3,2,1,0:T(8,128)(2,1)} %get-tuple-element.104.a0_ref.a1_ref, bf16[2,2,256,1024]{3,2,1,0:T(8,128)(2,1)} %copy-done.4, bf16[2,2,256,1024]{3,2,1,0:T(8,128)(2,1)} %get-tuple-element.104.a0_ref.a1_ref, bf16[2,2,256,1024]{3,2,1,0:T(8,128)(2,1)} %copy-done.4), custom_call_target="tpu_custom_call" | custom-call | bytes 8000000 | tf_op jit(solution)/shard_map/pallas_call | solution.py:968
  151.6 4.0 %all-to-all-done.5.b_ref.image_ref = bf16[4,2176,256]{2,1,0:T(8,128)(2,1)} async-done(((bf16[4,2176,256]{2,1,0:T(8,128)(2,1)}), bf16[4,2176,256]{2,1,0:T(8,128)(2,1)}, u32[]{:S(2)}, u32[]{:S(2)}) %all-to-all-start.5) | async-done | bytes 4456480 | tf_op jit(solution)/shard_map/all_to_all | solution.py:61
  155.7 4.6 %shard_map.273 = bf16[4,896,256]{2,1,0:T(8,128)(2,1)} custom-call(bf16[4,256,256]{2,1,0:T(8,128)(2,1)} %shard_map.271.early_ref, bf16[4,2176,256]{2,1,0:T(8,128)(2,1)} %all-to-all-done.5.b_ref.image_ref, bf16[4,2176,256]{2,1,0:T(8,128)(2,1)} %all-to-all-done.5.b_ref.image_ref), custom_call_target="tpu_custom_call" | custom-call | bytes 6000000 | tf_op jit(solution)/shard_map/pallas_call | solution.py:1040
  160.2 3.6 %all-to-all-start.6 = ((bf16[4,896,256]{2,1,0:T(8,128)(2,1)}), bf16[4,896,256]{2,1,0:T(8,128)(2,1)S(1)}, u32[]{:S(2)}, u32[]{:S(2)}) async-start(bf16[4,896,256]{2,1,0:T(8,128)(2,1)} %shard_map.273), calls=%async_computation.6 | async-start | bytes 3670016 | tf_op jit(solution)/shard_map/all_to_all | solution.py:61
  163.8 0.0 copy-start.1
  163.9 0.4 collective-permute-start.8
  164.2 13.8 %all-to-all-done.6.in_ref = bf16[4,896,256]{2,1,0:T(8,128)(2,1)S(1)} async-done(((bf16[4,896,256]{2,1,0:T(8,128)(2,1)}), bf16[4,896,256]{2,1,0:T(8,128)(2,1)S(1)}, u32[]{:S(2)}, u32[]{:S(2)}) %all-to-all-start.6) | async-done | bytes 1835040 | tf_op jit(solution)/shard_map/all_to_all | solution.py:61
  178.1 1.2 shard_map.274
  179.3 7.0 %all-to-all-start.7 = ((bf16[8,8,2816]{2,1,0:T(8,128)(2,1)}), bf16[8,8,2816]{2,1,0:T(8,128)(2,1)S(1)}, u32[]{:S(2)}, u32[]{:S(2)}) async-start(bf16[8,8,2816]{2,1,0:T(8,128)(2,1)} %get-tuple-element.115), calls=%async_computation.7 | async-start | bytes 720896 | tf_op jit(solution)/shard_map/all_to_all | solution.py:61
  186.3 2.9 %collective-permute-start.9 = (bf16[40,1024]{1,0:T(8,128)(2,1)}, bf16[40,1024]{1,0:T(8,128)(2,1)S(1)}, u32[]{:S(2)}, u32[]{:S(2)}) collective-permute-start(bf16[40,1024]{1,0:T(8,128)(2,1)} %get-tuple-element.117), channel_id=1, source_target_pairs={{0,1},{1,0},{2,3},{3,2},{4,5},{5,4},{6,7},{7,6},{8,9},{9,8},{10,11... | collective-permute-start | bytes 245768 | tf_op jit(solution)/shard_map/ppermute | solution.py:73
  189.2 1.0 copy-done.5
  190.2 4.6 %shard_map.272 = (bf16[256,1024]{1,0:T(8,128)(2,1)}, f32[256,1024]{1,0:T(8,128)}) custom-call(s32[1,8]{1,0:T(1,128)S(1)} %copy-done.1, bf16[256,1024]{1,0:T(8,128)(2,1)} %x_ref.1, bf16[256,1024]{1,0:T(8,128)(2,1)} %cot_ref.1, f32[1,2,256,1024]{3,2,1,0:T(8,128)} %get-tuple-element.106.kept_ref, bf16[1,2,256,1024]{3,2,1,0:T(8,128)(2,1)} %copy-done.5, ...), custom_call_target="tpu_custom_call" | custom-call | bytes 6000000 | tf_op jit(solution)/shard_map/pallas_call | solution.py:995
  194.9 1.0 collective-permute-done.9.got_ref
  195.8 0.6 shard_map.275
  196.5 0.6 copy.35
  197.1 0.7 copy.30
  197.7 0.7 copy.32
  198.4 0.7 copy.33
  (20 shorter events, 0.0 us)
Async XLA Ops:
  5.6 21.1 %copy-start.6 = (bf16[256,1024]{1,0:T(8,128)(2,1)S(1)}, bf16[256,1024]{1,0:T(8,128)(2,1)}, u32[]{:S(2)}) copy-start(bf16[256,1024]{1,0:T(8,128)(2,1)} %x_ref.1) | copy-start | bytes 1572868
  5.6 15.2 %all-to-all-start = ((bf16[8,8,1920]{2,1,0:T(8,128)(2,1)}), bf16[8,8,1920]{2,1,0:T(8,128)(2,1)S(1)}, u32[]{:S(2)}, u32[]{:S(2)}) async-start(bf16[8,8,1920]{2,1,0:T(8,128)(2,1)} %get-tuple-element.72), calls=%async_computation | async-start | bytes 491520 | tf_op jit(solution)/shard_map/all_to_all | solution.py:61
  12.6 8.2 %collective-permute-start = (bf16[40,1024]{1,0:T(8,128)(2,1)S(1)}, bf16[40,1024]{1,0:T(8,128)(2,1)S(1)}, u32[]{:S(2)}, u32[]{:S(2)}) collective-permute-start(bf16[40,1024]{1,0:T(8,128)(2,1)S(1)} %get-tuple-element.73.mine_ref), channel_id=1, source_target_pairs={{0,1},{1,0},{2,3},{3,2},{4,5},{5,4},{6,7},{7,6},{8,9},{9,8},{10,11... | collective-permute-start | bytes 245768 | tf_op jit(solution)/shard_map/ppermute | solution.py:73
  22.6 17.7 %all-to-all-start.1 = ((bf16[4,832,256]{2,1,0:T(8,128)(2,1)}), bf16[4,832,256]{2,1,0:T(8,128)(2,1)S(1)}, u32[]{:S(2)}, u32[]{:S(2)}) async-start(bf16[4,832,256]{2,1,0:T(8,128)(2,1)} %get-tuple-element.76), calls=%async_computation.1 | async-start | bytes 3407872 | tf_op jit(solution)/shard_map/all_to_all | solution.py:61
  26.8 12.4 %collective-permute-start.1 = (bf16[256,1024]{1,0:T(8,128)(2,1)S(1)}, bf16[256,1024]{1,0:T(8,128)(2,1)S(1)}, u32[]{:S(2)}, u32[]{:S(2)}) collective-permute-start(bf16[256,1024]{1,0:T(8,128)(2,1)S(1)} %copy-done.6), channel_id=1, source_target_pairs={{0,64},{64,0},{32,96},{96,32},{1,65},{65,1},{33,97},{97,33},{2,66}... | collective-permute-start | bytes 1572872 | tf_op jit(solution)/shard_map/ppermute | solution.py:69
  39.2 1.1 copy-start.8
  41.9 4.6 %copy-start.7 = (bf16[256,1024]{1,0:T(8,128)(2,1)S(1)}, bf16[256,1024]{1,0:T(8,128)(2,1)}, u32[]{:S(2)}) copy-start(bf16[256,1024]{1,0:T(8,128)(2,1)} %cot_ref.1) | copy-start | bytes 1572868
  41.9 23.2 %all-to-all-start.2 = ((bf16[4,1088,256]{2,1,0:T(8,128)(2,1)}), bf16[4,1088,256]{2,1,0:T(8,128)(2,1)}, u32[]{:S(2)}, u32[]{:S(2)}) async-start(bf16[4,1088,256]{2,1,0:T(8,128)(2,1)} %shard_map.266), calls=%async_computation.2 | async-start | bytes 4456448 | tf_op jit(solution)/shard_map/all_to_all | solution.py:61
  46.5 11.8 %collective-permute-start.4 = (bf16[256,1024]{1,0:T(8,128)(2,1)S(1)}, bf16[256,1024]{1,0:T(8,128)(2,1)S(1)}, u32[]{:S(2)}, u32[]{:S(2)}) collective-permute-start(bf16[256,1024]{1,0:T(8,128)(2,1)S(1)} %copy-done.7), channel_id=1, source_target_pairs={{0,64},{64,0},{32,96},{96,32},{1,65},{65,1},{33,97},{97,33},{2,66}... | collective-permute-start | bytes 1572872 | tf_op jit(solution)/shard_map/ppermute | solution.py:69
  46.9 16.3 %collective-permute-start.2 = (bf16[256,1024]{1,0:T(8,128)(2,1)S(1)}, bf16[256,1024]{1,0:T(8,128)(2,1)S(1)}, u32[]{:S(2)}, u32[]{:S(2)}) collective-permute-start(bf16[256,1024]{1,0:T(8,128)(2,1)S(1)} %copy-done.6), channel_id=1, source_target_pairs={{0,32},{32,0},{64,96},{96,64},{1,33},{33,1},{65,97},{97,65},{2,34}... | collective-permute-start | bytes 1572872 | tf_op jit(solution)/shard_map/ppermute | solution.py:65
  49.0 14.2 %collective-permute-start.5 = (bf16[256,1024]{1,0:T(8,128)(2,1)S(1)}, bf16[256,1024]{1,0:T(8,128)(2,1)S(1)}, u32[]{:S(2)}, u32[]{:S(2)}) collective-permute-start(bf16[256,1024]{1,0:T(8,128)(2,1)S(1)} %copy-done.7), channel_id=1, source_target_pairs={{0,32},{32,0},{64,96},{96,64},{1,33},{33,1},{65,97},{97,65},{2,34}... | collective-permute-start | bytes 1572872 | tf_op jit(solution)/shard_map/ppermute | solution.py:65
  49.0 14.2 %collective-permute-start.3 = (bf16[256,1024]{1,0:T(8,128)(2,1)}, bf16[256,1024]{1,0:T(8,128)(2,1)S(1)}, u32[]{:S(2)}, u32[]{:S(2)}) collective-permute-start(bf16[256,1024]{1,0:T(8,128)(2,1)} %copy-done.8), channel_id=1, source_target_pairs={{0,32},{32,0},{64,96},{96,64},{1,33},{33,1},{65,97},{97,65},{2,34}... | collective-permute-start | bytes 1572872 | tf_op jit(solution)/shard_map/ppermute | solution.py:65
  58.3 4.9 %copy-start.9 = (bf16[256,1024]{1,0:T(8,128)(2,1)}, bf16[256,1024]{1,0:T(8,128)(2,1)S(1)}, u32[]{:S(2)}) copy-start(bf16[256,1024]{1,0:T(8,128)(2,1)S(1)} %collective-permute-done.4.c1) | copy-start | bytes 1572868
  58.3 6.8 %collective-permute-start.6 = (bf16[256,1024]{1,0:T(8,128)(2,1)S(1)}, bf16[256,1024]{1,0:T(8,128)(2,1)}, u32[]{:S(2)}, u32[]{:S(2)}) collective-permute-start(bf16[256,1024]{1,0:T(8,128)(2,1)S(1)} %collective-permute-done.4.c1), channel_id=1, source_target_pairs={{0,32},{32,0},{64,96},{96,64},{1,33},{33,1},{65,97},{97,65},{2,34}... | collective-permute-start | bytes 1572872 | tf_op jit(solution)/shard_map/ppermute | solution.py:65
  63.2 6.8 %copy-start.2 = (bf16[256,768]{1,0:T(8,128)(2,1)S(1)}, bf16[256,768]{1,0:T(8,128)(2,1)}, u32[]{:S(2)}) copy-start(bf16[256,768]{1,0:T(8,128)(2,1)} %constant.26.clone.rot_ref) | copy-start | bytes 1179652
  63.2 0.8 copy-start.10
  63.2 1.0 copy-start.12
  64.2 0.8 copy-start.11
  65.0 31.8 %all-to-all-start.3 = ((bf16[4,2048,256]{2,1,0:T(8,128)(2,1)}), bf16[4,2048,256]{2,1,0:T(8,128)(2,1)}, u32[]{:S(2)}, u32[]{:S(2)}) async-start(bf16[4,2048,256]{2,1,0:T(8,128)(2,1)} %shard_map.265), calls=%async_computation.3 | async-start | bytes 8388608 | tf_op jit(solution)/shard_map/all_to_all | solution.py:61
  96.8 24.3 %all-to-all-start.4 = ((bf16[4,4,256,256]{3,2,1,0:T(8,128)(2,1)}), bf16[4,4,256,256]{3,2,1,0:T(8,128)(2,1)S(1)}, u32[]{:S(2)}, u32[]{:S(2)}) async-start(bf16[4,4,256,256]{3,2,1,0:T(8,128)(2,1)} %get-tuple-element.107), calls=%async_computation.4 | async-start | bytes 4194304 | tf_op jit(solution)/shard_map/all_to_all | solution.py:61
  121.1 1.3 copy-start.3
  122.4 33.2 %all-to-all-start.5 = ((bf16[4,2176,256]{2,1,0:T(8,128)(2,1)}), bf16[4,2176,256]{2,1,0:T(8,128)(2,1)}, u32[]{:S(2)}, u32[]{:S(2)}) async-start(bf16[4,2176,256]{2,1,0:T(8,128)(2,1)} %get-tuple-element.109), calls=%async_computation.5 | async-start | bytes 8912896 | tf_op jit(solution)/shard_map/all_to_all | solution.py:61
  140.4 5.5 %collective-permute-start.7 = (bf16[2,2,256,1024]{3,2,1,0:T(8,128)(2,1)}, bf16[2,2,256,1024]{3,2,1,0:T(8,128)(2,1)S(1)}, u32[]{:S(2)}, u32[]{:S(2)}) collective-permute-start(bf16[2,2,256,1024]{3,2,1,0:T(8,128)(2,1)} %get-tuple-element.105), channel_id=1, source_target_pairs={{0,32},{32,0},{64,96},{96,64},{1,33},{33,1},{65,97},{97,65},{2,34}... | collective-permute-start | bytes 6291464 | tf_op jit(solution)/shard_map/ppermute | solution.py:65
  145.9 1.4 copy-start.4
  160.2 17.8 %all-to-all-start.6 = ((bf16[4,896,256]{2,1,0:T(8,128)(2,1)}), bf16[4,896,256]{2,1,0:T(8,128)(2,1)S(1)}, u32[]{:S(2)}, u32[]{:S(2)}) async-start(bf16[4,896,256]{2,1,0:T(8,128)(2,1)} %shard_map.273), calls=%async_computation.6 | async-start | bytes 3670016 | tf_op jit(solution)/shard_map/all_to_all | solution.py:61
  163.8 26.4 %copy-start.1 = (s32[1,8]{1,0:T(1,128)S(1)}, s32[1,8]{1,0:T(1,128)}, u32[]{:S(2)}) copy-start(s32[1,8]{1,0:T(1,128)} %len_ref.1) | copy-start | bytes 100
  163.9 25.4 %collective-permute-start.8 = (bf16[1,2,256,1024]{3,2,1,0:T(8,128)(2,1)}, bf16[1,2,256,1024]{3,2,1,0:T(8,128)(2,1)S(1)}, u32[]{:S(2)}, u32[]{:S(2)}) collective-permute-start(bf16[1,2,256,1024]{3,2,1,0:T(8,128)(2,1)} %get-tuple-element.110), channel_id=1, source_target_pairs={{0,64},{64,0},{32,96},{96,32},{1,65},{65,1},{33,97},{97,33},{2,66}... | collective-permute-start | bytes 3145736 | tf_op jit(solution)/shard_map/ppermute | solution.py:69
  179.3 16.5 %all-to-all-start.7 = ((bf16[8,8,2816]{2,1,0:T(8,128)(2,1)}), bf16[8,8,2816]{2,1,0:T(8,128)(2,1)S(1)}, u32[]{:S(2)}, u32[]{:S(2)}) async-start(bf16[8,8,2816]{2,1,0:T(8,128)(2,1)} %get-tuple-element.115), calls=%async_computation.7 | async-start | bytes 720896 | tf_op jit(solution)/shard_map/all_to_all | solution.py:61
  186.3 9.5 %collective-permute-start.9 = (bf16[40,1024]{1,0:T(8,128)(2,1)}, bf16[40,1024]{1,0:T(8,128)(2,1)S(1)}, u32[]{:S(2)}, u32[]{:S(2)}) collective-permute-start(bf16[40,1024]{1,0:T(8,128)(2,1)} %get-tuple-element.117), channel_id=1, source_target_pairs={{0,1},{1,0},{2,3},{3,2},{4,5},{5,4},{6,7},{7,6},{8,9},{9,8},{10,11... | collective-permute-start | bytes 245768 | tf_op jit(solution)/shard_map/ppermute | solution.py:73
  189.2 1.0 copy-start.5
  190.2 5.6 %copy-start = (f32[40,1024]{1,0:T(8,128)S(1)}, f32[40,1024]{1,0:T(8,128)}, u32[]{:S(2)}) copy-start(f32[40,1024]{1,0:T(8,128)} %get-tuple-element.116.keep_ref) | copy-start | bytes 491524

commit v4 on v3

--- a/solution.py
+++ b/solution.py
@@ -55,6 +55,22 @@
     return [
         [dev(d, y, x, zh) for y in range(4) for x in range(4)] for d in range(4) for zh in range(2)
     ]
+
+
+def ring(values, groups, step):
+    pairs = [(g[i], g[(i + step) % 4]) for g in groups for i in range(4)]
+    return lax.ppermute(values, AXES, pairs)
+
+
+STEPS = (0, 1, 3, 2)
+
+
+def gather(values, groups):
+    return [values] + [ring(values, groups, k) for k in STEPS[1:]]
+
+
+def scatter(values, groups):
+    return [values[0]] + [ring(v, groups, k) for v, k in zip(values[1:], STEPS[1:])]
 
 
 def a2a(values, groups):
@@ -225,26 +241,25 @@
                     image_ref[pl.ds(row + 1, 1), :] += values[:, 256:]
     lens_ref[...] = jnp.concatenate(lens, axis=1).astype(jnp.int32)
     image = image_ref[...].astype(bf16)
-    for i in range(4):
-        for d in range(4):
-            for p in range(3):
-                row = (d * 3 + p) * 16
-                out_ref[i, row : row + 16, :] = first_ref[d, :, p * 256 : (p + 1) * 256]
-            for cg in range(4):
-                row = 256 + (d * 4 + cg) * 16
-                at = QC + cg * 256
-                out_ref[i, row : row + 16, :] = first_ref[d, :, at : at + 256]
+    for d in range(4):
+        for p in range(3):
+            row = (d * 3 + p) * 16
+            out_ref[row : row + 16, :] = first_ref[d, :, p * 256 : (p + 1) * 256]
         for cg in range(4):
-            at = slice(cg * 256, (cg + 1) * 256)
-            out_ref[i, 192 + cg * 16 : 208 + cg * 16, :] = dense[:, at]
-            out_ref[i, 512 + cg * 64 : 576 + cg * 64, :] = down[:, at]
-        out_ref[i, 768 : 768 + IMAGE, :] = image
+            row = 256 + (d * 4 + cg) * 16
+            at = QC + cg * 256
+            out_ref[row : row + 16, :] = first_ref[d, :, at : at + 256]
+    for cg in range(4):
+        at = slice(cg * 256, (cg + 1) * 256)
+        out_ref[192 + cg * 16 : 208 + cg * 16, :] = dense[:, at]
+        out_ref[512 + cg * 64 : 576 + cg * 64, :] = down[:, at]
+    out_ref[768 : 768 + IMAGE, :] = image
 
 
 def spread(index, first, mine, theirs):
     return call(
         spread_kernel,
-        [shaped(4, 768 + IMAGE, 256), shaped(1, 64, dtype=jnp.int32)],
+        [shaped(768 + IMAGE, 256), shaped(1, 64, dtype=jnp.int32)],
         index,
         first,
         mine,
@@ -254,31 +269,29 @@
     )
 
 
-def widen_a_kernel(in_ref, out_ref):
-    image = sum([in_ref[a, 768 : 768 + IMAGE, :].astype(f32) for a in range(4)]).astype(bf16)
-    for i in range(4):
-        for a in range(4):
-            out_ref[i, a * 256 : (a + 1) * 256, :] = in_ref[a, 0:256, :]
-        out_ref[i, 1024 : 1024 + IMAGE, :] = image
-
-
-def widen_a(second):
+def merge_a_kernel(place_ref, b0, b1, b2, b3, out_ref):
+    blocks = (b0, b1, b2, b3)
+    for block, step in zip(blocks, STEPS):
+        a = (place_ref[0] + 4 - step) % 4
+        out_ref[tile(a), :] = block[0:256, :]
+    total = sum([block[768 : 768 + IMAGE, :].astype(f32) for block in blocks])
+    out_ref[1024 : 1024 + IMAGE, :] = total.astype(bf16)
+
+
+def merge_a(place, blocks):
     return call(
-        widen_a_kernel, [shaped(4, 1024 + IMAGE, 256)], second, places="v", outs="u", nbytes=4e6
+        merge_a_kernel, [shaped(1024 + IMAGE, 256)], place, *blocks, outs="u", nbytes=1e6
     )[0]
 
 
-def widen_b_kernel(in_ref, out_ref):
-    @pl.loop(0, 4)
-    def _(i):
-        for a in range(4):
-            out_ref[i, a * 512 : (a + 1) * 512, :] = in_ref[a, 256:768, :]
-
-
-def widen_b(second):
-    return call(
-        widen_b_kernel, [shaped(4, 2048, 256)], second, places="v", outs="u", nbytes=6e6
-    )[0]
+def merge_b_kernel(place_ref, b0, b1, b2, b3, out_ref):
+    for block, step in zip((b0, b1, b2, b3), STEPS):
+        a = (place_ref[0] + 4 - step) % 4
+        out_ref[pl.ds(pl.multiple_of(a * 512, 512), 512), :] = block[256:768, :]
+
+
+def merge_b(place, blocks):
+    return call(merge_b_kernel, [shaped(2048, 256)], place, *blocks, outs="u", nbytes=2e6)[0]
 
 
 def assemble_a(me, buf_ref, wqkv_ref, wd_ref):
@@ -384,7 +397,10 @@
     c1,
     c2,
     c3,
-    buf_ref,
+    w0,
+    w1,
+    w2,
+    w3,
     rot_ref,
     sent_out,
     min_out,
@@ -413,14 +429,25 @@
     weight_sem,
     sent_sem,
     vec_col_ref,
+    buf_ref,
+    buf_sem,
 ):
     me = info_ref[64]
+    place = info_ref[66]
+    parts = []
+    for n, (src, step) in enumerate(zip((w0, w1, w2, w3), STEPS)):
+        b = (place + 4 - step) % 4
+        parts.append(pltpu.make_async_copy(src, buf_ref.at[b], buf_sem.at[n]))
+    for copy in parts:
+        copy.start()
     loads = []
     for i, (one, other) in enumerate(zip((x0, x1, x2, x3), (c0, c1, c2, c3))):
         loads.append(pltpu.make_async_copy(one, x_ref.at[i], in_sem.at[i, 0]))
         loads.append(pltpu.make_async_copy(other, cot_ref.at[i], in_sem.at[i, 1]))
     for load in loads[:2]:
         load.start()
+    for copy in parts:
+        copy.wait()
     assemble_a(me, buf_ref, wqkv_ref, wd_ref)
     for load in loads[2:]:
         load.start()
@@ -566,7 +593,7 @@
         sent(i, 1).wait()
 
 
-def attention(info, xs, cots, buf):
+def attention(info, xs, cots, blocks):
     tokens = TP * ROW
     dma = pltpu.SemaphoreType.DMA
     return call(
@@ -587,10 +614,10 @@
         info,
         *xs,
         *cots,
-        buf,
+        *blocks,
         jnp.asarray(rotary_tables()),
-        places="s" + "h" * 8 + "vv",
-        outs="hhhhhhhhvvv",
+        places="s" + "h" * 12 + "v",
+        outs="h" * 8 + "vvv",
         scratch=[
             pltpu.VMEM((TP, ROW, D), bf16),
             pltpu.VMEM((TP, ROW, D), bf16),
@@ -608,6 +635,8 @@
             dma((2,)),
             dma((4, 2)),
             pltpu.VMEM((D, 8), f32),
+            pltpu.VMEM((4, 1024 + IMAGE, 256), bf16),
+            dma((4,)),
         ],
         flops=6e9,
         nbytes=2e7,
@@ -616,8 +645,11 @@
 
 
 def mlp_kernel(
-    me_ref,
-    buf_in,
+    info_ref,
+    w0,
+    w1,
+    w2,
+    w3,
     min_in,
     gb_in,
     xhat_in,
@@ -649,9 +681,12 @@
     sent_sem,
     image_sem,
 ):
-    me = me_ref[0]
+    me, place = info_ref[64], info_ref[66]
     c = me % 2
-    parts = [pltpu.make_async_copy(buf_in.at[b], buf_ref.at[b], buf_sem.at[b]) for b in range(4)]
+    parts = []
+    for n, (src, step) in enumerate(zip((w0, w1, w2, w3), STEPS)):
+        b = (place + 4 - step) % 4
+        parts.append(pltpu.make_async_copy(src, buf_ref.at[b], buf_sem.at[n]))
 
     def load(t, n):
         src, dst = ((min_in, min_ref), (gb_in, gb_ref), (xhat_in, xhat_ref))[n]
@@ -794,7 +829,7 @@
         copy.wait()
 
 
-def mlp(me, buf, mlp_in, gb, xhat, ub, vec, sums):
+def mlp(info, blocks, mlp_in, gb, xhat, ub, vec, sums):
     tokens = TP * ROW
     dma = pltpu.SemaphoreType.DMA
     return call(
@@ -806,16 +841,16 @@
             shaped(D, HC),
             shaped(HC, D),
         ],
-        me,
-        buf,
+        info,
+        *blocks,
         mlp_in,
         gb,
         xhat,
         ub,
         vec,
         sums,
-        places="s" + "h" * 4 + "vvv",
-        outs="hhhhh",
+        places="s" + "h" * 7 + "vvv",
+        outs="h" * 5,
         scratch=[
             pltpu.VMEM((4, 2048, 256), bf16),
             pltpu.VMEM((tokens, D), bf16),
@@ -1019,38 +1054,61 @@
     )(in_hbm(sent_a))
 
 
-def add(early, sent_b):
+def add_kernel(place_ref, early_ref, b_ref, image_ref, o0, o1, o2, o3, sums_ref, both_ref, sem):
+    n = pl.program_id(0)
+    total = sum([b_ref[i].astype(f32) for i in range(4)]).astype(bf16)
+
+    @pl.when(n == 0)
+    def _():
+        image = sum([image_ref[i].astype(f32) for i in range(4)])
+        image = image[:IMAGE] + image[IMAGE:]
+        high = image.astype(bf16)
+        sums_ref[0:IMAGE, :] = high
+        sums_ref[IMAGE : 2 * IMAGE, :] = (image - high.astype(f32)).astype(bf16)
+
+    both_ref[n, 0:256, :] = early_ref[0]
+    both_ref[n, 256:768, :] = total
+    both_ref[n, 768 : 768 + 2 * IMAGE, :] = sums_ref[...]
+    copies = [
+        pltpu.make_async_copy(both_ref.at[k], out, sem.at[k]) for k, out in enumerate((o0, o1, o2, o3))
+    ]
+    for k, copy in enumerate(copies):
+        pl.when(n == k)(copy.start)
+
+    @pl.when(n == 3)
+    def _():
+        for copy in copies:
+            copy.wait()
+
+
+def step_of(n):
+    return jnp.where(n < 2, n, 5 - n)
+
+
+def add(place, early, sent_b):
     rows = 768 + 2 * IMAGE
-
-    def kernel(early_ref, b_ref, image_ref, out_ref, sums_ref):
-        out_ref[0, 0:256, :] = early_ref[0]
-        total = sum([b_ref[i].astype(f32) for i in range(4)])
-        out_ref[0, 256:768, :] = total.astype(bf16)
-
-        @pl.when(pl.program_id(0) == 0)
-        def _():
-            image = sum([image_ref[i].astype(f32) for i in range(4)])
-            image = image[:IMAGE] + image[IMAGE:]
-            high = image.astype(bf16)
-            sums_ref[0:IMAGE, :] = high
-            sums_ref[IMAGE : 2 * IMAGE, :] = (image - high.astype(f32)).astype(bf16)
-
-        out_ref[0, 768:rows, :] = sums_ref[...]
-
+    sent_b = in_hbm(sent_b)
     return pl.pallas_call(
-        kernel,
-        grid=(4,),
-        in_specs=[
-            pl.BlockSpec((1, 256, 256), lambda a: (a, 0, 0)),
-            pl.BlockSpec((4, 512, 256), lambda a: (0, a, 0)),
-            pl.BlockSpec((4, 2 * IMAGE, 256), lambda a: (0, 2048 // (2 * IMAGE), 0)),
-        ],
-        out_specs=pl.BlockSpec((1, rows, 256), lambda a: (a, 0, 0)),
-        out_shape=pltpu.HBM((4, rows, 256), bf16),
-        scratch_shapes=[pltpu.VMEM((2 * IMAGE, 256), bf16)],
+        add_kernel,
+        grid_spec=pltpu.PrefetchScalarGridSpec(
+            num_scalar_prefetch=1,
+            grid=(4,),
+            in_specs=[
+                pl.BlockSpec((1, 256, 256), lambda n, p: ((p[0] + step_of(n)) % 4, 0, 0)),
+                pl.BlockSpec((4, 512, 256), lambda n, p: (0, (p[0] + step_of(n)) % 4, 0)),
+                pl.BlockSpec((4, 2 * IMAGE, 256), lambda n, p: (0, 2048 // (2 * IMAGE), 0)),
+            ],
+            out_specs=[HBM_SPEC] * 4,
+            scratch_shapes=[
+                pltpu.VMEM((2 * IMAGE, 256), bf16),
+                pltpu.VMEM((4, rows, 256), bf16),
+                pltpu.SemaphoreType.DMA((4,)),
+            ],
+        ),
+        out_shape=[pltpu.HBM((rows, 256), bf16)] * 4,
         compiler_params=pltpu.CompilerParams(vmem_limit_bytes=VMEM),
         cost_estimate=pl.CostEstimate(flops=0, bytes_accessed=6000000, transcendentals=0),
-    )(in_hbm(early), in_hbm(sent_b), in_hbm(sent_b))
+    )(place, in_hbm(early), sent_b, sent_b)
 
 
 LAST = QC + HC + 4 * 256
@@ -1062,9 +1120,9 @@
     ] + [16 + 3 * d + i for i in range(3)]
 
 
-def part_kernel(far_ref, in_ref, slots_ref, keep_ref, send_ref, total_ref, rows_ref):
+def part_kernel(far_ref, r0, r1, r2, r3, slots_ref, keep_ref, send_ref, total_ref, rows_ref):
     far = far_ref[0]
-    total_ref[...] = sum([in_ref[i].astype(f32) for i in range(4)])
+    total_ref[...] = sum([ref[...].astype(f32) for ref in (r0, r1, r2, r3)])
     rows_ref[...] = jnp.zeros_like(rows_ref)
     for d in range(4):
         for i, row in enumerate(image_rows(d)):
@@ -1100,7 +1158,7 @@
         part_kernel,
         [shaped(8, 8, LAST), shaped(40, D, dtype=f32), shaped(40, D)],
         far,
-        received,
+        *received,
         outs="uuu",
         scratch=[pltpu.VMEM((768 + 2 * IMAGE, 256), f32), pltpu.VMEM((4, 16, 256), f32)],
         nbytes=4e6,
@@ -1201,37 +1259,46 @@
     far_pieces = flip_far(pieces)
     first = a2a(slots, stack_groups())
     block, lens = spread(index[None], first.reshape(4, 16, SLOT), pieces, far_pieces)
-    info = jnp.concatenate([lens[0], me1, far])
-
-    block, x0 = lax.optimization_barrier((block, inputs))
-    x1 = flip_chip(x0)
-    second = a2a(block, inner)
-    second, x1, c0 = lax.optimization_barrier((second, x1, cotangent))
-    c1 = flip_chip(c0)
-    third_a = a2a(widen_a(second), outer)
+    along_x, along_y = index // 2 % 4, index // 8
+    core = me % 2 == 1
+    near = jnp.where(core, along_x, along_y)[None]
+    deep = jnp.where(core, along_y, along_x)[None]
+    info = jnp.concatenate([lens[0], me1, far, near])
+
+    block, x0, c0 = lax.optimization_barrier((block, inputs, cotangent))
+    x1, c1 = flip_chip(x0), flip_chip(c0)
+    second = gather(block, inner)
+    second, x0, c0 = lax.optimization_barrier((second, x0, c0))
+    third_a = gather(merge_a(deep, second), outer)
     x2, x3 = flip_core(x0), flip_core(x1)
     c2, c3 = flip_core(c0), flip_core(c1)
     xs, cots = (x0, x1, x2, x3), (c0, c1, c2, c3)
-    wide_b, xs, cots = lax.optimization_barrier((widen_b(second), xs, cots))
-    third_b = a2a(wide_b, outer)
+    wide_b, third_a, xs, cots = lax.optimization_barrier(
+        (merge_b(deep, second), third_a, xs, cots)
+    )
+    third_b = gather(wide_b, outer)
 
     sent_a, mlp_in, gb, ctx, dqkv, wd, wqkv, xhat, vec, up_b, sums = attention(
         info, xs, cots, third_a
     )
     sent_a = a2a(sent_a, outer)
-    sent_b, hidden, dpre, wup, wdown = mlp(me1, third_b, mlp_in, gb, xhat, up_b, vec, sums)
+    sent_b, hidden, dpre, wup, wdown = mlp(info, third_b, mlp_in, gb, xhat, up_b, vec, sums)
     sent_b = a2a(sent_b, outer)
 
     theirs, mine = outputs(ctx, hidden, dqkv, dpre, wd, wdown, wqkv, wup, vec)
     kept, send = half_sum(mine, flip_core(theirs))
 
-    early, send, sent_b = lax.optimization_barrier((add_early(sent_a), send, sent_b))
     got = flip_chip(send)
-    fourth = a2a(add(early, sent_b), inner)
+    early, send = lax.optimization_barrier((add_early(sent_a), send))
+    fourth = scatter(add(deep, early, sent_b), inner)
+    fourth, got = lax.optimization_barrier((fourth, got))
     slots, keep, rest = part(far, fourth)
     block_output, input_grad = close(lengths, inputs, cotangent, kept, got, vec)
     place = (me * 32 + index)[None]
-    results = finish(place, a2a(slots, stack_groups()), keep, flip_far(rest))
+    slots, rest, block_output, input_grad = lax.optimization_barrier(
+        (a2a(slots, stack_groups()), flip_far(rest), block_output, input_grad)
+    )
+    results = finish(place, slots, keep, rest)
     flat = [r.reshape(-1) for r in results]
     return (
         block_output,

time: 200 us -> 186 us (0.930)
  waiting for transfers between devices: 54.2 us -> 45.4 us
  Pallas kernels: 79.1 us -> 76.7 us
    all_to_all x8 -> x4, waiting for transfers between devices: 26.5 us -> 0.51 us  [a2a(): lax.all_to_all(values, AXES, 0, 0, tiled=True, axis_index_groups=groups)]
    ppermute x0 -> x12, starting transfers between devices: none -> 18.8 us  [ring(): return lax.ppermute(values, AXES, pairs)]
    all_to_all x8 -> x4, starting transfers between devices: 39.9 us -> 21.7 us  [a2a(): lax.all_to_all(values, AXES, 0, 0, tiled=True, axis_index_groups=groups)]
    ppermute x0 -> x12, waiting for transfers between devices: none -> 14.1 us  [ring(): return lax.ppermute(values, AXES, pairs)]
    ppermute x5, waiting for transfers between devices: 0.44 us -> 4.01 us  [flip_core(): return lax.ppermute(values, 'dp', [(0, 1), (1, 0), (2, 3), (3, 2)])]
    ppermute x5, starting transfers between devices: 6.81 us -> 3.68 us  [flip_core(): return lax.ppermute(values, 'dp', [(0, 1), (1, 0), (2, 3), (3, 2)])]
    pallas_call x9, Pallas kernels: 62 us -> 59.5 us  [call(): pl.pallas_call(kernel, in_specs=[SPECS[p] for p in places], out_specs=out...]
    unnamed x30 -> x24, local copies, waits for them, and re-layouts: 8.15 us -> 6.7 us
  transfers between devices with their start and end apart: 18 -> 26, of which waited for: 9 -> 10; matrix products, arithmetic and copies ran while one was open for 0% -> 0% of each run, Pallas kernels for 35% -> 39%
where the time goes in v4:
time: 186 us; the launch traced here: 185 us
  Pallas kernels  76.7 us (41%)
  starting transfers between devices  51.8 us (28%)
  waiting for transfers between devices  45.4 us (24%)
  local copies, waits for them, and re-layouts  10 us (5%)
    pallas_call x9, Pallas kernels, call(): pl.pallas_call(kernel, in_specs=[SPECS[p] for p in places], out_specs=out...  59.5 us
    all_to_all x4, starting transfers between devices, a2a(): lax.all_to_all(values, AXES, 0, 0, tiled=True, axis_index_groups=groups)  21.7 us
    ppermute x3, waiting for transfers between devices, flip_chip(): return lax.ppermute(values, 'dp', [(0, 2), (2, 0), (1, 3), (3, 1)])  19.5 us
    ppermute x12, starting transfers between devices, ring(): return lax.ppermute(values, AXES, pairs)  18.8 us
    ppermute x12, waiting for transfers between devices, ring(): return lax.ppermute(values, AXES, pairs)  14.1 us
    ppermute x2, waiting for transfers between devices, flip_far(): return lax.ppermute(values, 'fsdp', [(i, i ^ 1) for i in range(32)])  7.31 us
    unnamed x24, local copies, waits for them, and re-layouts  6.7 us
    ppermute x2, starting transfers between devices, flip_far(): return lax.ppermute(values, 'fsdp', [(i, i ^ 1) for i in range(32)])  5.77 us
  transfers between devices with their start and end apart: 26, of which 10 were waited for; matrix products, arithmetic and copies ran while one was open for 0% of the time, Pallas kernels for 39%

profile of v4, /device:TPU:1, one launch (start us, length us, event | category | flops | bytes accessed | tf_op | source)
XLA Modules:
  0.0 184.8 jit_solution(1553780891910416238)
XLA Ops:
  0.6 0.7 reshape.81.dense_in
  1.4 0.8 reshape.79.qkv_ref
  2.2 0.9 reshape.80.up_ref
  3.1 0.9 reshape.82.down_in
  4.0 1.6 shard_map.263
  5.6 6.8 %all-to-all-start = ((bf16[8,8,1920]{2,1,0:T(8,128)(2,1)}), bf16[8,8,1920]{2,1,0:T(8,128)(2,1)S(1)}, u32[]{:S(2)}, u32[]{:S(2)}) async-start(bf16[8,8,1920]{2,1,0:T(8,128)(2,1)} %get-tuple-element.91), calls=%async_computation | async-start | bytes 491520 | tf_op jit(solution)/shard_map/all_to_all | solution.py:77
  12.4 2.9 %collective-permute-start = (bf16[40,1024]{1,0:T(8,128)(2,1)S(1)}, bf16[40,1024]{1,0:T(8,128)(2,1)S(1)}, u32[]{:S(2)}, u32[]{:S(2)}) collective-permute-start(bf16[40,1024]{1,0:T(8,128)(2,1)S(1)} %get-tuple-element.92.mine_ref), channel_id=1, source_target_pairs={{0,1},{1,0},{2,3},{3,2},{4,5},{5,4},{6,7},{7,6},{8,9},{9,8},{10,11... | collective-permute-start | bytes 245768 | tf_op jit(solution)/shard_map/ppermute | solution.py:89
  15.3 5.4 %collective-permute-done.theirs_ref = bf16[40,1024]{1,0:T(8,128)(2,1)S(1)} collective-permute-done((bf16[40,1024]{1,0:T(8,128)(2,1)S(1)}, bf16[40,1024]{1,0:T(8,128)(2,1)S(1)}, u32[]{:S(2)}, u32[]{:S(2)}) %collective-permute-start) | collective-permute-done | bytes 81952 | tf_op jit(solution)/shard_map/ppermute | solution.py:89
  20.7 0.0 all-to-all-done
  20.7 0.5 shard_map.264
  21.2 3.0 %collective-permute-start.3 = (bf16[832,256]{1,0:T(8,128)(2,1)S(1)}, bf16[832,256]{1,0:T(8,128)(2,1)S(1)}, u32[]{:S(2)}, u32[]{:S(2)}) collective-permute-start(bf16[832,256]{1,0:T(8,128)(2,1)S(1)} %get-tuple-element.98.b0), channel_id=1, source_target_pairs={{0,4},{2,6},{4,0},{6,2},{1,5},{3,7},{5,1},{7,3},{8,12},{10,14},{12... | collective-permute-start | bytes 1277960 | tf_op jit(solution)/shard_map/ppermute | solution.py:62
  24.2 0.8 collective-permute-start.2
  24.9 0.7 collective-permute-start.1
  25.6 0.3 collective-permute-start.7
  25.9 1.2 collective-permute-start.10
  27.1 2.9 %collective-permute-done.3.b3 = bf16[832,256]{1,0:T(8,128)(2,1)S(1)} collective-permute-done((bf16[832,256]{1,0:T(8,128)(2,1)S(1)}, bf16[832,256]{1,0:T(8,128)(2,1)S(1)}, u32[]{:S(2)}, u32[]{:S(2)}) %collective-permute-start.3) | collective-permute-done | bytes 426016 | tf_op jit(solution)/shard_map/ppermute | solution.py:62
  30.0 5.1 %collective-permute-done.2.b2 = bf16[832,256]{1,0:T(8,128)(2,1)S(1)} collective-permute-done((bf16[832,256]{1,0:T(8,128)(2,1)S(1)}, bf16[832,256]{1,0:T(8,128)(2,1)S(1)}, u32[]{:S(2)}, u32[]{:S(2)}) %collective-permute-start.2) | collective-permute-done | bytes 426016 | tf_op jit(solution)/shard_map/ppermute | solution.py:62
  35.1 1.4 collective-permute-start.8
  36.4 0.0 collective-permute-start.11
  36.4 0.9 shard_map.266.w0
  37.3 2.6 %collective-permute-start.6 = (bf16[1088,256]{1,0:T(8,128)(2,1)}, bf16[1088,256]{1,0:T(8,128)(2,1)S(1)}, u32[]{:S(2)}, u32[]{:S(2)}) collective-permute-start(bf16[1088,256]{1,0:T(8,128)(2,1)} %shard_map.266.w0), channel_id=1, source_target_pairs={{0,16},{8,24},{16,0},{24,8},{1,17},{9,25},{17,1},{25,9},{2,18},{10... | collective-permute-start | bytes 1671176 | tf_op jit(solution)/shard_map/ppermute | solution.py:62
  39.9 0.9 collective-permute-start.5
  40.9 8.2 %collective-permute-done.10.c1 = bf16[256,1024]{1,0:T(8,128)(2,1)} collective-permute-done((bf16[256,1024]{1,0:T(8,128)(2,1)}, bf16[256,1024]{1,0:T(8,128)(2,1)}, u32[]{:S(2)}, u32[]{:S(2)}) %collective-permute-start.10) | collective-permute-done | bytes 524320 | tf_op jit(solution)/shard_map/ppermute | solution.py:85
  49.0 2.2 %collective-permute-start.4 = (bf16[1088,256]{1,0:T(8,128)(2,1)}, bf16[1088,256]{1,0:T(8,128)(2,1)}, u32[]{:S(2)}, u32[]{:S(2)}) collective-permute-start(bf16[1088,256]{1,0:T(8,128)(2,1)} %shard_map.266.w0), channel_id=1, source_target_pairs={{0,8},{8,16},{16,24},{24,0},{1,9},{9,17},{17,25},{25,1},{2,10},{10... | collective-permute-start | bytes 1671176 | tf_op jit(solution)/shard_map/ppermute | solution.py:62
  51.2 1.0 collective-permute-start.9
  52.2 0.1 collective-permute-start.12
  52.3 0.1 pad_add_fusion.info_ref
  52.4 1.0 shard_map.265.w0
  53.4 0.3 collective-permute-done.5.w2
  53.7 5.8 %collective-permute-done.4.w1 = bf16[1088,256]{1,0:T(8,128)(2,1)} collective-permute-done((bf16[1088,256]{1,0:T(8,128)(2,1)}, bf16[1088,256]{1,0:T(8,128)(2,1)}, u32[]{:S(2)}, u32[]{:S(2)}) %collective-permute-start.4) | collective-permute-done | bytes 557088 | tf_op jit(solution)/shard_map/ppermute | solution.py:62
  59.5 3.0 %collective-permute-start.15 = (bf16[2048,256]{1,0:T(8,128)(2,1)}, bf16[2048,256]{1,0:T(8,128)(2,1)S(1)}, u32[]{:S(2)}, u32[]{:S(2)}) collective-permute-start(bf16[2048,256]{1,0:T(8,128)(2,1)} %shard_map.265.w0), channel_id=1, source_target_pairs={{0,16},{8,24},{16,0},{24,8},{1,17},{9,25},{17,1},{25,9},{2,18},{10... | collective-permute-start | bytes 3145736 | tf_op jit(solution)/shard_map/ppermute | solution.py:62
  62.5 0.2 collective-permute-start.14
  62.7 1.2 collective-permute-start.13
  63.9 19.4 %shard_map.267 = (bf16[4,4,256,256]{3,2,1,0:T(8,128)(2,1)}, bf16[1024,1024]{1,0:T(8,128)(2,1)}, bf16[1024,1024]{1,0:T(8,128)(2,1)}, bf16[1024,256]{1,0:T(8,128)(...) custom-call(s32[67]{0:T(128)S(1)} %pad_add_fusion.info_ref, ...), custom_call_target="tpu_custom_call" | custom-call | flops 6000000000 | bytes 20000000 | tf_op jit(solution)/shard_map/pallas_call | solution.py:123
  83.3 4.6 %all-to-all-start.1 = ((bf16[4,4,256,256]{3,2,1,0:T(8,128)(2,1)}), bf16[4,4,256,256]{3,2,1,0:T(8,128)(2,1)}, u32[]{:S(2)}, u32[]{:S(2)}) async-start(bf16[4,4,256,256]{3,2,1,0:T(8,128)(2,1)} %get-tuple-element.116), calls=%async_computation.1 | async-start | bytes 4194304 | tf_op jit(solution)/shard_map/all_to_all | solution.py:77
  88.0 1.0 copy-done.6
  89.0 0.4 copy-done.7
  89.4 21.1 %shard_map.269 = (bf16[4,2176,256]{2,1,0:T(8,128)(2,1)}, bf16[1024,1024]{1,0:T(8,128)(2,1)}, bf16[1024,1024]{1,0:T(8,128)(2,1)}, bf16[1024,1024]{1,0:T(8,128)(2,1)}, bf16[1024,1024]{1,0:T(8,128)(2,1)}) custom-call(s32[67]{0:T(128)S(1)} %pad_add_fusion.info_ref, bf16[2048,256]{1,0:T(8,128)(2,1)} %shard_map.265.w0, ...), custom_call_target="tpu_custom_call" | custom-call | flops 8999999488 | bytes 20000000 | tf_op jit(solution)/shard_map/pallas_call | solution.py:123
  110.5 4.9 %all-to-all-start.2 = ((bf16[4,2176,256]{2,1,0:T(8,128)(2,1)}), bf16[4,2176,256]{2,1,0:T(8,128)(2,1)}, u32[]{:S(2)}, u32[]{:S(2)}) async-start(bf16[4,2176,256]{2,1,0:T(8,128)(2,1)} %get-tuple-element.136), calls=%async_computation.2 | async-start | bytes 8912896 | tf_op jit(solution)/shard_map/all_to_all | solution.py:77
  115.4 13.1 %shard_map.270 = (bf16[2,2,256,1024]{3,2,1,0:T(8,128)(2,1)}, bf16[2,2,256,1024]{3,2,1,0:T(8,128)(2,1)}) custom-call(bf16[1024,256]{1,0:T(8,128)(2,1)} %get-tuple-element.117.ctx_in, bf16[1024,1024]{1,0:T(8,128)(2,1)} %get-tuple-element.125.hidden_in, bf16[1024,768]{1,0:T(8,128)(2,1)} %get-tuple-element.126.dqkv_in, ...), custom_call_target="tpu_custom_call" | custom-call | flops 6499999744 | bytes 16000000 | tf_op jit(solution)/shard_map/pallas_call | solution.py:123
  128.6 1.2 collective-permute-start.16
  129.8 4.0 %collective-permute-done.16.b0_ref.b1_ref = bf16[2,2,256,1024]{3,2,1,0:T(8,128)(2,1)S(1)} collective-permute-done((bf16[2,2,256,1024]{3,2,1,0:T(8,128)(2,1)}, bf16[2,2,256,1024]{3,2,1,0:T(8,128)(2,1)S(1)}, u32[]{:S(2)}, u32[]{:S(2)}) %collective-permute-start.16) | collective-permute-done | bytes 2097184 | tf_op jit(solution)/shard_map/ppermute | solution.py:81
  133.8 1.3 copy-done.4
  135.1 4.3 %shard_map.271 = (f32[1,2,256,1024]{3,2,1,0:T(8,128)}, bf16[1,2,256,1024]{3,2,1,0:T(8,128)(2,1)}) custom-call(bf16[2,2,256,1024]{3,2,1,0:T(8,128)(2,1)} %get-tuple-element.132.a0_ref.a1_ref, bf16[2,2,256,1024]{3,2,1,0:T(8,128)(2,1)} %copy-done.4, bf16[2,2,256,1024]{3,2,1,0:T(8,128)(2,1)} %get-tuple-element.132.a0_ref.a1_ref, bf16[2,2,256,1024]{3,2,1,0:T(8,128)(2,1)} %copy-done.4), custom_call_target="tpu_custom_call" | custom-call | bytes 8000000 | tf_op jit(solution)/shard_map/pallas_call | solution.py:1003
  139.4 0.3 collective-permute-start.20
  139.7 3.6 %shard_map.268.early_ref = bf16[4,256,256]{2,1,0:T(8,128)(2,1)} custom-call(bf16[4,4,256,256]{3,2,1,0:T(8,128)(2,1)} %all-to-all-done.1.a_ref), custom_call_target="tpu_custom_call" | custom-call | bytes 3000000 | tf_op jit(solution)/shard_map/pallas_call | solution.py:1046
  143.3 0.5 all-to-all-done.2.b_ref.image_ref
  143.8 4.7 %shard_map.272 = (bf16[896,256]{1,0:T(8,128)(2,1)}, bf16[896,256]{1,0:T(8,128)(2,1)}, bf16[896,256]{1,0:T(8,128)(2,1)}, bf16[896,256]{1,0:T(8,128)(2,1)}) custom-call(s32[1]{0:T(128)} %bitcast.1.place_ref, bf16[4,256,256]{2,1,0:T(8,128)(2,1)} %shard_map.268.early_ref, bf16[4,2176,256]{2,1,0:T(8,128)(2,1)} %all-to-all-done.2.b_ref.image_ref, ...), custom_call_target="tpu_custom_call" | custom-call | bytes 6000000 | tf_op jit(solution)/shard_map/pallas_call | solution.py:1091
  148.5 0.0 copy-start.2
  148.5 1.3 collective-permute-start.17
  149.8 1.5 collective-permute-start.18
  151.3 1.5 collective-permute-start.19
  152.7 11.3 %collective-permute-done.20.got_ref = bf16[1,2,256,1024]{3,2,1,0:T(8,128)(2,1)S(1)} collective-permute-done((bf16[1,2,256,1024]{3,2,1,0:T(8,128)(2,1)}, bf16[1,2,256,1024]{3,2,1,0:T(8,128)(2,1)S(1)}, u32[]{:S(2)}, u32[]{:S(2)}) %collective-permute-start.20) | collective-permute-done | bytes 1048608 | tf_op jit(solution)/shard_map/ppermute | solution.py:85
  164.0 1.4 copy-done
  165.4 1.2 shard_map.273
  166.7 5.4 %all-to-all-start.3 = ((bf16[8,8,2816]{2,1,0:T(8,128)(2,1)}), bf16[8,8,2816]{2,1,0:T(8,128)(2,1)S(1)}, u32[]{:S(2)}, u32[]{:S(2)}) async-start(bf16[8,8,2816]{2,1,0:T(8,128)(2,1)} %get-tuple-element.145), calls=%async_computation.3 | async-start | bytes 720896 | tf_op jit(solution)/shard_map/all_to_all | solution.py:77
  172.0 2.9 %collective-permute-start.21 = (bf16[40,1024]{1,0:T(8,128)(2,1)}, bf16[40,1024]{1,0:T(8,128)(2,1)S(1)}, u32[]{:S(2)}, u32[]{:S(2)}) collective-permute-start(bf16[40,1024]{1,0:T(8,128)(2,1)} %get-tuple-element.146), channel_id=1, source_target_pairs={{0,1},{1,0},{2,3},{3,2},{4,5},{5,4},{6,7},{7,6},{8,9},{9,8},{10,11... | collective-permute-start | bytes 245768 | tf_op jit(solution)/shard_map/ppermute | solution.py:89
  174.9 4.6 %shard_map.274 = (bf16[256,1024]{1,0:T(8,128)(2,1)}, f32[256,1024]{1,0:T(8,128)}) custom-call(s32[1,8]{1,0:T(1,128)S(1)} %copy-done.2, bf16[256,1024]{1,0:T(8,128)(2,1)} %x_ref.1, bf16[256,1024]{1,0:T(8,128)(2,1)} %cot_ref.1, f32[1,2,256,1024]{3,2,1,0:T(8,128)} %get-tuple-element.147.kept_ref, bf16[1,2,256,1024]{3,2,1,0:T(8,128)(2,1)} %copy-done.5, ...), custom_call_target="tpu_custom_call" | custom-call | bytes 6000000 | tf_op jit(solution)/shard_map/pallas_call | solution.py:1030
  179.5 1.9 %collective-permute-done.21.got_ref = bf16[40,1024]{1,0:T(8,128)(2,1)S(1)} collective-permute-done((bf16[40,1024]{1,0:T(8,128)(2,1)}, bf16[40,1024]{1,0:T(8,128)(2,1)S(1)}, u32[]{:S(2)}, u32[]{:S(2)}) %collective-permute-start.21) | collective-permute-done | bytes 81952 | tf_op jit(solution)/shard_map/ppermute | solution.py:89
  181.5 0.6 shard_map.275
  182.1 0.6 copy.35
  182.7 0.7 copy.30
  183.4 0.7 copy.32
  184.1 0.7 copy.33
  (30 shorter events, 0.1 us)
Async XLA Ops:
  5.6 15.1 %all-to-all-start = ((bf16[8,8,1920]{2,1,0:T(8,128)(2,1)}), bf16[8,8,1920]{2,1,0:T(8,128)(2,1)S(1)}, u32[]{:S(2)}, u32[]{:S(2)}) async-start(bf16[8,8,1920]{2,1,0:T(8,128)(2,1)} %get-tuple-element.91), calls=%async_computation | async-start | bytes 491520 | tf_op jit(solution)/shard_map/all_to_all | solution.py:77
  12.4 8.2 %collective-permute-start = (bf16[40,1024]{1,0:T(8,128)(2,1)S(1)}, bf16[40,1024]{1,0:T(8,128)(2,1)S(1)}, u32[]{:S(2)}, u32[]{:S(2)}) collective-permute-start(bf16[40,1024]{1,0:T(8,128)(2,1)S(1)} %get-tuple-element.92.mine_ref), channel_id=1, source_target_pairs={{0,1},{1,0},{2,3},{3,2},{4,5},{5,4},{6,7},{7,6},{8,9},{9,8},{10,11... | collective-permute-start | bytes 245768 | tf_op jit(solution)/shard_map/ppermute | solution.py:89
  21.2 8.9 %collective-permute-start.3 = (bf16[832,256]{1,0:T(8,128)(2,1)S(1)}, bf16[832,256]{1,0:T(8,128)(2,1)S(1)}, u32[]{:S(2)}, u32[]{:S(2)}) collective-permute-start(bf16[832,256]{1,0:T(8,128)(2,1)S(1)} %get-tuple-element.98.b0), channel_id=1, source_target_pairs={{0,4},{2,6},{4,0},{6,2},{1,5},{3,7},{5,1},{7,3},{8,12},{10,14},{12... | collective-permute-start | bytes 1277960 | tf_op jit(solution)/shard_map/ppermute | solution.py:62
  24.2 10.9 %collective-permute-start.2 = (bf16[832,256]{1,0:T(8,128)(2,1)S(1)}, bf16[832,256]{1,0:T(8,128)(2,1)S(1)}, u32[]{:S(2)}, u32[]{:S(2)}) collective-permute-start(bf16[832,256]{1,0:T(8,128)(2,1)S(1)} %get-tuple-element.98.b0), channel_id=1, source_target_pairs={{0,6},{2,0},{4,2},{6,4},{1,7},{3,1},{5,3},{7,5},{8,14},{10,8},{12,... | collective-permute-start | bytes 1277960 | tf_op jit(solution)/shard_map/ppermute | solution.py:62
  24.9 10.1 %collective-permute-start.1 = (bf16[832,256]{1,0:T(8,128)(2,1)S(1)}, bf16[832,256]{1,0:T(8,128)(2,1)S(1)}, u32[]{:S(2)}, u32[]{:S(2)}) collective-permute-start(bf16[832,256]{1,0:T(8,128)(2,1)S(1)} %get-tuple-element.98.b0), channel_id=1, source_target_pairs={{0,2},{2,4},{4,6},{6,0},{1,3},{3,5},{5,7},{7,1},{8,10},{10,12},{12... | collective-permute-start | bytes 1277960 | tf_op jit(solution)/shard_map/ppermute | solution.py:62
  25.6 14.3 %collective-permute-start.7 = (bf16[256,1024]{1,0:T(8,128)(2,1)}, bf16[256,1024]{1,0:T(8,128)(2,1)}, u32[]{:S(2)}, u32[]{:S(2)}) collective-permute-start(bf16[256,1024]{1,0:T(8,128)(2,1)} %x_ref.1), channel_id=1, source_target_pairs={{0,64},{64,0},{32,96},{96,32},{1,65},{65,1},{33,97},{97,33},{2,66}... | collective-permute-start | bytes 1572872 | tf_op jit(solution)/shard_map/ppermute | solution.py:85
  25.9 23.1 %collective-permute-start.10 = (bf16[256,1024]{1,0:T(8,128)(2,1)}, bf16[256,1024]{1,0:T(8,128)(2,1)}, u32[]{:S(2)}, u32[]{:S(2)}) collective-permute-start(bf16[256,1024]{1,0:T(8,128)(2,1)} %cot_ref.1), channel_id=1, source_target_pairs={{0,64},{64,0},{32,96},{96,32},{1,65},{65,1},{33,97},{97,33},{2,66}... | collective-permute-start | bytes 1572872 | tf_op jit(solution)/shard_map/ppermute | solution.py:85
  35.1 16.1 %collective-permute-start.8 = (bf16[256,1024]{1,0:T(8,128)(2,1)}, bf16[256,1024]{1,0:T(8,128)(2,1)}, u32[]{:S(2)}, u32[]{:S(2)}) collective-permute-start(bf16[256,1024]{1,0:T(8,128)(2,1)} %x_ref.1), channel_id=1, source_target_pairs={{0,32},{32,0},{64,96},{96,64},{1,33},{33,1},{65,97},{97,65},{2,34}... | collective-permute-start | bytes 1572872 | tf_op jit(solution)/shard_map/ppermute | solution.py:81
  36.4 15.8 %collective-permute-start.11 = (bf16[256,1024]{1,0:T(8,128)(2,1)}, bf16[256,1024]{1,0:T(8,128)(2,1)}, u32[]{:S(2)}, u32[]{:S(2)}) collective-permute-start(bf16[256,1024]{1,0:T(8,128)(2,1)} %cot_ref.1), channel_id=1, source_target_pairs={{0,32},{32,0},{64,96},{96,64},{1,33},{33,1},{65,97},{97,65},{2,34}... | collective-permute-start | bytes 1572872 | tf_op jit(solution)/shard_map/ppermute | solution.py:81
  36.4 27.5 %copy-start.3 = (bf16[256,768]{1,0:T(8,128)(2,1)S(1)}, bf16[256,768]{1,0:T(8,128)(2,1)}, u32[]{:S(2)}) copy-start(bf16[256,768]{1,0:T(8,128)(2,1)} %constant.62.clone.rot_ref) | copy-start | bytes 1179652
  37.3 16.1 %collective-permute-start.6 = (bf16[1088,256]{1,0:T(8,128)(2,1)}, bf16[1088,256]{1,0:T(8,128)(2,1)S(1)}, u32[]{:S(2)}, u32[]{:S(2)}) collective-permute-start(bf16[1088,256]{1,0:T(8,128)(2,1)} %shard_map.266.w0), channel_id=1, source_target_pairs={{0,16},{8,24},{16,0},{24,8},{1,17},{9,25},{17,1},{25,9},{2,18},{10... | collective-permute-start | bytes 1671176 | tf_op jit(solution)/shard_map/ppermute | solution.py:62
  39.9 13.7 %collective-permute-start.5 = (bf16[1088,256]{1,0:T(8,128)(2,1)}, bf16[1088,256]{1,0:T(8,128)(2,1)S(1)}, u32[]{:S(2)}, u32[]{:S(2)}) collective-permute-start(bf16[1088,256]{1,0:T(8,128)(2,1)} %shard_map.266.w0), channel_id=1, source_target_pairs={{0,24},{8,0},{16,8},{24,16},{1,25},{9,1},{17,9},{25,17},{2,26},{10... | collective-permute-start | bytes 1671176 | tf_op jit(solution)/shard_map/ppermute | solution.py:62
  49.0 10.4 %collective-permute-start.4 = (bf16[1088,256]{1,0:T(8,128)(2,1)}, bf16[1088,256]{1,0:T(8,128)(2,1)}, u32[]{:S(2)}, u32[]{:S(2)}) collective-permute-start(bf16[1088,256]{1,0:T(8,128)(2,1)} %shard_map.266.w0), channel_id=1, source_target_pairs={{0,8},{8,16},{16,24},{24,0},{1,9},{9,17},{17,25},{25,1},{2,10},{10... | collective-permute-start | bytes 1671176 | tf_op jit(solution)/shard_map/ppermute | solution.py:62
  51.2 8.2 %collective-permute-start.9 = (bf16[256,1024]{1,0:T(8,128)(2,1)}, bf16[256,1024]{1,0:T(8,128)(2,1)}, u32[]{:S(2)}, u32[]{:S(2)}) collective-permute-start(bf16[256,1024]{1,0:T(8,128)(2,1)} %collective-permute-done.7.x1), channel_id=1, source_target_pairs={{0,32},{32,0},{64,96},{96,64},{1,33},{33,1},{65,97},{97,65},{2,34}... | collective-permute-start | bytes 1572872 | tf_op jit(solution)/shard_map/ppermute | solution.py:81
  52.2 7.3 %collective-permute-start.12 = (bf16[256,1024]{1,0:T(8,128)(2,1)}, bf16[256,1024]{1,0:T(8,128)(2,1)}, u32[]{:S(2)}, u32[]{:S(2)}) collective-permute-start(bf16[256,1024]{1,0:T(8,128)(2,1)} %collective-permute-done.10.c1), channel_id=1, source_target_pairs={{0,32},{32,0},{64,96},{96,64},{1,33},{33,1},{65,97},{97,65},{2,34}... | collective-permute-start | bytes 1572872 | tf_op jit(solution)/shard_map/ppermute | solution.py:81
  53.4 6.1 %copy-start.8 = (bf16[1088,256]{1,0:T(8,128)(2,1)}, bf16[1088,256]{1,0:T(8,128)(2,1)S(1)}, u32[]{:S(2)}) copy-start(bf16[1088,256]{1,0:T(8,128)(2,1)S(1)} %collective-permute-done.6.w3) | copy-start | bytes 1671172
  53.7 5.8 %copy-start.9 = (bf16[1088,256]{1,0:T(8,128)(2,1)}, bf16[1088,256]{1,0:T(8,128)(2,1)S(1)}, u32[]{:S(2)}) copy-start(bf16[1088,256]{1,0:T(8,128)(2,1)S(1)} %collective-permute-done.5.w2) | copy-start | bytes 1671172
  59.5 28.5 %collective-permute-start.15 = (bf16[2048,256]{1,0:T(8,128)(2,1)}, bf16[2048,256]{1,0:T(8,128)(2,1)S(1)}, u32[]{:S(2)}, u32[]{:S(2)}) collective-permute-start(bf16[2048,256]{1,0:T(8,128)(2,1)} %shard_map.265.w0), channel_id=1, source_target_pairs={{0,16},{8,24},{16,0},{24,8},{1,17},{9,25},{17,1},{25,9},{2,18},{10... | collective-permute-start | bytes 3145736 | tf_op jit(solution)/shard_map/ppermute | solution.py:62
  62.5 25.5 %collective-permute-start.14 = (bf16[2048,256]{1,0:T(8,128)(2,1)}, bf16[2048,256]{1,0:T(8,128)(2,1)S(1)}, u32[]{:S(2)}, u32[]{:S(2)}) collective-permute-start(bf16[2048,256]{1,0:T(8,128)(2,1)} %shard_map.265.w0), channel_id=1, source_target_pairs={{0,24},{8,0},{16,8},{24,16},{1,25},{9,1},{17,9},{25,17},{2,26},{10... | collective-permute-start | bytes 3145736 | tf_op jit(solution)/shard_map/ppermute | solution.py:62
  62.7 25.3 %collective-permute-start.13 = (bf16[2048,256]{1,0:T(8,128)(2,1)}, bf16[2048,256]{1,0:T(8,128)(2,1)}, u32[]{:S(2)}, u32[]{:S(2)}) collective-permute-start(bf16[2048,256]{1,0:T(8,128)(2,1)} %shard_map.265.w0), channel_id=1, source_target_pairs={{0,8},{8,16},{16,24},{24,0},{1,9},{9,17},{17,25},{25,1},{2,10},{10... | collective-permute-start | bytes 3145736 | tf_op jit(solution)/shard_map/ppermute | solution.py:62
  83.3 27.2 %all-to-all-start.1 = ((bf16[4,4,256,256]{3,2,1,0:T(8,128)(2,1)}), bf16[4,4,256,256]{3,2,1,0:T(8,128)(2,1)}, u32[]{:S(2)}, u32[]{:S(2)}) async-start(bf16[4,4,256,256]{3,2,1,0:T(8,128)(2,1)} %get-tuple-element.116), calls=%async_computation.1 | async-start | bytes 4194304 | tf_op jit(solution)/shard_map/all_to_all | solution.py:77
  88.0 1.0 copy-start.6
  88.0 1.4 copy-start.7
  110.5 33.3 %all-to-all-start.2 = ((bf16[4,2176,256]{2,1,0:T(8,128)(2,1)}), bf16[4,2176,256]{2,1,0:T(8,128)(2,1)}, u32[]{:S(2)}, u32[]{:S(2)}) async-start(bf16[4,2176,256]{2,1,0:T(8,128)(2,1)} %get-tuple-element.136), calls=%async_computation.2 | async-start | bytes 8912896 | tf_op jit(solution)/shard_map/all_to_all | solution.py:77
  128.6 5.2 %collective-permute-start.16 = (bf16[2,2,256,1024]{3,2,1,0:T(8,128)(2,1)}, bf16[2,2,256,1024]{3,2,1,0:T(8,128)(2,1)S(1)}, u32[]{:S(2)}, u32[]{:S(2)}) collective-permute-start(bf16[2,2,256,1024]{3,2,1,0:T(8,128)(2,1)} %get-tuple-element.133), channel_id=1, source_target_pairs={{0,32},{32,0},{64,96},{96,64},{1,33},{33,1},{65,97},{97,65},{2,34}... | collective-permute-start | bytes 6291464 | tf_op jit(solution)/shard_map/ppermute | solution.py:81
  133.8 1.3 copy-start.4
  139.4 24.6 %collective-permute-start.20 = (bf16[1,2,256,1024]{3,2,1,0:T(8,128)(2,1)}, bf16[1,2,256,1024]{3,2,1,0:T(8,128)(2,1)S(1)}, u32[]{:S(2)}, u32[]{:S(2)}) collective-permute-start(bf16[1,2,256,1024]{3,2,1,0:T(8,128)(2,1)} %get-tuple-element.134), channel_id=1, source_target_pairs={{0,64},{64,0},{32,96},{96,32},{1,65},{65,1},{33,97},{97,33},{2,66}... | collective-permute-start | bytes 3145736 | tf_op jit(solution)/shard_map/ppermute | solution.py:85
  148.5 26.4 %copy-start.2 = (s32[1,8]{1,0:T(1,128)S(1)}, s32[1,8]{1,0:T(1,128)}, u32[]{:S(2)}) copy-start(s32[1,8]{1,0:T(1,128)} %len_ref.1) | copy-start | bytes 100
  148.5 15.5 %collective-permute-start.17 = (bf16[896,256]{1,0:T(8,128)(2,1)}, bf16[896,256]{1,0:T(8,128)(2,1)S(1)}, u32[]{:S(2)}, u32[]{:S(2)}) collective-permute-start(bf16[896,256]{1,0:T(8,128)(2,1)} %get-tuple-element.138), channel_id=1, source_target_pairs={{0,2},{2,4},{4,6},{6,0},{1,3},{3,5},{5,7},{7,1},{8,10},{10,12},{12... | collective-permute-start | bytes 1376264 | tf_op jit(solution)/shard_map/ppermute | solution.py:62
  149.8 14.3 %collective-permute-start.18 = (bf16[896,256]{1,0:T(8,128)(2,1)}, bf16[896,256]{1,0:T(8,128)(2,1)S(1)}, u32[]{:S(2)}, u32[]{:S(2)}) collective-permute-start(bf16[896,256]{1,0:T(8,128)(2,1)} %get-tuple-element.139), channel_id=1, source_target_pairs={{0,6},{2,0},{4,2},{6,4},{1,7},{3,1},{5,3},{7,5},{8,14},{10,8},{12,... | collective-permute-start | bytes 1376264 | tf_op jit(solution)/shard_map/ppermute | solution.py:62
  151.3 12.8 %collective-permute-start.19 = (bf16[896,256]{1,0:T(8,128)(2,1)}, bf16[896,256]{1,0:T(8,128)(2,1)S(1)}, u32[]{:S(2)}, u32[]{:S(2)}) collective-permute-start(bf16[896,256]{1,0:T(8,128)(2,1)} %get-tuple-element.140), channel_id=1, source_target_pairs={{0,4},{2,6},{4,0},{6,2},{1,5},{3,7},{5,1},{7,3},{8,12},{10,14},{12... | collective-permute-start | bytes 1376264 | tf_op jit(solution)/shard_map/ppermute | solution.py:62
  164.0 10.9 %copy-start.5 = (bf16[1,2,256,1024]{3,2,1,0:T(8,128)(2,1)}, bf16[1,2,256,1024]{3,2,1,0:T(8,128)(2,1)S(1)}, u32[]{:S(2)}) copy-start(bf16[1,2,256,1024]{3,2,1,0:T(8,128)(2,1)S(1)} %collective-permute-done.20.got_ref) | copy-start | bytes 3145732
  164.0 1.4 copy-start
  166.7 14.8 %all-to-all-start.3 = ((bf16[8,8,2816]{2,1,0:T(8,128)(2,1)}), bf16[8,8,2816]{2,1,0:T(8,128)(2,1)S(1)}, u32[]{:S(2)}, u32[]{:S(2)}) async-start(bf16[8,8,2816]{2,1,0:T(8,128)(2,1)} %get-tuple-element.145), calls=%async_computation.3 | async-start | bytes 720896 | tf_op jit(solution)/shard_map/all_to_all | solution.py:77
  172.0 9.5 %collective-permute-start.21 = (bf16[40,1024]{1,0:T(8,128)(2,1)}, bf16[40,1024]{1,0:T(8,128)(2,1)S(1)}, u32[]{:S(2)}, u32[]{:S(2)}) collective-permute-start(bf16[40,1024]{1,0:T(8,128)(2,1)} %get-tuple-element.146), channel_id=1, source_target_pairs={{0,1},{1,0},{2,3},{3,2},{4,5},{5,4},{6,7},{7,6},{8,9},{9,8},{10,11... | collective-permute-start | bytes 245768 | tf_op jit(solution)/shard_map/ppermute | solution.py:89
  174.9 6.6 %copy-start.1 = (f32[40,1024]{1,0:T(8,128)S(1)}, f32[40,1024]{1,0:T(8,128)}, u32[]{:S(2)}) copy-start(f32[40,1024]{1,0:T(8,128)} %get-tuple-element.154.keep_ref) | copy-start | bytes 491524

commit v5 on v4

--- a/solution.py
+++ b/solution.py
@@ -18,6 +18,7 @@
 QC = 3 * D // TP
 HC = FF // TP
 LOCAL_HEADS = HEADS // TP
+STRIP = 32
 AXES = ("dp", "fsdp")
 VMEM = 44 * 1024 * 1024
 
@@ -108,7 +109,7 @@
 VMEM_SPEC = pl.BlockSpec(memory_space=pltpu.VMEM)
 SMEM_SPEC = pl.BlockSpec(memory_space=pltpu.SMEM)
 HBM_SPEC = pl.BlockSpec(memory_space=pltpu.HBM)
-SPECS = {"s": SMEM_SPEC, "v": VMEM_SPEC, "u": VMEM_SPEC, "h": HBM_SPEC}
+SPECS = {"a": pl.BlockSpec(memory_space=pl.ANY), "s": SMEM_SPEC, "v": VMEM_SPEC, "u": VMEM_SPEC, "h": HBM_SPEC}
 
 
 def call(kernel, out_shape, *args, places=None, outs=None, scratch=(), flops=0, nbytes=0, trans=0):
@@ -401,14 +402,11 @@
     w1,
     w2,
     w3,
-    rot_ref,
+    rot_in,
     sent_out,
-    min_out,
     gb_out,
     ctx_out,
     dqkv_out,
-    wd_out,
-    wqkv_out,
     xhat_out,
     vec_ref,
     ub_ref,
@@ -418,7 +416,6 @@
     wqkv_ref,
     wd_ref,
     qb_ref,
-    min_ref,
     gb_ref,
     ctx_ref,
     dqkv_ref,
@@ -426,11 +423,12 @@
     sent_ref,
     in_sem,
     out_sem,
-    weight_sem,
     sent_sem,
     vec_col_ref,
     buf_ref,
     buf_sem,
+    rot_ref,
+    rot_sem,
 ):
     me = info_ref[64]
     place = info_ref[66]
@@ -449,17 +447,13 @@
     for copy in parts:
         copy.wait()
     assemble_a(me, buf_ref, wqkv_ref, wd_ref)
+    rotary = pltpu.make_async_copy(rot_in, rot_ref, rot_sem)
+    rotary.start()
     for load in loads[2:]:
         load.start()
     read_vectors(me, buf_ref, vec_ref, qb_ref, ub_ref)
-    weights = [
-        pltpu.make_async_copy(wd_ref, wd_out, weight_sem.at[0]),
-        pltpu.make_async_copy(wqkv_ref, wqkv_out, weight_sem.at[1]),
-    ]
-    for copy in weights:
-        copy.start()
+    rotary.wait()
     stores = (
-        (min_ref, min_out),
         (gb_ref, gb_out),
         (ctx_ref, ctx_out),
         (xhat_ref, xhat_out),
@@ -481,7 +475,6 @@
         xhat, _ = normalize(x_ref[r].astype(f32))
         xhat_ref[here, :] = xhat.astype(bf16)
         attn_in = (xhat * vec_ref[0:1] + vec_ref[1:2]).astype(bf16)
-        min_ref[here, :] = (xhat * vec_ref[2:3] + vec_ref[3:4]).astype(bf16)
         qkv = dot(attn_in, wqkv_ref[...]) + qb_ref[...]
         d = me ^ ((r & 1) * 2 + r // 2)
         base = (d * 2 + info_ref[65]) * SEGS
@@ -545,7 +538,7 @@
             sums_ref[0:1, :] = jnp.sum(kept, axis=0, keepdims=True)
 
         sums_ref[1:2, 0:QC] += jnp.sum(dqkv.astype(f32), axis=0, keepdims=True)
-        for n in range(5):
+        for n in range(4):
             store(n, r).start()
 
     c = me % 2
@@ -582,12 +575,9 @@
         sent(d, 0).start()
         sent(d, 1).start()
 
-    for copy in weights:
-        copy.wait()
-
     @pl.loop(0, 4)
     def _(i):
-        for n in range(5):
+        for n in range(4):
             store(n, i).wait()
         sent(i, 0).wait()
         sent(i, 1).wait()
@@ -601,11 +591,8 @@
         [
             shaped(4, 4, 256, 256),
             shaped(tokens, D),
-            shaped(tokens, D),
             shaped(tokens, 256),
             shaped(tokens, QC),
-            shaped(D // TP, D),
-            shaped(D, QC),
             shaped(tokens, D),
             shaped(8, D, dtype=f32),
             shaped(1, HC, dtype=f32),
@@ -616,8 +603,8 @@
         *cots,
         *blocks,
         jnp.asarray(rotary_tables()),
-        places="s" + "h" * 12 + "v",
-        outs="h" * 8 + "vvv",
+        places="s" + "a" * 12 + "h",
+        outs="h" * 5 + "vvv",
         scratch=[
             pltpu.VMEM((TP, ROW, D), bf16),
             pltpu.VMEM((TP, ROW, D), bf16),
@@ -625,18 +612,18 @@
             pltpu.VMEM((D // TP, D), bf16),
             pltpu.VMEM((1, QC), f32),
             pltpu.VMEM((tokens, D), bf16),
-            pltpu.VMEM((tokens, D), bf16),
             pltpu.VMEM((tokens, 256), bf16),
             pltpu.VMEM((tokens, QC), bf16),
             pltpu.VMEM((tokens, D), bf16),
             pltpu.VMEM((4, 4, 256, 256), bf16),
             dma((4, 2)),
-            dma((5, 4)),
-            dma((2,)),
+            dma((4, 4)),
             dma((4, 2)),
             pltpu.VMEM((D, 8), f32),
             pltpu.VMEM((4, 1024 + IMAGE, 256), bf16),
             dma((4,)),
+            pltpu.VMEM((ROW, 768), bf16),
+            dma,
         ],
         flops=6e9,
         nbytes=2e7,
@@ -650,7 +637,6 @@
     w1,
     w2,
     w3,
-    min_in,
     gb_in,
     xhat_in,
     ub_ref,
@@ -659,10 +645,7 @@
     sent_out,
     hidden_out,
     dpre_out,
-    wup_out,
-    wdown_out,
     buf_ref,
-    min_ref,
     gb_ref,
     wup_ref,
     wdown_ref,
@@ -672,12 +655,13 @@
     xhat_ref,
     sums_ref,
     image_ref,
-    parts_ref,
     vec_col_ref,
+    min_ref,
+    rows_ref,
+    turned_ref,
     buf_sem,
     in_sem,
     out_sem,
-    weight_sem,
     sent_sem,
     image_sem,
 ):
@@ -689,7 +673,7 @@
         parts.append(pltpu.make_async_copy(src, buf_ref.at[b], buf_sem.at[n]))
 
     def load(t, n):
-        src, dst = ((min_in, min_ref), (gb_in, gb_ref), (xhat_in, xhat_ref))[n]
+        src, dst = ((gb_in, gb_ref), (xhat_in, xhat_ref))[n]
         return pltpu.make_async_copy(src.at[tile(t), :], dst.at[tile(t), :], in_sem.at[t, n])
 
     for part in parts:
@@ -699,98 +683,119 @@
             load(t, n).start()
     for part in parts:
         part.wait()
-    for t in range(4):
-        load(t, 2).start()
     assemble_b(me, buf_ref, wup_ref, wdown_ref)
-    weights = [
-        pltpu.make_async_copy(wup_ref, wup_out, weight_sem.at[0]),
-        pltpu.make_async_copy(wdown_ref, wdown_out, weight_sem.at[1]),
-    ]
-    for copy in weights:
-        copy.start()
     sums_ref[...] = jnp.zeros_like(sums_ref)
 
-    def store(t, n):
+    vec_col_ref[...] = jnp.transpose(vec_ref[...])
+    rows_ref[...] = jnp.zeros_like(rows_ref)
+
+    def store(j, n):
         src, dst = ((hidden_ref, hidden_out), (dpre_ref, dpre_out))[n]
-        return pltpu.make_async_copy(src.at[tile(t), :], dst.at[tile(t), :], out_sem.at[t, n])
-
-    @pl.loop(0, TP)
-    def _(tn):
-        t = tile(tn)
-        load(tn, 0).wait()
-        load(tn, 1).wait()
-
-        def products(n):
-            at = slice(n * 256, (n + 1) * 256)
-            pre = dot(min_ref[t, :], wup_ref[:, at]) + ub_ref[:, at]
-            return pre, dot_nt(gb_ref[t, :], wdown_ref[at, :])
-
-        ahead = products(0)
-        for n in range(4):
-            at = slice(n * 256, (n + 1) * 256)
-            pre, back = ahead
-            if n < 3:
-                ahead = products(n + 1)
-            size = jnp.abs(pre) * 0.7071067811865476
-            bell = jnp.exp(-0.5 * pre * pre)
+        return pltpu.make_async_copy(src.at[:, tile(j)], dst.at[:, tile(j)], out_sem.at[j, n])
+
+    def sent_up(j):
+        rows = pl.ds(pl.multiple_of(j * 64, 64), 64)
+        return pltpu.make_async_copy(
+            sent_ref.at[:, :, rows, :], sent_out.at[:, :, rows, :], sent_sem.at[j, 4]
+        )
+
+    def sent_down(j, x):
+        b, a = swapped(j, x, c)
+        rows = pl.ds(256, 256)
+        return pltpu.make_async_copy(
+            sent_ref.at[b, a, rows, :], sent_out.at[b, a, rows, :], sent_sem.at[j, x]
+        )
+
+    def hidden_tile(j, t):
+        at = pl.ds(t * ROW, ROW)
+        pre = dot(min_ref[at, :], wup_ref[:, tile(j)]) + ub_ref[:, tile(j)]
+        return pre, dot_nt(gb_ref[at, :], wdown_ref[tile(j), :])
+
+    def activate(j, t, pre, back):
+        total = jnp.zeros((8, 256), f32)
+        for i in range(0, ROW, STRIP):
+            at = pl.ds(t * ROW + i, STRIP)
+            a, b = pre[i : i + STRIP], back[i : i + STRIP]
+            size = jnp.abs(a) * 0.7071067811865476
+            bell = jnp.exp(-0.5 * a * a)
             s = 1.0 / (1.0 + 0.3275911 * size)
             poly = s * (
                 0.127414796
                 + s * (-0.142248368 + s * (0.7107068705 + s * (-0.7265760135 + s * 0.5307027145)))
             )
             tail = poly * bell
-            cumul = jnp.where(pre >= 0.0, 1.0 - tail, tail)
-            hidden_ref[t, at] = (pre * cumul).astype(bf16)
-            dpre = (back * (cumul + pre * (bell * 0.3989422804014327))).astype(bf16)
-            dpre_ref[t, at] = dpre
-            sums_ref[0:1, at] += jnp.sum(dpre.astype(f32), axis=0, keepdims=True)
-        store(tn, 0).start()
-        store(tn, 1).start()
-
-    @pl.loop(0, 4)
-    def _(y):
-        grad = dot_tn(hidden_ref[:, tile(y)], gb_ref[...]).astype(bf16)
+            cumul = jnp.where(a >= 0.0, 1.0 - tail, tail)
+            hidden_ref[at, tile(j)] = (a * cumul).astype(bf16)
+            dpre = (b * (cumul + a * (bell * 0.3989422804014327))).astype(bf16)
+            dpre_ref[at, tile(j)] = dpre
+            total += jnp.sum(dpre.astype(f32).reshape(STRIP // 8, 8, 256), axis=0)
+        return jnp.sum(total, axis=0, keepdims=True)
+
+    def put_down(j):
+        down = dot_tn(hidden_ref[:, tile(j)], gb_ref[...]).astype(bf16)
         for x in range(4):
-            b, a = swapped(y, x, c)
+            b, a = swapped(j, x, c)
             for cg in range(4):
-                sent_ref[b, a, 256 + cg * 64 : 256 + (cg + 1) * 64, :] = grad[
+                sent_ref[b, a, 256 + cg * 64 : 256 + (cg + 1) * 64, :] = down[
                     x * 64 : (x + 1) * 64, cg * 256 : (cg + 1) * 256
                 ]
 
-    def sent(a, rows, n):
-        base = a * 512 + rows.start
-        return pltpu.make_async_copy(
-            sent_ref.at[:, a, rows, :],
-            sent_out.at[:, pl.ds(pl.multiple_of(base, 16), rows.size), :],
-            sent_sem.at[a, n],
-        )
-
-    for a in range(4):
-        sent(a, pl.ds(256, 256), 4).start()
-
-    sums_ref[2:3, :] = through(sums_ref[0:1, :], wup_ref[...])
-    vec_col_ref[...] = jnp.transpose(vec_ref[...])
-    for t in range(4):
-        load(t, 2).wait()
-
-    def above(a, d):
-        return sent(a, pl.ds(pl.multiple_of(d * 64, 64), 64), d)
-
-    @pl.loop(0, 4)
-    def _(d):
-        raw = dot_tn(xhat_ref[:, tile(d)], dpre_ref[...])
-        gain, bias = vec_col_ref[tile(d), 2:3], vec_col_ref[tile(d), 3:4]
-        grad = (raw * gain + bias * sums_ref[0:1, :]).astype(bf16)
-        sums_ref[1:2, tile(d)] = row_sums(raw * wup_ref[tile(d), :].astype(f32))
+    def put_up(j, t, raw):
+        row = pl.multiple_of(j * 64 + t * 16, 16)
+        sums = sums_ref[0:1, tile(j)]
         for y in range(4):
             for x in range(4):
                 b, a = swapped(y, x, c)
-                at = slice((y * 4 + x) * 16, (y * 4 + x + 1) * 16)
-                for cg in range(4):
-                    row = pl.multiple_of(d * 64 + cg * 16, 16)
-                    sent_ref[b, a, pl.ds(row, 16), :] = grad[at, cg * 256 : (cg + 1) * 256]
-        for a in range(4):
-            above(a, d).start()
+                i = (y * 4 + x) * 16
+                at = slice(t * 256 + i, t * 256 + i + 16)
+                part = raw[i : i + 16]
+                product = part * wup_ref[at, tile(j)].astype(f32)
+                rows_ref[at, :] += product[:, :128] + product[:, 128:]
+                gain, bias = vec_col_ref[at, 2:3], vec_col_ref[at, 3:4]
+                sent_ref[b, a, pl.ds(row, 16), :] = (part * gain + bias * sums).astype(bf16)
+
+    def step(j, last=False, first=False):
+        if not last:
+            total = jnp.zeros((1, 256), f32)
+        for t in range(TP):
+            if first:
+                at = pl.ds(t * ROW, ROW)
+                load(t, 0).wait()
+                load(t, 1).wait()
+                for i in range(0, ROW, 16):
+                    strip = pl.ds(t * ROW + i, 16)
+                    values = xhat_ref[strip, :].astype(f32)
+                    min_ref[strip, :] = (values * vec_ref[2:3] + vec_ref[3:4]).astype(bf16)
+                turned_ref[:, at] = jnp.transpose(xhat_ref[at, :])
+            if not last:
+                pre, back = hidden_tile(j, t)
+            if not first:
+                if t == 0:
+                    put_down(j - 1)
+                raw = dot(turned_ref[t * 256 : (t + 1) * 256, :], dpre_ref[:, tile(j - 1)])
+            if not last:
+                total += activate(j, t, pre, back)
+            if not first:
+                put_up(j - 1, t, raw)
+        if not last:
+            sums_ref[0:1, tile(j)] = total
+            store(j, 0).start()
+            store(j, 1).start()
+        if not first:
+            sent_up(j - 1).start()
+            for x in range(4):
+                sent_down(j - 1, x).start()
+
+    step(0, first=True)
+
+    @pl.loop(1, 4)
+    def _(j):
+        step(j)
+
+    step(4, last=True)
+    total = jnp.sum(rows_ref[...], axis=1, keepdims=True)
+    sums_ref[1:2, :] = jnp.transpose(jnp.broadcast_to(total, (D, 128)))[0:1, :]
+    sums_ref[2:3, :] = through(sums_ref[0:1, :], wup_ref[...])
 
     image_ref[...] = jnp.zeros_like(image_ref)
 
@@ -809,68 +814,64 @@
     put(48, sums_a_ref, 0, 4)
     image = image_ref[...]
     high = image.astype(bf16)
-    parts_ref[0:IMAGE, :] = high
-    parts_ref[IMAGE : 2 * IMAGE, :] = (image - high.astype(f32)).astype(bf16)
-    images = [
-        pltpu.make_async_copy(parts_ref, sent_out.at[b, pl.ds(2048, 2 * IMAGE), :], image_sem.at[b])
-        for b in range(4)
-    ]
-    for copy in images:
-        copy.start()
-    for copy in weights:
-        copy.wait()
+    low = (image - high.astype(f32)).astype(bf16)
+    for b in range(4):
+        for a in range(4):
+            half = (high, low)[a // 2]
+            sent_ref[b, a, 512 : 512 + IMAGE // 2, :] = half[a % 2 * 32 : a % 2 * 32 + 32]
+    rows = pl.ds(512, IMAGE // 2)
+    images = pltpu.make_async_copy(
+        sent_ref.at[:, :, rows, :], sent_out.at[:, :, rows, :], image_sem
+    )
+    images.start()
     for i in range(TP):
         store(i, 0).wait()
         store(i, 1).wait()
-        for n in range(4):
-            above(i, n).wait()
-        sent(i, pl.ds(256, 256), 4).wait()
-    for copy in images:
-        copy.wait()
-
-
-def mlp(info, blocks, mlp_in, gb, xhat, ub, vec, sums):
+        sent_up(i).wait()
+        for x in range(4):
+            sent_down(i, x).wait()
+    images.wait()
+
+
+def mlp(info, blocks, gb, xhat, ub, vec, sums):
     tokens = TP * ROW
     dma = pltpu.SemaphoreType.DMA
     return call(
         mlp_kernel,
         [
-            shaped(4, 2048 + 2 * IMAGE, 256),
+            shaped(4, 4, 512 + IMAGE // 2, 256),
             shaped(tokens, HC),
             shaped(tokens, HC),
-            shaped(D, HC),
-            shaped(HC, D),
         ],
         info,
         *blocks,
-        mlp_in,
         gb,
         xhat,
         ub,
         vec,
         sums,
-        places="s" + "h" * 7 + "vvv",
-        outs="h" * 5,
+        places="s" + "a" * 4 + "hhvvv",
+        outs="hhh",
         scratch=[
             pltpu.VMEM((4, 2048, 256), bf16),
-            pltpu.VMEM((tokens, D), bf16),
             pltpu.VMEM((tokens, D), bf16),
             pltpu.VMEM((D, HC), bf16),
             pltpu.VMEM((HC, D), bf16),
             pltpu.VMEM((tokens, HC), bf16),
             pltpu.VMEM((tokens, HC), bf16),
-            pltpu.VMEM((4, 4, 512, 256), bf16),
+            pltpu.VMEM((4, 4, 512 + IMAGE // 2, 256), bf16),
             pltpu.VMEM((tokens, D), bf16),
             pltpu.VMEM((8, D), f32),
             pltpu.VMEM((IMAGE, 256), f32),
-            pltpu.VMEM((2 * IMAGE, 256), bf16),
             pltpu.VMEM((D, 8), f32),
+            pltpu.VMEM((tokens, D), bf16),
+            pltpu.VMEM((D, 128), f32),
+            pltpu.VMEM((D, tokens), bf16),
             dma((4,)),
-            dma((4, 3)),
             dma((4, 2)),
-            dma((2,)),
+            dma((4, 2)),
             dma((4, 5)),
-            dma((4,)),
+            dma,
         ],
         flops=9e9,
         nbytes=2e7,
@@ -879,14 +880,19 @@
 
 
 def outputs_kernel(
+    info_ref,
     ctx_in,
     hidden_in,
     dqkv_in,
     dpre_in,
-    wd_in,
-    wdown_in,
-    wqkv_in,
-    wup_in,
+    a0,
+    a1,
+    a2,
+    a3,
+    b0,
+    b1,
+    b2,
+    b3,
     vec_ref,
     theirs_out,
     mine_out,
@@ -899,14 +905,19 @@
     wqkv_ref,
     wup_ref,
     both_ref,
+    buf_a_ref,
+    buf_b_ref,
     weight_sem,
     in_sem,
     out_sem,
 ):
-    pairs = ((wqkv_in, wqkv_ref), (wup_in, wup_ref), (wd_in, wd_ref), (wdown_in, wdown_ref))
-    weights = [
-        pltpu.make_async_copy(src, dst, weight_sem.at[i]) for i, (src, dst) in enumerate(pairs)
-    ]
+    me, place = info_ref[64], info_ref[66]
+    weights = []
+    for n, step in enumerate(STEPS):
+        b = (place + 4 - step) % 4
+        pairs = (((a0, a1, a2, a3)[n], buf_a_ref), ((b0, b1, b2, b3)[n], buf_b_ref))
+        for i, (src, dst) in enumerate(pairs):
+            weights.append(pltpu.make_async_copy(src, dst.at[b], weight_sem.at[n, i]))
     inputs = (
         (dqkv_in, dqkv_ref),
         (dpre_in, dpre_ref),
@@ -922,13 +933,15 @@
         dst = (theirs_out, mine_out)[n]
         return pltpu.make_async_copy(both_ref.at[i], dst.at[i - 2 * n], out_sem.at[i])
 
+    for weight in weights:
+        weight.start()
     for i in range(TP):
         for n in range(4):
             load((i + 2) % 4, n).start()
-            if i == 0:
-                weights[n].start()
     for weight in weights:
         weight.wait()
+    assemble_a(me, buf_a_ref, wqkv_ref, wd_ref)
+    assemble_b(me, buf_b_ref, wup_ref, wdown_ref)
 
     @pl.loop(0, TP)
     def _(i):
@@ -954,22 +967,21 @@
         finished(i, i // 2).wait()
 
 
-def outputs(ctx, hidden, dqkv, dpre, wd, wdown, wqkv, wup, vec):
+def outputs(info, ctx, hidden, dqkv, dpre, blocks_a, blocks_b, vec):
     tokens = TP * ROW
     dma = pltpu.SemaphoreType.DMA
     return call(
         outputs_kernel,
         [shaped(2, 2, ROW, D), shaped(2, 2, ROW, D)],
+        info,
         ctx,
         hidden,
         dqkv,
         dpre,
-        wd,
-        wdown,
-        wqkv,
-        wup,
+        *blocks_a,
+        *blocks_b,
         vec,
-        places="h" * 8 + "v",
+        places="s" + "a" * 12 + "v",
         outs="hh",
         scratch=[
             pltpu.VMEM((tokens, 256), bf16),
@@ -981,7 +993,9 @@
             pltpu.VMEM((D, QC), bf16),
             pltpu.VMEM((D, HC), bf16),
             pltpu.VMEM((TP, 2, ROW, D), bf16),
-            dma((4,)),
+            pltpu.VMEM((4, 1024 + IMAGE, 256), bf16),
+            pltpu.VMEM((4, 2048, 256), bf16),
+            dma((4, 2)),
             dma((4, 4)),
             dma((4,)),
         ],
@@ -990,25 +1004,49 @@
     )
 
 
-def half_kernel(a0_ref, b0_ref, a1_ref, b1_ref, kept_ref, send_ref):
-    kept_ref[...] = a0_ref[...].astype(f32) + b0_ref[...].astype(f32)
-    send_ref[...] = (a1_ref[...].astype(f32) + b1_ref[...].astype(f32)).astype(bf16)
+def half_kernel(mine_in, got_in, kept_out, send_out, mine_ref, got_ref, kept_ref, send_ref, in_sem, out_sem):
+    loads = []
+    for i in (1, 0):
+        for n in range(2):
+            pair = (
+                pltpu.make_async_copy(mine_in.at[i, n], mine_ref.at[i, n], in_sem.at[i, n, 0]),
+                pltpu.make_async_copy(got_in.at[i, n], got_ref.at[i, n], in_sem.at[i, n, 1]),
+            )
+            loads.append((i, n, pair))
+            for copy in pair:
+                copy.start()
+    stores = []
+    for i, n, pair in loads:
+        for copy in pair:
+            copy.wait()
+        total = mine_ref[i, n].astype(f32) + got_ref[i, n].astype(f32)
+        ref, out = ((kept_ref, kept_out), (send_ref, send_out))[i]
+        ref[n] = total.astype(ref.dtype)
+        stores.append(pltpu.make_async_copy(ref.at[n], out.at[0, n], out_sem.at[i, n]))
+        stores[-1].start()
+    for store in stores:
+        store.wait()
 
 
 def half_sum(mine, got):
-    mine, got = in_hbm(mine), in_hbm(got)
-    first = pl.BlockSpec((1, 1, ROW // 2, D), lambda n, k: (0, n, k, 0))
-    second = pl.BlockSpec((1, 1, ROW // 2, D), lambda n, k: (1, n, k, 0))
-    out = pl.BlockSpec((1, 1, ROW // 2, D), lambda n, k: (0, n, k, 0))
-    return pl.pallas_call(
+    dma = pltpu.SemaphoreType.DMA
+    return call(
         half_kernel,
-        grid=(2, 2),
-        in_specs=[first, first, second, second],
-        out_specs=[out, out],
-        out_shape=[pltpu.HBM((1, 2, ROW, D), f32), pltpu.HBM((1, 2, ROW, D), bf16)],
-        compiler_params=pltpu.CompilerParams(vmem_limit_bytes=VMEM),
-        cost_estimate=pl.CostEstimate(flops=0, bytes_accessed=8000000, transcendentals=0),
-    )(mine, got, mine, got)
+        [shaped(1, 2, ROW, D, dtype=f32), shaped(1, 2, ROW, D)],
+        mine,
+        got,
+        places="ha",
+        outs="hh",
+        scratch=[
+            pltpu.VMEM((2, 2, ROW, D), bf16),
+            pltpu.VMEM((2, 2, ROW, D), bf16),
+            pltpu.VMEM((2, ROW, D), f32),
+            pltpu.VMEM((2, ROW, D), bf16),
+            dma((2, 2, 2)),
+            dma((2, 2)),
+        ],
+        nbytes=8e6,
+    )
 
 
 def close_kernel(len_ref, x_ref, cot_ref, kept_ref, got_ref, vec_ref, out_ref, grad_ref):
@@ -1051,64 +1089,84 @@
         out_shape=pltpu.HBM((4, 256, 256), bf16),
         compiler_params=pltpu.CompilerParams(vmem_limit_bytes=VMEM),
         cost_estimate=pl.CostEstimate(flops=0, bytes_accessed=3000000, transcendentals=0),
-    )(in_hbm(sent_a))
-
-
-def add_kernel(place_ref, early_ref, b_ref, image_ref, o0, o1, o2, o3, sums_ref, both_ref, sem):
-    n = pl.program_id(0)
-    total = sum([b_ref[i].astype(f32) for i in range(4)]).astype(bf16)
-
-    @pl.when(n == 0)
-    def _():
-        image = sum([image_ref[i].astype(f32) for i in range(4)])
-        image = image[:IMAGE] + image[IMAGE:]
-        high = image.astype(bf16)
-        sums_ref[0:IMAGE, :] = high
-        sums_ref[IMAGE : 2 * IMAGE, :] = (image - high.astype(f32)).astype(bf16)
-
-    both_ref[n, 0:256, :] = early_ref[0]
-    both_ref[n, 256:768, :] = total
-    both_ref[n, 768 : 768 + 2 * IMAGE, :] = sums_ref[...]
-    copies = [
-        pltpu.make_async_copy(both_ref.at[k], out, sem.at[k]) for k, out in enumerate((o0, o1, o2, o3))
+    )(sent_a)
+
+
+def add_kernel(
+    place_ref, early_in, b_in, o0, o1, o2, o3, early_ref, b_ref, image_ref, both_ref, early_sem, b_sem, image_sem, sem
+):
+    place = place_ref[0]
+
+    def load(n, i):
+        a = (place + STEPS[n]) % 4
+        return pltpu.make_async_copy(
+            b_in.at[i, a, pl.ds(0, 512), :], b_ref.at[n, i], b_sem.at[n, i]
+        )
+
+    images = [
+        pltpu.make_async_copy(
+            b_in.at[i, :, pl.ds(512, IMAGE // 2), :], image_ref.at[i], image_sem.at[i]
+        )
+        for i in range(4)
     ]
-    for k, copy in enumerate(copies):
-        pl.when(n == k)(copy.start)
-
-    @pl.when(n == 3)
-    def _():
-        for copy in copies:
-            copy.wait()
-
-
-def step_of(n):
-    return jnp.where(n < 2, n, 5 - n)
+    early = [
+        pltpu.make_async_copy(
+            early_in.at[(place + step) % 4], early_ref.at[n], early_sem.at[n]
+        )
+        for n, step in enumerate(STEPS)
+    ]
+    for copy in images:
+        copy.start()
+    for n in range(4):
+        early[n].start()
+        for i in range(4):
+            load(n, i).start()
+    for copy in images:
+        copy.wait()
+    image = sum([image_ref[i].astype(f32) for i in range(4)]).reshape(2, IMAGE, 256)
+    image = image[0] + image[1]
+    high = image.astype(bf16)
+    low = (image - high.astype(f32)).astype(bf16)
+    stores = [
+        pltpu.make_async_copy(both_ref.at[n], out, sem.at[n]) for n, out in enumerate((o0, o1, o2, o3))
+    ]
+    for n in range(4):
+        both_ref[n, 768 : 768 + IMAGE, :] = high
+        both_ref[n, 768 + IMAGE : 768 + 2 * IMAGE, :] = low
+        early[n].wait()
+        both_ref[n, 0:256, :] = early_ref[n]
+        for i in range(4):
+            load(n, i).wait()
+        total = sum([b_ref[n, i].astype(f32) for i in range(4)])
+        both_ref[n, 256:768, :] = total.astype(bf16)
+        stores[n].start()
+    for store in stores:
+        store.wait()
 
 
 def add(place, early, sent_b):
     rows = 768 + 2 * IMAGE
-    sent_b = in_hbm(sent_b)
-    return pl.pallas_call(
+    dma = pltpu.SemaphoreType.DMA
+    return call(
         add_kernel,
-        grid_spec=pltpu.PrefetchScalarGridSpec(
-            num_scalar_prefetch=1,
-            grid=(4,),
-            in_specs=[
-                pl.BlockSpec((1, 256, 256), lambda n, p: ((p[0] + step_of(n)) % 4, 0, 0)),
-                pl.BlockSpec((4, 512, 256), lambda n, p: (0, (p[0] + step_of(n)) % 4, 0)),
-                pl.BlockSpec((4, 2 * IMAGE, 256), lambda n, p: (0, 2048 // (2 * IMAGE), 0)),
-            ],
-            out_specs=[HBM_SPEC] * 4,
-            scratch_shapes=[
-                pltpu.VMEM((2 * IMAGE, 256), bf16),
-                pltpu.VMEM((4, rows, 256), bf16),
-                pltpu.SemaphoreType.DMA((4,)),
-            ],
-        ),
-        out_shape=[pltpu.HBM((rows, 256), bf16)] * 4,
-        compiler_params=pltpu.CompilerParams(vmem_limit_bytes=VMEM),
-        cost_estimate=pl.CostEstimate(flops=0, bytes_accessed=6000000, transcendentals=0),
-    )(place, in_hbm(early), sent_b, sent_b)
+        [shaped(rows, 256)] * 4,
+        place,
+        early,
+        sent_b,
+        places="shh",
+        outs="hhhh",
+        scratch=[
+            pltpu.VMEM((4, 256, 256), bf16),
+            pltpu.VMEM((4, 4, 512, 256), bf16),
+            pltpu.VMEM((4, 4, IMAGE // 2, 256), bf16),
+            pltpu.VMEM((4, rows, 256), bf16),
+            dma((4,)),
+            dma((4, 4)),
+            dma((4,)),
+            dma((4,)),
+        ],
+        nbytes=6e6,
+    )
 
 
 LAST = QC + HC + 4 * 256
@@ -1120,9 +1178,18 @@
     ] + [16 + 3 * d + i for i in range(3)]
 
 
-def part_kernel(far_ref, r0, r1, r2, r3, slots_ref, keep_ref, send_ref, total_ref, rows_ref):
+def part_kernel(
+    far_ref, r0, r1, r2, r3, slots_ref, keep_ref, send_ref, total_ref, rows_ref, in_ref, sem
+):
     far = far_ref[0]
-    total_ref[...] = sum([ref[...].astype(f32) for ref in (r0, r1, r2, r3)])
+    loads = [
+        pltpu.make_async_copy(r, in_ref.at[i], sem.at[i]) for i, r in enumerate((r0, r1, r2, r3))
+    ]
+    for load in loads:
+        load.start()
+    for load in loads:
+        load.wait()
+    total_ref[...] = sum([in_ref[i].astype(f32) for i in range(4)])
     rows_ref[...] = jnp.zeros_like(rows_ref)
     for d in range(4):
         for i, row in enumerate(image_rows(d)):
@@ -1138,7 +1205,7 @@
                 row = (d * 3 + p) * 16 + zh * 8
                 slots_ref[s, :, p * 256 : (p + 1) * 256] = total_ref[row : row + 8, :].astype(bf16)
             for cg in range(4):
-                row = 256 + (d * 4 + cg) * 16 + zh * 8
+                row = 256 + (cg * 4 + d) * 16 + zh * 8
                 at = QC + cg * 256
                 slots_ref[s, :, at : at + 256] = total_ref[row : row + 8, :].astype(bf16)
             for n, block in enumerate((high[:8], high[8:], low[:8], low[8:])):
@@ -1159,8 +1226,14 @@
         [shaped(8, 8, LAST), shaped(40, D, dtype=f32), shaped(40, D)],
         far,
         *received,
+        places="saaaa",
         outs="uuu",
-        scratch=[pltpu.VMEM((768 + 2 * IMAGE, 256), f32), pltpu.VMEM((4, 16, 256), f32)],
+        scratch=[
+            pltpu.VMEM((768 + 2 * IMAGE, 256), f32),
+            pltpu.VMEM((4, 16, 256), f32),
+            pltpu.VMEM((4, 768 + 2 * IMAGE, 256), bf16),
+            pltpu.SemaphoreType.DMA((4,)),
+        ],
         nbytes=4e6,
     )
 
@@ -1248,6 +1321,7 @@
         up_bias,
         down_bias,
     )
+    x2, c2 = flip_core(inputs), flip_core(cotangent)
     slots, pieces = prepare(
         qkv_weight.reshape(8, 3 * D),
         up_weight.reshape(8, FF),
@@ -1256,6 +1330,7 @@
         lengths,
         vectors,
     )
+    slots, x2, c2 = lax.optimization_barrier((slots, x2, c2))
     far_pieces = flip_far(pieces)
     first = a2a(slots, stack_groups())
     block, lens = spread(index[None], first.reshape(4, 16, SLOT), pieces, far_pieces)
@@ -1268,30 +1343,24 @@
     block, x0, c0 = lax.optimization_barrier((block, inputs, cotangent))
     x1, c1 = flip_chip(x0), flip_chip(c0)
     second = gather(block, inner)
-    second, x0, c0 = lax.optimization_barrier((second, x0, c0))
+    second, x1 = lax.optimization_barrier((second, x1))
     third_a = gather(merge_a(deep, second), outer)
-    x2, x3 = flip_core(x0), flip_core(x1)
-    c2, c3 = flip_core(c0), flip_core(c1)
+    x3, c3 = flip_core(x1), flip_core(c1)
     xs, cots = (x0, x1, x2, x3), (c0, c1, c2, c3)
-    wide_b, third_a, xs, cots = lax.optimization_barrier(
-        (merge_b(deep, second), third_a, xs, cots)
-    )
+    wide_b, xs, cots = lax.optimization_barrier((merge_b(deep, second), xs, cots))
     third_b = gather(wide_b, outer)
 
-    sent_a, mlp_in, gb, ctx, dqkv, wd, wqkv, xhat, vec, up_b, sums = attention(
-        info, xs, cots, third_a
-    )
+    sent_a, gb, ctx, dqkv, xhat, vec, up_b, sums = attention(info, xs, cots, third_a)
     sent_a = a2a(sent_a, outer)
-    sent_b, hidden, dpre, wup, wdown = mlp(info, third_b, mlp_in, gb, xhat, up_b, vec, sums)
+    sent_b, hidden, dpre = mlp(info, third_b, gb, xhat, up_b, vec, sums)
     sent_b = a2a(sent_b, outer)
 
-    theirs, mine = outputs(ctx, hidden, dqkv, dpre, wd, wdown, wqkv, wup, vec)
+    theirs, mine = outputs(info, ctx, hidden, dqkv, dpre, third_a, third_b, vec)
     kept, send = half_sum(mine, flip_core(theirs))
 
     got = flip_chip(send)
     early, send = lax.optimization_barrier((add_early(sent_a), send))
     fourth = scatter(add(deep, early, sent_b), inner)
-    fourth, got = lax.optimization_barrier((fourth, got))
     slots, keep, rest = part(far, fourth)
     block_output, input_grad = close(lengths, inputs, cotangent, kept, got, vec)
     place = (me * 32 + index)[None]

time: 186 us -> 177 us (0.952)
  waiting for transfers between devices: 45.4 us -> 32.8 us
  starting transfers between devices: 51.8 us -> 57.6 us
  Pallas kernels: 76.7 us -> 72.1 us
  local copies, waits for them, and re-layouts: 10 us -> 12.3 us
    ppermute x3, waiting for transfers between devices: 19.5 us -> 0.75 us  [flip_chip(): return lax.ppermute(values, 'dp', [(0, 2), (2, 0), (1, 3), (3, 1)])]
    pallas_call x2 -> x0, Pallas kernels: 9.01 us -> none  [the longest x1 4.7 us: add(): pl.pallas_call(add_kernel, grid_spec=pltpu.PrefetchScalarGridSpec(num_sca...]
    ppermute x12, waiting for transfers between devices: 14.1 us -> 21 us  [ring(): return lax.ppermute(values, AXES, pairs)]
    pallas_call x9 -> x11, Pallas kernels: 59.5 us -> 65.8 us  [call(): pl.pallas_call(kernel, in_specs=[SPECS[p] for p in places], out_specs=out...]
    ppermute x5, starting transfers between devices: 3.68 us -> 9.63 us  [flip_core(): return lax.ppermute(values, 'dp', [(0, 1), (1, 0), (2, 3), (3, 2)])]
    unnamed x24 -> x34, local copies, waits for them, and re-layouts: 6.7 us -> 8.97 us
    pallas_call x1, Pallas kernels: 3.56 us -> 1.65 us  [add_early(): pl.pallas_call(add_early_kernel, grid=(4,), in_specs=[pl.BlockSpec((4, 1,...]
  transfers between devices with their start and end apart: 26 -> 26, of which waited for: 10 -> 11; matrix products, arithmetic and copies ran while one was open for 0% -> 2% of each run, Pallas kernels for 39% -> 40%
where the time goes in v5:
time: 177 us; the launch traced here: 176 us
  Pallas kernels  72.1 us (41%)
  starting transfers between devices  57.6 us (33%)
  waiting for transfers between devices  32.8 us (19%)
  local copies, waits for them, and re-layouts  12.3 us (7%)
    pallas_call x11, Pallas kernels, call(): pl.pallas_call(kernel, in_specs=[SPECS[p] for p in places], out_specs=out...  65.8 us
    all_to_all x4, starting transfers between devices, a2a(): lax.all_to_all(values, AXES, 0, 0, tiled=True, axis_index_groups=groups)  22.5 us
    ppermute x12, waiting for transfers between devices, ring(): return lax.ppermute(values, AXES, pairs)  21 us
    ppermute x12, starting transfers between devices, ring(): return lax.ppermute(values, AXES, pairs)  17.5 us
    ppermute x5, starting transfers between devices, flip_core(): return lax.ppermute(values, 'dp', [(0, 1), (1, 0), (2, 3), (3, 2)])  9.63 us
    unnamed x34, local copies, waits for them, and re-layouts  8.97 us
    ppermute x2, waiting for transfers between devices, flip_far(): return lax.ppermute(values, 'fsdp', [(i, i ^ 1) for i in range(32)])  6.32 us
    ppermute x2, starting transfers between devices, flip_far(): return lax.ppermute(values, 'fsdp', [(i, i ^ 1) for i in range(32)])  5.77 us
  transfers between devices with their start and end apart: 26, of which 11 were waited for; matrix products, arithmetic and copies ran while one was open for 2% of the time, Pallas kernels for 40%

profile of v5, /device:TPU:1, one launch (start us, length us, event | category | flops | bytes accessed | tf_op | source)
XLA Modules:
  0.0 175.7 jit_solution(5515334672672481514)
XLA Ops:
  0.6 1.5 collective-permute-start
  2.1 0.1 collective-permute-start.1
  2.2 0.7 reshape.81.dense_in
  3.0 0.8 reshape.79.qkv_ref
  3.8 0.9 reshape.80.up_ref
  4.7 0.9 reshape.82.down_in
  5.6 1.6 shard_map.263
  7.2 0.8 copy-done.8
  8.0 5.8 %all-to-all-start = ((bf16[8,8,1920]{2,1,0:T(8,128)(2,1)}), bf16[8,8,1920]{2,1,0:T(8,128)(2,1)S(1)}, u32[]{:S(2)}, u32[]{:S(2)}) async-start(bf16[8,8,1920]{2,1,0:T(8,128)(2,1)} %get-tuple-element.80), calls=%async_computation | async-start | bytes 491520 | tf_op jit(solution)/shard_map/all_to_all | solution.py:78
  13.8 2.9 %collective-permute-start.2 = (bf16[40,1024]{1,0:T(8,128)(2,1)S(1)}, bf16[40,1024]{1,0:T(8,128)(2,1)S(1)}, u32[]{:S(2)}, u32[]{:S(2)}) collective-permute-start(bf16[40,1024]{1,0:T(8,128)(2,1)S(1)} %get-tuple-element.81.mine_ref), channel_id=1, source_target_pairs={{0,1},{1,0},{2,3},{3,2},{4,5},{5,4},{6,7},{7,6},{8,9},{9,8},{10,11... | collective-permute-start | bytes 245768 | tf_op jit(solution)/shard_map/ppermute | solution.py:90
  16.7 5.4 %collective-permute-done.2.theirs_ref = bf16[40,1024]{1,0:T(8,128)(2,1)S(1)} collective-permute-done((bf16[40,1024]{1,0:T(8,128)(2,1)S(1)}, bf16[40,1024]{1,0:T(8,128)(2,1)S(1)}, u32[]{:S(2)}, u32[]{:S(2)}) %collective-permute-start.2) | collective-permute-done | bytes 81952 | tf_op jit(solution)/shard_map/ppermute | solution.py:90
  22.1 0.5 shard_map.264
  22.6 0.4 collective-permute-start.6
  22.9 1.2 collective-permute-start.8
  24.1 2.9 %collective-permute-start.5 = (bf16[832,256]{1,0:T(8,128)(2,1)S(1)}, bf16[832,256]{1,0:T(8,128)(2,1)S(1)}, u32[]{:S(2)}, u32[]{:S(2)}) collective-permute-start(bf16[832,256]{1,0:T(8,128)(2,1)S(1)} %get-tuple-element.86.b0), channel_id=1, source_target_pairs={{0,4},{2,6},{4,0},{6,2},{1,5},{3,7},{5,1},{7,3},{8,12},{10,14},{12... | collective-permute-start | bytes 1277960 | tf_op jit(solution)/shard_map/ppermute | solution.py:63
  27.0 0.8 collective-permute-start.4
  27.8 0.7 collective-permute-start.3
  28.5 4.4 %collective-permute-done.5.b3 = bf16[832,256]{1,0:T(8,128)(2,1)S(1)} collective-permute-done((bf16[832,256]{1,0:T(8,128)(2,1)S(1)}, bf16[832,256]{1,0:T(8,128)(2,1)S(1)}, u32[]{:S(2)}, u32[]{:S(2)}) %collective-permute-start.5) | collective-permute-done | bytes 426016 | tf_op jit(solution)/shard_map/ppermute | solution.py:63
  32.9 5.1 %collective-permute-done.4.b2 = bf16[832,256]{1,0:T(8,128)(2,1)S(1)} collective-permute-done((bf16[832,256]{1,0:T(8,128)(2,1)S(1)}, bf16[832,256]{1,0:T(8,128)(2,1)S(1)}, u32[]{:S(2)}, u32[]{:S(2)}) %collective-permute-start.4) | collective-permute-done | bytes 426016 | tf_op jit(solution)/shard_map/ppermute | solution.py:63
  38.0 0.9 shard_map.266.w0.a0
  38.9 2.7 %collective-permute-start.12 = (bf16[1088,256]{1,0:T(8,128)(2,1)}, bf16[1088,256]{1,0:T(8,128)(2,1)}, u32[]{:S(2)}, u32[]{:S(2)}) collective-permute-start(bf16[1088,256]{1,0:T(8,128)(2,1)} %shard_map.266.w0.a0), channel_id=1, source_target_pairs={{0,16},{8,24},{16,0},{24,8},{1,17},{9,25},{17,1},{25,9},{2,18},{10... | collective-permute-start | bytes 1671176 | tf_op jit(solution)/shard_map/ppermute | solution.py:63
  41.6 0.9 collective-permute-start.11
  42.5 0.6 collective-permute-start.10
  43.1 2.9 %collective-permute-start.7 = (bf16[256,1024]{1,0:T(8,128)(2,1)}, bf16[256,1024]{1,0:T(8,128)(2,1)}, u32[]{:S(2)}, u32[]{:S(2)}) collective-permute-start(bf16[256,1024]{1,0:T(8,128)(2,1)} %collective-permute-done.6.x1), channel_id=1, source_target_pairs={{0,32},{32,0},{64,96},{96,64},{1,33},{33,1},{65,97},{97,65},{2,34}... | collective-permute-start | bytes 1572872 | tf_op jit(solution)/shard_map/ppermute | solution.py:82
  46.0 0.7 collective-permute-done.8.c1
  46.8 1.8 %collective-permute-start.9 = (bf16[256,1024]{1,0:T(8,128)(2,1)}, bf16[256,1024]{1,0:T(8,128)(2,1)}, u32[]{:S(2)}, u32[]{:S(2)}) collective-permute-start(bf16[256,1024]{1,0:T(8,128)(2,1)} %collective-permute-done.8.c1), channel_id=1, source_target_pairs={{0,32},{32,0},{64,96},{96,64},{1,33},{33,1},{65,97},{97,65},{2,34}... | collective-permute-start | bytes 1572872 | tf_op jit(solution)/shard_map/ppermute | solution.py:82
  48.6 1.0 shard_map.265.w0.b0
  49.7 0.7 collective-permute-done.9.c3
  50.4 2.7 %collective-permute-start.15 = (bf16[2048,256]{1,0:T(8,128)(2,1)}, bf16[2048,256]{1,0:T(8,128)(2,1)}, u32[]{:S(2)}, u32[]{:S(2)}) collective-permute-start(bf16[2048,256]{1,0:T(8,128)(2,1)} %shard_map.265.w0.b0), channel_id=1, source_target_pairs={{0,16},{8,24},{16,0},{24,8},{1,17},{9,25},{17,1},{25,9},{2,18},{10... | collective-permute-start | bytes 3145736 | tf_op jit(solution)/shard_map/ppermute | solution.py:63
  53.1 0.9 collective-permute-start.14
  54.0 0.6 collective-permute-start.13
  54.6 0.8 collective-permute-done.11.w2.a2
  55.5 19.9 %shard_map.267 = (bf16[4,4,256,256]{3,2,1,0:T(8,128)(2,1)}, bf16[1024,1024]{1,0:T(8,128)(2,1)}, bf16[1024,256]{1,0:T(8,128)(2,1)}, bf16[1024,768]{1,0:T(8,128)(2...) custom-call(s32[67]{0:T(128)S(1)} %pad_add_fusion.info_ref, ...), custom_call_target="tpu_custom_call" | custom-call | flops 6000000000 | bytes 20000000 | tf_op jit(solution)/shard_map/pallas_call | solution.py:124
  75.4 4.0 %all-to-all-start.1 = ((bf16[4,4,256,256]{3,2,1,0:T(8,128)(2,1)}), bf16[4,4,256,256]{3,2,1,0:T(8,128)(2,1)S(1)}, u32[]{:S(2)}, u32[]{:S(2)}) async-start(bf16[4,4,256,256]{3,2,1,0:T(8,128)(2,1)} %get-tuple-element.102), calls=%async_computation.1 | async-start | bytes 4194304 | tf_op jit(solution)/shard_map/all_to_all | solution.py:78
  79.5 19.6 %shard_map.269 = (bf16[4,4,544,256]{3,2,1,0:T(8,128)(2,1)}, bf16[1024,1024]{1,0:T(8,128)(2,1)}, bf16[1024,1024]{1,0:T(8,128)(2,1)}) custom-call(s32[67]{0:T(128)S(1)} %pad_add_fusion.info_ref, bf16[2048,256]{1,0:T(8,128)(2,1)S(1)} %copy-done, bf16[2048,256]{1,0:T(8,128)(2,1)} %collective-permute-done.13.w1.b1, ...), custom_call_target="tpu_custom_call" | custom-call | flops 8999999488 | bytes 20000000 | tf_op jit(solution)/shard_map/pallas_call | solution.py:124
  99.1 5.0 %all-to-all-start.2 = ((bf16[4,4,544,256]{3,2,1,0:T(8,128)(2,1)}), bf16[4,4,544,256]{3,2,1,0:T(8,128)(2,1)}, u32[]{:S(2)}, u32[]{:S(2)}) async-start(bf16[4,4,544,256]{3,2,1,0:T(8,128)(2,1)} %get-tuple-element.117), calls=%async_computation.2 | async-start | bytes 8912896 | tf_op jit(solution)/shard_map/all_to_all | solution.py:78
  104.0 1.0 copy-done.2
  105.1 1.4 copy-done.12
  106.5 1.0 copy-done.13
  107.5 12.4 %shard_map.270 = (bf16[2,2,256,1024]{3,2,1,0:T(8,128)(2,1)}, bf16[2,2,256,1024]{3,2,1,0:T(8,128)(2,1)}) custom-call(s32[67]{0:T(128)S(1)} %pad_add_fusion.info_ref, bf16[1024,256]{1,0:T(8,128)(2,1)S(1)} %copy-done.13, bf16[1024,1024]{1,0:T(8,128)(2,1)} %get-tuple-element.110.hidden_in, bf16[1024,768]{1,0:T(8,128)(2,1)S(1)} %copy-done.12, ...), custom_call_target="tpu_custom_call" | custom-call | flops 6499999744 | bytes 16000000 | tf_op jit(solution)/shard_map/pallas_call | solution.py:124
  119.9 3.3 %collective-permute-start.16 = (bf16[2,2,256,1024]{3,2,1,0:T(8,128)(2,1)}, bf16[2,2,256,1024]{3,2,1,0:T(8,128)(2,1)S(1)}, u32[]{:S(2)}, u32[]{:S(2)}) collective-permute-start(bf16[2,2,256,1024]{3,2,1,0:T(8,128)(2,1)} %get-tuple-element.114), channel_id=1, source_target_pairs={{0,32},{32,0},{64,96},{96,64},{1,33},{33,1},{65,97},{97,65},{2,34}... | collective-permute-start | bytes 6291464 | tf_op jit(solution)/shard_map/ppermute | solution.py:82
  123.2 4.0 %collective-permute-done.16.got_in = bf16[2,2,256,1024]{3,2,1,0:T(8,128)(2,1)S(1)} collective-permute-done((bf16[2,2,256,1024]{3,2,1,0:T(8,128)(2,1)}, bf16[2,2,256,1024]{3,2,1,0:T(8,128)(2,1)S(1)}, u32[]{:S(2)}, u32[]{:S(2)}) %collective-permute-start.16) | collective-permute-done | bytes 2097184 | tf_op jit(solution)/shard_map/ppermute | solution.py:82
  127.2 2.9 %shard_map.271 = (f32[1,2,256,1024]{3,2,1,0:T(8,128)}, bf16[1,2,256,1024]{3,2,1,0:T(8,128)(2,1)}) custom-call(bf16[2,2,256,1024]{3,2,1,0:T(8,128)(2,1)} %get-tuple-element.113.mine_in, bf16[2,2,256,1024]{3,2,1,0:T(8,128)(2,1)S(1)} %collective-permute-done.16.got_in), custom_call_target="tpu_custom_call" | custom-call | bytes 8000000 | tf_op jit(solution)/shard_map/pallas_call | solution.py:124
  130.2 0.6 collective-permute-start.21
  130.7 1.6 shard_map.268.early_in
  132.4 3.9 %shard_map.272 = (bf16[896,256]{1,0:T(8,128)(2,1)}, bf16[896,256]{1,0:T(8,128)(2,1)}, bf16[896,256]{1,0:T(8,128)(2,1)}, bf16[896,256]{1,0:T(8,128)(2,1)}) custom-call(s32[1]{0:T(128)} %bitcast.1.place_ref, bf16[4,256,256]{2,1,0:T(8,128)(2,1)} %shard_map.268.early_in, bf16[4,4,544,256]{3,2,1,0:T(8,128)(2,1)} %all-to-all-done.2.b_in), custom_call_target="tpu_custom_call" | custom-call | bytes 6000000 | tf_op jit(solution)/shard_map/pallas_call | solution.py:124
  136.3 1.8 %collective-permute-start.17 = (bf16[896,256]{1,0:T(8,128)(2,1)}, bf16[896,256]{1,0:T(8,128)(2,1)S(1)}, u32[]{:S(2)}, u32[]{:S(2)}) collective-permute-start(bf16[896,256]{1,0:T(8,128)(2,1)} %get-tuple-element.119), channel_id=1, source_target_pairs={{0,2},{2,4},{4,6},{6,0},{1,3},{3,5},{5,7},{7,1},{8,10},{10,12},{12... | collective-permute-start | bytes 1376264 | tf_op jit(solution)/shard_map/ppermute | solution.py:63
  138.1 1.3 collective-permute-start.18
  139.4 1.7 collective-permute-start.19
  141.0 4.6 %collective-permute-done.17.r1 = bf16[896,256]{1,0:T(8,128)(2,1)S(1)} collective-permute-done((bf16[896,256]{1,0:T(8,128)(2,1)}, bf16[896,256]{1,0:T(8,128)(2,1)S(1)}, u32[]{:S(2)}, u32[]{:S(2)}) %collective-permute-start.17) | collective-permute-done | bytes 458784 | tf_op jit(solution)/shard_map/ppermute | solution.py:63
  145.7 0.2 collective-permute-done.18.r2
  145.9 5.8 %collective-permute-done.19.r3 = bf16[896,256]{1,0:T(8,128)(2,1)S(1)} collective-permute-done((bf16[896,256]{1,0:T(8,128)(2,1)}, bf16[896,256]{1,0:T(8,128)(2,1)S(1)}, u32[]{:S(2)}, u32[]{:S(2)}) %collective-permute-start.19) | collective-permute-done | bytes 458784 | tf_op jit(solution)/shard_map/ppermute | solution.py:63
  151.8 1.0 copy-done.5
  152.8 2.5 %shard_map.273 = (bf16[8,8,2816]{2,1,0:T(8,128)(2,1)}, f32[40,1024]{1,0:T(8,128)}, bf16[40,1024]{1,0:T(8,128)(2,1)}) custom-call(s32[1]{0:T(128)} %bitcast.far_ref, bf16[896,256]{1,0:T(8,128)(2,1)S(1)} %copy-done.5, bf16[896,256]{1,0:T(8,128)(2,1)S(1)} %collective-permute-done.17.r1, bf16[896,256]{1,0:T(8,128)(2,1)S(1)} %collective-permute-done.18.r2, ...), custom_call_target="tpu_custom_call" | custom-call | bytes 4000000 | tf_op jit(solution)/shard_map/pallas_call | solution.py:124
  155.2 7.7 %all-to-all-start.3 = ((bf16[8,8,2816]{2,1,0:T(8,128)(2,1)}), bf16[8,8,2816]{2,1,0:T(8,128)(2,1)S(1)}, u32[]{:S(2)}, u32[]{:S(2)}) async-start(bf16[8,8,2816]{2,1,0:T(8,128)(2,1)} %get-tuple-element.122), calls=%async_computation.3 | async-start | bytes 720896 | tf_op jit(solution)/shard_map/all_to_all | solution.py:78
  163.0 2.9 %collective-permute-start.20 = (bf16[40,1024]{1,0:T(8,128)(2,1)}, bf16[40,1024]{1,0:T(8,128)(2,1)S(1)}, u32[]{:S(2)}, u32[]{:S(2)}) collective-permute-start(bf16[40,1024]{1,0:T(8,128)(2,1)} %get-tuple-element.123), channel_id=1, source_target_pairs={{0,1},{1,0},{2,3},{3,2},{4,5},{5,4},{6,7},{7,6},{8,9},{9,8},{10,11... | collective-permute-start | bytes 245768 | tf_op jit(solution)/shard_map/ppermute | solution.py:90
  165.8 1.0 copy-done.14
  166.8 4.6 %shard_map.274 = (bf16[256,1024]{1,0:T(8,128)(2,1)}, f32[256,1024]{1,0:T(8,128)}) custom-call(s32[1,8]{1,0:T(1,128)S(1)} %copy-done.7, bf16[256,1024]{1,0:T(8,128)(2,1)} %x_ref.1, bf16[256,1024]{1,0:T(8,128)(2,1)} %cot_ref.1, f32[1,2,256,1024]{3,2,1,0:T(8,128)} %get-tuple-element.124.kept_ref, bf16[1,2,256,1024]{3,2,1,0:T(8,128)(2,1)} %copy-done.14, ...), custom_call_target="tpu_custom_call" | custom-call | bytes 6000000 | tf_op jit(solution)/shard_map/pallas_call | solution.py:1068
  171.5 1.0 collective-permute-done.20.got_ref
  172.4 0.6 shard_map.275
  173.1 0.6 copy.35
  173.7 0.7 copy.30
  174.3 0.7 copy.32
  175.0 0.7 copy.33
  (40 shorter events, 0.2 us)
Async XLA Ops:
  0.6 6.6 %collective-permute-start = (bf16[256,1024]{1,0:T(8,128)(2,1)}, bf16[256,1024]{1,0:T(8,128)(2,1)S(1)}, u32[]{:S(2)}, u32[]{:S(2)}) collective-permute-start(bf16[256,1024]{1,0:T(8,128)(2,1)} %x_ref.1), channel_id=1, source_target_pairs={{0,32},{32,0},{64,96},{96,64},{1,33},{33,1},{65,97},{97,65},{2,34}... | collective-permute-start | bytes 1572872 | tf_op jit(solution)/shard_map/ppermute | solution.py:82
  2.1 5.9 %collective-permute-start.1 = (bf16[256,1024]{1,0:T(8,128)(2,1)}, bf16[256,1024]{1,0:T(8,128)(2,1)S(1)}, u32[]{:S(2)}, u32[]{:S(2)}) collective-permute-start(bf16[256,1024]{1,0:T(8,128)(2,1)} %cot_ref.1), channel_id=1, source_target_pairs={{0,32},{32,0},{64,96},{96,64},{1,33},{33,1},{65,97},{97,65},{2,34}... | collective-permute-start | bytes 1572872 | tf_op jit(solution)/shard_map/ppermute | solution.py:82
  7.2 0.8 copy-start.8
  8.0 19.0 %copy-start.10 = (bf16[256,1024]{1,0:T(8,128)(2,1)}, bf16[256,1024]{1,0:T(8,128)(2,1)S(1)}, u32[]{:S(2)}) copy-start(bf16[256,1024]{1,0:T(8,128)(2,1)S(1)} %collective-permute-done.1.c2) | copy-start | bytes 1572868
  8.0 14.1 %all-to-all-start = ((bf16[8,8,1920]{2,1,0:T(8,128)(2,1)}), bf16[8,8,1920]{2,1,0:T(8,128)(2,1)S(1)}, u32[]{:S(2)}, u32[]{:S(2)}) async-start(bf16[8,8,1920]{2,1,0:T(8,128)(2,1)} %get-tuple-element.80), calls=%async_computation | async-start | bytes 491520 | tf_op jit(solution)/shard_map/all_to_all | solution.py:78
  13.8 8.2 %collective-permute-start.2 = (bf16[40,1024]{1,0:T(8,128)(2,1)S(1)}, bf16[40,1024]{1,0:T(8,128)(2,1)S(1)}, u32[]{:S(2)}, u32[]{:S(2)}) collective-permute-start(bf16[40,1024]{1,0:T(8,128)(2,1)S(1)} %get-tuple-element.81.mine_ref), channel_id=1, source_target_pairs={{0,1},{1,0},{2,3},{3,2},{4,5},{5,4},{6,7},{7,6},{8,9},{9,8},{10,11... | collective-permute-start | bytes 245768 | tf_op jit(solution)/shard_map/ppermute | solution.py:90
  22.6 15.4 %collective-permute-start.6 = (bf16[256,1024]{1,0:T(8,128)(2,1)}, bf16[256,1024]{1,0:T(8,128)(2,1)}, u32[]{:S(2)}, u32[]{:S(2)}) collective-permute-start(bf16[256,1024]{1,0:T(8,128)(2,1)} %x_ref.1), channel_id=1, source_target_pairs={{0,64},{64,0},{32,96},{96,32},{1,65},{65,1},{33,97},{97,33},{2,66}... | collective-permute-start | bytes 1572872 | tf_op jit(solution)/shard_map/ppermute | solution.py:86
  22.9 23.8 %collective-permute-start.8 = (bf16[256,1024]{1,0:T(8,128)(2,1)}, bf16[256,1024]{1,0:T(8,128)(2,1)}, u32[]{:S(2)}, u32[]{:S(2)}) collective-permute-start(bf16[256,1024]{1,0:T(8,128)(2,1)} %cot_ref.1), channel_id=1, source_target_pairs={{0,64},{64,0},{32,96},{96,32},{1,65},{65,1},{33,97},{97,33},{2,66}... | collective-permute-start | bytes 1572872 | tf_op jit(solution)/shard_map/ppermute | solution.py:86
  24.1 8.8 %collective-permute-start.5 = (bf16[832,256]{1,0:T(8,128)(2,1)S(1)}, bf16[832,256]{1,0:T(8,128)(2,1)S(1)}, u32[]{:S(2)}, u32[]{:S(2)}) collective-permute-start(bf16[832,256]{1,0:T(8,128)(2,1)S(1)} %get-tuple-element.86.b0), channel_id=1, source_target_pairs={{0,4},{2,6},{4,0},{6,2},{1,5},{3,7},{5,1},{7,3},{8,12},{10,14},{12... | collective-permute-start | bytes 1277960 | tf_op jit(solution)/shard_map/ppermute | solution.py:63
  27.0 10.9 %collective-permute-start.4 = (bf16[832,256]{1,0:T(8,128)(2,1)S(1)}, bf16[832,256]{1,0:T(8,128)(2,1)S(1)}, u32[]{:S(2)}, u32[]{:S(2)}) collective-permute-start(bf16[832,256]{1,0:T(8,128)(2,1)S(1)} %get-tuple-element.86.b0), channel_id=1, source_target_pairs={{0,6},{2,0},{4,2},{6,4},{1,7},{3,1},{5,3},{7,5},{8,14},{10,8},{12,... | collective-permute-start | bytes 1277960 | tf_op jit(solution)/shard_map/ppermute | solution.py:63
  27.8 10.1 %collective-permute-start.3 = (bf16[832,256]{1,0:T(8,128)(2,1)S(1)}, bf16[832,256]{1,0:T(8,128)(2,1)S(1)}, u32[]{:S(2)}, u32[]{:S(2)}) collective-permute-start(bf16[832,256]{1,0:T(8,128)(2,1)S(1)} %get-tuple-element.86.b0), channel_id=1, source_target_pairs={{0,2},{2,4},{4,6},{6,0},{1,3},{3,5},{5,7},{7,1},{8,10},{10,12},{12... | collective-permute-start | bytes 1277960 | tf_op jit(solution)/shard_map/ppermute | solution.py:63
  37.9 17.5 %copy-start.3 = (bf16[256,1024]{1,0:T(8,128)(2,1)S(1)}, bf16[256,1024]{1,0:T(8,128)(2,1)}, u32[]{:S(2)}) copy-start(bf16[256,1024]{1,0:T(8,128)(2,1)} %x_ref.1) | copy-start | bytes 1572868
  37.9 17.5 %copy-start.4 = (bf16[256,1024]{1,0:T(8,128)(2,1)S(1)}, bf16[256,1024]{1,0:T(8,128)(2,1)}, u32[]{:S(2)}) copy-start(bf16[256,1024]{1,0:T(8,128)(2,1)} %cot_ref.1) | copy-start | bytes 1572868
  38.9 16.6 %copy-start.1 = (bf16[1088,256]{1,0:T(8,128)(2,1)S(1)}, bf16[1088,256]{1,0:T(8,128)(2,1)}, u32[]{:S(2)}) copy-start(bf16[1088,256]{1,0:T(8,128)(2,1)} %shard_map.266.w0.a0) | copy-start | bytes 1671172
  38.9 15.2 %collective-permute-start.12 = (bf16[1088,256]{1,0:T(8,128)(2,1)}, bf16[1088,256]{1,0:T(8,128)(2,1)}, u32[]{:S(2)}, u32[]{:S(2)}) collective-permute-start(bf16[1088,256]{1,0:T(8,128)(2,1)} %shard_map.266.w0.a0), channel_id=1, source_target_pairs={{0,16},{8,24},{16,0},{24,8},{1,17},{9,25},{17,1},{25,9},{2,18},{10... | collective-permute-start | bytes 1671176 | tf_op jit(solution)/shard_map/ppermute | solution.py:63
  41.6 13.9 %collective-permute-start.11 = (bf16[1088,256]{1,0:T(8,128)(2,1)}, bf16[1088,256]{1,0:T(8,128)(2,1)}, u32[]{:S(2)}, u32[]{:S(2)}) collective-permute-start(bf16[1088,256]{1,0:T(8,128)(2,1)} %shard_map.266.w0.a0), channel_id=1, source_target_pairs={{0,24},{8,0},{16,8},{24,16},{1,25},{9,1},{17,9},{25,17},{2,26},{10... | collective-permute-start | bytes 1671176 | tf_op jit(solution)/shard_map/ppermute | solution.py:63
  42.5 13.0 %collective-permute-start.10 = (bf16[1088,256]{1,0:T(8,128)(2,1)}, bf16[1088,256]{1,0:T(8,128)(2,1)}, u32[]{:S(2)}, u32[]{:S(2)}) collective-permute-start(bf16[1088,256]{1,0:T(8,128)(2,1)} %shard_map.266.w0.a0), channel_id=1, source_target_pairs={{0,8},{8,16},{16,24},{24,0},{1,9},{9,17},{17,25},{25,1},{2,10},{10... | collective-permute-start | bytes 1671176 | tf_op jit(solution)/shard_map/ppermute | solution.py:63
  43.1 6.6 %collective-permute-start.7 = (bf16[256,1024]{1,0:T(8,128)(2,1)}, bf16[256,1024]{1,0:T(8,128)(2,1)}, u32[]{:S(2)}, u32[]{:S(2)}) collective-permute-start(bf16[256,1024]{1,0:T(8,128)(2,1)} %collective-permute-done.6.x1), channel_id=1, source_target_pairs={{0,32},{32,0},{64,96},{96,64},{1,33},{33,1},{65,97},{97,65},{2,34}... | collective-permute-start | bytes 1572872 | tf_op jit(solution)/shard_map/ppermute | solution.py:82
  46.8 3.7 %collective-permute-start.9 = (bf16[256,1024]{1,0:T(8,128)(2,1)}, bf16[256,1024]{1,0:T(8,128)(2,1)}, u32[]{:S(2)}, u32[]{:S(2)}) collective-permute-start(bf16[256,1024]{1,0:T(8,128)(2,1)} %collective-permute-done.8.c1), channel_id=1, source_target_pairs={{0,32},{32,0},{64,96},{96,64},{1,33},{33,1},{65,97},{97,65},{2,34}... | collective-permute-start | bytes 1572872 | tf_op jit(solution)/shard_map/ppermute | solution.py:82
  48.5 6.9 %copy-start.9 = (bf16[256,1024]{1,0:T(8,128)(2,1)S(1)}, bf16[256,1024]{1,0:T(8,128)(2,1)}, u32[]{:S(2)}) copy-start(bf16[256,1024]{1,0:T(8,128)(2,1)} %copy-done.8) | copy-start | bytes 1572868
  48.5 7.0 %copy-start.11 = (bf16[256,1024]{1,0:T(8,128)(2,1)S(1)}, bf16[256,1024]{1,0:T(8,128)(2,1)}, u32[]{:S(2)}) copy-start(bf16[256,1024]{1,0:T(8,128)(2,1)} %copy-done.10) | copy-start | bytes 1572868
  50.4 29.0 %collective-permute-start.15 = (bf16[2048,256]{1,0:T(8,128)(2,1)}, bf16[2048,256]{1,0:T(8,128)(2,1)}, u32[]{:S(2)}, u32[]{:S(2)}) collective-permute-start(bf16[2048,256]{1,0:T(8,128)(2,1)} %shard_map.265.w0.b0), channel_id=1, source_target_pairs={{0,16},{8,24},{16,0},{24,8},{1,17},{9,25},{17,1},{25,9},{2,18},{10... | collective-permute-start | bytes 3145736 | tf_op jit(solution)/shard_map/ppermute | solution.py:63
  53.1 26.3 %collective-permute-start.14 = (bf16[2048,256]{1,0:T(8,128)(2,1)}, bf16[2048,256]{1,0:T(8,128)(2,1)}, u32[]{:S(2)}, u32[]{:S(2)}) collective-permute-start(bf16[2048,256]{1,0:T(8,128)(2,1)} %shard_map.265.w0.b0), channel_id=1, source_target_pairs={{0,24},{8,0},{16,8},{24,16},{1,25},{9,1},{17,9},{25,17},{2,26},{10... | collective-permute-start | bytes 3145736 | tf_op jit(solution)/shard_map/ppermute | solution.py:63
  54.0 25.4 %collective-permute-start.13 = (bf16[2048,256]{1,0:T(8,128)(2,1)}, bf16[2048,256]{1,0:T(8,128)(2,1)}, u32[]{:S(2)}, u32[]{:S(2)}) collective-permute-start(bf16[2048,256]{1,0:T(8,128)(2,1)} %shard_map.265.w0.b0), channel_id=1, source_target_pairs={{0,8},{8,16},{16,24},{24,0},{1,9},{9,17},{17,25},{25,1},{2,10},{10... | collective-permute-start | bytes 3145736 | tf_op jit(solution)/shard_map/ppermute | solution.py:63
  75.4 4.1 %copy-start = (bf16[2048,256]{1,0:T(8,128)(2,1)S(1)}, bf16[2048,256]{1,0:T(8,128)(2,1)}, u32[]{:S(2)}) copy-start(bf16[2048,256]{1,0:T(8,128)(2,1)} %shard_map.265.w0.b0) | copy-start | bytes 3145732
  75.4 23.6 %all-to-all-start.1 = ((bf16[4,4,256,256]{3,2,1,0:T(8,128)(2,1)}), bf16[4,4,256,256]{3,2,1,0:T(8,128)(2,1)S(1)}, u32[]{:S(2)}, u32[]{:S(2)}) async-start(bf16[4,4,256,256]{3,2,1,0:T(8,128)(2,1)} %get-tuple-element.102), calls=%async_computation.1 | async-start | bytes 4194304 | tf_op jit(solution)/shard_map/all_to_all | solution.py:78
  99.1 33.3 %all-to-all-start.2 = ((bf16[4,4,544,256]{3,2,1,0:T(8,128)(2,1)}), bf16[4,4,544,256]{3,2,1,0:T(8,128)(2,1)}, u32[]{:S(2)}, u32[]{:S(2)}) async-start(bf16[4,4,544,256]{3,2,1,0:T(8,128)(2,1)} %get-tuple-element.117), calls=%async_computation.2 | async-start | bytes 8912896 | tf_op jit(solution)/shard_map/all_to_all | solution.py:78
  104.0 1.1 copy-start.2
  105.1 1.4 copy-start.12
  106.5 1.0 copy-start.13
  119.9 7.3 %collective-permute-start.16 = (bf16[2,2,256,1024]{3,2,1,0:T(8,128)(2,1)}, bf16[2,2,256,1024]{3,2,1,0:T(8,128)(2,1)S(1)}, u32[]{:S(2)}, u32[]{:S(2)}) collective-permute-start(bf16[2,2,256,1024]{3,2,1,0:T(8,128)(2,1)} %get-tuple-element.114), channel_id=1, source_target_pairs={{0,32},{32,0},{64,96},{96,64},{1,33},{33,1},{65,97},{97,65},{2,34}... | collective-permute-start | bytes 6291464 | tf_op jit(solution)/shard_map/ppermute | solution.py:82
  130.2 35.7 %collective-permute-start.21 = (bf16[1,2,256,1024]{3,2,1,0:T(8,128)(2,1)}, bf16[1,2,256,1024]{3,2,1,0:T(8,128)(2,1)S(1)}, u32[]{:S(2)}, u32[]{:S(2)}) collective-permute-start(bf16[1,2,256,1024]{3,2,1,0:T(8,128)(2,1)} %get-tuple-element.115), channel_id=1, source_target_pairs={{0,64},{64,0},{32,96},{96,32},{1,65},{65,1},{33,97},{97,33},{2,66}... | collective-permute-start | bytes 3145736 | tf_op jit(solution)/shard_map/ppermute | solution.py:86
  136.3 30.5 %copy-start.7 = (s32[1,8]{1,0:T(1,128)S(1)}, s32[1,8]{1,0:T(1,128)}, u32[]{:S(2)}) copy-start(s32[1,8]{1,0:T(1,128)} %len_ref.1) | copy-start | bytes 100
  136.3 9.4 %collective-permute-start.17 = (bf16[896,256]{1,0:T(8,128)(2,1)}, bf16[896,256]{1,0:T(8,128)(2,1)S(1)}, u32[]{:S(2)}, u32[]{:S(2)}) collective-permute-start(bf16[896,256]{1,0:T(8,128)(2,1)} %get-tuple-element.119), channel_id=1, source_target_pairs={{0,2},{2,4},{4,6},{6,0},{1,3},{3,5},{5,7},{7,1},{8,10},{10,12},{12... | collective-permute-start | bytes 1376264 | tf_op jit(solution)/shard_map/ppermute | solution.py:63
  138.1 7.8 %collective-permute-start.18 = (bf16[896,256]{1,0:T(8,128)(2,1)}, bf16[896,256]{1,0:T(8,128)(2,1)S(1)}, u32[]{:S(2)}, u32[]{:S(2)}) collective-permute-start(bf16[896,256]{1,0:T(8,128)(2,1)} %get-tuple-element.120), channel_id=1, source_target_pairs={{0,6},{2,0},{4,2},{6,4},{1,7},{3,1},{5,3},{7,5},{8,14},{10,8},{12,... | collective-permute-start | bytes 1376264 | tf_op jit(solution)/shard_map/ppermute | solution.py:63
  139.4 12.4 %collective-permute-start.19 = (bf16[896,256]{1,0:T(8,128)(2,1)}, bf16[896,256]{1,0:T(8,128)(2,1)S(1)}, u32[]{:S(2)}, u32[]{:S(2)}) collective-permute-start(bf16[896,256]{1,0:T(8,128)(2,1)} %get-tuple-element.121), channel_id=1, source_target_pairs={{0,4},{2,6},{4,0},{6,2},{1,5},{3,7},{5,1},{7,3},{8,12},{10,14},{12... | collective-permute-start | bytes 1376264 | tf_op jit(solution)/shard_map/ppermute | solution.py:63
  151.8 1.0 copy-start.5
  155.2 17.2 %all-to-all-start.3 = ((bf16[8,8,2816]{2,1,0:T(8,128)(2,1)}), bf16[8,8,2816]{2,1,0:T(8,128)(2,1)S(1)}, u32[]{:S(2)}, u32[]{:S(2)}) async-start(bf16[8,8,2816]{2,1,0:T(8,128)(2,1)} %get-tuple-element.122), calls=%async_computation.3 | async-start | bytes 720896 | tf_op jit(solution)/shard_map/all_to_all | solution.py:78
  163.0 9.5 %collective-permute-start.20 = (bf16[40,1024]{1,0:T(8,128)(2,1)}, bf16[40,1024]{1,0:T(8,128)(2,1)S(1)}, u32[]{:S(2)}, u32[]{:S(2)}) collective-permute-start(bf16[40,1024]{1,0:T(8,128)(2,1)} %get-tuple-element.123), channel_id=1, source_target_pairs={{0,1},{1,0},{2,3},{3,2},{4,5},{5,4},{6,7},{7,6},{8,9},{9,8},{10,11... | collective-permute-start | bytes 245768 | tf_op jit(solution)/shard_map/ppermute | solution.py:90
  165.8 1.0 copy-start.14
  166.8 5.6 %copy-start.6 = (f32[40,1024]{1,0:T(8,128)S(1)}, f32[40,1024]{1,0:T(8,128)}, u32[]{:S(2)}) copy-start(f32[40,1024]{1,0:T(8,128)} %get-tuple-element.130.keep_ref) | copy-start | bytes 491524

commit v6 on v5

--- a/solution.py
+++ b/solution.py
@@ -1178,18 +1178,9 @@
     ] + [16 + 3 * d + i for i in range(3)]
 
 
-def part_kernel(
-    far_ref, r0, r1, r2, r3, slots_ref, keep_ref, send_ref, total_ref, rows_ref, in_ref, sem
-):
+def part_kernel(far_ref, r0, r1, r2, r3, slots_ref, keep_ref, send_ref, total_ref, rows_ref):
     far = far_ref[0]
-    loads = [
-        pltpu.make_async_copy(r, in_ref.at[i], sem.at[i]) for i, r in enumerate((r0, r1, r2, r3))
-    ]
-    for load in loads:
-        load.start()
-    for load in loads:
-        load.wait()
-    total_ref[...] = sum([in_ref[i].astype(f32) for i in range(4)])
+    total_ref[...] = sum([ref[...].astype(f32) for ref in (r0, r1, r2, r3)])
     rows_ref[...] = jnp.zeros_like(rows_ref)
     for d in range(4):
         for i, row in enumerate(image_rows(d)):
@@ -1226,20 +1217,17 @@
         [shaped(8, 8, LAST), shaped(40, D, dtype=f32), shaped(40, D)],
         far,
         *received,
-        places="saaaa",
         outs="uuu",
-        scratch=[
-            pltpu.VMEM((768 + 2 * IMAGE, 256), f32),
-            pltpu.VMEM((4, 16, 256), f32),
-            pltpu.VMEM((4, 768 + 2 * IMAGE, 256), bf16),
-            pltpu.SemaphoreType.DMA((4,)),
-        ],
+        scratch=[pltpu.VMEM((768 + 2 * IMAGE, 256), f32), pltpu.VMEM((4, 16, 256), f32)],
         nbytes=4e6,
     )
 
 
-def finish_kernel(place_ref, slots_ref, keep_ref, got_ref, qkv_ref, up_ref, dense_ref, down_ref, *rest):
-    tiny_refs, image_ref = rest[:8], rest[8]
+def finish_kernel(
+    place_ref, slots_ref, keep_ref, got_ref, qkv_out, up_out, dense_out, down_out, *rest
+):
+    tiny_refs = rest[:8]
+    image_ref, qkv_ref, up_ref, dense_ref, down_ref, sem = rest[8:]
     image = [jnp.zeros((8, 256), f32)] * 2
     for s in range(8):
         for n in range(4):
@@ -1247,17 +1235,31 @@
             image[n % 2] = image[n % 2] + slots_ref[s, :, at : at + 256].astype(f32)
     image_ref[0:8, :] = image[0]
     image_ref[8:16, :] = image[1]
+    def rows_out(ref, out, first):
+        width = ref.shape[2]
+        copies = [
+            pltpu.make_async_copy(
+                ref.at[r, 0], out.at[pl.ds(r * width, width)], sem.at[first + r]
+            )
+            for r in range(ref.shape[0])
+        ]
+        for copy in copies:
+            copy.start()
+        return copies
+
+    total = keep_ref[...] + got_ref[...].astype(f32)
+    dense_ref[:, 0, :] = total[32:40]
+    down_ref[:, 0, :] = total[0:32]
+    copies = rows_out(dense_ref, dense_out, 0) + rows_out(down_ref, down_out, 8)
     for d in range(4):
         both = slots_ref[2 * d, :, 0 : QC + HC].astype(f32) + slots_ref[
             2 * d + 1, :, 0 : QC + HC
         ].astype(f32)
         for p in range(3):
             at = p * D + d * 256
-            qkv_ref[:, at : at + 256] = both[:, p * 256 : (p + 1) * 256]
-        up_ref[:, d * HC : (d + 1) * HC] = both[:, QC:]
-    total = keep_ref[...] + got_ref[...].astype(f32)
-    dense_ref[...] = total[32:40]
-    down_ref[...] = total[0:32]
+            qkv_ref[:, 0, at : at + 256] = both[:, p * 256 : (p + 1) * 256]
+        up_ref[:, 0, d * HC : (d + 1) * HC] = both[:, QC:]
+    copies += rows_out(qkv_ref, qkv_out, 40) + rows_out(up_ref, up_out, 48)
     p = place_ref[0]
     f = p % 32
     lines = (0, 1, 2, 3, 10 + f * 24 // 256, 4, 6 + f // 8, 5)
@@ -1267,23 +1269,33 @@
         if size == 24:
             values = jnp.concatenate([values, image_ref[pl.ds(line + 1, 1), :]], axis=1)
         ref[...] = pltpu.roll(values, values.shape[1] - lane, 1)[:, :size]
+    for copy in copies:
+        copy.wait()
 
 
 def finish(place, slots, keep, got):
     return call(
         finish_kernel,
         [
-            shaped(8, 3 * D, dtype=f32),
-            shaped(8, FF, dtype=f32),
-            shaped(8, D, dtype=f32),
-            shaped(32, D, dtype=f32),
+            shaped(8 * 3 * D, dtype=f32),
+            shaped(8 * FF, dtype=f32),
+            shaped(8 * D, dtype=f32),
+            shaped(32 * D, dtype=f32),
         ]
         + [shaped(1, size, dtype=f32) for size in SIZES],
         place,
         slots,
         keep,
         got,
-        scratch=[pltpu.VMEM((16, 256), f32)],
+        outs="hhhh" + "v" * 8,
+        scratch=[
+            pltpu.VMEM((16, 256), f32),
+            pltpu.VMEM((8, 1, 3 * D), f32),
+            pltpu.VMEM((8, 1, FF), f32),
+            pltpu.VMEM((8, 1, D), f32),
+            pltpu.VMEM((32, 1, D), f32),
+            pltpu.SemaphoreType.DMA((56,)),
+        ],
         nbytes=2e6,
     )
 

time: 177 us -> 174 us (0.983)
  local copies, waits for them, and re-layouts: 12.3 us -> 9.64 us
    unnamed x34 -> x30, local copies, waits for them, and re-layouts: 8.97 us -> 6.33 us
where the time goes in v6:
time: 174 us; the launch traced here: 173 us
  Pallas kernels  72.2 us (41%)
  starting transfers between devices  57.6 us (33%)
  waiting for transfers between devices  32.8 us (19%)
  local copies, waits for them, and re-layouts  9.64 us (6%)
    pallas_call x11, Pallas kernels, call(): pl.pallas_call(kernel, in_specs=[SPECS[p] for p in places], out_specs=out...  65.9 us
    all_to_all x4, starting transfers between devices, a2a(): lax.all_to_all(values, AXES, 0, 0, tiled=True, axis_index_groups=groups)  22.5 us
    ppermute x12, waiting for transfers between devices, ring(): return lax.ppermute(values, AXES, pairs)  21 us
    ppermute x12, starting transfers between devices, ring(): return lax.ppermute(values, AXES, pairs)  17.5 us
    ppermute x5, starting transfers between devices, flip_core(): return lax.ppermute(values, 'dp', [(0, 1), (1, 0), (2, 3), (3, 2)])  9.61 us
    unnamed x30, local copies, waits for them, and re-layouts  6.33 us
    ppermute x2, waiting for transfers between devices, flip_far(): return lax.ppermute(values, 'fsdp', [(i, i ^ 1) for i in range(32)])  6.32 us
    ppermute x2, starting transfers between devices, flip_far(): return lax.ppermute(values, 'fsdp', [(i, i ^ 1) for i in range(32)])  5.77 us
  transfers between devices with their start and end apart: 26, of which 11 were waited for; matrix products, arithmetic and copies ran while one was open for 2% of the time, Pallas kernels for 40%

profile of v6, /device:TPU:1, one launch (start us, length us, event | category | flops | bytes accessed | tf_op | source)
XLA Modules:
  0.0 173.3 jit_solution(17308671501646553545)
XLA Ops:
  0.6 1.5 collective-permute-start
  2.1 0.1 collective-permute-start.1
  2.2 0.7 reshape.69.dense_in
  3.0 0.8 reshape.67.qkv_ref
  3.8 0.9 reshape.68.up_ref
  4.7 0.9 reshape.70.down_in
  5.6 1.6 shard_map.263
  7.2 0.0 copy-start.8
  7.2 0.8 copy-done.8
  8.0 5.8 %all-to-all-start = ((bf16[8,8,1920]{2,1,0:T(8,128)(2,1)}), bf16[8,8,1920]{2,1,0:T(8,128)(2,1)S(1)}, u32[]{:S(2)}, u32[]{:S(2)}) async-start(bf16[8,8,1920]{2,1,0:T(8,128)(2,1)} %get-tuple-element.80), calls=%async_computation | async-start | bytes 491520 | tf_op jit(solution)/shard_map/all_to_all | solution.py:78
  13.8 2.9 %collective-permute-start.2 = (bf16[40,1024]{1,0:T(8,128)(2,1)S(1)}, bf16[40,1024]{1,0:T(8,128)(2,1)S(1)}, u32[]{:S(2)}, u32[]{:S(2)}) collective-permute-start(bf16[40,1024]{1,0:T(8,128)(2,1)S(1)} %get-tuple-element.81.mine_ref), channel_id=1, source_target_pairs={{0,1},{1,0},{2,3},{3,2},{4,5},{5,4},{6,7},{7,6},{8,9},{9,8},{10,11... | collective-permute-start | bytes 245768 | tf_op jit(solution)/shard_map/ppermute | solution.py:90
  16.7 5.4 %collective-permute-done.2.theirs_ref = bf16[40,1024]{1,0:T(8,128)(2,1)S(1)} collective-permute-done((bf16[40,1024]{1,0:T(8,128)(2,1)S(1)}, bf16[40,1024]{1,0:T(8,128)(2,1)S(1)}, u32[]{:S(2)}, u32[]{:S(2)}) %collective-permute-start.2) | collective-permute-done | bytes 81952 | tf_op jit(solution)/shard_map/ppermute | solution.py:90
  22.1 0.5 shard_map.264
  22.6 0.4 collective-permute-start.6
  22.9 1.2 collective-permute-start.8
  24.1 2.9 %collective-permute-start.5 = (bf16[832,256]{1,0:T(8,128)(2,1)S(1)}, bf16[832,256]{1,0:T(8,128)(2,1)S(1)}, u32[]{:S(2)}, u32[]{:S(2)}) collective-permute-start(bf16[832,256]{1,0:T(8,128)(2,1)S(1)} %get-tuple-element.86.b0), channel_id=1, source_target_pairs={{0,4},{2,6},{4,0},{6,2},{1,5},{3,7},{5,1},{7,3},{8,12},{10,14},{12... | collective-permute-start | bytes 1277960 | tf_op jit(solution)/shard_map/ppermute | solution.py:63
  27.0 0.8 collective-permute-start.4
  27.8 0.7 collective-permute-start.3
  28.5 4.4 %collective-permute-done.5.b3 = bf16[832,256]{1,0:T(8,128)(2,1)S(1)} collective-permute-done((bf16[832,256]{1,0:T(8,128)(2,1)S(1)}, bf16[832,256]{1,0:T(8,128)(2,1)S(1)}, u32[]{:S(2)}, u32[]{:S(2)}) %collective-permute-start.5) | collective-permute-done | bytes 426016 | tf_op jit(solution)/shard_map/ppermute | solution.py:63
  32.9 5.1 %collective-permute-done.4.b2 = bf16[832,256]{1,0:T(8,128)(2,1)S(1)} collective-permute-done((bf16[832,256]{1,0:T(8,128)(2,1)S(1)}, bf16[832,256]{1,0:T(8,128)(2,1)S(1)}, u32[]{:S(2)}, u32[]{:S(2)}) %collective-permute-start.4) | collective-permute-done | bytes 426016 | tf_op jit(solution)/shard_map/ppermute | solution.py:63
  38.0 0.9 shard_map.266.w0.a0
  38.9 2.7 %collective-permute-start.12 = (bf16[1088,256]{1,0:T(8,128)(2,1)}, bf16[1088,256]{1,0:T(8,128)(2,1)}, u32[]{:S(2)}, u32[]{:S(2)}) collective-permute-start(bf16[1088,256]{1,0:T(8,128)(2,1)} %shard_map.266.w0.a0), channel_id=1, source_target_pairs={{0,16},{8,24},{16,0},{24,8},{1,17},{9,25},{17,1},{25,9},{2,18},{10... | collective-permute-start | bytes 1671176 | tf_op jit(solution)/shard_map/ppermute | solution.py:63
  41.6 0.9 collective-permute-start.11
  42.5 0.6 collective-permute-start.10
  43.1 2.9 %collective-permute-start.7 = (bf16[256,1024]{1,0:T(8,128)(2,1)}, bf16[256,1024]{1,0:T(8,128)(2,1)}, u32[]{:S(2)}, u32[]{:S(2)}) collective-permute-start(bf16[256,1024]{1,0:T(8,128)(2,1)} %collective-permute-done.6.x1), channel_id=1, source_target_pairs={{0,32},{32,0},{64,96},{96,64},{1,33},{33,1},{65,97},{97,65},{2,34}... | collective-permute-start | bytes 1572872 | tf_op jit(solution)/shard_map/ppermute | solution.py:82
  46.0 0.7 collective-permute-done.8.c1
  46.8 1.8 %collective-permute-start.9 = (bf16[256,1024]{1,0:T(8,128)(2,1)}, bf16[256,1024]{1,0:T(8,128)(2,1)}, u32[]{:S(2)}, u32[]{:S(2)}) collective-permute-start(bf16[256,1024]{1,0:T(8,128)(2,1)} %collective-permute-done.8.c1), channel_id=1, source_target_pairs={{0,32},{32,0},{64,96},{96,64},{1,33},{33,1},{65,97},{97,65},{2,34}... | collective-permute-start | bytes 1572872 | tf_op jit(solution)/shard_map/ppermute | solution.py:82
  48.5 0.1 pad_add_fusion.info_ref
  48.6 1.0 shard_map.265.w0.b0
  49.7 0.7 collective-permute-done.9.c3
  50.4 2.7 %collective-permute-start.15 = (bf16[2048,256]{1,0:T(8,128)(2,1)}, bf16[2048,256]{1,0:T(8,128)(2,1)}, u32[]{:S(2)}, u32[]{:S(2)}) collective-permute-start(bf16[2048,256]{1,0:T(8,128)(2,1)} %shard_map.265.w0.b0), channel_id=1, source_target_pairs={{0,16},{8,24},{16,0},{24,8},{1,17},{9,25},{17,1},{25,9},{2,18},{10... | collective-permute-start | bytes 3145736 | tf_op jit(solution)/shard_map/ppermute | solution.py:63
  53.1 0.9 collective-permute-start.14
  54.0 0.6 collective-permute-start.13
  54.6 0.8 collective-permute-done.11.w2.a2
  55.5 19.9 %shard_map.267 = (bf16[4,4,256,256]{3,2,1,0:T(8,128)(2,1)}, bf16[1024,1024]{1,0:T(8,128)(2,1)}, bf16[1024,256]{1,0:T(8,128)(2,1)}, bf16[1024,768]{1,0:T(8,128)(2...) custom-call(s32[67]{0:T(128)S(1)} %pad_add_fusion.info_ref, ...), custom_call_target="tpu_custom_call" | custom-call | flops 6000000000 | bytes 20000000 | tf_op jit(solution)/shard_map/pallas_call | solution.py:124
  75.4 4.0 %all-to-all-start.1 = ((bf16[4,4,256,256]{3,2,1,0:T(8,128)(2,1)}), bf16[4,4,256,256]{3,2,1,0:T(8,128)(2,1)S(1)}, u32[]{:S(2)}, u32[]{:S(2)}) async-start(bf16[4,4,256,256]{3,2,1,0:T(8,128)(2,1)} %get-tuple-element.102), calls=%async_computation.1 | async-start | bytes 4194304 | tf_op jit(solution)/shard_map/all_to_all | solution.py:78
  79.5 19.6 %shard_map.269 = (bf16[4,4,544,256]{3,2,1,0:T(8,128)(2,1)}, bf16[1024,1024]{1,0:T(8,128)(2,1)}, bf16[1024,1024]{1,0:T(8,128)(2,1)}) custom-call(s32[67]{0:T(128)S(1)} %pad_add_fusion.info_ref, bf16[2048,256]{1,0:T(8,128)(2,1)S(1)} %copy-done, bf16[2048,256]{1,0:T(8,128)(2,1)} %collective-permute-done.13.w1.b1, ...), custom_call_target="tpu_custom_call" | custom-call | flops 8999999488 | bytes 20000000 | tf_op jit(solution)/shard_map/pallas_call | solution.py:124
  99.1 5.0 %all-to-all-start.2 = ((bf16[4,4,544,256]{3,2,1,0:T(8,128)(2,1)}), bf16[4,4,544,256]{3,2,1,0:T(8,128)(2,1)}, u32[]{:S(2)}, u32[]{:S(2)}) async-start(bf16[4,4,544,256]{3,2,1,0:T(8,128)(2,1)} %get-tuple-element.117), calls=%async_computation.2 | async-start | bytes 8912896 | tf_op jit(solution)/shard_map/all_to_all | solution.py:78
  104.1 1.0 copy-done.2
  105.1 1.4 copy-done.12
  106.5 1.0 copy-done.13
  107.5 12.4 %shard_map.270 = (bf16[2,2,256,1024]{3,2,1,0:T(8,128)(2,1)}, bf16[2,2,256,1024]{3,2,1,0:T(8,128)(2,1)}) custom-call(s32[67]{0:T(128)S(1)} %pad_add_fusion.info_ref, bf16[1024,256]{1,0:T(8,128)(2,1)S(1)} %copy-done.13, bf16[1024,1024]{1,0:T(8,128)(2,1)} %get-tuple-element.110.hidden_in, bf16[1024,768]{1,0:T(8,128)(2,1)S(1)} %copy-done.12, ...), custom_call_target="tpu_custom_call" | custom-call | flops 6499999744 | bytes 16000000 | tf_op jit(solution)/shard_map/pallas_call | solution.py:124
  119.9 3.3 %collective-permute-start.16 = (bf16[2,2,256,1024]{3,2,1,0:T(8,128)(2,1)}, bf16[2,2,256,1024]{3,2,1,0:T(8,128)(2,1)S(1)}, u32[]{:S(2)}, u32[]{:S(2)}) collective-permute-start(bf16[2,2,256,1024]{3,2,1,0:T(8,128)(2,1)} %get-tuple-element.114), channel_id=1, source_target_pairs={{0,32},{32,0},{64,96},{96,64},{1,33},{33,1},{65,97},{97,65},{2,34}... | collective-permute-start | bytes 6291464 | tf_op jit(solution)/shard_map/ppermute | solution.py:82
  123.2 4.0 %collective-permute-done.16.got_in = bf16[2,2,256,1024]{3,2,1,0:T(8,128)(2,1)S(1)} collective-permute-done((bf16[2,2,256,1024]{3,2,1,0:T(8,128)(2,1)}, bf16[2,2,256,1024]{3,2,1,0:T(8,128)(2,1)S(1)}, u32[]{:S(2)}, u32[]{:S(2)}) %collective-permute-start.16) | collective-permute-done | bytes 2097184 | tf_op jit(solution)/shard_map/ppermute | solution.py:82
  127.2 2.9 %shard_map.271 = (f32[1,2,256,1024]{3,2,1,0:T(8,128)}, bf16[1,2,256,1024]{3,2,1,0:T(8,128)(2,1)}) custom-call(bf16[2,2,256,1024]{3,2,1,0:T(8,128)(2,1)} %get-tuple-element.113.mine_in, bf16[2,2,256,1024]{3,2,1,0:T(8,128)(2,1)S(1)} %collective-permute-done.16.got_in), custom_call_target="tpu_custom_call" | custom-call | bytes 8000000 | tf_op jit(solution)/shard_map/pallas_call | solution.py:124
  130.2 0.6 collective-permute-start.21
  130.7 1.6 shard_map.268.early_in
  132.4 0.0 all-to-all-done.2.b_in
  132.4 3.9 %shard_map.272 = (bf16[896,256]{1,0:T(8,128)(2,1)}, bf16[896,256]{1,0:T(8,128)(2,1)}, bf16[896,256]{1,0:T(8,128)(2,1)}, bf16[896,256]{1,0:T(8,128)(2,1)}) custom-call(s32[1]{0:T(128)} %bitcast.1.place_ref, bf16[4,256,256]{2,1,0:T(8,128)(2,1)} %shard_map.268.early_in, bf16[4,4,544,256]{3,2,1,0:T(8,128)(2,1)} %all-to-all-done.2.b_in), custom_call_target="tpu_custom_call" | custom-call | bytes 6000000 | tf_op jit(solution)/shard_map/pallas_call | solution.py:124
  136.3 0.0 copy-start.7
  136.3 1.8 %collective-permute-start.17 = (bf16[896,256]{1,0:T(8,128)(2,1)}, bf16[896,256]{1,0:T(8,128)(2,1)S(1)}, u32[]{:S(2)}, u32[]{:S(2)}) collective-permute-start(bf16[896,256]{1,0:T(8,128)(2,1)} %get-tuple-element.119), channel_id=1, source_target_pairs={{0,2},{2,4},{4,6},{6,0},{1,3},{3,5},{5,7},{7,1},{8,10},{10,12},{12... | collective-permute-start | bytes 1376264 | tf_op jit(solution)/shard_map/ppermute | solution.py:63
  138.1 1.3 collective-permute-start.18
  139.4 1.7 collective-permute-start.19
  141.0 4.6 %collective-permute-done.17.r1 = bf16[896,256]{1,0:T(8,128)(2,1)S(1)} collective-permute-done((bf16[896,256]{1,0:T(8,128)(2,1)}, bf16[896,256]{1,0:T(8,128)(2,1)S(1)}, u32[]{:S(2)}, u32[]{:S(2)}) %collective-permute-start.17) | collective-permute-done | bytes 458784 | tf_op jit(solution)/shard_map/ppermute | solution.py:63
  145.7 0.2 collective-permute-done.18.r2
  145.9 5.8 %collective-permute-done.19.r3 = bf16[896,256]{1,0:T(8,128)(2,1)S(1)} collective-permute-done((bf16[896,256]{1,0:T(8,128)(2,1)}, bf16[896,256]{1,0:T(8,128)(2,1)S(1)}, u32[]{:S(2)}, u32[]{:S(2)}) %collective-permute-start.19) | collective-permute-done | bytes 458784 | tf_op jit(solution)/shard_map/ppermute | solution.py:63
  151.7 1.0 copy-done.5
  152.8 1.3 shard_map.273
  154.0 7.7 %all-to-all-start.3 = ((bf16[8,8,2816]{2,1,0:T(8,128)(2,1)}), bf16[8,8,2816]{2,1,0:T(8,128)(2,1)S(1)}, u32[]{:S(2)}, u32[]{:S(2)}) async-start(bf16[8,8,2816]{2,1,0:T(8,128)(2,1)} %get-tuple-element.122), calls=%async_computation.3 | async-start | bytes 720896 | tf_op jit(solution)/shard_map/all_to_all | solution.py:78
  161.8 2.9 %collective-permute-start.20 = (bf16[40,1024]{1,0:T(8,128)(2,1)}, bf16[40,1024]{1,0:T(8,128)(2,1)S(1)}, u32[]{:S(2)}, u32[]{:S(2)}) collective-permute-start(bf16[40,1024]{1,0:T(8,128)(2,1)} %get-tuple-element.123), channel_id=1, source_target_pairs={{0,1},{1,0},{2,3},{3,2},{4,5},{5,4},{6,7},{7,6},{8,9},{9,8},{10,11... | collective-permute-start | bytes 245768 | tf_op jit(solution)/shard_map/ppermute | solution.py:90
  164.7 1.0 copy-done.14
  165.7 4.6 %shard_map.274 = (bf16[256,1024]{1,0:T(8,128)(2,1)}, f32[256,1024]{1,0:T(8,128)}) custom-call(s32[1,8]{1,0:T(1,128)S(1)} %copy-done.7, bf16[256,1024]{1,0:T(8,128)(2,1)} %x_ref.1, bf16[256,1024]{1,0:T(8,128)(2,1)} %cot_ref.1, f32[1,2,256,1024]{3,2,1,0:T(8,128)} %get-tuple-element.124.kept_ref, bf16[1,2,256,1024]{3,2,1,0:T(8,128)(2,1)} %copy-done.14, ...), custom_call_target="tpu_custom_call" | custom-call | bytes 6000000 | tf_op jit(solution)/shard_map/pallas_call | solution.py:1068
  170.3 1.0 collective-permute-done.20.got_ref
  171.2 1.9 %shard_map.275 = (f32[24576]{0:T(1024)}, f32[32768]{0:T(1024)}, f32[8192]{0:T(1024)}, f32[32768]{0:T(1024)}, f32[1,8]{1,0:T(1,128)}, /*index=5*/f32[1,8]{1,0:T(1...) custom-call(s32[1]{0:T(128)} %bitcast.15.place_ref, ...), custom_call_target="tpu_custom_call" | custom-call | bytes 2000000 | tf_op jit(solution)/shard_map/pallas_call | solution.py:124
  (36 shorter events, 0.1 us)
Async XLA Ops:
  0.6 6.6 %collective-permute-start = (bf16[256,1024]{1,0:T(8,128)(2,1)}, bf16[256,1024]{1,0:T(8,128)(2,1)S(1)}, u32[]{:S(2)}, u32[]{:S(2)}) collective-permute-start(bf16[256,1024]{1,0:T(8,128)(2,1)} %x_ref.1), channel_id=1, source_target_pairs={{0,32},{32,0},{64,96},{96,64},{1,33},{33,1},{65,97},{97,65},{2,34}... | collective-permute-start | bytes 1572872 | tf_op jit(solution)/shard_map/ppermute | solution.py:82
  2.1 5.9 %collective-permute-start.1 = (bf16[256,1024]{1,0:T(8,128)(2,1)}, bf16[256,1024]{1,0:T(8,128)(2,1)S(1)}, u32[]{:S(2)}, u32[]{:S(2)}) collective-permute-start(bf16[256,1024]{1,0:T(8,128)(2,1)} %cot_ref.1), channel_id=1, source_target_pairs={{0,32},{32,0},{64,96},{96,64},{1,33},{33,1},{65,97},{97,65},{2,34}... | collective-permute-start | bytes 1572872 | tf_op jit(solution)/shard_map/ppermute | solution.py:82
  7.2 0.8 copy-start.8
  8.0 19.0 %copy-start.10 = (bf16[256,1024]{1,0:T(8,128)(2,1)}, bf16[256,1024]{1,0:T(8,128)(2,1)S(1)}, u32[]{:S(2)}) copy-start(bf16[256,1024]{1,0:T(8,128)(2,1)S(1)} %collective-permute-done.1.c2) | copy-start | bytes 1572868
  8.0 14.1 %all-to-all-start = ((bf16[8,8,1920]{2,1,0:T(8,128)(2,1)}), bf16[8,8,1920]{2,1,0:T(8,128)(2,1)S(1)}, u32[]{:S(2)}, u32[]{:S(2)}) async-start(bf16[8,8,1920]{2,1,0:T(8,128)(2,1)} %get-tuple-element.80), calls=%async_computation | async-start | bytes 491520 | tf_op jit(solution)/shard_map/all_to_all | solution.py:78
  13.8 8.2 %collective-permute-start.2 = (bf16[40,1024]{1,0:T(8,128)(2,1)S(1)}, bf16[40,1024]{1,0:T(8,128)(2,1)S(1)}, u32[]{:S(2)}, u32[]{:S(2)}) collective-permute-start(bf16[40,1024]{1,0:T(8,128)(2,1)S(1)} %get-tuple-element.81.mine_ref), channel_id=1, source_target_pairs={{0,1},{1,0},{2,3},{3,2},{4,5},{5,4},{6,7},{7,6},{8,9},{9,8},{10,11... | collective-permute-start | bytes 245768 | tf_op jit(solution)/shard_map/ppermute | solution.py:90
  22.6 15.4 %collective-permute-start.6 = (bf16[256,1024]{1,0:T(8,128)(2,1)}, bf16[256,1024]{1,0:T(8,128)(2,1)}, u32[]{:S(2)}, u32[]{:S(2)}) collective-permute-start(bf16[256,1024]{1,0:T(8,128)(2,1)} %x_ref.1), channel_id=1, source_target_pairs={{0,64},{64,0},{32,96},{96,32},{1,65},{65,1},{33,97},{97,33},{2,66}... | collective-permute-start | bytes 1572872 | tf_op jit(solution)/shard_map/ppermute | solution.py:86
  22.9 23.8 %collective-permute-start.8 = (bf16[256,1024]{1,0:T(8,128)(2,1)}, bf16[256,1024]{1,0:T(8,128)(2,1)}, u32[]{:S(2)}, u32[]{:S(2)}) collective-permute-start(bf16[256,1024]{1,0:T(8,128)(2,1)} %cot_ref.1), channel_id=1, source_target_pairs={{0,64},{64,0},{32,96},{96,32},{1,65},{65,1},{33,97},{97,33},{2,66}... | collective-permute-start | bytes 1572872 | tf_op jit(solution)/shard_map/ppermute | solution.py:86
  24.1 8.8 %collective-permute-start.5 = (bf16[832,256]{1,0:T(8,128)(2,1)S(1)}, bf16[832,256]{1,0:T(8,128)(2,1)S(1)}, u32[]{:S(2)}, u32[]{:S(2)}) collective-permute-start(bf16[832,256]{1,0:T(8,128)(2,1)S(1)} %get-tuple-element.86.b0), channel_id=1, source_target_pairs={{0,4},{2,6},{4,0},{6,2},{1,5},{3,7},{5,1},{7,3},{8,12},{10,14},{12... | collective-permute-start | bytes 1277960 | tf_op jit(solution)/shard_map/ppermute | solution.py:63
  27.0 10.9 %collective-permute-start.4 = (bf16[832,256]{1,0:T(8,128)(2,1)S(1)}, bf16[832,256]{1,0:T(8,128)(2,1)S(1)}, u32[]{:S(2)}, u32[]{:S(2)}) collective-permute-start(bf16[832,256]{1,0:T(8,128)(2,1)S(1)} %get-tuple-element.86.b0), channel_id=1, source_target_pairs={{0,6},{2,0},{4,2},{6,4},{1,7},{3,1},{5,3},{7,5},{8,14},{10,8},{12,... | collective-permute-start | bytes 1277960 | tf_op jit(solution)/shard_map/ppermute | solution.py:63
  27.8 10.1 %collective-permute-start.3 = (bf16[832,256]{1,0:T(8,128)(2,1)S(1)}, bf16[832,256]{1,0:T(8,128)(2,1)S(1)}, u32[]{:S(2)}, u32[]{:S(2)}) collective-permute-start(bf16[832,256]{1,0:T(8,128)(2,1)S(1)} %get-tuple-element.86.b0), channel_id=1, source_target_pairs={{0,2},{2,4},{4,6},{6,0},{1,3},{3,5},{5,7},{7,1},{8,10},{10,12},{12... | collective-permute-start | bytes 1277960 | tf_op jit(solution)/shard_map/ppermute | solution.py:63
  37.9 17.5 %copy-start.3 = (bf16[256,1024]{1,0:T(8,128)(2,1)S(1)}, bf16[256,1024]{1,0:T(8,128)(2,1)}, u32[]{:S(2)}) copy-start(bf16[256,1024]{1,0:T(8,128)(2,1)} %x_ref.1) | copy-start | bytes 1572868
  37.9 17.5 %copy-start.4 = (bf16[256,1024]{1,0:T(8,128)(2,1)S(1)}, bf16[256,1024]{1,0:T(8,128)(2,1)}, u32[]{:S(2)}) copy-start(bf16[256,1024]{1,0:T(8,128)(2,1)} %cot_ref.1) | copy-start | bytes 1572868
  38.9 16.6 %copy-start.1 = (bf16[1088,256]{1,0:T(8,128)(2,1)S(1)}, bf16[1088,256]{1,0:T(8,128)(2,1)}, u32[]{:S(2)}) copy-start(bf16[1088,256]{1,0:T(8,128)(2,1)} %shard_map.266.w0.a0) | copy-start | bytes 1671172
  38.9 15.2 %collective-permute-start.12 = (bf16[1088,256]{1,0:T(8,128)(2,1)}, bf16[1088,256]{1,0:T(8,128)(2,1)}, u32[]{:S(2)}, u32[]{:S(2)}) collective-permute-start(bf16[1088,256]{1,0:T(8,128)(2,1)} %shard_map.266.w0.a0), channel_id=1, source_target_pairs={{0,16},{8,24},{16,0},{24,8},{1,17},{9,25},{17,1},{25,9},{2,18},{10... | collective-permute-start | bytes 1671176 | tf_op jit(solution)/shard_map/ppermute | solution.py:63
  41.6 13.9 %collective-permute-start.11 = (bf16[1088,256]{1,0:T(8,128)(2,1)}, bf16[1088,256]{1,0:T(8,128)(2,1)}, u32[]{:S(2)}, u32[]{:S(2)}) collective-permute-start(bf16[1088,256]{1,0:T(8,128)(2,1)} %shard_map.266.w0.a0), channel_id=1, source_target_pairs={{0,24},{8,0},{16,8},{24,16},{1,25},{9,1},{17,9},{25,17},{2,26},{10... | collective-permute-start | bytes 1671176 | tf_op jit(solution)/shard_map/ppermute | solution.py:63
  42.5 13.0 %collective-permute-start.10 = (bf16[1088,256]{1,0:T(8,128)(2,1)}, bf16[1088,256]{1,0:T(8,128)(2,1)}, u32[]{:S(2)}, u32[]{:S(2)}) collective-permute-start(bf16[1088,256]{1,0:T(8,128)(2,1)} %shard_map.266.w0.a0), channel_id=1, source_target_pairs={{0,8},{8,16},{16,24},{24,0},{1,9},{9,17},{17,25},{25,1},{2,10},{10... | collective-permute-start | bytes 1671176 | tf_op jit(solution)/shard_map/ppermute | solution.py:63
  43.1 6.6 %collective-permute-start.7 = (bf16[256,1024]{1,0:T(8,128)(2,1)}, bf16[256,1024]{1,0:T(8,128)(2,1)}, u32[]{:S(2)}, u32[]{:S(2)}) collective-permute-start(bf16[256,1024]{1,0:T(8,128)(2,1)} %collective-permute-done.6.x1), channel_id=1, source_target_pairs={{0,32},{32,0},{64,96},{96,64},{1,33},{33,1},{65,97},{97,65},{2,34}... | collective-permute-start | bytes 1572872 | tf_op jit(solution)/shard_map/ppermute | solution.py:82
  46.8 3.7 %collective-permute-start.9 = (bf16[256,1024]{1,0:T(8,128)(2,1)}, bf16[256,1024]{1,0:T(8,128)(2,1)}, u32[]{:S(2)}, u32[]{:S(2)}) collective-permute-start(bf16[256,1024]{1,0:T(8,128)(2,1)} %collective-permute-done.8.c1), channel_id=1, source_target_pairs={{0,32},{32,0},{64,96},{96,64},{1,33},{33,1},{65,97},{97,65},{2,34}... | collective-permute-start | bytes 1572872 | tf_op jit(solution)/shard_map/ppermute | solution.py:82
  48.5 6.9 %copy-start.9 = (bf16[256,1024]{1,0:T(8,128)(2,1)S(1)}, bf16[256,1024]{1,0:T(8,128)(2,1)}, u32[]{:S(2)}) copy-start(bf16[256,1024]{1,0:T(8,128)(2,1)} %copy-done.8) | copy-start | bytes 1572868
  48.5 7.0 %copy-start.11 = (bf16[256,1024]{1,0:T(8,128)(2,1)S(1)}, bf16[256,1024]{1,0:T(8,128)(2,1)}, u32[]{:S(2)}) copy-start(bf16[256,1024]{1,0:T(8,128)(2,1)} %copy-done.10) | copy-start | bytes 1572868
  50.4 29.1 %collective-permute-start.15 = (bf16[2048,256]{1,0:T(8,128)(2,1)}, bf16[2048,256]{1,0:T(8,128)(2,1)}, u32[]{:S(2)}, u32[]{:S(2)}) collective-permute-start(bf16[2048,256]{1,0:T(8,128)(2,1)} %shard_map.265.w0.b0), channel_id=1, source_target_pairs={{0,16},{8,24},{16,0},{24,8},{1,17},{9,25},{17,1},{25,9},{2,18},{10... | collective-permute-start | bytes 3145736 | tf_op jit(solution)/shard_map/ppermute | solution.py:63
  53.1 26.3 %collective-permute-start.14 = (bf16[2048,256]{1,0:T(8,128)(2,1)}, bf16[2048,256]{1,0:T(8,128)(2,1)}, u32[]{:S(2)}, u32[]{:S(2)}) collective-permute-start(bf16[2048,256]{1,0:T(8,128)(2,1)} %shard_map.265.w0.b0), channel_id=1, source_target_pairs={{0,24},{8,0},{16,8},{24,16},{1,25},{9,1},{17,9},{25,17},{2,26},{10... | collective-permute-start | bytes 3145736 | tf_op jit(solution)/shard_map/ppermute | solution.py:63
  54.0 25.5 %collective-permute-start.13 = (bf16[2048,256]{1,0:T(8,128)(2,1)}, bf16[2048,256]{1,0:T(8,128)(2,1)}, u32[]{:S(2)}, u32[]{:S(2)}) collective-permute-start(bf16[2048,256]{1,0:T(8,128)(2,1)} %shard_map.265.w0.b0), channel_id=1, source_target_pairs={{0,8},{8,16},{16,24},{24,0},{1,9},{9,17},{17,25},{25,1},{2,10},{10... | collective-permute-start | bytes 3145736 | tf_op jit(solution)/shard_map/ppermute | solution.py:63
  75.4 4.1 %copy-start = (bf16[2048,256]{1,0:T(8,128)(2,1)S(1)}, bf16[2048,256]{1,0:T(8,128)(2,1)}, u32[]{:S(2)}) copy-start(bf16[2048,256]{1,0:T(8,128)(2,1)} %shard_map.265.w0.b0) | copy-start | bytes 3145732
  75.4 23.7 %all-to-all-start.1 = ((bf16[4,4,256,256]{3,2,1,0:T(8,128)(2,1)}), bf16[4,4,256,256]{3,2,1,0:T(8,128)(2,1)S(1)}, u32[]{:S(2)}, u32[]{:S(2)}) async-start(bf16[4,4,256,256]{3,2,1,0:T(8,128)(2,1)} %get-tuple-element.102), calls=%async_computation.1 | async-start | bytes 4194304 | tf_op jit(solution)/shard_map/all_to_all | solution.py:78
  99.1 33.3 %all-to-all-start.2 = ((bf16[4,4,544,256]{3,2,1,0:T(8,128)(2,1)}), bf16[4,4,544,256]{3,2,1,0:T(8,128)(2,1)}, u32[]{:S(2)}, u32[]{:S(2)}) async-start(bf16[4,4,544,256]{3,2,1,0:T(8,128)(2,1)} %get-tuple-element.117), calls=%async_computation.2 | async-start | bytes 8912896 | tf_op jit(solution)/shard_map/all_to_all | solution.py:78
  104.0 1.1 copy-start.2
  105.1 1.4 copy-start.12
  106.5 1.0 copy-start.13
  119.9 7.3 %collective-permute-start.16 = (bf16[2,2,256,1024]{3,2,1,0:T(8,128)(2,1)}, bf16[2,2,256,1024]{3,2,1,0:T(8,128)(2,1)S(1)}, u32[]{:S(2)}, u32[]{:S(2)}) collective-permute-start(bf16[2,2,256,1024]{3,2,1,0:T(8,128)(2,1)} %get-tuple-element.114), channel_id=1, source_target_pairs={{0,32},{32,0},{64,96},{96,64},{1,33},{33,1},{65,97},{97,65},{2,34}... | collective-permute-start | bytes 6291464 | tf_op jit(solution)/shard_map/ppermute | solution.py:82
  130.2 34.5 %collective-permute-start.21 = (bf16[1,2,256,1024]{3,2,1,0:T(8,128)(2,1)}, bf16[1,2,256,1024]{3,2,1,0:T(8,128)(2,1)S(1)}, u32[]{:S(2)}, u32[]{:S(2)}) collective-permute-start(bf16[1,2,256,1024]{3,2,1,0:T(8,128)(2,1)} %get-tuple-element.115), channel_id=1, source_target_pairs={{0,64},{64,0},{32,96},{96,32},{1,65},{65,1},{33,97},{97,33},{2,66}... | collective-permute-start | bytes 3145736 | tf_op jit(solution)/shard_map/ppermute | solution.py:86
  136.3 29.4 %copy-start.7 = (s32[1,8]{1,0:T(1,128)S(1)}, s32[1,8]{1,0:T(1,128)}, u32[]{:S(2)}) copy-start(s32[1,8]{1,0:T(1,128)} %len_ref.1) | copy-start | bytes 100
  136.3 9.3 %collective-permute-start.17 = (bf16[896,256]{1,0:T(8,128)(2,1)}, bf16[896,256]{1,0:T(8,128)(2,1)S(1)}, u32[]{:S(2)}, u32[]{:S(2)}) collective-permute-start(bf16[896,256]{1,0:T(8,128)(2,1)} %get-tuple-element.119), channel_id=1, source_target_pairs={{0,2},{2,4},{4,6},{6,0},{1,3},{3,5},{5,7},{7,1},{8,10},{10,12},{12... | collective-permute-start | bytes 1376264 | tf_op jit(solution)/shard_map/ppermute | solution.py:63
  138.1 7.8 %collective-permute-start.18 = (bf16[896,256]{1,0:T(8,128)(2,1)}, bf16[896,256]{1,0:T(8,128)(2,1)S(1)}, u32[]{:S(2)}, u32[]{:S(2)}) collective-permute-start(bf16[896,256]{1,0:T(8,128)(2,1)} %get-tuple-element.120), channel_id=1, source_target_pairs={{0,6},{2,0},{4,2},{6,4},{1,7},{3,1},{5,3},{7,5},{8,14},{10,8},{12,... | collective-permute-start | bytes 1376264 | tf_op jit(solution)/shard_map/ppermute | solution.py:63
  139.4 12.4 %collective-permute-start.19 = (bf16[896,256]{1,0:T(8,128)(2,1)}, bf16[896,256]{1,0:T(8,128)(2,1)S(1)}, u32[]{:S(2)}, u32[]{:S(2)}) collective-permute-start(bf16[896,256]{1,0:T(8,128)(2,1)} %get-tuple-element.121), channel_id=1, source_target_pairs={{0,4},{2,6},{4,0},{6,2},{1,5},{3,7},{5,1},{7,3},{8,12},{10,14},{12... | collective-permute-start | bytes 1376264 | tf_op jit(solution)/shard_map/ppermute | solution.py:63
  151.7 1.0 copy-start.5
  154.0 17.2 %all-to-all-start.3 = ((bf16[8,8,2816]{2,1,0:T(8,128)(2,1)}), bf16[8,8,2816]{2,1,0:T(8,128)(2,1)S(1)}, u32[]{:S(2)}, u32[]{:S(2)}) async-start(bf16[8,8,2816]{2,1,0:T(8,128)(2,1)} %get-tuple-element.122), calls=%async_computation.3 | async-start | bytes 720896 | tf_op jit(solution)/shard_map/all_to_all | solution.py:78
  161.8 9.5 %collective-permute-start.20 = (bf16[40,1024]{1,0:T(8,128)(2,1)}, bf16[40,1024]{1,0:T(8,128)(2,1)S(1)}, u32[]{:S(2)}, u32[]{:S(2)}) collective-permute-start(bf16[40,1024]{1,0:T(8,128)(2,1)} %get-tuple-element.123), channel_id=1, source_target_pairs={{0,1},{1,0},{2,3},{3,2},{4,5},{5,4},{6,7},{7,6},{8,9},{9,8},{10,11... | collective-permute-start | bytes 245768 | tf_op jit(solution)/shard_map/ppermute | solution.py:90
  164.7 1.0 copy-start.14
  165.6 5.6 %copy-start.6 = (f32[40,1024]{1,0:T(8,128)S(1)}, f32[40,1024]{1,0:T(8,128)}, u32[]{:S(2)}) copy-start(f32[40,1024]{1,0:T(8,128)} %get-tuple-element.130.keep_ref) | copy-start | bytes 491524

commit v7 on v6

--- a/solution.py
+++ b/solution.py
@@ -386,6 +386,11 @@
     both = jnp.concatenate([high.astype(f32), low.astype(f32)] + [jnp.zeros_like(sums)] * 6, axis=0)
     out = dot_nt(both.astype(bf16), matrix)
     return out[0:1] + out[1:2]
+
+
+def in_turn(rows):
+    while rows:
+        rows = [row for row in rows if next(row, "end") != "end"]
 
 
 def attention_kernel(
@@ -467,14 +472,14 @@
 
     sums_ref[...] = jnp.zeros_like(sums_ref)
 
-    @pl.loop(0, TP)
-    def _(r):
+    def one_row(r):
         pltpu.make_async_copy(x0, x_ref.at[r], in_sem.at[r, 0]).wait()
         pltpu.make_async_copy(c0, cot_ref.at[r], in_sem.at[r, 1]).wait()
         here = pl.ds(pl.multiple_of(r * ROW, ROW), ROW)
         xhat, _ = normalize(x_ref[r].astype(f32))
         xhat_ref[here, :] = xhat.astype(bf16)
         attn_in = (xhat * vec_ref[0:1] + vec_ref[1:2]).astype(bf16)
+        yield
         qkv = dot(attn_in, wqkv_ref[...]) + qb_ref[...]
         d = me ^ ((r & 1) * 2 + r // 2)
         base = (d * 2 + info_ref[65]) * SEGS
@@ -493,8 +498,10 @@
         kept = jnp.where(rows < ends[-1], cot_ref[r].astype(f32), 0.0)
         gb = kept.astype(bf16)
         gb_ref[here, :] = gb
+        yield
         dctx = dot_nt(gb, wd_ref[...]).astype(bf16)
         chosen = ((rows - start) == cols).astype(f32).astype(bf16)
+        yield
         table = dot(chosen, rot_ref[...])
         pair = lambda n: table[:, n * 256 : n * 256 + 128] + table[:, n * 256 + 128 : n * 256 + 256]
         cosine, left, right = [jnp.concatenate([pair(n)] * 2, axis=1) for n in range(3)]
@@ -502,6 +509,7 @@
         q = (turn(qkv[:, 0:256], cosine, left, right).astype(bf16).astype(f32) * scale).astype(bf16)
         k = turn(qkv[:, 256:512], cosine, left, right).astype(bf16)
         v = qkv[:, 512:768].astype(bf16)
+        yield
         lanes = lax.broadcasted_iota(jnp.int32, (1, 256), 1) // HEAD_DIM
         ctx, dq, dk, dv = [jnp.zeros((ROW, 256), f32)] * 4
         heads = range(LOCAL_HEADS)
@@ -509,37 +517,43 @@
         qs, dcs = [q * m for m in only], [dctx * m for m in only]
         s_all = dot_nt(k, jnp.concatenate(qs, axis=0))
         dp_all = dot_nt(v, jnp.concatenate(dcs, axis=0))
+        yield
         cut = [slice(h * ROW, (h + 1) * ROW) for h in heads]
         scores = [jnp.where(allowed, s_all[:, c], -1000000000.0) for c in cut]
         dprobs = [dp_all[:, c] for c in cut]
         probs = []
         for h in heads:
+            yield
             shifted = jnp.exp(scores[h] - jnp.max(scores[h], axis=0, keepdims=True))
             probs.append(shifted * (1.0 / jnp.sum(shifted, axis=0, keepdims=True)))
+        yield
         lows = [p.astype(bf16) for p in probs]
         ds = []
         for h in heads:
+            yield
             inner = jnp.sum(dprobs[h] * probs[h], axis=0, keepdims=True)
             ds.append((probs[h] * (dprobs[h] - inner)).astype(bf16))
+        yield
         p_all = jnp.concatenate(lows, axis=0)
         ds_all = jnp.concatenate(ds, axis=0)
         ctx = dot_tn(p_all, jnp.concatenate([v * m for m in only], axis=0))
         dq = dot_tn(ds_all, jnp.concatenate([k * m for m in only], axis=0))
         dv = dot(jnp.concatenate(lows, axis=1), jnp.concatenate(dcs, axis=0))
         dk = dot(jnp.concatenate(ds, axis=1), jnp.concatenate(qs, axis=0))
+        yield
         ctx_ref[here, :] = ctx.astype(bf16)
         dqs = turn(dq * scale, cosine, -left, -right)
         dks = turn(dk, cosine, -left, -right)
         dqkv = jnp.concatenate([dqs, dks, dv], axis=1).astype(bf16)
         dqkv_ref[here, :] = dqkv
 
-        @pl.when(r == 0)
-        def _():
-            sums_ref[0:1, :] = jnp.sum(kept, axis=0, keepdims=True)
-
+        first = jnp.where(r == 0, 1.0, 0.0)
+        sums_ref[0:1, :] += first * jnp.sum(kept, axis=0, keepdims=True)
         sums_ref[1:2, 0:QC] += jnp.sum(dqkv.astype(f32), axis=0, keepdims=True)
         for n in range(4):
             store(n, r).start()
+
+    in_turn([one_row(r) for r in range(TP)])
 
     c = me % 2
     sums_ref[3:4, :] = through(sums_ref[1:2, 0:QC], wqkv_ref[...])
@@ -1268,7 +1282,8 @@
         values = image_ref[pl.ds(line, 1), :]
         if size == 24:
             values = jnp.concatenate([values, image_ref[pl.ds(line + 1, 1), :]], axis=1)
-        ref[...] = pltpu.roll(values, values.shape[1] - lane, 1)[:, :size]
+        width = values.shape[1]
+        ref[...] = pltpu.roll(values, (width - lane) % width, 1)[:, :size]
     for copy in copies:
         copy.wait()
 
@@ -1342,9 +1357,9 @@
         lengths,
         vectors,
     )
-    slots, x2, c2 = lax.optimization_barrier((slots, x2, c2))
     far_pieces = flip_far(pieces)
     first = a2a(slots, stack_groups())
+    first, x2, c2 = lax.optimization_barrier((first, x2, c2))
     block, lens = spread(index[None], first.reshape(4, 16, SLOT), pieces, far_pieces)
     along_x, along_y = index // 2 % 4, index // 8
     core = me % 2 == 1
@@ -1359,7 +1374,7 @@
     third_a = gather(merge_a(deep, second), outer)
     x3, c3 = flip_core(x1), flip_core(c1)
     xs, cots = (x0, x1, x2, x3), (c0, c1, c2, c3)
-    wide_b, xs, cots = lax.optimization_barrier((merge_b(deep, second), xs, cots))
+    wide_b, xs = lax.optimization_barrier((merge_b(deep, second), xs))
     third_b = gather(wide_b, outer)
 
     sent_a, gb, ctx, dqkv, xhat, vec, up_b, sums = attention(info, xs, cots, third_a)

time: 174 us -> 173 us (level)
    ppermute x2, waiting for transfers between devices: 6.32 us -> 1.07 us  [flip_far(): return lax.ppermute(values, 'fsdp', [(i, i ^ 1) for i in range(32)])]
    all_to_all x4, waiting for transfers between devices: 0.02 us -> 3.65 us  [a2a(): lax.all_to_all(values, AXES, 0, 0, tiled=True, axis_index_groups=groups)]
where the time goes in v7:
time: 173 us; the launch traced here: 172 us
  Pallas kernels  71.5 us (41%)
  starting transfers between devices  57.8 us (33%)
  waiting for transfers between devices  31.2 us (18%)
  local copies, waits for them, and re-layouts  10.4 us (6%)
    pallas_call x11, Pallas kernels, call(): pl.pallas_call(kernel, in_specs=[SPECS[p] for p in places], out_specs=out...  65.2 us
    all_to_all x4, starting transfers between devices, a2a(): lax.all_to_all(values, AXES, 0, 0, tiled=True, axis_index_groups=groups)  22.7 us
    ppermute x12, waiting for transfers between devices, ring(): return lax.ppermute(values, AXES, pairs)  21.7 us
    ppermute x12, starting transfers between devices, ring(): return lax.ppermute(values, AXES, pairs)  17.5 us
    ppermute x5, starting transfers between devices, flip_core(): return lax.ppermute(values, 'dp', [(0, 1), (1, 0), (2, 3), (3, 2)])  9.6 us
    unnamed x30, local copies, waits for them, and re-layouts  7.13 us
    ppermute x2, starting transfers between devices, flip_far(): return lax.ppermute(values, 'fsdp', [(i, i ^ 1) for i in range(32)])  5.77 us
    pallas_call x1, Pallas kernels, close(): pl.pallas_call(close_kernel, grid=(4,), in_specs=[SMEM_SPEC, row, row, bo...  4.63 us
  transfers between devices with their start and end apart: 26, of which 11 were waited for; matrix products, arithmetic and copies ran while one was open for 2% of the time, Pallas kernels for 40%

profile of v7, /device:TPU:1, one launch (start us, length us, event | category | flops | bytes accessed | tf_op | source)
XLA Modules:
  0.0 172.1 jit_solution(10184096730408495115)
XLA Ops:
  0.6 1.5 collective-permute-start
  2.1 0.1 collective-permute-start.1
  2.2 0.7 reshape.69.dense_in
  3.0 0.8 reshape.67.qkv_ref
  3.8 0.9 reshape.68.up_ref
  4.7 0.9 reshape.70.down_in
  5.6 1.6 shard_map.263
  7.2 5.8 %all-to-all-start = ((bf16[8,8,1920]{2,1,0:T(8,128)(2,1)}), bf16[8,8,1920]{2,1,0:T(8,128)(2,1)S(1)}, u32[]{:S(2)}, u32[]{:S(2)}) async-start(bf16[8,8,1920]{2,1,0:T(8,128)(2,1)} %get-tuple-element.75), calls=%async_computation | async-start | bytes 491520 | tf_op jit(solution)/shard_map/all_to_all | solution.py:78
  13.0 2.9 %collective-permute-start.2 = (bf16[40,1024]{1,0:T(8,128)(2,1)S(1)}, bf16[40,1024]{1,0:T(8,128)(2,1)S(1)}, u32[]{:S(2)}, u32[]{:S(2)}) collective-permute-start(bf16[40,1024]{1,0:T(8,128)(2,1)S(1)} %get-tuple-element.77.mine_ref), channel_id=1, source_target_pairs={{0,1},{1,0},{2,3},{3,2},{4,5},{5,4},{6,7},{7,6},{8,9},{9,8},{10,11... | collective-permute-start | bytes 245768 | tf_op jit(solution)/shard_map/ppermute | solution.py:90
  15.9 3.6 %all-to-all-done = bf16[8,8,1920]{2,1,0:T(8,128)(2,1)S(1)} async-done(((bf16[8,8,1920]{2,1,0:T(8,128)(2,1)}), bf16[8,8,1920]{2,1,0:T(8,128)(2,1)S(1)}, u32[]{:S(2)}, u32[]{:S(2)}) %all-to-all-start) | async-done | bytes 245792 | tf_op jit(solution)/shard_map/all_to_all | solution.py:78
  19.6 0.8 copy-done.8
  20.4 0.8 copy-done.10
  21.2 0.1 collective-permute-done.2.theirs_ref
  21.3 0.5 shard_map.264
  21.7 0.4 collective-permute-start.6
  22.1 1.2 collective-permute-start.8
  23.3 2.9 %collective-permute-start.5 = (bf16[832,256]{1,0:T(8,128)(2,1)S(1)}, bf16[832,256]{1,0:T(8,128)(2,1)S(1)}, u32[]{:S(2)}, u32[]{:S(2)}) collective-permute-start(bf16[832,256]{1,0:T(8,128)(2,1)S(1)} %get-tuple-element.82.b0), channel_id=1, source_target_pairs={{0,4},{2,6},{4,0},{6,2},{1,5},{3,7},{5,1},{7,3},{8,12},{10,14},{12... | collective-permute-start | bytes 1277960 | tf_op jit(solution)/shard_map/ppermute | solution.py:63
  26.2 0.8 collective-permute-start.4
  27.0 0.7 collective-permute-start.3
  27.7 4.4 %collective-permute-done.5.b3 = bf16[832,256]{1,0:T(8,128)(2,1)S(1)} collective-permute-done((bf16[832,256]{1,0:T(8,128)(2,1)S(1)}, bf16[832,256]{1,0:T(8,128)(2,1)S(1)}, u32[]{:S(2)}, u32[]{:S(2)}) %collective-permute-start.5) | collective-permute-done | bytes 426016 | tf_op jit(solution)/shard_map/ppermute | solution.py:63
  32.1 5.1 %collective-permute-done.4.b2 = bf16[832,256]{1,0:T(8,128)(2,1)S(1)} collective-permute-done((bf16[832,256]{1,0:T(8,128)(2,1)S(1)}, bf16[832,256]{1,0:T(8,128)(2,1)S(1)}, u32[]{:S(2)}, u32[]{:S(2)}) %collective-permute-start.4) | collective-permute-done | bytes 426016 | tf_op jit(solution)/shard_map/ppermute | solution.py:63
  37.1 0.0 copy-start.4
  37.2 0.9 shard_map.266.w0.a0
  38.0 2.7 %collective-permute-start.12 = (bf16[1088,256]{1,0:T(8,128)(2,1)}, bf16[1088,256]{1,0:T(8,128)(2,1)}, u32[]{:S(2)}, u32[]{:S(2)}) collective-permute-start(bf16[1088,256]{1,0:T(8,128)(2,1)} %shard_map.266.w0.a0), channel_id=1, source_target_pairs={{0,16},{8,24},{16,0},{24,8},{1,17},{9,25},{17,1},{25,9},{2,18},{10... | collective-permute-start | bytes 1671176 | tf_op jit(solution)/shard_map/ppermute | solution.py:63
  40.8 0.9 collective-permute-start.11
  41.7 0.6 collective-permute-start.10
  42.3 2.9 %collective-permute-start.7 = (bf16[256,1024]{1,0:T(8,128)(2,1)}, bf16[256,1024]{1,0:T(8,128)(2,1)}, u32[]{:S(2)}, u32[]{:S(2)}) collective-permute-start(bf16[256,1024]{1,0:T(8,128)(2,1)} %collective-permute-done.6.x1), channel_id=1, source_target_pairs={{0,32},{32,0},{64,96},{96,64},{1,33},{33,1},{65,97},{97,65},{2,34}... | collective-permute-start | bytes 1572872 | tf_op jit(solution)/shard_map/ppermute | solution.py:82
  45.2 0.7 collective-permute-done.8.c1
  45.9 1.8 %collective-permute-start.9 = (bf16[256,1024]{1,0:T(8,128)(2,1)}, bf16[256,1024]{1,0:T(8,128)(2,1)}, u32[]{:S(2)}, u32[]{:S(2)}) collective-permute-start(bf16[256,1024]{1,0:T(8,128)(2,1)} %collective-permute-done.8.c1), channel_id=1, source_target_pairs={{0,32},{32,0},{64,96},{96,64},{1,33},{33,1},{65,97},{97,65},{2,34}... | collective-permute-start | bytes 1572872 | tf_op jit(solution)/shard_map/ppermute | solution.py:82
  47.7 0.1 pad_add_fusion.info_ref
  47.8 1.0 shard_map.265.w0.b0
  48.8 2.7 %collective-permute-start.15 = (bf16[2048,256]{1,0:T(8,128)(2,1)}, bf16[2048,256]{1,0:T(8,128)(2,1)}, u32[]{:S(2)}, u32[]{:S(2)}) collective-permute-start(bf16[2048,256]{1,0:T(8,128)(2,1)} %shard_map.265.w0.b0), channel_id=1, source_target_pairs={{0,16},{8,24},{16,0},{24,8},{1,17},{9,25},{17,1},{25,9},{2,18},{10... | collective-permute-start | bytes 3145736 | tf_op jit(solution)/shard_map/ppermute | solution.py:63
  51.6 0.9 collective-permute-start.14
  52.5 0.6 collective-permute-start.13
  53.1 1.6 collective-permute-done.11.w2.a2
  54.7 19.2 %shard_map.267 = (bf16[4,4,256,256]{3,2,1,0:T(8,128)(2,1)}, bf16[1024,1024]{1,0:T(8,128)(2,1)}, bf16[1024,256]{1,0:T(8,128)(2,1)}, bf16[1024,768]{1,0:T(8,128)(2...) custom-call(s32[67]{0:T(128)S(1)} %pad_add_fusion.info_ref, ...), custom_call_target="tpu_custom_call" | custom-call | flops 6000000000 | bytes 20000000 | tf_op jit(solution)/shard_map/pallas_call | solution.py:124
  74.0 4.2 %all-to-all-start.1 = ((bf16[4,4,256,256]{3,2,1,0:T(8,128)(2,1)}), bf16[4,4,256,256]{3,2,1,0:T(8,128)(2,1)S(1)}, u32[]{:S(2)}, u32[]{:S(2)}) async-start(bf16[4,4,256,256]{3,2,1,0:T(8,128)(2,1)} %get-tuple-element.94), calls=%async_computation.1 | async-start | bytes 4194304 | tf_op jit(solution)/shard_map/all_to_all | solution.py:78
  78.2 19.6 %shard_map.269 = (bf16[4,4,544,256]{3,2,1,0:T(8,128)(2,1)}, bf16[1024,1024]{1,0:T(8,128)(2,1)}, bf16[1024,1024]{1,0:T(8,128)(2,1)}) custom-call(s32[67]{0:T(128)S(1)} %pad_add_fusion.info_ref, bf16[2048,256]{1,0:T(8,128)(2,1)S(1)} %copy-done, bf16[2048,256]{1,0:T(8,128)(2,1)} %collective-permute-done.13.w1.b1, ...), custom_call_target="tpu_custom_call" | custom-call | flops 8999999488 | bytes 20000000 | tf_op jit(solution)/shard_map/pallas_call | solution.py:124
  97.8 5.0 %all-to-all-start.2 = ((bf16[4,4,544,256]{3,2,1,0:T(8,128)(2,1)}), bf16[4,4,544,256]{3,2,1,0:T(8,128)(2,1)}, u32[]{:S(2)}, u32[]{:S(2)}) async-start(bf16[4,4,544,256]{3,2,1,0:T(8,128)(2,1)} %get-tuple-element.109), calls=%async_computation.2 | async-start | bytes 8912896 | tf_op jit(solution)/shard_map/all_to_all | solution.py:78
  102.8 1.0 copy-done.2
  103.8 1.4 copy-done.12
  105.2 1.0 copy-done.13
  106.3 12.4 %shard_map.270 = (bf16[2,2,256,1024]{3,2,1,0:T(8,128)(2,1)}, bf16[2,2,256,1024]{3,2,1,0:T(8,128)(2,1)}) custom-call(s32[67]{0:T(128)S(1)} %pad_add_fusion.info_ref, bf16[1024,256]{1,0:T(8,128)(2,1)S(1)} %copy-done.13, bf16[1024,1024]{1,0:T(8,128)(2,1)} %get-tuple-element.102.hidden_in, bf16[1024,768]{1,0:T(8,128)(2,1)S(1)} %copy-done.12, ...), custom_call_target="tpu_custom_call" | custom-call | flops 6499999744 | bytes 16000000 | tf_op jit(solution)/shard_map/pallas_call | solution.py:124
  118.7 3.3 %collective-permute-start.16 = (bf16[2,2,256,1024]{3,2,1,0:T(8,128)(2,1)}, bf16[2,2,256,1024]{3,2,1,0:T(8,128)(2,1)S(1)}, u32[]{:S(2)}, u32[]{:S(2)}) collective-permute-start(bf16[2,2,256,1024]{3,2,1,0:T(8,128)(2,1)} %get-tuple-element.106), channel_id=1, source_target_pairs={{0,32},{32,0},{64,96},{96,64},{1,33},{33,1},{65,97},{97,65},{2,34}... | collective-permute-start | bytes 6291464 | tf_op jit(solution)/shard_map/ppermute | solution.py:82
  121.9 4.0 %collective-permute-done.16.got_in = bf16[2,2,256,1024]{3,2,1,0:T(8,128)(2,1)S(1)} collective-permute-done((bf16[2,2,256,1024]{3,2,1,0:T(8,128)(2,1)}, bf16[2,2,256,1024]{3,2,1,0:T(8,128)(2,1)S(1)}, u32[]{:S(2)}, u32[]{:S(2)}) %collective-permute-start.16) | collective-permute-done | bytes 2097184 | tf_op jit(solution)/shard_map/ppermute | solution.py:82
  125.9 2.9 %shard_map.271 = (f32[1,2,256,1024]{3,2,1,0:T(8,128)}, bf16[1,2,256,1024]{3,2,1,0:T(8,128)(2,1)}) custom-call(bf16[2,2,256,1024]{3,2,1,0:T(8,128)(2,1)} %get-tuple-element.105.mine_in, bf16[2,2,256,1024]{3,2,1,0:T(8,128)(2,1)S(1)} %collective-permute-done.16.got_in), custom_call_target="tpu_custom_call" | custom-call | bytes 8000000 | tf_op jit(solution)/shard_map/pallas_call | solution.py:124
  128.9 0.6 collective-permute-start.21
  129.5 1.6 shard_map.268.early_in
  131.2 3.9 %shard_map.272 = (bf16[896,256]{1,0:T(8,128)(2,1)}, bf16[896,256]{1,0:T(8,128)(2,1)}, bf16[896,256]{1,0:T(8,128)(2,1)}, bf16[896,256]{1,0:T(8,128)(2,1)}) custom-call(s32[1]{0:T(128)} %bitcast.1.place_ref, bf16[4,256,256]{2,1,0:T(8,128)(2,1)} %shard_map.268.early_in, bf16[4,4,544,256]{3,2,1,0:T(8,128)(2,1)} %all-to-all-done.2.b_in), custom_call_target="tpu_custom_call" | custom-call | bytes 6000000 | tf_op jit(solution)/shard_map/pallas_call | solution.py:124
  135.1 0.0 copy-start.7
  135.1 1.8 %collective-permute-start.17 = (bf16[896,256]{1,0:T(8,128)(2,1)}, bf16[896,256]{1,0:T(8,128)(2,1)S(1)}, u32[]{:S(2)}, u32[]{:S(2)}) collective-permute-start(bf16[896,256]{1,0:T(8,128)(2,1)} %get-tuple-element.111), channel_id=1, source_target_pairs={{0,2},{2,4},{4,6},{6,0},{1,3},{3,5},{5,7},{7,1},{8,10},{10,12},{12... | collective-permute-start | bytes 1376264 | tf_op jit(solution)/shard_map/ppermute | solution.py:63
  136.8 1.3 collective-permute-start.18
  138.1 1.7 collective-permute-start.19
  139.8 4.6 %collective-permute-done.17.r1 = bf16[896,256]{1,0:T(8,128)(2,1)S(1)} collective-permute-done((bf16[896,256]{1,0:T(8,128)(2,1)}, bf16[896,256]{1,0:T(8,128)(2,1)S(1)}, u32[]{:S(2)}, u32[]{:S(2)}) %collective-permute-start.17) | collective-permute-done | bytes 458784 | tf_op jit(solution)/shard_map/ppermute | solution.py:63
  144.4 0.2 collective-permute-done.18.r2
  144.7 5.8 %collective-permute-done.19.r3 = bf16[896,256]{1,0:T(8,128)(2,1)S(1)} collective-permute-done((bf16[896,256]{1,0:T(8,128)(2,1)}, bf16[896,256]{1,0:T(8,128)(2,1)S(1)}, u32[]{:S(2)}, u32[]{:S(2)}) %collective-permute-start.19) | collective-permute-done | bytes 458784 | tf_op jit(solution)/shard_map/ppermute | solution.py:63
  150.5 1.0 copy-done.5
  151.6 1.3 shard_map.273
  152.8 7.7 %all-to-all-start.3 = ((bf16[8,8,2816]{2,1,0:T(8,128)(2,1)}), bf16[8,8,2816]{2,1,0:T(8,128)(2,1)S(1)}, u32[]{:S(2)}, u32[]{:S(2)}) async-start(bf16[8,8,2816]{2,1,0:T(8,128)(2,1)} %get-tuple-element.114), calls=%async_computation.3 | async-start | bytes 720896 | tf_op jit(solution)/shard_map/all_to_all | solution.py:78
  160.5 2.9 %collective-permute-start.20 = (bf16[40,1024]{1,0:T(8,128)(2,1)}, bf16[40,1024]{1,0:T(8,128)(2,1)S(1)}, u32[]{:S(2)}, u32[]{:S(2)}) collective-permute-start(bf16[40,1024]{1,0:T(8,128)(2,1)} %get-tuple-element.115), channel_id=1, source_target_pairs={{0,1},{1,0},{2,3},{3,2},{4,5},{5,4},{6,7},{7,6},{8,9},{9,8},{10,11... | collective-permute-start | bytes 245768 | tf_op jit(solution)/shard_map/ppermute | solution.py:90
  163.4 1.0 copy-done.14
  164.4 4.6 %shard_map.274 = (bf16[256,1024]{1,0:T(8,128)(2,1)}, f32[256,1024]{1,0:T(8,128)}) custom-call(s32[1,8]{1,0:T(1,128)S(1)} %copy-done.7, bf16[256,1024]{1,0:T(8,128)(2,1)} %x_ref.1, bf16[256,1024]{1,0:T(8,128)(2,1)} %cot_ref.1, f32[1,2,256,1024]{3,2,1,0:T(8,128)} %get-tuple-element.116.kept_ref, bf16[1,2,256,1024]{3,2,1,0:T(8,128)(2,1)} %copy-done.14, ...), custom_call_target="tpu_custom_call" | custom-call | bytes 6000000 | tf_op jit(solution)/shard_map/pallas_call | solution.py:1082
  169.0 1.0 collective-permute-done.20.got_ref
  170.0 1.9 %shard_map.275 = (f32[24576]{0:T(1024)}, f32[32768]{0:T(1024)}, f32[8192]{0:T(1024)}, f32[32768]{0:T(1024)}, f32[1,8]{1,0:T(1,128)}, /*index=5*/f32[1,8]{1,0:T(1...) custom-call(s32[1]{0:T(128)} %bitcast.15.place_ref, ...), custom_call_target="tpu_custom_call" | custom-call | bytes 2000000 | tf_op jit(solution)/shard_map/pallas_call | solution.py:124
  (36 shorter events, 0.1 us)
Async XLA Ops:
  0.6 18.9 %collective-permute-start = (bf16[256,1024]{1,0:T(8,128)(2,1)}, bf16[256,1024]{1,0:T(8,128)(2,1)S(1)}, u32[]{:S(2)}, u32[]{:S(2)}) collective-permute-start(bf16[256,1024]{1,0:T(8,128)(2,1)} %x_ref.1), channel_id=1, source_target_pairs={{0,32},{32,0},{64,96},{96,64},{1,33},{33,1},{65,97},{97,65},{2,34}... | collective-permute-start | bytes 1572872 | tf_op jit(solution)/shard_map/ppermute | solution.py:82
  2.1 18.2 %collective-permute-start.1 = (bf16[256,1024]{1,0:T(8,128)(2,1)}, bf16[256,1024]{1,0:T(8,128)(2,1)S(1)}, u32[]{:S(2)}, u32[]{:S(2)}) collective-permute-start(bf16[256,1024]{1,0:T(8,128)(2,1)} %cot_ref.1), channel_id=1, source_target_pairs={{0,32},{32,0},{64,96},{96,64},{1,33},{33,1},{65,97},{97,65},{2,34}... | collective-permute-start | bytes 1572872 | tf_op jit(solution)/shard_map/ppermute | solution.py:82
  7.2 12.4 %all-to-all-start = ((bf16[8,8,1920]{2,1,0:T(8,128)(2,1)}), bf16[8,8,1920]{2,1,0:T(8,128)(2,1)S(1)}, u32[]{:S(2)}, u32[]{:S(2)}) async-start(bf16[8,8,1920]{2,1,0:T(8,128)(2,1)} %get-tuple-element.75), calls=%async_computation | async-start | bytes 491520 | tf_op jit(solution)/shard_map/all_to_all | solution.py:78
  13.0 8.2 %collective-permute-start.2 = (bf16[40,1024]{1,0:T(8,128)(2,1)S(1)}, bf16[40,1024]{1,0:T(8,128)(2,1)S(1)}, u32[]{:S(2)}, u32[]{:S(2)}) collective-permute-start(bf16[40,1024]{1,0:T(8,128)(2,1)S(1)} %get-tuple-element.77.mine_ref), channel_id=1, source_target_pairs={{0,1},{1,0},{2,3},{3,2},{4,5},{5,4},{6,7},{7,6},{8,9},{9,8},{10,11... | collective-permute-start | bytes 245768 | tf_op jit(solution)/shard_map/ppermute | solution.py:90
  19.6 0.8 copy-start.8
  20.4 0.8 copy-start.10
  21.7 15.4 %collective-permute-start.6 = (bf16[256,1024]{1,0:T(8,128)(2,1)}, bf16[256,1024]{1,0:T(8,128)(2,1)}, u32[]{:S(2)}, u32[]{:S(2)}) collective-permute-start(bf16[256,1024]{1,0:T(8,128)(2,1)} %x_ref.1), channel_id=1, source_target_pairs={{0,64},{64,0},{32,96},{96,32},{1,65},{65,1},{33,97},{97,33},{2,66}... | collective-permute-start | bytes 1572872 | tf_op jit(solution)/shard_map/ppermute | solution.py:86
  22.1 23.8 %collective-permute-start.8 = (bf16[256,1024]{1,0:T(8,128)(2,1)}, bf16[256,1024]{1,0:T(8,128)(2,1)}, u32[]{:S(2)}, u32[]{:S(2)}) collective-permute-start(bf16[256,1024]{1,0:T(8,128)(2,1)} %cot_ref.1), channel_id=1, source_target_pairs={{0,64},{64,0},{32,96},{96,32},{1,65},{65,1},{33,97},{97,33},{2,66}... | collective-permute-start | bytes 1572872 | tf_op jit(solution)/shard_map/ppermute | solution.py:86
  23.3 8.8 %collective-permute-start.5 = (bf16[832,256]{1,0:T(8,128)(2,1)S(1)}, bf16[832,256]{1,0:T(8,128)(2,1)S(1)}, u32[]{:S(2)}, u32[]{:S(2)}) collective-permute-start(bf16[832,256]{1,0:T(8,128)(2,1)S(1)} %get-tuple-element.82.b0), channel_id=1, source_target_pairs={{0,4},{2,6},{4,0},{6,2},{1,5},{3,7},{5,1},{7,3},{8,12},{10,14},{12... | collective-permute-start | bytes 1277960 | tf_op jit(solution)/shard_map/ppermute | solution.py:63
  26.2 10.9 %collective-permute-start.4 = (bf16[832,256]{1,0:T(8,128)(2,1)S(1)}, bf16[832,256]{1,0:T(8,128)(2,1)S(1)}, u32[]{:S(2)}, u32[]{:S(2)}) collective-permute-start(bf16[832,256]{1,0:T(8,128)(2,1)S(1)} %get-tuple-element.82.b0), channel_id=1, source_target_pairs={{0,6},{2,0},{4,2},{6,4},{1,7},{3,1},{5,3},{7,5},{8,14},{10,8},{12,... | collective-permute-start | bytes 1277960 | tf_op jit(solution)/shard_map/ppermute | solution.py:63
  27.0 10.1 %collective-permute-start.3 = (bf16[832,256]{1,0:T(8,128)(2,1)S(1)}, bf16[832,256]{1,0:T(8,128)(2,1)S(1)}, u32[]{:S(2)}, u32[]{:S(2)}) collective-permute-start(bf16[832,256]{1,0:T(8,128)(2,1)S(1)} %get-tuple-element.82.b0), channel_id=1, source_target_pairs={{0,2},{2,4},{4,6},{6,0},{1,3},{3,5},{5,7},{7,1},{8,10},{10,12},{12... | collective-permute-start | bytes 1277960 | tf_op jit(solution)/shard_map/ppermute | solution.py:63
  37.1 17.5 %copy-start.3 = (bf16[256,1024]{1,0:T(8,128)(2,1)S(1)}, bf16[256,1024]{1,0:T(8,128)(2,1)}, u32[]{:S(2)}) copy-start(bf16[256,1024]{1,0:T(8,128)(2,1)} %x_ref.1) | copy-start | bytes 1572868
  37.1 17.5 %copy-start.4 = (bf16[256,1024]{1,0:T(8,128)(2,1)S(1)}, bf16[256,1024]{1,0:T(8,128)(2,1)}, u32[]{:S(2)}) copy-start(bf16[256,1024]{1,0:T(8,128)(2,1)} %cot_ref.1) | copy-start | bytes 1572868
  38.0 16.6 %copy-start.1 = (bf16[1088,256]{1,0:T(8,128)(2,1)S(1)}, bf16[1088,256]{1,0:T(8,128)(2,1)}, u32[]{:S(2)}) copy-start(bf16[1088,256]{1,0:T(8,128)(2,1)} %shard_map.266.w0.a0) | copy-start | bytes 1671172
  38.0 14.4 %collective-permute-start.12 = (bf16[1088,256]{1,0:T(8,128)(2,1)}, bf16[1088,256]{1,0:T(8,128)(2,1)}, u32[]{:S(2)}, u32[]{:S(2)}) collective-permute-start(bf16[1088,256]{1,0:T(8,128)(2,1)} %shard_map.266.w0.a0), channel_id=1, source_target_pairs={{0,16},{8,24},{16,0},{24,8},{1,17},{9,25},{17,1},{25,9},{2,18},{10... | collective-permute-start | bytes 1671176 | tf_op jit(solution)/shard_map/ppermute | solution.py:63
  40.8 13.9 %collective-permute-start.11 = (bf16[1088,256]{1,0:T(8,128)(2,1)}, bf16[1088,256]{1,0:T(8,128)(2,1)}, u32[]{:S(2)}, u32[]{:S(2)}) collective-permute-start(bf16[1088,256]{1,0:T(8,128)(2,1)} %shard_map.266.w0.a0), channel_id=1, source_target_pairs={{0,24},{8,0},{16,8},{24,16},{1,25},{9,1},{17,9},{25,17},{2,26},{10... | collective-permute-start | bytes 1671176 | tf_op jit(solution)/shard_map/ppermute | solution.py:63
  41.7 13.0 %collective-permute-start.10 = (bf16[1088,256]{1,0:T(8,128)(2,1)}, bf16[1088,256]{1,0:T(8,128)(2,1)}, u32[]{:S(2)}, u32[]{:S(2)}) collective-permute-start(bf16[1088,256]{1,0:T(8,128)(2,1)} %shard_map.266.w0.a0), channel_id=1, source_target_pairs={{0,8},{8,16},{16,24},{24,0},{1,9},{9,17},{17,25},{25,1},{2,10},{10... | collective-permute-start | bytes 1671176 | tf_op jit(solution)/shard_map/ppermute | solution.py:63
  42.3 6.6 %collective-permute-start.7 = (bf16[256,1024]{1,0:T(8,128)(2,1)}, bf16[256,1024]{1,0:T(8,128)(2,1)}, u32[]{:S(2)}, u32[]{:S(2)}) collective-permute-start(bf16[256,1024]{1,0:T(8,128)(2,1)} %collective-permute-done.6.x1), channel_id=1, source_target_pairs={{0,32},{32,0},{64,96},{96,64},{1,33},{33,1},{65,97},{97,65},{2,34}... | collective-permute-start | bytes 1572872 | tf_op jit(solution)/shard_map/ppermute | solution.py:82
  45.9 5.6 %collective-permute-start.9 = (bf16[256,1024]{1,0:T(8,128)(2,1)}, bf16[256,1024]{1,0:T(8,128)(2,1)}, u32[]{:S(2)}, u32[]{:S(2)}) collective-permute-start(bf16[256,1024]{1,0:T(8,128)(2,1)} %collective-permute-done.8.c1), channel_id=1, source_target_pairs={{0,32},{32,0},{64,96},{96,64},{1,33},{33,1},{65,97},{97,65},{2,34}... | collective-permute-start | bytes 1572872 | tf_op jit(solution)/shard_map/ppermute | solution.py:82
  47.7 6.9 %copy-start.9 = (bf16[256,1024]{1,0:T(8,128)(2,1)S(1)}, bf16[256,1024]{1,0:T(8,128)(2,1)}, u32[]{:S(2)}) copy-start(bf16[256,1024]{1,0:T(8,128)(2,1)} %copy-done.8) | copy-start | bytes 1572868
  47.7 7.0 %copy-start.11 = (bf16[256,1024]{1,0:T(8,128)(2,1)S(1)}, bf16[256,1024]{1,0:T(8,128)(2,1)}, u32[]{:S(2)}) copy-start(bf16[256,1024]{1,0:T(8,128)(2,1)} %copy-done.10) | copy-start | bytes 1572868
  48.8 29.3 %collective-permute-start.15 = (bf16[2048,256]{1,0:T(8,128)(2,1)}, bf16[2048,256]{1,0:T(8,128)(2,1)}, u32[]{:S(2)}, u32[]{:S(2)}) collective-permute-start(bf16[2048,256]{1,0:T(8,128)(2,1)} %shard_map.265.w0.b0), channel_id=1, source_target_pairs={{0,16},{8,24},{16,0},{24,8},{1,17},{9,25},{17,1},{25,9},{2,18},{10... | collective-permute-start | bytes 3145736 | tf_op jit(solution)/shard_map/ppermute | solution.py:63
  51.6 26.6 %collective-permute-start.14 = (bf16[2048,256]{1,0:T(8,128)(2,1)}, bf16[2048,256]{1,0:T(8,128)(2,1)}, u32[]{:S(2)}, u32[]{:S(2)}) collective-permute-start(bf16[2048,256]{1,0:T(8,128)(2,1)} %shard_map.265.w0.b0), channel_id=1, source_target_pairs={{0,24},{8,0},{16,8},{24,16},{1,25},{9,1},{17,9},{25,17},{2,26},{10... | collective-permute-start | bytes 3145736 | tf_op jit(solution)/shard_map/ppermute | solution.py:63
  52.5 25.7 %collective-permute-start.13 = (bf16[2048,256]{1,0:T(8,128)(2,1)}, bf16[2048,256]{1,0:T(8,128)(2,1)}, u32[]{:S(2)}, u32[]{:S(2)}) collective-permute-start(bf16[2048,256]{1,0:T(8,128)(2,1)} %shard_map.265.w0.b0), channel_id=1, source_target_pairs={{0,8},{8,16},{16,24},{24,0},{1,9},{9,17},{17,25},{25,1},{2,10},{10... | collective-permute-start | bytes 3145736 | tf_op jit(solution)/shard_map/ppermute | solution.py:63
  73.9 4.3 %copy-start = (bf16[2048,256]{1,0:T(8,128)(2,1)S(1)}, bf16[2048,256]{1,0:T(8,128)(2,1)}, u32[]{:S(2)}) copy-start(bf16[2048,256]{1,0:T(8,128)(2,1)} %shard_map.265.w0.b0) | copy-start | bytes 3145732
  74.0 23.9 %all-to-all-start.1 = ((bf16[4,4,256,256]{3,2,1,0:T(8,128)(2,1)}), bf16[4,4,256,256]{3,2,1,0:T(8,128)(2,1)S(1)}, u32[]{:S(2)}, u32[]{:S(2)}) async-start(bf16[4,4,256,256]{3,2,1,0:T(8,128)(2,1)} %get-tuple-element.94), calls=%async_computation.1 | async-start | bytes 4194304 | tf_op jit(solution)/shard_map/all_to_all | solution.py:78
  97.8 33.4 %all-to-all-start.2 = ((bf16[4,4,544,256]{3,2,1,0:T(8,128)(2,1)}), bf16[4,4,544,256]{3,2,1,0:T(8,128)(2,1)}, u32[]{:S(2)}, u32[]{:S(2)}) async-start(bf16[4,4,544,256]{3,2,1,0:T(8,128)(2,1)} %get-tuple-element.109), calls=%async_computation.2 | async-start | bytes 8912896 | tf_op jit(solution)/shard_map/all_to_all | solution.py:78
  102.8 1.1 copy-start.2
  103.8 1.4 copy-start.12
  105.2 1.0 copy-start.13
  118.7 7.3 %collective-permute-start.16 = (bf16[2,2,256,1024]{3,2,1,0:T(8,128)(2,1)}, bf16[2,2,256,1024]{3,2,1,0:T(8,128)(2,1)S(1)}, u32[]{:S(2)}, u32[]{:S(2)}) collective-permute-start(bf16[2,2,256,1024]{3,2,1,0:T(8,128)(2,1)} %get-tuple-element.106), channel_id=1, source_target_pairs={{0,32},{32,0},{64,96},{96,64},{1,33},{33,1},{65,97},{97,65},{2,34}... | collective-permute-start | bytes 6291464 | tf_op jit(solution)/shard_map/ppermute | solution.py:82
  128.9 34.5 %collective-permute-start.21 = (bf16[1,2,256,1024]{3,2,1,0:T(8,128)(2,1)}, bf16[1,2,256,1024]{3,2,1,0:T(8,128)(2,1)S(1)}, u32[]{:S(2)}, u32[]{:S(2)}) collective-permute-start(bf16[1,2,256,1024]{3,2,1,0:T(8,128)(2,1)} %get-tuple-element.107), channel_id=1, source_target_pairs={{0,64},{64,0},{32,96},{96,32},{1,65},{65,1},{33,97},{97,33},{2,66}... | collective-permute-start | bytes 3145736 | tf_op jit(solution)/shard_map/ppermute | solution.py:86
  135.1 29.3 %copy-start.7 = (s32[1,8]{1,0:T(1,128)S(1)}, s32[1,8]{1,0:T(1,128)}, u32[]{:S(2)}) copy-start(s32[1,8]{1,0:T(1,128)} %len_ref.1) | copy-start | bytes 100
  135.1 9.4 %collective-permute-start.17 = (bf16[896,256]{1,0:T(8,128)(2,1)}, bf16[896,256]{1,0:T(8,128)(2,1)S(1)}, u32[]{:S(2)}, u32[]{:S(2)}) collective-permute-start(bf16[896,256]{1,0:T(8,128)(2,1)} %get-tuple-element.111), channel_id=1, source_target_pairs={{0,2},{2,4},{4,6},{6,0},{1,3},{3,5},{5,7},{7,1},{8,10},{10,12},{12... | collective-permute-start | bytes 1376264 | tf_op jit(solution)/shard_map/ppermute | solution.py:63
  136.8 7.8 %collective-permute-start.18 = (bf16[896,256]{1,0:T(8,128)(2,1)}, bf16[896,256]{1,0:T(8,128)(2,1)S(1)}, u32[]{:S(2)}, u32[]{:S(2)}) collective-permute-start(bf16[896,256]{1,0:T(8,128)(2,1)} %get-tuple-element.112), channel_id=1, source_target_pairs={{0,6},{2,0},{4,2},{6,4},{1,7},{3,1},{5,3},{7,5},{8,14},{10,8},{12,... | collective-permute-start | bytes 1376264 | tf_op jit(solution)/shard_map/ppermute | solution.py:63
  138.1 12.4 %collective-permute-start.19 = (bf16[896,256]{1,0:T(8,128)(2,1)}, bf16[896,256]{1,0:T(8,128)(2,1)S(1)}, u32[]{:S(2)}, u32[]{:S(2)}) collective-permute-start(bf16[896,256]{1,0:T(8,128)(2,1)} %get-tuple-element.113), channel_id=1, source_target_pairs={{0,4},{2,6},{4,0},{6,2},{1,5},{3,7},{5,1},{7,3},{8,12},{10,14},{12... | collective-permute-start | bytes 1376264 | tf_op jit(solution)/shard_map/ppermute | solution.py:63
  150.5 1.0 copy-start.5
  152.8 17.2 %all-to-all-start.3 = ((bf16[8,8,2816]{2,1,0:T(8,128)(2,1)}), bf16[8,8,2816]{2,1,0:T(8,128)(2,1)S(1)}, u32[]{:S(2)}, u32[]{:S(2)}) async-start(bf16[8,8,2816]{2,1,0:T(8,128)(2,1)} %get-tuple-element.114), calls=%async_computation.3 | async-start | bytes 720896 | tf_op jit(solution)/shard_map/all_to_all | solution.py:78
  160.5 9.5 %collective-permute-start.20 = (bf16[40,1024]{1,0:T(8,128)(2,1)}, bf16[40,1024]{1,0:T(8,128)(2,1)S(1)}, u32[]{:S(2)}, u32[]{:S(2)}) collective-permute-start(bf16[40,1024]{1,0:T(8,128)(2,1)} %get-tuple-element.115), channel_id=1, source_target_pairs={{0,1},{1,0},{2,3},{3,2},{4,5},{5,4},{6,7},{7,6},{8,9},{9,8},{10,11... | collective-permute-start | bytes 245768 | tf_op jit(solution)/shard_map/ppermute | solution.py:90
  163.4 1.0 copy-start.14
  164.4 5.6 %copy-start.6 = (f32[40,1024]{1,0:T(8,128)S(1)}, f32[40,1024]{1,0:T(8,128)}, u32[]{:S(2)}) copy-start(f32[40,1024]{1,0:T(8,128)} %get-tuple-element.122.keep_ref) | copy-start | bytes 491524

commit v8 on v7

--- a/solution.py
+++ b/solution.py
@@ -1367,7 +1367,7 @@
     deep = jnp.where(core, along_y, along_x)[None]
     info = jnp.concatenate([lens[0], me1, far, near])
 
-    block, x0, c0 = lax.optimization_barrier((block, inputs, cotangent))
+    info, x0, c0 = lax.optimization_barrier((info, inputs, cotangent))
     x1, c1 = flip_chip(x0), flip_chip(c0)
     second = gather(block, inner)
     second, x1 = lax.optimization_barrier((second, x1))

time: 173 us -> 172 us (level)
  starting transfers between devices: 57.8 us -> 54.5 us
  local copies, waits for them, and re-layouts: 10.4 us -> 12.8 us
    all_to_all x4, starting transfers between devices: 22.7 us -> 19.7 us  [a2a(): lax.all_to_all(values, AXES, 0, 0, tiled=True, axis_index_groups=groups)]
    unnamed x30 -> x38, local copies, waits for them, and re-layouts: 7.13 us -> 9.47 us
  transfers between devices with their start and end apart: 26 -> 26, of which waited for: 11 -> 12; matrix products, arithmetic and copies ran while one was open for 2% -> 2% of each run, Pallas kernels for 40% -> 40%
where the time goes in v8:
time: 172 us; the launch traced here: 171 us
  Pallas kernels  70.1 us (41%)
  starting transfers between devices  54.5 us (32%)
  waiting for transfers between devices  32.4 us (19%)
  local copies, waits for them, and re-layouts  12.8 us (7%)
    pallas_call x11, Pallas kernels, call(): pl.pallas_call(kernel, in_specs=[SPECS[p] for p in places], out_specs=out...  63.8 us
    ppermute x12, waiting for transfers between devices, ring(): return lax.ppermute(values, AXES, pairs)  22.1 us
    all_to_all x4, starting transfers between devices, a2a(): lax.all_to_all(values, AXES, 0, 0, tiled=True, axis_index_groups=groups)  19.7 us
    ppermute x12, starting transfers between devices, ring(): return lax.ppermute(values, AXES, pairs)  17.5 us
    unnamed x38, local copies, waits for them, and re-layouts  9.47 us
    ppermute x5, starting transfers between devices, flip_core(): return lax.ppermute(values, 'dp', [(0, 1), (1, 0), (2, 3), (3, 2)])  9.43 us
    ppermute x2, starting transfers between devices, flip_far(): return lax.ppermute(values, 'fsdp', [(i, i ^ 1) for i in range(32)])  5.77 us
    pallas_call x1, Pallas kernels, close(): pl.pallas_call(close_kernel, grid=(4,), in_specs=[SMEM_SPEC, row, row, bo...  4.63 us
  transfers between devices with their start and end apart: 26, of which 12 were waited for; matrix products, arithmetic and copies ran while one was open for 2% of the time, Pallas kernels for 40%

profile of v8, /device:TPU:1, one launch (start us, length us, event | category | flops | bytes accessed | tf_op | source)
XLA Modules:
  0.0 170.9 jit_solution(2410567088228680430)
XLA Ops:
  0.6 1.5 collective-permute-start
  2.1 0.1 collective-permute-start.1
  2.2 0.7 reshape.69.dense_in
  3.0 0.8 reshape.67.qkv_ref
  3.8 0.9 reshape.68.up_ref
  4.7 0.9 reshape.70.down_in
  5.6 1.6 shard_map.263
  7.2 5.8 %all-to-all-start = ((bf16[8,8,1920]{2,1,0:T(8,128)(2,1)}), bf16[8,8,1920]{2,1,0:T(8,128)(2,1)S(1)}, u32[]{:S(2)}, u32[]{:S(2)}) async-start(bf16[8,8,1920]{2,1,0:T(8,128)(2,1)} %get-tuple-element.75), calls=%async_computation | async-start | bytes 491520 | tf_op jit(solution)/shard_map/all_to_all | solution.py:78
  13.0 2.9 %collective-permute-start.2 = (bf16[40,1024]{1,0:T(8,128)(2,1)S(1)}, bf16[40,1024]{1,0:T(8,128)(2,1)S(1)}, u32[]{:S(2)}, u32[]{:S(2)}) collective-permute-start(bf16[40,1024]{1,0:T(8,128)(2,1)S(1)} %get-tuple-element.77.mine_ref), channel_id=1, source_target_pairs={{0,1},{1,0},{2,3},{3,2},{4,5},{5,4},{6,7},{7,6},{8,9},{9,8},{10,11... | collective-permute-start | bytes 245768 | tf_op jit(solution)/shard_map/ppermute | solution.py:90
  15.9 3.6 %all-to-all-done = bf16[8,8,1920]{2,1,0:T(8,128)(2,1)S(1)} async-done(((bf16[8,8,1920]{2,1,0:T(8,128)(2,1)}), bf16[8,8,1920]{2,1,0:T(8,128)(2,1)S(1)}, u32[]{:S(2)}, u32[]{:S(2)}) %all-to-all-start) | async-done | bytes 245792 | tf_op jit(solution)/shard_map/all_to_all | solution.py:78
  19.6 0.8 copy-done.14
  20.4 0.9 collective-permute-done.2.theirs_ref
  21.3 0.5 shard_map.264
  21.8 0.3 collective-permute-start.6
  22.1 1.2 collective-permute-start.8
  23.3 2.9 %collective-permute-start.5 = (bf16[832,256]{1,0:T(8,128)(2,1)S(1)}, bf16[832,256]{1,0:T(8,128)(2,1)S(1)}, u32[]{:S(2)}, u32[]{:S(2)}) collective-permute-start(bf16[832,256]{1,0:T(8,128)(2,1)S(1)} %get-tuple-element.82.b0), channel_id=1, source_target_pairs={{0,4},{2,6},{4,0},{6,2},{1,5},{3,7},{5,1},{7,3},{8,12},{10,14},{12... | collective-permute-start | bytes 1277960 | tf_op jit(solution)/shard_map/ppermute | solution.py:63
  26.2 0.8 collective-permute-start.4
  27.0 0.7 collective-permute-start.3
  27.7 4.4 %collective-permute-done.5.b3 = bf16[832,256]{1,0:T(8,128)(2,1)S(1)} collective-permute-done((bf16[832,256]{1,0:T(8,128)(2,1)S(1)}, bf16[832,256]{1,0:T(8,128)(2,1)S(1)}, u32[]{:S(2)}, u32[]{:S(2)}) %collective-permute-start.5) | collective-permute-done | bytes 426016 | tf_op jit(solution)/shard_map/ppermute | solution.py:63
  32.1 5.1 %collective-permute-done.4.b2 = bf16[832,256]{1,0:T(8,128)(2,1)S(1)} collective-permute-done((bf16[832,256]{1,0:T(8,128)(2,1)S(1)}, bf16[832,256]{1,0:T(8,128)(2,1)S(1)}, u32[]{:S(2)}, u32[]{:S(2)}) %collective-permute-start.4) | collective-permute-done | bytes 426016 | tf_op jit(solution)/shard_map/ppermute | solution.py:63
  37.2 0.9 shard_map.266.w0.a0
  38.1 2.7 %collective-permute-start.12 = (bf16[1088,256]{1,0:T(8,128)(2,1)}, bf16[1088,256]{1,0:T(8,128)(2,1)S(1)}, u32[]{:S(2)}, u32[]{:S(2)}) collective-permute-start(bf16[1088,256]{1,0:T(8,128)(2,1)} %shard_map.266.w0.a0), channel_id=1, source_target_pairs={{0,16},{8,24},{16,0},{24,8},{1,17},{9,25},{17,1},{25,9},{2,18},{10... | collective-permute-start | bytes 1671176 | tf_op jit(solution)/shard_map/ppermute | solution.py:63
  40.9 0.9 collective-permute-start.11
  41.7 0.6 collective-permute-start.10
  42.3 2.9 %collective-permute-start.7 = (bf16[256,1024]{1,0:T(8,128)(2,1)}, bf16[256,1024]{1,0:T(8,128)(2,1)S(1)}, u32[]{:S(2)}, u32[]{:S(2)}) collective-permute-start(bf16[256,1024]{1,0:T(8,128)(2,1)} %collective-permute-done.6.x1), channel_id=1, source_target_pairs={{0,32},{32,0},{64,96},{96,64},{1,33},{33,1},{65,97},{97,65},{2,34}... | collective-permute-start | bytes 1572872 | tf_op jit(solution)/shard_map/ppermute | solution.py:82
  45.3 0.7 collective-permute-done.8.c1
  46.0 1.8 %collective-permute-start.9 = (bf16[256,1024]{1,0:T(8,128)(2,1)}, bf16[256,1024]{1,0:T(8,128)(2,1)S(1)}, u32[]{:S(2)}, u32[]{:S(2)}) collective-permute-start(bf16[256,1024]{1,0:T(8,128)(2,1)} %collective-permute-done.8.c1), channel_id=1, source_target_pairs={{0,32},{32,0},{64,96},{96,64},{1,33},{33,1},{65,97},{97,65},{2,34}... | collective-permute-start | bytes 1572872 | tf_op jit(solution)/shard_map/ppermute | solution.py:82
  47.7 1.0 shard_map.265.w0.b0
  48.8 2.7 %collective-permute-start.15 = (bf16[2048,256]{1,0:T(8,128)(2,1)}, bf16[2048,256]{1,0:T(8,128)(2,1)}, u32[]{:S(2)}, u32[]{:S(2)}) collective-permute-start(bf16[2048,256]{1,0:T(8,128)(2,1)} %shard_map.265.w0.b0), channel_id=1, source_target_pairs={{0,16},{8,24},{16,0},{24,8},{1,17},{9,25},{17,1},{25,9},{2,18},{10... | collective-permute-start | bytes 3145736 | tf_op jit(solution)/shard_map/ppermute | solution.py:63
  51.5 0.9 collective-permute-start.14
  52.4 0.6 collective-permute-start.13
  53.0 1.6 collective-permute-done.11.w2.a2
  54.7 18.2 %shard_map.267 = (bf16[4,4,256,256]{3,2,1,0:T(8,128)(2,1)}, bf16[1024,1024]{1,0:T(8,128)(2,1)}, bf16[1024,256]{1,0:T(8,128)(2,1)}, bf16[1024,768]{1,0:T(8,128)(2...) custom-call(s32[67]{0:T(128)S(1)} %pad_add_fusion.info_ref, ...), custom_call_target="tpu_custom_call" | custom-call | flops 6000000000 | bytes 20000000 | tf_op jit(solution)/shard_map/pallas_call | solution.py:124
  72.9 4.0 %all-to-all-start.1 = ((bf16[4,4,256,256]{3,2,1,0:T(8,128)(2,1)}), bf16[4,4,256,256]{3,2,1,0:T(8,128)(2,1)S(1)}, u32[]{:S(2)}, u32[]{:S(2)}) async-start(bf16[4,4,256,256]{3,2,1,0:T(8,128)(2,1)} %get-tuple-element.94), calls=%async_computation.1 | async-start | bytes 4194304 | tf_op jit(solution)/shard_map/all_to_all | solution.py:78
  76.9 0.3 collective-permute-done.14.w2.b2
  77.2 19.5 %shard_map.269 = (bf16[4,4,544,256]{3,2,1,0:T(8,128)(2,1)}, bf16[1024,1024]{1,0:T(8,128)(2,1)}, bf16[1024,1024]{1,0:T(8,128)(2,1)}) custom-call(s32[67]{0:T(128)S(1)} %pad_add_fusion.info_ref, bf16[2048,256]{1,0:T(8,128)(2,1)S(1)} %copy-done, bf16[2048,256]{1,0:T(8,128)(2,1)} %collective-permute-done.13.w1.b1, ...), custom_call_target="tpu_custom_call" | custom-call | flops 8999999488 | bytes 20000000 | tf_op jit(solution)/shard_map/pallas_call | solution.py:124
  96.8 4.9 %all-to-all-start.2 = ((bf16[4,4,544,256]{3,2,1,0:T(8,128)(2,1)}), bf16[4,4,544,256]{3,2,1,0:T(8,128)(2,1)}, u32[]{:S(2)}, u32[]{:S(2)}) async-start(bf16[4,4,544,256]{3,2,1,0:T(8,128)(2,1)} %get-tuple-element.109), calls=%async_computation.2 | async-start | bytes 8912896 | tf_op jit(solution)/shard_map/all_to_all | solution.py:78
  101.7 1.0 copy-done.2
  102.8 1.1 copy-done.9
  103.8 1.1 copy-done.11
  104.9 1.1 copy-done.13
  105.9 1.4 copy-done.16
  107.3 1.0 copy-done.17
  108.4 12.0 %shard_map.270 = (bf16[2,2,256,1024]{3,2,1,0:T(8,128)(2,1)}, bf16[2,2,256,1024]{3,2,1,0:T(8,128)(2,1)}) custom-call(s32[67]{0:T(128)S(1)} %pad_add_fusion.info_ref, bf16[1024,256]{1,0:T(8,128)(2,1)S(1)} %copy-done.17, bf16[1024,1024]{1,0:T(8,128)(2,1)} %get-tuple-element.102.hidden_in, bf16[1024,768]{1,0:T(8,128)(2,1)S(1)} %copy-done.16, ...), custom_call_target="tpu_custom_call" | custom-call | flops 6499999744 | bytes 16000000 | tf_op jit(solution)/shard_map/pallas_call | solution.py:124
  120.4 3.1 %collective-permute-start.16 = (bf16[2,2,256,1024]{3,2,1,0:T(8,128)(2,1)}, bf16[2,2,256,1024]{3,2,1,0:T(8,128)(2,1)S(1)}, u32[]{:S(2)}, u32[]{:S(2)}) collective-permute-start(bf16[2,2,256,1024]{3,2,1,0:T(8,128)(2,1)} %get-tuple-element.106), channel_id=1, source_target_pairs={{0,32},{32,0},{64,96},{96,64},{1,33},{33,1},{65,97},{97,65},{2,34}... | collective-permute-start | bytes 6291464 | tf_op jit(solution)/shard_map/ppermute | solution.py:82
  123.5 4.0 %collective-permute-done.16.got_in = bf16[2,2,256,1024]{3,2,1,0:T(8,128)(2,1)S(1)} collective-permute-done((bf16[2,2,256,1024]{3,2,1,0:T(8,128)(2,1)}, bf16[2,2,256,1024]{3,2,1,0:T(8,128)(2,1)S(1)}, u32[]{:S(2)}, u32[]{:S(2)}) %collective-permute-start.16) | collective-permute-done | bytes 2097184 | tf_op jit(solution)/shard_map/ppermute | solution.py:82
  127.5 2.9 %shard_map.271 = (f32[1,2,256,1024]{3,2,1,0:T(8,128)}, bf16[1,2,256,1024]{3,2,1,0:T(8,128)(2,1)}) custom-call(bf16[2,2,256,1024]{3,2,1,0:T(8,128)(2,1)} %get-tuple-element.105.mine_in, bf16[2,2,256,1024]{3,2,1,0:T(8,128)(2,1)S(1)} %collective-permute-done.16.got_in), custom_call_target="tpu_custom_call" | custom-call | bytes 8000000 | tf_op jit(solution)/shard_map/pallas_call | solution.py:124
  130.4 0.6 collective-permute-start.21
  131.0 1.6 shard_map.268.early_in
  132.7 3.9 %shard_map.272 = (bf16[896,256]{1,0:T(8,128)(2,1)}, bf16[896,256]{1,0:T(8,128)(2,1)}, bf16[896,256]{1,0:T(8,128)(2,1)}, bf16[896,256]{1,0:T(8,128)(2,1)}) custom-call(s32[1]{0:T(128)} %bitcast.1.place_ref, bf16[4,256,256]{2,1,0:T(8,128)(2,1)} %shard_map.268.early_in, bf16[4,4,544,256]{3,2,1,0:T(8,128)(2,1)} %all-to-all-done.2.b_in), custom_call_target="tpu_custom_call" | custom-call | bytes 6000000 | tf_op jit(solution)/shard_map/pallas_call | solution.py:124
  136.6 1.8 %collective-permute-start.17 = (bf16[896,256]{1,0:T(8,128)(2,1)}, bf16[896,256]{1,0:T(8,128)(2,1)S(1)}, u32[]{:S(2)}, u32[]{:S(2)}) collective-permute-start(bf16[896,256]{1,0:T(8,128)(2,1)} %get-tuple-element.111), channel_id=1, source_target_pairs={{0,2},{2,4},{4,6},{6,0},{1,3},{3,5},{5,7},{7,1},{8,10},{10,12},{12... | collective-permute-start | bytes 1376264 | tf_op jit(solution)/shard_map/ppermute | solution.py:63
  138.4 1.3 collective-permute-start.18
  139.7 1.7 collective-permute-start.19
  141.4 4.6 %collective-permute-done.17.r1 = bf16[896,256]{1,0:T(8,128)(2,1)S(1)} collective-permute-done((bf16[896,256]{1,0:T(8,128)(2,1)}, bf16[896,256]{1,0:T(8,128)(2,1)S(1)}, u32[]{:S(2)}, u32[]{:S(2)}) %collective-permute-start.17) | collective-permute-done | bytes 458784 | tf_op jit(solution)/shard_map/ppermute | solution.py:63
  146.0 0.2 collective-permute-done.18.r2
  146.2 5.8 %collective-permute-done.19.r3 = bf16[896,256]{1,0:T(8,128)(2,1)S(1)} collective-permute-done((bf16[896,256]{1,0:T(8,128)(2,1)}, bf16[896,256]{1,0:T(8,128)(2,1)S(1)}, u32[]{:S(2)}, u32[]{:S(2)}) %collective-permute-start.19) | collective-permute-done | bytes 458784 | tf_op jit(solution)/shard_map/ppermute | solution.py:63
  152.1 1.0 copy-done.5
  153.1 1.3 shard_map.273
  154.4 4.9 %all-to-all-start.3 = ((bf16[8,8,2816]{2,1,0:T(8,128)(2,1)}), bf16[8,8,2816]{2,1,0:T(8,128)(2,1)S(1)}, u32[]{:S(2)}, u32[]{:S(2)}) async-start(bf16[8,8,2816]{2,1,0:T(8,128)(2,1)} %get-tuple-element.114), calls=%async_computation.3 | async-start | bytes 720896 | tf_op jit(solution)/shard_map/all_to_all | solution.py:78
  159.3 2.9 %collective-permute-start.20 = (bf16[40,1024]{1,0:T(8,128)(2,1)}, bf16[40,1024]{1,0:T(8,128)(2,1)S(1)}, u32[]{:S(2)}, u32[]{:S(2)}) collective-permute-start(bf16[40,1024]{1,0:T(8,128)(2,1)} %get-tuple-element.115), channel_id=1, source_target_pairs={{0,1},{1,0},{2,3},{3,2},{4,5},{5,4},{6,7},{7,6},{8,9},{9,8},{10,11... | collective-permute-start | bytes 245768 | tf_op jit(solution)/shard_map/ppermute | solution.py:90
  162.2 1.0 copy-done.18
  163.1 4.6 %shard_map.274 = (bf16[256,1024]{1,0:T(8,128)(2,1)}, f32[256,1024]{1,0:T(8,128)}) custom-call(s32[1,8]{1,0:T(1,128)S(1)} %copy-done.7, bf16[256,1024]{1,0:T(8,128)(2,1)} %x_ref.1, bf16[256,1024]{1,0:T(8,128)(2,1)} %cot_ref.1, f32[1,2,256,1024]{3,2,1,0:T(8,128)} %get-tuple-element.116.kept_ref, bf16[1,2,256,1024]{3,2,1,0:T(8,128)(2,1)} %copy-done.18, ...), custom_call_target="tpu_custom_call" | custom-call | bytes 6000000 | tf_op jit(solution)/shard_map/pallas_call | solution.py:1082
  167.8 1.0 collective-permute-done.20.got_ref
  168.8 1.9 %shard_map.275 = (f32[24576]{0:T(1024)}, f32[32768]{0:T(1024)}, f32[8192]{0:T(1024)}, f32[32768]{0:T(1024)}, f32[1,8]{1,0:T(1,128)}, /*index=5*/f32[1,8]{1,0:T(1...) custom-call(s32[1]{0:T(128)} %bitcast.15.place_ref, ...), custom_call_target="tpu_custom_call" | custom-call | bytes 2000000 | tf_op jit(solution)/shard_map/pallas_call | solution.py:124
  (44 shorter events, 0.2 us)
Async XLA Ops:
  0.6 18.9 %collective-permute-start = (bf16[256,1024]{1,0:T(8,128)(2,1)}, bf16[256,1024]{1,0:T(8,128)(2,1)S(1)}, u32[]{:S(2)}, u32[]{:S(2)}) collective-permute-start(bf16[256,1024]{1,0:T(8,128)(2,1)} %x_ref.1), channel_id=1, source_target_pairs={{0,32},{32,0},{64,96},{96,64},{1,33},{33,1},{65,97},{97,65},{2,34}... | collective-permute-start | bytes 1572872 | tf_op jit(solution)/shard_map/ppermute | solution.py:82
  2.1 17.4 %collective-permute-start.1 = (bf16[256,1024]{1,0:T(8,128)(2,1)}, bf16[256,1024]{1,0:T(8,128)(2,1)S(1)}, u32[]{:S(2)}, u32[]{:S(2)}) collective-permute-start(bf16[256,1024]{1,0:T(8,128)(2,1)} %cot_ref.1), channel_id=1, source_target_pairs={{0,32},{32,0},{64,96},{96,64},{1,33},{33,1},{65,97},{97,65},{2,34}... | collective-permute-start | bytes 1572872 | tf_op jit(solution)/shard_map/ppermute | solution.py:82
  7.2 12.4 %all-to-all-start = ((bf16[8,8,1920]{2,1,0:T(8,128)(2,1)}), bf16[8,8,1920]{2,1,0:T(8,128)(2,1)S(1)}, u32[]{:S(2)}, u32[]{:S(2)}) async-start(bf16[8,8,1920]{2,1,0:T(8,128)(2,1)} %get-tuple-element.75), calls=%async_computation | async-start | bytes 491520 | tf_op jit(solution)/shard_map/all_to_all | solution.py:78
  13.0 8.2 %collective-permute-start.2 = (bf16[40,1024]{1,0:T(8,128)(2,1)S(1)}, bf16[40,1024]{1,0:T(8,128)(2,1)S(1)}, u32[]{:S(2)}, u32[]{:S(2)}) collective-permute-start(bf16[40,1024]{1,0:T(8,128)(2,1)S(1)} %get-tuple-element.77.mine_ref), channel_id=1, source_target_pairs={{0,1},{1,0},{2,3},{3,2},{4,5},{5,4},{6,7},{7,6},{8,9},{9,8},{10,11... | collective-permute-start | bytes 245768 | tf_op jit(solution)/shard_map/ppermute | solution.py:90
  19.6 0.8 copy-start.14
  21.8 15.3 %collective-permute-start.6 = (bf16[256,1024]{1,0:T(8,128)(2,1)}, bf16[256,1024]{1,0:T(8,128)(2,1)}, u32[]{:S(2)}, u32[]{:S(2)}) collective-permute-start(bf16[256,1024]{1,0:T(8,128)(2,1)} %x_ref.1), channel_id=1, source_target_pairs={{0,64},{64,0},{32,96},{96,32},{1,65},{65,1},{33,97},{97,33},{2,66}... | collective-permute-start | bytes 1572872 | tf_op jit(solution)/shard_map/ppermute | solution.py:86
  22.1 23.8 %collective-permute-start.8 = (bf16[256,1024]{1,0:T(8,128)(2,1)}, bf16[256,1024]{1,0:T(8,128)(2,1)}, u32[]{:S(2)}, u32[]{:S(2)}) collective-permute-start(bf16[256,1024]{1,0:T(8,128)(2,1)} %cot_ref.1), channel_id=1, source_target_pairs={{0,64},{64,0},{32,96},{96,32},{1,65},{65,1},{33,97},{97,33},{2,66}... | collective-permute-start | bytes 1572872 | tf_op jit(solution)/shard_map/ppermute | solution.py:86
  23.3 8.8 %collective-permute-start.5 = (bf16[832,256]{1,0:T(8,128)(2,1)S(1)}, bf16[832,256]{1,0:T(8,128)(2,1)S(1)}, u32[]{:S(2)}, u32[]{:S(2)}) collective-permute-start(bf16[832,256]{1,0:T(8,128)(2,1)S(1)} %get-tuple-element.82.b0), channel_id=1, source_target_pairs={{0,4},{2,6},{4,0},{6,2},{1,5},{3,7},{5,1},{7,3},{8,12},{10,14},{12... | collective-permute-start | bytes 1277960 | tf_op jit(solution)/shard_map/ppermute | solution.py:63
  26.2 10.9 %collective-permute-start.4 = (bf16[832,256]{1,0:T(8,128)(2,1)S(1)}, bf16[832,256]{1,0:T(8,128)(2,1)S(1)}, u32[]{:S(2)}, u32[]{:S(2)}) collective-permute-start(bf16[832,256]{1,0:T(8,128)(2,1)S(1)} %get-tuple-element.82.b0), channel_id=1, source_target_pairs={{0,6},{2,0},{4,2},{6,4},{1,7},{3,1},{5,3},{7,5},{8,14},{10,8},{12,... | collective-permute-start | bytes 1277960 | tf_op jit(solution)/shard_map/ppermute | solution.py:63
  27.0 10.1 %collective-permute-start.3 = (bf16[832,256]{1,0:T(8,128)(2,1)S(1)}, bf16[832,256]{1,0:T(8,128)(2,1)S(1)}, u32[]{:S(2)}, u32[]{:S(2)}) collective-permute-start(bf16[832,256]{1,0:T(8,128)(2,1)S(1)} %get-tuple-element.82.b0), channel_id=1, source_target_pairs={{0,2},{2,4},{4,6},{6,0},{1,3},{3,5},{5,7},{7,1},{8,10},{10,12},{12... | collective-permute-start | bytes 1277960 | tf_op jit(solution)/shard_map/ppermute | solution.py:63
  37.2 17.5 %copy-start.3 = (bf16[256,1024]{1,0:T(8,128)(2,1)S(1)}, bf16[256,1024]{1,0:T(8,128)(2,1)}, u32[]{:S(2)}) copy-start(bf16[256,1024]{1,0:T(8,128)(2,1)} %x_ref.1) | copy-start | bytes 1572868
  37.2 17.5 %copy-start.4 = (bf16[256,1024]{1,0:T(8,128)(2,1)S(1)}, bf16[256,1024]{1,0:T(8,128)(2,1)}, u32[]{:S(2)}) copy-start(bf16[256,1024]{1,0:T(8,128)(2,1)} %cot_ref.1) | copy-start | bytes 1572868
  37.2 17.5 %copy-start.15 = (bf16[256,1024]{1,0:T(8,128)(2,1)S(1)}, bf16[256,1024]{1,0:T(8,128)(2,1)}, u32[]{:S(2)}) copy-start(bf16[256,1024]{1,0:T(8,128)(2,1)} %copy-done.14) | copy-start | bytes 1572868
  38.1 16.5 %copy-start.1 = (bf16[1088,256]{1,0:T(8,128)(2,1)S(1)}, bf16[1088,256]{1,0:T(8,128)(2,1)}, u32[]{:S(2)}) copy-start(bf16[1088,256]{1,0:T(8,128)(2,1)} %shard_map.266.w0.a0) | copy-start | bytes 1671172
  38.1 14.3 %collective-permute-start.12 = (bf16[1088,256]{1,0:T(8,128)(2,1)}, bf16[1088,256]{1,0:T(8,128)(2,1)S(1)}, u32[]{:S(2)}, u32[]{:S(2)}) collective-permute-start(bf16[1088,256]{1,0:T(8,128)(2,1)} %shard_map.266.w0.a0), channel_id=1, source_target_pairs={{0,16},{8,24},{16,0},{24,8},{1,17},{9,25},{17,1},{25,9},{2,18},{10... | collective-permute-start | bytes 1671176 | tf_op jit(solution)/shard_map/ppermute | solution.py:63
  40.9 13.7 %collective-permute-start.11 = (bf16[1088,256]{1,0:T(8,128)(2,1)}, bf16[1088,256]{1,0:T(8,128)(2,1)S(1)}, u32[]{:S(2)}, u32[]{:S(2)}) collective-permute-start(bf16[1088,256]{1,0:T(8,128)(2,1)} %shard_map.266.w0.a0), channel_id=1, source_target_pairs={{0,24},{8,0},{16,8},{24,16},{1,25},{9,1},{17,9},{25,17},{2,26},{10... | collective-permute-start | bytes 1671176 | tf_op jit(solution)/shard_map/ppermute | solution.py:63
  41.7 12.9 %collective-permute-start.10 = (bf16[1088,256]{1,0:T(8,128)(2,1)}, bf16[1088,256]{1,0:T(8,128)(2,1)S(1)}, u32[]{:S(2)}, u32[]{:S(2)}) collective-permute-start(bf16[1088,256]{1,0:T(8,128)(2,1)} %shard_map.266.w0.a0), channel_id=1, source_target_pairs={{0,8},{8,16},{16,24},{24,0},{1,9},{9,17},{17,25},{25,1},{2,10},{10... | collective-permute-start | bytes 1671176 | tf_op jit(solution)/shard_map/ppermute | solution.py:63
  42.3 6.5 %collective-permute-start.7 = (bf16[256,1024]{1,0:T(8,128)(2,1)}, bf16[256,1024]{1,0:T(8,128)(2,1)S(1)}, u32[]{:S(2)}, u32[]{:S(2)}) collective-permute-start(bf16[256,1024]{1,0:T(8,128)(2,1)} %collective-permute-done.6.x1), channel_id=1, source_target_pairs={{0,32},{32,0},{64,96},{96,64},{1,33},{33,1},{65,97},{97,65},{2,34}... | collective-permute-start | bytes 1572872 | tf_op jit(solution)/shard_map/ppermute | solution.py:82
  46.0 5.6 %collective-permute-start.9 = (bf16[256,1024]{1,0:T(8,128)(2,1)}, bf16[256,1024]{1,0:T(8,128)(2,1)S(1)}, u32[]{:S(2)}, u32[]{:S(2)}) collective-permute-start(bf16[256,1024]{1,0:T(8,128)(2,1)} %collective-permute-done.8.c1), channel_id=1, source_target_pairs={{0,32},{32,0},{64,96},{96,64},{1,33},{33,1},{65,97},{97,65},{2,34}... | collective-permute-start | bytes 1572872 | tf_op jit(solution)/shard_map/ppermute | solution.py:82
  48.8 28.1 %collective-permute-start.15 = (bf16[2048,256]{1,0:T(8,128)(2,1)}, bf16[2048,256]{1,0:T(8,128)(2,1)}, u32[]{:S(2)}, u32[]{:S(2)}) collective-permute-start(bf16[2048,256]{1,0:T(8,128)(2,1)} %shard_map.265.w0.b0), channel_id=1, source_target_pairs={{0,16},{8,24},{16,0},{24,8},{1,17},{9,25},{17,1},{25,9},{2,18},{10... | collective-permute-start | bytes 3145736 | tf_op jit(solution)/shard_map/ppermute | solution.py:63
  51.5 25.7 %collective-permute-start.14 = (bf16[2048,256]{1,0:T(8,128)(2,1)}, bf16[2048,256]{1,0:T(8,128)(2,1)}, u32[]{:S(2)}, u32[]{:S(2)}) collective-permute-start(bf16[2048,256]{1,0:T(8,128)(2,1)} %shard_map.265.w0.b0), channel_id=1, source_target_pairs={{0,24},{8,0},{16,8},{24,16},{1,25},{9,1},{17,9},{25,17},{2,26},{10... | collective-permute-start | bytes 3145736 | tf_op jit(solution)/shard_map/ppermute | solution.py:63
  52.4 20.4 %copy-start.8 = (bf16[1088,256]{1,0:T(8,128)(2,1)}, bf16[1088,256]{1,0:T(8,128)(2,1)S(1)}, u32[]{:S(2)}) copy-start(bf16[1088,256]{1,0:T(8,128)(2,1)S(1)} %collective-permute-done.12.w3.a3) | copy-start | bytes 1671172
  52.4 24.8 %collective-permute-start.13 = (bf16[2048,256]{1,0:T(8,128)(2,1)}, bf16[2048,256]{1,0:T(8,128)(2,1)}, u32[]{:S(2)}, u32[]{:S(2)}) collective-permute-start(bf16[2048,256]{1,0:T(8,128)(2,1)} %shard_map.265.w0.b0), channel_id=1, source_target_pairs={{0,8},{8,16},{16,24},{24,0},{1,9},{9,17},{17,25},{25,1},{2,10},{10... | collective-permute-start | bytes 3145736 | tf_op jit(solution)/shard_map/ppermute | solution.py:63
  54.6 18.3 %copy-start.10 = (bf16[1088,256]{1,0:T(8,128)(2,1)}, bf16[1088,256]{1,0:T(8,128)(2,1)S(1)}, u32[]{:S(2)}) copy-start(bf16[1088,256]{1,0:T(8,128)(2,1)S(1)} %collective-permute-done.11.w2.a2) | copy-start | bytes 1671172
  54.6 18.2 %copy-start.12 = (bf16[1088,256]{1,0:T(8,128)(2,1)}, bf16[1088,256]{1,0:T(8,128)(2,1)S(1)}, u32[]{:S(2)}) copy-start(bf16[1088,256]{1,0:T(8,128)(2,1)S(1)} %collective-permute-done.10.w1.a1) | copy-start | bytes 1671172
  72.9 4.4 %copy-start = (bf16[2048,256]{1,0:T(8,128)(2,1)S(1)}, bf16[2048,256]{1,0:T(8,128)(2,1)}, u32[]{:S(2)}) copy-start(bf16[2048,256]{1,0:T(8,128)(2,1)} %shard_map.265.w0.b0) | copy-start | bytes 3145732
  72.9 23.9 %all-to-all-start.1 = ((bf16[4,4,256,256]{3,2,1,0:T(8,128)(2,1)}), bf16[4,4,256,256]{3,2,1,0:T(8,128)(2,1)S(1)}, u32[]{:S(2)}, u32[]{:S(2)}) async-start(bf16[4,4,256,256]{3,2,1,0:T(8,128)(2,1)} %get-tuple-element.94), calls=%async_computation.1 | async-start | bytes 4194304 | tf_op jit(solution)/shard_map/all_to_all | solution.py:78
  96.8 35.9 %all-to-all-start.2 = ((bf16[4,4,544,256]{3,2,1,0:T(8,128)(2,1)}), bf16[4,4,544,256]{3,2,1,0:T(8,128)(2,1)}, u32[]{:S(2)}, u32[]{:S(2)}) async-start(bf16[4,4,544,256]{3,2,1,0:T(8,128)(2,1)} %get-tuple-element.109), calls=%async_computation.2 | async-start | bytes 8912896 | tf_op jit(solution)/shard_map/all_to_all | solution.py:78
  101.7 1.1 copy-start.2
  102.8 1.1 copy-start.9
  103.8 1.1 copy-start.11
  104.9 1.1 copy-start.13
  105.9 1.4 copy-start.16
  107.3 1.0 copy-start.17
  120.4 7.1 %collective-permute-start.16 = (bf16[2,2,256,1024]{3,2,1,0:T(8,128)(2,1)}, bf16[2,2,256,1024]{3,2,1,0:T(8,128)(2,1)S(1)}, u32[]{:S(2)}, u32[]{:S(2)}) collective-permute-start(bf16[2,2,256,1024]{3,2,1,0:T(8,128)(2,1)} %get-tuple-element.106), channel_id=1, source_target_pairs={{0,32},{32,0},{64,96},{96,64},{1,33},{33,1},{65,97},{97,65},{2,34}... | collective-permute-start | bytes 6291464 | tf_op jit(solution)/shard_map/ppermute | solution.py:82
  130.4 31.8 %collective-permute-start.21 = (bf16[1,2,256,1024]{3,2,1,0:T(8,128)(2,1)}, bf16[1,2,256,1024]{3,2,1,0:T(8,128)(2,1)S(1)}, u32[]{:S(2)}, u32[]{:S(2)}) collective-permute-start(bf16[1,2,256,1024]{3,2,1,0:T(8,128)(2,1)} %get-tuple-element.107), channel_id=1, source_target_pairs={{0,64},{64,0},{32,96},{96,32},{1,65},{65,1},{33,97},{97,33},{2,66}... | collective-permute-start | bytes 3145736 | tf_op jit(solution)/shard_map/ppermute | solution.py:86
  136.6 26.5 %copy-start.7 = (s32[1,8]{1,0:T(1,128)S(1)}, s32[1,8]{1,0:T(1,128)}, u32[]{:S(2)}) copy-start(s32[1,8]{1,0:T(1,128)} %len_ref.1) | copy-start | bytes 100
  136.6 9.4 %collective-permute-start.17 = (bf16[896,256]{1,0:T(8,128)(2,1)}, bf16[896,256]{1,0:T(8,128)(2,1)S(1)}, u32[]{:S(2)}, u32[]{:S(2)}) collective-permute-start(bf16[896,256]{1,0:T(8,128)(2,1)} %get-tuple-element.111), channel_id=1, source_target_pairs={{0,2},{2,4},{4,6},{6,0},{1,3},{3,5},{5,7},{7,1},{8,10},{10,12},{12... | collective-permute-start | bytes 1376264 | tf_op jit(solution)/shard_map/ppermute | solution.py:63
  138.4 7.8 %collective-permute-start.18 = (bf16[896,256]{1,0:T(8,128)(2,1)}, bf16[896,256]{1,0:T(8,128)(2,1)S(1)}, u32[]{:S(2)}, u32[]{:S(2)}) collective-permute-start(bf16[896,256]{1,0:T(8,128)(2,1)} %get-tuple-element.112), channel_id=1, source_target_pairs={{0,6},{2,0},{4,2},{6,4},{1,7},{3,1},{5,3},{7,5},{8,14},{10,8},{12,... | collective-permute-start | bytes 1376264 | tf_op jit(solution)/shard_map/ppermute | solution.py:63
  139.7 12.4 %collective-permute-start.19 = (bf16[896,256]{1,0:T(8,128)(2,1)}, bf16[896,256]{1,0:T(8,128)(2,1)S(1)}, u32[]{:S(2)}, u32[]{:S(2)}) collective-permute-start(bf16[896,256]{1,0:T(8,128)(2,1)} %get-tuple-element.113), channel_id=1, source_target_pairs={{0,4},{2,6},{4,0},{6,2},{1,5},{3,7},{5,1},{7,3},{8,12},{10,14},{12... | collective-permute-start | bytes 1376264 | tf_op jit(solution)/shard_map/ppermute | solution.py:63
  152.1 1.0 copy-start.5
  154.4 14.4 %all-to-all-start.3 = ((bf16[8,8,2816]{2,1,0:T(8,128)(2,1)}), bf16[8,8,2816]{2,1,0:T(8,128)(2,1)S(1)}, u32[]{:S(2)}, u32[]{:S(2)}) async-start(bf16[8,8,2816]{2,1,0:T(8,128)(2,1)} %get-tuple-element.114), calls=%async_computation.3 | async-start | bytes 720896 | tf_op jit(solution)/shard_map/all_to_all | solution.py:78
  159.3 9.5 %collective-permute-start.20 = (bf16[40,1024]{1,0:T(8,128)(2,1)}, bf16[40,1024]{1,0:T(8,128)(2,1)S(1)}, u32[]{:S(2)}, u32[]{:S(2)}) collective-permute-start(bf16[40,1024]{1,0:T(8,128)(2,1)} %get-tuple-element.115), channel_id=1, source_target_pairs={{0,1},{1,0},{2,3},{3,2},{4,5},{5,4},{6,7},{7,6},{8,9},{9,8},{10,11... | collective-permute-start | bytes 245768 | tf_op jit(solution)/shard_map/ppermute | solution.py:90
  162.2 1.0 copy-start.18
  163.1 5.6 %copy-start.6 = (f32[40,1024]{1,0:T(8,128)S(1)}, f32[40,1024]{1,0:T(8,128)}, u32[]{:S(2)}) copy-start(f32[40,1024]{1,0:T(8,128)} %get-tuple-element.122.keep_ref) | copy-start | bytes 491524
